TPU v7x, 32 devices: a whole 2x2x4 slice. The times are simulated.
32 devices in a mesh: grp: 4 (over y, x), blk: 8 (over z, core).
Axes of the slice: x: 2, y: 2, z: 4, core: 2. Of those that a mesh axis runs over, the one named last changes fastest.
Arguments:
- queries: bfloat16 [4096, 4096], P(('grp', 'blk')), may hold values from -4 to 4
- passages: bfloat16 [4096, 4096], P(('grp', 'blk')), may hold values from -1 to 1
- hard_index: int32 [4096, 3], P(('grp', 'blk')), may hold values from 0 to 4095, as said below
- weights: float32 [4096], P(('grp', 'blk')), may hold values from 0.5 to 2
Outputs:
- loss_rows: float32 [4096], P(('grp', 'blk'))
- grad_queries: bfloat16 [4096, 4096], P(('grp', 'blk'))
- grad_passages: bfloat16 [4096, 4096], P(('grp', 'blk'))
Inputs may be any that keep to these rules, and one draw needn't show every extreme that they name: `hard_index`: the three entries of query i name passages of the block at the same index of blk as query i in three different groups, none its own; among the queries of one device at most 128 entries name one group, and in every device exactly 128 entries name some group.
All inputs are finite; a program needn't handle non-finite values.
Results may differ from a plain program's by a relative error of at most 0.0065.
Values may be sent and summed in bfloat16 or wider, within the bound.
No kernel may reach another device: no remote copies, remote signals or barrier semaphores. Data moves between devices by JAX's collectives and lax.ppermute only.
A program may use at most 64 MiB of HBM per device.

v0:
```python
import functools
import math

import jax
import jax.numpy as jnp
from jax import lax
from jax.experimental import pallas as pl
from jax.experimental.pallas import tpu as pltpu
from jax.sharding import PartitionSpec as P

INV_TEMP = 50.0
BF16 = jnp.bfloat16
F32 = jnp.float32
CHUNK = 512
TAIL = 16
LONG, SOME = 5 * 10**10, 16 * 10**9
VMEM = pl.BlockSpec(memory_space=pltpu.VMEM)
HBM = pl.BlockSpec(memory_space=pltpu.HBM)
TOKEN = jax.ShapeDtypeStruct((8, 128), F32)


def dot(left, right, dims):
    return lax.dot_general(left, right, (dims, ((), ())), preferred_element_type=F32)


def size_of(arrays):
    return sum(math.prod(a.shape) * jnp.dtype(a.dtype).itemsize for a in arrays)


def local_call(body, out_shape, *args, flops=0, in_specs=None, out_specs=None, scratch=(), limit=20):
    return pl.pallas_call(
        body,
        out_shape=out_shape,
        in_specs=in_specs or [VMEM] * len(args),
        out_specs=out_specs or [VMEM] * len(out_shape),
        scratch_shapes=list(scratch),
        cost_estimate=pl.CostEstimate(
            flops=flops, bytes_accessed=size_of(args) + size_of(out_shape), transcendentals=0
        ),
        compiler_params=pltpu.CompilerParams(vmem_limit_bytes=limit * 2**20),
    )(*args)


def signal(token):
    token[...] = jnp.zeros(token.shape, token.dtype)


def split_index(index, rows, group_rows):
    if group_rows & (group_rows - 1) or rows & (rows - 1):
        return index // group_rows, index % rows
    return index >> (group_rows.bit_length() - 1), index & (rows - 1)


def load_body(groups, group_rows, q_hbm, p_hbm, index_hbm, *refs):
    pieces, (token, index_ref, sems) = refs[:groups], refs[groups:]
    rows = q_hbm.shape[0]
    cols = pieces[0].shape[1]
    g = lax.axis_index("grp")
    index_copy = pltpu.make_async_copy(index_hbm, index_ref, sems.at[2 * groups])
    index_copy.start()
    copies = []
    for r, piece in enumerate(pieces):
        at = pl.ds(pl.multiple_of((g ^ r) * cols, 128), cols)
        for n, source in enumerate((q_hbm, p_hbm)):
            target = piece.at[pl.ds(n * rows, rows)]
            copies.append(pltpu.make_async_copy(source.at[:, at], target, sems.at[2 * r + n]))
            copies[-1].start()
    signal(token)
    index_copy.wait()
    index = jnp.concatenate([index_ref[...], jnp.zeros((TAIL - 3, rows), jnp.int32)], axis=0)
    named_group, named_row = split_index(index, rows, group_rows)
    named_group = named_group.astype(F32).astype(BF16)
    named_row = named_row.astype(F32).astype(BF16)
    for piece in pieces:
        piece[2 * rows :, :rows] = named_group
        piece[2 * rows :, rows : 2 * rows] = named_row
        if cols > 2 * rows:
            piece[2 * rows :, 2 * rows :] = jnp.zeros((TAIL, cols - 2 * rows), BF16)
    for copy in copies:
        copy.wait()


def places_of(piece_ref, rows):
    tail = piece_ref[2 * rows :, : 2 * rows].astype(F32).astype(jnp.int32)
    g = lax.axis_index("grp")
    return [(tail[k : k + 1, :rows] ^ g) * rows + tail[k : k + 1, rows:] for k in range(3)]


def hard_scores_body(groups, *refs):
    pieces, outs = refs[:groups], refs[groups + 1 :]
    rows = outs[0].shape[1]
    ids = lax.broadcasted_iota(jnp.int32, (groups * rows, rows), 0)
    p_all = jnp.concatenate([piece[rows : 2 * rows] for piece in pieces], axis=0)
    for r in range(groups):
        places = places_of(pieces[r], rows)
        dots = dot(p_all, pieces[r][:rows], ((1,), (1,)))
        for k in range(3):
            hit = jnp.where(ids == places[k], dots, 0.0)
            outs[r][k : k + 1] = jnp.sum(hit, axis=0, keepdims=True)


def hard_grads_body(groups, *refs):
    pieces, coefs, outs = refs[:groups], refs[groups : 2 * groups], refs[2 * groups + 1 : 3 * groups + 1]
    token, matrix, matrix_t = refs[3 * groups + 1 :]
    rows = coefs[0].shape[1]
    cols = outs[0].shape[1]
    signal(token)
    ids = lax.broadcasted_iota(jnp.int32, (groups * rows, rows), 0)
    for r in range(groups):
        places = places_of(pieces[r], rows)
        total = jnp.zeros(ids.shape, F32)
        for k in range(3):
            total += jnp.where(ids == places[k], coefs[r][k : k + 1], 0.0)
        mine = slice(r * rows, (r + 1) * rows)
        matrix[:, mine] = total.astype(BF16)
        matrix_t[mine] = total.T.astype(BF16)
    step = min(cols, 256)
    for c in range(0, cols, step):
        at = slice(c, c + step)
        q_all = jnp.concatenate([piece[:rows, at] for piece in pieces], axis=0)
        p_all = jnp.concatenate([piece[rows : 2 * rows, at] for piece in pieces], axis=0)
        grad_q = dot(matrix_t[...], p_all, ((1,), (0,))).astype(BF16)
        grad_p = dot(matrix[...], q_all, ((1,), (0,))).astype(BF16)
        for r in range(groups):
            mine = slice(r * rows, (r + 1) * rows)
            outs[r][:rows, at] = grad_q[mine]
            outs[r][rows:, at] = grad_p[mine]


def pass_body(source, token, out):
    out[...] = source[...]


def choose_body(n1_ref, e3_ref, q_ref, out):
    width = q_ref.shape[1]
    odd = lax.axis_index("blk") % 2 == 1
    out[:, width:] = q_ref[...]

    @pl.when(odd)
    def _():
        out[:, :width] = n1_ref[...]

    @pl.when(jnp.logical_not(odd))
    def _():
        out[:, :width] = e3_ref[...]


def scores_body(q_ref, *refs):
    half = len(refs) // 2
    for block, out in zip(refs[:half], refs[half:]):
        out[...] = dot(block[...], q_ref[...], ((1,), (1,)))


def last_score_body(q_ref, pair_ref, out):
    out[...] = dot(pair_ref[:, : q_ref.shape[1]], q_ref[...], ((1,), (1,)))


def weigh_body(
    groups, q_ref, s0_ref, s1_ref, s2_ref, s3_ref, last_ref, w_ref, *refs
):
    parts, (loss_ref, coef_ref, hard_out, swap_ref, term3_ref) = refs[:groups], refs[groups:]
    rows, width = q_ref.shape
    w = w_ref[...]
    s3 = INV_TEMP * (s3_ref[...] + dot(last_ref[...], q_ref[...], ((1,), (1,))))
    scores = [INV_TEMP * s0_ref[...], INV_TEMP * s1_ref[...], INV_TEMP * s2_ref[...], s3]
    hard = parts[0][...]
    for other in parts[1:]:
        hard = hard + other[...]
    hard = INV_TEMP * hard
    largest = jnp.max(hard, axis=0, keepdims=True)
    for block in scores:
        largest = jnp.maximum(largest, jnp.max(block, axis=0, keepdims=True))
    summed = jnp.sum(jnp.exp(hard - largest), axis=0, keepdims=True)
    for block in scores:
        summed = summed + jnp.sum(jnp.exp(block - largest), axis=0, keepdims=True)
    log_total = largest + jnp.log(summed)
    for s, block in enumerate(scores):
        coef = (w * jnp.exp(block - log_total)).astype(BF16)
        coef_ref[:, s * rows : (s + 1) * rows] = coef
        if s in (1, 2):
            swap_ref[:, (s - 1) * rows : s * rows] = coef
    coef3 = coef_ref[:, 3 * rows :]
    for c in range(0, width, CHUNK):
        at = slice(c, c + CHUNK)
        term3_ref[:, at] = dot(coef3, q_ref[:, at], ((1,), (0,))).astype(BF16)
    hard_out[...] = (w * jnp.exp(hard - log_total)).astype(BF16).astype(F32)
    eye = lax.broadcasted_iota(jnp.int32, (rows, rows), 0) == lax.broadcasted_iota(
        jnp.int32, (rows, rows), 1
    )
    loss_ref[...] = log_total - jnp.sum(jnp.where(eye, scores[0], 0.0), axis=0, keepdims=True)


def sums_body(q_ref, pair_ref, coef_ref, swap_ref, sent3, partial1, token):
    signal(token)
    rows, width = q_ref.shape
    odd = lax.axis_index("blk") % 2 == 1
    mine = jnp.where(odd, coef_ref[:, rows : 2 * rows], coef_ref[:, 3 * rows :])
    coef = jnp.concatenate([mine, swap_ref[:, rows:]], axis=1)
    for c in range(0, width, CHUNK):
        at = slice(c, c + CHUNK)
        held = jnp.concatenate([q_ref[:, at], pair_ref[:, width + c : width + c + CHUNK]], axis=0)
        total = dot(coef, held, ((1,), (0,)))
        sent3[:, at] = total.astype(BF16)
        partial1[:, at] = total


def relay_body(partial1, got3_ref, out, done):
    signal(done)
    out[...] = (partial1[...] + got3_ref[...].astype(F32)).astype(BF16)


def base_body(
    q_ref, pair_ref, p_ref, n1_ref, e3_ref, o3_ref, coef_ref, swap_ref, w_ref, own3_ref,
    token, pulled, base, coef_t,
):
    rows, width = q_ref.shape
    w = jnp.broadcast_to(w_ref[...], (rows, rows)).T[:, :1]
    odd = lax.axis_index("blk") % 2 == 1
    blocks = (p_ref, n1_ref, pair_ref, e3_ref, o3_ref)
    for s in range(5):
        k = min(s, 3) * rows
        coef_t[:, s * rows : (s + 1) * rows] = coef_ref[:, k : k + rows].astype(F32).T.astype(BF16)
    coef = [coef_ref[:, :rows], jnp.where(odd, swap_ref[:, :rows], jnp.zeros((rows, rows), BF16))]
    coef = jnp.concatenate(coef, axis=1)
    for c in range(0, width, CHUNK):
        at = slice(c, c + CHUNK)
        held = jnp.concatenate([block[:, at] for block in blocks], axis=0)
        pulled[:, at] = dot(coef_t[...], held, ((1,), (0,))) - w * p_ref[:, at].astype(F32)
        held = jnp.concatenate([q_ref[:, at], pair_ref[:, width + c : width + c + CHUNK]], axis=0)
        own = dot(coef, held, ((1,), (0,))) + own3_ref[:, at].astype(F32)
        base[:, at] = own - w * q_ref[:, at].astype(F32)


def finish_body(groups, pulled, base, own1, *refs):
    backs = refs[:groups]
    q_out, p_out, q_held, p_held, sems = refs[groups:]
    rows, cols = pulled.shape[0], backs[0].shape[1]
    g = lax.axis_index("grp")
    copies = []
    for r, back in enumerate(backs):
        at = pl.ds(pl.multiple_of((g ^ r) * cols, 128), cols)
        q_held[:, at] = (INV_TEMP * (pulled[:, at] + back[:rows].astype(F32))).astype(BF16)
        copies.append(pltpu.make_async_copy(q_held.at[:, at], q_out.at[:, at], sems.at[2 * r]))
        copies[-1].start()
        total = base[:, at] + back[rows:].astype(F32) + own1[:, at].astype(F32)
        p_held[:, at] = (INV_TEMP * total).astype(BF16)
        copies.append(pltpu.make_async_copy(p_held.at[:, at], p_out.at[:, at], sems.at[2 * r + 1]))
        copies[-1].start()
    for copy in copies:
        copy.wait()


def per_device(queries, passages, hard_index, weights):
    rows, width = queries.shape
    groups = lax.axis_size("grp")
    loop = lax.axis_size("blk")
    cols = width // groups

    def shift(array, by, which=(0, 1)):
        pairs = [(i, (i + by) % loop) for i in range(loop) if i % 2 in which]
        return lax.ppermute(array, "blk", pairs)

    def swap(array):
        return lax.ppermute(array, "blk", [(i, i ^ 1) for i in range(loop)])

    def over_groups(array, r):
        return lax.ppermute(array, "grp", [(i, i ^ r) for i in range(groups)])

    def exchange(arrays):
        out = list(arrays)
        for r in reversed(range(1, groups)):
            out[r] = over_groups(arrays[r], r)
        return out

    def like(*shape, dtype=BF16):
        return jax.ShapeDtypeStruct(shape, dtype)

    block, block32 = like(rows, width), like(rows, width, dtype=F32)
    square, triple = like(rows, rows, dtype=F32), like(3, rows, dtype=F32)
    piece, back = like(2 * rows + TAIL, cols), like(2 * rows, cols)

    next1 = shift(passages, -1)

    *pieces, token = local_call(
        functools.partial(load_body, groups, loop * rows), [piece] * groups + [TOKEN],
        queries, passages, hard_index.T, in_specs=[HBM, HBM, HBM],
        scratch=[pltpu.VMEM((3, rows), jnp.int32), pltpu.SemaphoreType.DMA((2 * groups + 1,))],
        limit=51,
    )
    pieces = exchange(pieces)

    next3_even = shift(passages, -3, (1,))
    (next1,) = local_call(pass_body, [block], next1, token, flops=LONG)
    next3_odd = shift(next1, -2, (1,))
    pair = swap(
        local_call(choose_body, [like(rows, 2 * width)], next1, next3_even, queries, flops=LONG)[0]
    )

    s0, s1, s3 = local_call(scores_body, [square] * 3, queries, passages, next1, next3_even)
    parts = local_call(
        functools.partial(hard_scores_body, groups), [triple] * groups, *pieces, s0, flops=LONG
    )
    (s2,) = local_call(last_score_body, [square], queries, pair)
    parts = exchange(parts)
    loss_rows, coef, hard_coef, to_core, term3 = local_call(
        functools.partial(weigh_body, groups),
        [like(1, rows, dtype=F32), like(rows, 4 * rows), triple, like(rows, 2 * rows), block],
        queries, s0, s1, s2, s3, next3_odd, weights[None, :], *parts,
    )

    got3 = shift(term3, 2, (1,))
    from_core = swap(to_core)
    sent3, partial1, token = local_call(
        sums_body, [block, block32, TOKEN], queries, pair, coef, from_core
    )
    own3 = shift(sent3, 3, (0,))

    hard_coefs = exchange([hard_coef] * groups)
    square_all = pltpu.VMEM((groups * rows, groups * rows), BF16)
    *backs, token = local_call(
        functools.partial(hard_grads_body, groups), [back] * groups + [TOKEN],
        *pieces, *hard_coefs, token, scratch=[square_all, square_all],
    )
    backs = exchange(backs)

    sent1, token = local_call(relay_body, [block, TOKEN], partial1, got3, flops=SOME)
    own1 = shift(sent1, 1, (1,))

    pulled, base = local_call(
        base_body, [block32, block32],
        queries, pair, passages, next1, next3_even, next3_odd, coef, from_core,
        weights[None, :], own3, token, flops=LONG, scratch=[pltpu.VMEM((rows, 5 * rows), BF16)],
    )
    grad_queries, grad_passages = local_call(
        functools.partial(finish_body, groups), [block, block], pulled, base, own1, *backs,
        out_specs=[HBM, HBM],
        scratch=[
            pltpu.VMEM((rows, width), BF16),
            pltpu.VMEM((rows, width), BF16),
            pltpu.SemaphoreType.DMA((2 * groups,)),
        ],
    )
    return loss_rows.reshape(rows), grad_queries, grad_passages


def solution(mesh):
    rows = P(("grp", "blk"))
    matrix = P(("grp", "blk"), None)
    return jax.shard_map(
        per_device,
        mesh=mesh,
        in_specs=(matrix, matrix, matrix, rows),
        out_specs=(rows, matrix, matrix),
        check_vma=False,
    )
```

profile of v0, /device:TPU:0, one launch (start us, length us, event | category | flops | bytes accessed | tf_op | source)
XLA Modules:
  0.0 88.0 jit_solution(17597901486602020855)
XLA Ops:
  0.6 4.5 %collective-permute-start = (bf16[128,4096]{1,0:T(8,128)(2,1)}, bf16[128,4096]{1,0:T(8,128)(2,1)S(1)}, u32[]{:S(2)}, u32[]{:S(2)}) collective-permute-start(bf16[128,4096]{1,0:T(8,128)(2,1)} %p_ref.1), channel_id=1, source_target_pairs={{0,7},{1,0},{2,1},{3,2},{4,3},{5,4},{6,5},{7,6},{8,15},{9,8},{10,9... | collective-permute-start | bytes 3145736 | tf_op jit(solution)/shard_map/ppermute | solution.py:261
  5.2 1.3 %collective-permute-start.1 = (bf16[128,4096]{1,0:T(8,128)(2,1)}, bf16[128,4096]{1,0:T(8,128)(2,1)S(1)}, u32[]{:S(2)}, u32[]{:S(2)}) collective-permute-start(bf16[128,4096]{1,0:T(8,128)(2,1)} %p_ref.1), channel_id=1, source_target_pairs={{1,6},{3,0},{5,2},{7,4},{9,14},{11,8},{13,10},{15,12},{17,22},{19,... | collective-permute-start | bytes 3145736 | tf_op jit(solution)/shard_map/ppermute | solution.py:261
  6.5 0.7 copy-done.2
  7.1 1.6 %shard_map.67 = (bf16[272,1024]{1,0:T(8,128)(2,1)S(1)}, bf16[272,1024]{1,0:T(8,128)(2,1)S(1)}, bf16[272,1024]{1,0:T(8,128)(2,1)S(1)}, bf16[272,1024]{1,0:T(8,128)(2,1)S(1)}, f32[8,128]{1,0:T(8,128)S(1)}) custom-call(bf16[128,4096]{1,0:T(8,128)(2,1)} %q_ref.11, bf16[128,4096]{1,0:T(8,128)(2,1)} %p_ref.1, s32[3,128]{1,0:T(4,128)S(1)} %bitcast.3), custom_call_target="tpu_custom_call" | custom-call | bytes 4331008 | tf_op jit(solution)/shard_map/pallas_call | solution.py:31
  8.7 1.6 %collective-permute-start.4 = (bf16[272,1024]{1,0:T(8,128)(2,1)S(1)}, bf16[272,1024]{1,0:T(8,128)(2,1)S(1)}, u32[]{:S(2)}, u32[]{:S(2)}) collective-permute-start(bf16[272,1024]{1,0:T(8,128)(2,1)S(1)} %get-tuple-element.38), channel_id=1, source_target_pairs={{0,8},{8,0},{16,24},{24,16},{1,9},{9,1},{17,25},{25,17},{2,10},{10... | collective-permute-start | bytes 1671176 | tf_op jit(solution)/shard_map/ppermute | solution.py:267
  10.3 1.5 %collective-permute-start.5 = (bf16[272,1024]{1,0:T(8,128)(2,1)S(1)}, bf16[272,1024]{1,0:T(8,128)(2,1)S(1)}, u32[]{:S(2)}, u32[]{:S(2)}) collective-permute-start(bf16[272,1024]{1,0:T(8,128)(2,1)S(1)} %get-tuple-element.39), channel_id=1, source_target_pairs={{0,16},{8,24},{16,0},{24,8},{1,17},{9,25},{17,1},{25,9},{2,18},{10... | collective-permute-start | bytes 1671176 | tf_op jit(solution)/shard_map/ppermute | solution.py:267
  12.3 14.8 %collective-permute-done.source = bf16[128,4096]{1,0:T(8,128)(2,1)S(1)} collective-permute-done((bf16[128,4096]{1,0:T(8,128)(2,1)}, bf16[128,4096]{1,0:T(8,128)(2,1)S(1)}, u32[]{:S(2)}, u32[]{:S(2)}) %collective-permute-start) | collective-permute-done | bytes 1048608 | tf_op jit(solution)/shard_map/ppermute | solution.py:261
  27.2 0.9 collective-permute-start.3
  28.4 5.0 %collective-permute-start.2 = (bf16[128,8192]{1,0:T(8,128)(2,1)S(1)}, bf16[128,8192]{1,0:T(8,128)(2,1)S(1)}, u32[]{:S(2)}, u32[]{:S(2)}) collective-permute-start(bf16[128,8192]{1,0:T(8,128)(2,1)S(1)} %shard_map.70), channel_id=1, source_target_pairs={{0,1},{1,0},{2,3},{3,2},{4,5},{5,4},{6,7},{7,6},{8,9},{9,8},{10,11... | collective-permute-start | bytes 6291464 | tf_op jit(solution)/shard_map/ppermute | solution.py:264
  33.5 1.0 %shard_map.69 = (f32[128,128]{1,0:T(8,128)S(1)}, f32[128,128]{1,0:T(8,128)S(1)}, f32[128,128]{1,0:T(8,128)S(1)}) custom-call(bf16[128,4096]{1,0:T(8,128)(2,1)S(1)} %copy-done, bf16[128,4096]{1,0:T(8,128)(2,1)S(1)} %copy-done.1, bf16[128,4096]{1,0:T(8,128)(2,1)S(1)} %shard_map.68.refs_1_.n1_ref, bf16[128,4096]{1,0:T(8,128)(2,1)S(1)} %collective-permute-done.1.refs_2_.e3_ref), custom_call_target="tpu_custom_call" | custom-call | bytes 4390912 | tf_op jit(solution)/shard_map/pallas_call | solution.py:31
  34.4 3.2 %collective-permute-done.5.refs_2_ = bf16[272,1024]{1,0:T(8,128)(2,1)S(1)} collective-permute-done((bf16[272,1024]{1,0:T(8,128)(2,1)S(1)}, bf16[272,1024]{1,0:T(8,128)(2,1)S(1)}, u32[]{:S(2)}, u32[]{:S(2)}) %collective-permute-start.5) | collective-permute-done | bytes 557088 | tf_op jit(solution)/shard_map/ppermute | solution.py:267
  37.6 1.4 %shard_map.72 = (f32[3,128]{1,0:T(4,128)S(1)}, f32[3,128]{1,0:T(4,128)S(1)}, f32[3,128]{1,0:T(4,128)S(1)}, f32[3,128]{1,0:T(4,128)S(1)}) custom-call(bf16[272,1024]{1,0:T(8,128)(2,1)S(1)} %get-tuple-element.37.refs_0_, bf16[272,1024]{1,0:T(8,128)(2,1)S(1)} %collective-permute-done.4.refs_1_, bf16[272,1024]{1,0:T(8,128)(2,1)S(1)} %collective-permute-done.5.refs_2_, ...), custom_call_target="tpu_custom_call" | custom-call | flops 49999998976 | bytes 2299904 | tf_op jit(solution)/shard_map/pallas_call | solution.py:31
  39.0 0.8 collective-permute-start.7
  39.9 1.3 %collective-permute-start.8 = (f32[3,128]{1,0:T(4,128)S(1)}, f32[3,128]{1,0:T(4,128)S(1)}, u32[]{:S(2)}, u32[]{:S(2)}) collective-permute-start(f32[3,128]{1,0:T(4,128)S(1)} %get-tuple-element.43), channel_id=1, source_target_pairs={{0,16},{8,24},{16,0},{24,8},{1,17},{9,25},{17,1},{25,9},{2,18},{10... | collective-permute-start | bytes 4616 | tf_op jit(solution)/shard_map/ppermute | solution.py:267
  41.2 1.4 %collective-permute-start.9 = (f32[3,128]{1,0:T(4,128)S(1)}, f32[3,128]{1,0:T(4,128)S(1)}, u32[]{:S(2)}, u32[]{:S(2)}) collective-permute-start(f32[3,128]{1,0:T(4,128)S(1)} %get-tuple-element.44), channel_id=1, source_target_pairs={{0,24},{8,16},{16,8},{24,0},{1,25},{9,17},{17,9},{25,1},{2,26},{10... | collective-permute-start | bytes 4616 | tf_op jit(solution)/shard_map/ppermute | solution.py:267
  43.4 2.2 %collective-permute-done.9.refs_3_ = f32[3,128]{1,0:T(4,128)S(1)} collective-permute-done((f32[3,128]{1,0:T(4,128)S(1)}, f32[3,128]{1,0:T(4,128)S(1)}, u32[]{:S(2)}, u32[]{:S(2)}) %collective-permute-start.9) | collective-permute-done | bytes 1568 | tf_op jit(solution)/shard_map/ppermute | solution.py:267
  45.7 1.1 %shard_map.73 = (f32[1,128]{1,0:T(1,128)}, bf16[128,512]{1,0:T(8,128)(2,1)S(1)}, f32[3,128]{1,0:T(4,128)S(1)}, bf16[128,256]{1,0:T(8,128)(2,1)S(1)}, bf16[128,4096]{1,0:T(8,128)(2,1)S(1)}) custom-call(bf16[128,4096]{1,0:T(8,128)(2,1)S(1)} %copy-done, f32[128,128]{1,0:T(8,128)S(1)} %get-tuple-element.34.refs_4_.s0_ref, ...), custom_call_target="tpu_custom_call" | custom-call | bytes 3613184 | tf_op jit(solution)/shard_map/pallas_call | solution.py:31
  46.8 0.7 collective-permute-start.12
  47.5 0.5 collective-permute-start.10
  48.0 1.5 %collective-permute-start.14 = (f32[3,128]{1,0:T(4,128)S(1)}, f32[3,128]{1,0:T(4,128)S(1)}, u32[]{:S(2)}, u32[]{:S(2)}) collective-permute-start(f32[3,128]{1,0:T(4,128)S(1)} %get-tuple-element.55.refs_4_), channel_id=1, source_target_pairs={{0,8},{8,0},{16,24},{24,16},{1,9},{9,1},{17,25},{25,17},{2,10},{10... | collective-permute-start | bytes 4616 | tf_op jit(solution)/shard_map/ppermute | solution.py:267
  49.5 1.5 %collective-permute-start.15 = (f32[3,128]{1,0:T(4,128)S(1)}, f32[3,128]{1,0:T(4,128)S(1)}, u32[]{:S(2)}, u32[]{:S(2)}) collective-permute-start(f32[3,128]{1,0:T(4,128)S(1)} %get-tuple-element.55.refs_4_), channel_id=1, source_target_pairs={{0,16},{8,24},{16,0},{24,8},{1,17},{9,25},{17,1},{25,9},{2,18},{10... | collective-permute-start | bytes 4616 | tf_op jit(solution)/shard_map/ppermute | solution.py:267
  52.0 2.1 %collective-permute-start.11 = (bf16[128,4096]{1,0:T(8,128)(2,1)S(1)}, bf16[128,4096]{1,0:T(8,128)(2,1)S(1)}, u32[]{:S(2)}, u32[]{:S(2)}) collective-permute-start(bf16[128,4096]{1,0:T(8,128)(2,1)S(1)} %get-tuple-element.48), channel_id=1, source_target_pairs={{0,3},{2,5},{4,7},{6,1},{8,11},{10,13},{12,15},{14,9},{16,19},{18,... | collective-permute-start | bytes 3145736 | tf_op jit(solution)/shard_map/ppermute | solution.py:261
  54.1 1.4 %collective-permute-done.16.refs_7_ = f32[3,128]{1,0:T(4,128)S(1)} collective-permute-done((f32[3,128]{1,0:T(4,128)S(1)}, f32[3,128]{1,0:T(4,128)S(1)}, u32[]{:S(2)}, u32[]{:S(2)}) %collective-permute-start.16) | collective-permute-done | bytes 1568 | tf_op jit(solution)/shard_map/ppermute | solution.py:267
  55.5 2.1 %shard_map.77 = (bf16[256,1024]{1,0:T(8,128)(2,1)S(1)}, bf16[256,1024]{1,0:T(8,128)(2,1)S(1)}, bf16[256,1024]{1,0:T(8,128)(2,1)S(1)}, bf16[256,1024]{1,0:T(8,128)(2,1)S(1)}, f32[8,128]{1,0:T(8,128)}) custom-call(bf16[272,1024]{1,0:T(8,128)(2,1)S(1)} %get-tuple-element.37.refs_0_, bf16[272,1024]{1,0:T(8,128)(2,1)S(1)} %collective-permute-done.4.refs_1_, ...), custom_call_target="tpu_custom_call" | custom-call | bytes 4339712 | tf_op jit(solution)/shard_map/pallas_call | solution.py:31
  58.1 1.1 %collective-permute-start.18 = (bf16[256,1024]{1,0:T(8,128)(2,1)S(1)}, bf16[256,1024]{1,0:T(8,128)(2,1)S(1)}, u32[]{:S(2)}, u32[]{:S(2)}) collective-permute-start(bf16[256,1024]{1,0:T(8,128)(2,1)S(1)} %get-tuple-element.59), channel_id=1, source_target_pairs={{0,16},{8,24},{16,0},{24,8},{1,17},{9,25},{17,1},{25,9},{2,18},{10... | collective-permute-start | bytes 1572872 | tf_op jit(solution)/shard_map/ppermute | solution.py:267
  59.2 1.9 %collective-permute-start.19 = (bf16[256,1024]{1,0:T(8,128)(2,1)S(1)}, bf16[256,1024]{1,0:T(8,128)(2,1)S(1)}, u32[]{:S(2)}, u32[]{:S(2)}) collective-permute-start(bf16[256,1024]{1,0:T(8,128)(2,1)S(1)} %get-tuple-element.60), channel_id=1, source_target_pairs={{0,24},{8,16},{16,8},{24,0},{1,25},{9,17},{17,9},{25,1},{2,26},{10... | collective-permute-start | bytes 1572872 | tf_op jit(solution)/shard_map/ppermute | solution.py:267
  61.3 1.3 %collective-permute-start.13 = (bf16[128,4096]{1,0:T(8,128)(2,1)S(1)}, bf16[128,4096]{1,0:T(8,128)(2,1)S(1)}, u32[]{:S(2)}, u32[]{:S(2)}) collective-permute-start(bf16[128,4096]{1,0:T(8,128)(2,1)S(1)} %get-tuple-element.54), channel_id=1, source_target_pairs={{1,2},{3,4},{5,6},{7,0},{9,10},{11,12},{13,14},{15,8},{17,18},{19,... | collective-permute-start | bytes 3145736 | tf_op jit(solution)/shard_map/ppermute | solution.py:261
  62.6 8.2 %collective-permute-done.11.own3_ref = bf16[128,4096]{1,0:T(8,128)(2,1)S(1)} collective-permute-done((bf16[128,4096]{1,0:T(8,128)(2,1)S(1)}, bf16[128,4096]{1,0:T(8,128)(2,1)S(1)}, u32[]{:S(2)}, u32[]{:S(2)}) %collective-permute-start.11) | collective-permute-done | bytes 1048608 | tf_op jit(solution)/shard_map/ppermute | solution.py:261
  70.8 1.7 %shard_map.76 = (f32[128,4096]{1,0:T(8,128)S(1)}, f32[128,4096]{1,0:T(8,128)S(1)}) custom-call(bf16[128,4096]{1,0:T(8,128)(2,1)S(1)} %copy-done, bf16[128,8192]{1,0:T(8,128)(2,1)S(1)} %collective-permute-done.2.pair_ref, bf16[128,4096]{1,0:T(8,128)(2,1)S(1)} %copy-done.1, bf16[128,4096]{1,0:T(8,128)(2,1)S(1)} %shard_map.68.refs_1_.n1_ref, ...), custom_call_target="tpu_custom_call" | custom-call | flops 49999998976 | bytes 12784128 | tf_op jit(solution)/shard_map/pallas_call | solution.py:31
  72.5 8.8 %collective-permute-done.18.refs_2_ = bf16[256,1024]{1,0:T(8,128)(2,1)S(1)} collective-permute-done((bf16[256,1024]{1,0:T(8,128)(2,1)S(1)}, bf16[256,1024]{1,0:T(8,128)(2,1)S(1)}, u32[]{:S(2)}, u32[]{:S(2)}) %collective-permute-start.18) | collective-permute-done | bytes 524320 | tf_op jit(solution)/shard_map/ppermute | solution.py:267
  81.3 5.2 %collective-permute-done.13.own1 = bf16[128,4096]{1,0:T(8,128)(2,1)S(1)} collective-permute-done((bf16[128,4096]{1,0:T(8,128)(2,1)S(1)}, bf16[128,4096]{1,0:T(8,128)(2,1)S(1)}, u32[]{:S(2)}, u32[]{:S(2)}) %collective-permute-start.13) | collective-permute-done | bytes 1048608 | tf_op jit(solution)/shard_map/ppermute | solution.py:261
  86.5 1.5 %shard_map.78 = (bf16[128,4096]{1,0:T(8,128)(2,1)}, bf16[128,4096]{1,0:T(8,128)(2,1)}) custom-call(f32[128,4096]{1,0:T(8,128)S(1)} %get-tuple-element.52.pulled, f32[128,4096]{1,0:T(8,128)S(1)} %get-tuple-element.53.base, bf16[128,4096]{1,0:T(8,128)(2,1)S(1)} %collective-permute-done.13.own1, bf16[256,1024]{1,0:T(8,128)(2,1)S(1)} %get-tuple-element.57.refs_0_, ...), custom_call_target="tpu_custom_call" | custom-call | bytes 9437184 | tf_op jit(solution)/shard_map/pallas_call | solution.py:31
  (28 shorter events, 3.5 us)
Async XLA Ops:
  0.6 26.4 %collective-permute-start = (bf16[128,4096]{1,0:T(8,128)(2,1)}, bf16[128,4096]{1,0:T(8,128)(2,1)S(1)}, u32[]{:S(2)}, u32[]{:S(2)}) collective-permute-start(bf16[128,4096]{1,0:T(8,128)(2,1)} %p_ref.1), channel_id=1, source_target_pairs={{0,7},{1,0},{2,1},{3,2},{4,3},{5,4},{6,5},{7,6},{8,15},{9,8},{10,9... | collective-permute-start | bytes 3145736 | tf_op jit(solution)/shard_map/ppermute | solution.py:261
  5.2 22.9 %collective-permute-start.1 = (bf16[128,4096]{1,0:T(8,128)(2,1)}, bf16[128,4096]{1,0:T(8,128)(2,1)S(1)}, u32[]{:S(2)}, u32[]{:S(2)}) collective-permute-start(bf16[128,4096]{1,0:T(8,128)(2,1)} %p_ref.1), channel_id=1, source_target_pairs={{1,6},{3,0},{5,2},{7,4},{9,14},{11,8},{13,10},{15,12},{17,22},{19,... | collective-permute-start | bytes 3145736 | tf_op jit(solution)/shard_map/ppermute | solution.py:261
  6.5 0.7 copy-start.2
  8.7 25.7 %collective-permute-start.4 = (bf16[272,1024]{1,0:T(8,128)(2,1)S(1)}, bf16[272,1024]{1,0:T(8,128)(2,1)S(1)}, u32[]{:S(2)}, u32[]{:S(2)}) collective-permute-start(bf16[272,1024]{1,0:T(8,128)(2,1)S(1)} %get-tuple-element.38), channel_id=1, source_target_pairs={{0,8},{8,0},{16,24},{24,16},{1,9},{9,1},{17,25},{25,17},{2,10},{10... | collective-permute-start | bytes 1671176 | tf_op jit(solution)/shard_map/ppermute | solution.py:267
  10.3 27.3 %collective-permute-start.5 = (bf16[272,1024]{1,0:T(8,128)(2,1)S(1)}, bf16[272,1024]{1,0:T(8,128)(2,1)S(1)}, u32[]{:S(2)}, u32[]{:S(2)}) collective-permute-start(bf16[272,1024]{1,0:T(8,128)(2,1)S(1)} %get-tuple-element.39), channel_id=1, source_target_pairs={{0,16},{8,24},{16,0},{24,8},{1,17},{9,25},{17,1},{25,9},{2,18},{10... | collective-permute-start | bytes 1671176 | tf_op jit(solution)/shard_map/ppermute | solution.py:267
  11.8 25.8 %collective-permute-start.6 = (bf16[272,1024]{1,0:T(8,128)(2,1)S(1)}, bf16[272,1024]{1,0:T(8,128)(2,1)S(1)}, u32[]{:S(2)}, u32[]{:S(2)}) collective-permute-start(bf16[272,1024]{1,0:T(8,128)(2,1)S(1)} %get-tuple-element.40), channel_id=1, source_target_pairs={{0,24},{8,16},{16,8},{24,0},{1,25},{9,17},{17,9},{25,1},{2,26},{10... | collective-permute-start | bytes 1671176 | tf_op jit(solution)/shard_map/ppermute | solution.py:267
  27.1 1.2 %copy-start = (bf16[128,4096]{1,0:T(8,128)(2,1)S(1)}, bf16[128,4096]{1,0:T(8,128)(2,1)}, u32[]{:S(2)}) copy-start(bf16[128,4096]{1,0:T(8,128)(2,1)} %q_ref.11) | copy-start | bytes 3145732
  27.1 6.3 %copy-start.1 = (bf16[128,4096]{1,0:T(8,128)(2,1)S(1)}, bf16[128,4096]{1,0:T(8,128)(2,1)}, u32[]{:S(2)}) copy-start(bf16[128,4096]{1,0:T(8,128)(2,1)} %p_ref.1) | copy-start | bytes 3145732
  27.2 18.5 %collective-permute-start.3 = (bf16[128,4096]{1,0:T(8,128)(2,1)S(1)}, bf16[128,4096]{1,0:T(8,128)(2,1)S(1)}, u32[]{:S(2)}, u32[]{:S(2)}) collective-permute-start(bf16[128,4096]{1,0:T(8,128)(2,1)S(1)} %shard_map.68.refs_1_.n1_ref), channel_id=1, source_target_pairs={{1,7},{3,1},{5,3},{7,5},{9,15},{11,9},{13,11},{15,13},{17,23},{19,... | collective-permute-start | bytes 3145736 | tf_op jit(solution)/shard_map/ppermute | solution.py:261
  28.4 14.2 %collective-permute-start.2 = (bf16[128,8192]{1,0:T(8,128)(2,1)S(1)}, bf16[128,8192]{1,0:T(8,128)(2,1)S(1)}, u32[]{:S(2)}, u32[]{:S(2)}) collective-permute-start(bf16[128,8192]{1,0:T(8,128)(2,1)S(1)} %shard_map.70), channel_id=1, source_target_pairs={{0,1},{1,0},{2,3},{3,2},{4,5},{5,4},{6,7},{7,6},{8,9},{9,8},{10,11... | collective-permute-start | bytes 6291464 | tf_op jit(solution)/shard_map/ppermute | solution.py:264
  39.0 6.6 %copy-start.3 = (f32[128]{0:T(128)S(1)}, f32[128]{0:T(128)}, u32[]{:S(2)}) copy-start(f32[128]{0:T(128)} %param.7) | copy-start | bytes 1540
  39.0 4.0 %collective-permute-start.7 = (f32[3,128]{1,0:T(4,128)S(1)}, f32[3,128]{1,0:T(4,128)S(1)}, u32[]{:S(2)}, u32[]{:S(2)}) collective-permute-start(f32[3,128]{1,0:T(4,128)S(1)} %get-tuple-element.42), channel_id=1, source_target_pairs={{0,8},{8,0},{16,24},{24,16},{1,9},{9,1},{17,25},{25,17},{2,10},{10... | collective-permute-start | bytes 4616 | tf_op jit(solution)/shard_map/ppermute | solution.py:267
  39.9 3.6 %collective-permute-start.8 = (f32[3,128]{1,0:T(4,128)S(1)}, f32[3,128]{1,0:T(4,128)S(1)}, u32[]{:S(2)}, u32[]{:S(2)}) collective-permute-start(f32[3,128]{1,0:T(4,128)S(1)} %get-tuple-element.43), channel_id=1, source_target_pairs={{0,16},{8,24},{16,0},{24,8},{1,17},{9,25},{17,1},{25,9},{2,18},{10... | collective-permute-start | bytes 4616 | tf_op jit(solution)/shard_map/ppermute | solution.py:267
  41.2 4.5 %collective-permute-start.9 = (f32[3,128]{1,0:T(4,128)S(1)}, f32[3,128]{1,0:T(4,128)S(1)}, u32[]{:S(2)}, u32[]{:S(2)}) collective-permute-start(f32[3,128]{1,0:T(4,128)S(1)} %get-tuple-element.44), channel_id=1, source_target_pairs={{0,24},{8,16},{16,8},{24,0},{1,25},{9,17},{17,9},{25,1},{2,26},{10... | collective-permute-start | bytes 4616 | tf_op jit(solution)/shard_map/ppermute | solution.py:267
  46.8 14.3 %collective-permute-start.12 = (bf16[128,4096]{1,0:T(8,128)(2,1)S(1)}, bf16[128,4096]{1,0:T(8,128)(2,1)S(1)}, u32[]{:S(2)}, u32[]{:S(2)}) collective-permute-start(bf16[128,4096]{1,0:T(8,128)(2,1)S(1)} %get-tuple-element.50), channel_id=1, source_target_pairs={{1,3},{3,5},{5,7},{7,1},{9,11},{11,13},{13,15},{15,9},{17,19},{19,... | collective-permute-start | bytes 3145736 | tf_op jit(solution)/shard_map/ppermute | solution.py:261
  47.5 4.0 %collective-permute-start.10 = (bf16[128,256]{1,0:T(8,128)(2,1)S(1)}, bf16[128,256]{1,0:T(8,128)(2,1)S(1)}, u32[]{:S(2)}, u32[]{:S(2)}) collective-permute-start(bf16[128,256]{1,0:T(8,128)(2,1)S(1)} %get-tuple-element.47), channel_id=1, source_target_pairs={{0,1},{1,0},{2,3},{3,2},{4,5},{5,4},{6,7},{7,6},{8,9},{9,8},{10,11... | collective-permute-start | bytes 196616 | tf_op jit(solution)/shard_map/ppermute | solution.py:264
  48.0 6.1 %collective-permute-start.14 = (f32[3,128]{1,0:T(4,128)S(1)}, f32[3,128]{1,0:T(4,128)S(1)}, u32[]{:S(2)}, u32[]{:S(2)}) collective-permute-start(f32[3,128]{1,0:T(4,128)S(1)} %get-tuple-element.55.refs_4_), channel_id=1, source_target_pairs={{0,8},{8,0},{16,24},{24,16},{1,9},{9,1},{17,25},{25,17},{2,10},{10... | collective-permute-start | bytes 4616 | tf_op jit(solution)/shard_map/ppermute | solution.py:267
  49.5 4.6 %collective-permute-start.15 = (f32[3,128]{1,0:T(4,128)S(1)}, f32[3,128]{1,0:T(4,128)S(1)}, u32[]{:S(2)}, u32[]{:S(2)}) collective-permute-start(f32[3,128]{1,0:T(4,128)S(1)} %get-tuple-element.55.refs_4_), channel_id=1, source_target_pairs={{0,16},{8,24},{16,0},{24,8},{1,17},{9,25},{17,1},{25,9},{2,18},{10... | collective-permute-start | bytes 4616 | tf_op jit(solution)/shard_map/ppermute | solution.py:267
  51.0 4.5 %collective-permute-start.16 = (f32[3,128]{1,0:T(4,128)S(1)}, f32[3,128]{1,0:T(4,128)S(1)}, u32[]{:S(2)}, u32[]{:S(2)}) collective-permute-start(f32[3,128]{1,0:T(4,128)S(1)} %get-tuple-element.55.refs_4_), channel_id=1, source_target_pairs={{0,24},{8,16},{16,8},{24,0},{1,25},{9,17},{17,9},{25,1},{2,26},{10... | collective-permute-start | bytes 4616 | tf_op jit(solution)/shard_map/ppermute | solution.py:267
  52.0 18.8 %collective-permute-start.11 = (bf16[128,4096]{1,0:T(8,128)(2,1)S(1)}, bf16[128,4096]{1,0:T(8,128)(2,1)S(1)}, u32[]{:S(2)}, u32[]{:S(2)}) collective-permute-start(bf16[128,4096]{1,0:T(8,128)(2,1)S(1)} %get-tuple-element.48), channel_id=1, source_target_pairs={{0,3},{2,5},{4,7},{6,1},{8,11},{10,13},{12,15},{14,9},{16,19},{18,... | collective-permute-start | bytes 3145736 | tf_op jit(solution)/shard_map/ppermute | solution.py:261
  57.6 14.9 %collective-permute-start.17 = (bf16[256,1024]{1,0:T(8,128)(2,1)S(1)}, bf16[256,1024]{1,0:T(8,128)(2,1)S(1)}, u32[]{:S(2)}, u32[]{:S(2)}) collective-permute-start(bf16[256,1024]{1,0:T(8,128)(2,1)S(1)} %get-tuple-element.58), channel_id=1, source_target_pairs={{0,8},{8,0},{16,24},{24,16},{1,9},{9,1},{17,25},{25,17},{2,10},{10... | collective-permute-start | bytes 1572872 | tf_op jit(solution)/shard_map/ppermute | solution.py:267
  58.1 23.2 %collective-permute-start.18 = (bf16[256,1024]{1,0:T(8,128)(2,1)S(1)}, bf16[256,1024]{1,0:T(8,128)(2,1)S(1)}, u32[]{:S(2)}, u32[]{:S(2)}) collective-permute-start(bf16[256,1024]{1,0:T(8,128)(2,1)S(1)} %get-tuple-element.59), channel_id=1, source_target_pairs={{0,16},{8,24},{16,0},{24,8},{1,17},{9,25},{17,1},{25,9},{2,18},{10... | collective-permute-start | bytes 1572872 | tf_op jit(solution)/shard_map/ppermute | solution.py:267
  59.2 22.1 %collective-permute-start.19 = (bf16[256,1024]{1,0:T(8,128)(2,1)S(1)}, bf16[256,1024]{1,0:T(8,128)(2,1)S(1)}, u32[]{:S(2)}, u32[]{:S(2)}) collective-permute-start(bf16[256,1024]{1,0:T(8,128)(2,1)S(1)} %get-tuple-element.60), channel_id=1, source_target_pairs={{0,24},{8,16},{16,8},{24,0},{1,25},{9,17},{17,9},{25,1},{2,26},{10... | collective-permute-start | bytes 1572872 | tf_op jit(solution)/shard_map/ppermute | solution.py:267
  61.3 25.2 %collective-permute-start.13 = (bf16[128,4096]{1,0:T(8,128)(2,1)S(1)}, bf16[128,4096]{1,0:T(8,128)(2,1)S(1)}, u32[]{:S(2)}, u32[]{:S(2)}) collective-permute-start(bf16[128,4096]{1,0:T(8,128)(2,1)S(1)} %get-tuple-element.54), channel_id=1, source_target_pairs={{1,2},{3,4},{5,6},{7,0},{9,10},{11,12},{13,14},{15,8},{17,18},{19,... | collective-permute-start | bytes 3145736 | tf_op jit(solution)/shard_map/ppermute | solution.py:261
where the time goes:
time: 88.3 us; the launch traced here: 88 us
  waiting for transfers between devices  44.2 us (50%)
  starting transfers between devices  30.4 us (34%)
  Pallas kernels  11.7 us (13%)
  local copies, waits for them, and re-layouts  0.95 us (1%)
    ppermute x6, waiting for transfers between devices, shift(): return lax.ppermute(array, 'blk', pairs)  28.2 us
    ppermute x12, waiting for transfers between devices, over_groups(): return lax.ppermute(array, 'grp', [(i, i ^ r) for i in range(groups)])  16 us
    ppermute x12, starting transfers between devices, over_groups(): return lax.ppermute(array, 'grp', [(i, i ^ r) for i in range(groups)])  14.1 us
    pallas_call x12, Pallas kernels, local_call(): pl.pallas_call(body, out_shape=out_shape, in_specs=in_specs or [VMEM] * l...  11.7 us
    ppermute x6, starting transfers between devices, shift(): return lax.ppermute(array, 'blk', pairs)  10.8 us
    ppermute x2, starting transfers between devices, swap(): return lax.ppermute(array, 'blk', [(i, i ^ 1) for i in range(loop)])  5.56 us
  transfers between devices with their start and end apart: 20, of which 8 were waited for; matrix products, arithmetic and copies ran while one was open for 0% of the time, Pallas kernels for 10%

commit v1 on v0

--- a/solution.py
+++ b/solution.py
@@ -156,9 +156,11 @@
 
 
 def weigh_body(
-    groups, q_ref, s0_ref, s1_ref, s2_ref, s3_ref, last_ref, w_ref, *refs
+    groups, *refs
 ):
-    parts, (loss_ref, coef_ref, hard_out, swap_ref, term3_ref) = refs[:groups], refs[groups:]
+    parts, refs = refs[:groups], refs[groups:]
+    q_ref, s0_ref, s1_ref, s2_ref, s3_ref, last_ref, w_ref, *refs = refs
+    loss_ref, coef_ref, hard_out, swap_ref, term3_ref = refs
     rows, width = q_ref.shape
     w = w_ref[...]
     s3 = INV_TEMP * (s3_ref[...] + dot(last_ref[...], q_ref[...], ((1,), (1,))))
@@ -289,7 +291,8 @@
     )
     pieces = exchange(pieces)
 
-    next3_even = shift(passages, -3, (1,))
+    (later_p,) = local_call(pass_body, [block], passages, token)
+    next3_even = shift(later_p, -3, (1,))
     (next1,) = local_call(pass_body, [block], next1, token, flops=LONG)
     next3_odd = shift(next1, -2, (1,))
     pair = swap(
@@ -305,7 +308,7 @@
     loss_rows, coef, hard_coef, to_core, term3 = local_call(
         functools.partial(weigh_body, groups),
         [like(1, rows, dtype=F32), like(rows, 4 * rows), triple, like(rows, 2 * rows), block],
-        queries, s0, s1, s2, s3, next3_odd, weights[None, :], *parts,
+        *parts, queries, s0, s1, s2, s3, next3_odd, weights[None, :],
     )
 
     got3 = shift(term3, 2, (1,))

time: 88.3 us -> 83.6 us (0.947)
  starting transfers between devices: 30.4 us -> 27.3 us
  waiting for transfers between devices: 44.2 us -> 42.9 us
    ppermute x2, starting transfers between devices: 5.56 us -> 2.12 us  [swap(): return lax.ppermute(array, 'blk', [(i, i ^ 1) for i in range(loop)])]
    ppermute x12, waiting for transfers between devices: 16 us -> 14.7 us  [over_groups(): return lax.ppermute(array, 'grp', [(i, i ^ r) for i in range(groups)])]
    pallas_call x12 -> x13, Pallas kernels: 11.7 us -> 11.7 us  [local_call(): pl.pallas_call(body, out_shape=out_shape, in_specs=in_specs or [VMEM] * l...]
  transfers between devices with their start and end apart: 20 -> 20, of which waited for: 8 -> 9; matrix products, arithmetic and copies ran while one was open for 0% -> 0% of each run, Pallas kernels for 10% -> 11%
where the time goes in v1:
time: 83.6 us; the launch traced here: 83.4 us
  waiting for transfers between devices  42.9 us (51%)
  starting transfers between devices  27.3 us (33%)
  Pallas kernels  11.7 us (14%)
    ppermute x6, waiting for transfers between devices, shift(): return lax.ppermute(array, 'blk', pairs)  28.1 us
    ppermute x12, waiting for transfers between devices, over_groups(): return lax.ppermute(array, 'grp', [(i, i ^ r) for i in range(groups)])  14.7 us
    ppermute x12, starting transfers between devices, over_groups(): return lax.ppermute(array, 'grp', [(i, i ^ r) for i in range(groups)])  14.1 us
    pallas_call x13, Pallas kernels, local_call(): pl.pallas_call(body, out_shape=out_shape, in_specs=in_specs or [VMEM] * l...  11.7 us
    ppermute x6, starting transfers between devices, shift(): return lax.ppermute(array, 'blk', pairs)  11.1 us
    ppermute x2, starting transfers between devices, swap(): return lax.ppermute(array, 'blk', [(i, i ^ 1) for i in range(loop)])  2.12 us
  transfers between devices with their start and end apart: 20, of which 9 were waited for; matrix products, arithmetic and copies ran while one was open for 0% of the time, Pallas kernels for 11%

profile of v1, /device:TPU:0, one launch (start us, length us, event | category | flops | bytes accessed | tf_op | source)
XLA Modules:
  0.0 83.4 jit_solution(11111450441129501973)
XLA Ops:
  0.6 4.5 %collective-permute-start.3 = (bf16[128,4096]{1,0:T(8,128)(2,1)}, bf16[128,4096]{1,0:T(8,128)(2,1)S(1)}, u32[]{:S(2)}, u32[]{:S(2)}) collective-permute-start(bf16[128,4096]{1,0:T(8,128)(2,1)} %p_ref.1), channel_id=1, source_target_pairs={{0,7},{1,0},{2,1},{3,2},{4,3},{5,4},{6,5},{7,6},{8,15},{9,8},{10,9... | collective-permute-start | bytes 3145736 | tf_op jit(solution)/shard_map/ppermute | solution.py:263
  5.9 1.6 %shard_map.67 = (bf16[272,1024]{1,0:T(8,128)(2,1)S(1)}, bf16[272,1024]{1,0:T(8,128)(2,1)S(1)}, bf16[272,1024]{1,0:T(8,128)(2,1)S(1)}, bf16[272,1024]{1,0:T(8,128)(2,1)S(1)}, f32[8,128]{1,0:T(8,128)S(1)}) custom-call(bf16[128,4096]{1,0:T(8,128)(2,1)} %q_ref.9, bf16[128,4096]{1,0:T(8,128)(2,1)} %p_ref.1, s32[3,128]{1,0:T(4,128)S(1)} %bitcast.3), custom_call_target="tpu_custom_call" | custom-call | bytes 4331008 | tf_op jit(solution)/shard_map/pallas_call | solution.py:31
  7.5 1.6 %collective-permute-start = (bf16[272,1024]{1,0:T(8,128)(2,1)S(1)}, bf16[272,1024]{1,0:T(8,128)(2,1)S(1)}, u32[]{:S(2)}, u32[]{:S(2)}) collective-permute-start(bf16[272,1024]{1,0:T(8,128)(2,1)S(1)} %get-tuple-element.34), channel_id=1, source_target_pairs={{0,8},{8,0},{16,24},{24,16},{1,9},{9,1},{17,25},{25,17},{2,10},{10... | collective-permute-start | bytes 1671176 | tf_op jit(solution)/shard_map/ppermute | solution.py:269
  9.0 1.5 %collective-permute-start.1 = (bf16[272,1024]{1,0:T(8,128)(2,1)S(1)}, bf16[272,1024]{1,0:T(8,128)(2,1)S(1)}, u32[]{:S(2)}, u32[]{:S(2)}) collective-permute-start(bf16[272,1024]{1,0:T(8,128)(2,1)S(1)} %get-tuple-element.35), channel_id=1, source_target_pairs={{0,16},{8,24},{16,0},{24,8},{1,17},{9,25},{17,1},{25,9},{2,18},{10... | collective-permute-start | bytes 1671176 | tf_op jit(solution)/shard_map/ppermute | solution.py:269
  11.1 1.4 %collective-permute-start.4 = (bf16[128,4096]{1,0:T(8,128)(2,1)S(1)}, bf16[128,4096]{1,0:T(8,128)(2,1)S(1)}, u32[]{:S(2)}, u32[]{:S(2)}) collective-permute-start(bf16[128,4096]{1,0:T(8,128)(2,1)S(1)} %shard_map.69), channel_id=1, source_target_pairs={{1,6},{3,0},{5,2},{7,4},{9,14},{11,8},{13,10},{15,12},{17,22},{19,... | collective-permute-start | bytes 3145736 | tf_op jit(solution)/shard_map/ppermute | solution.py:263
  12.5 8.6 %collective-permute-done.3.source = bf16[128,4096]{1,0:T(8,128)(2,1)S(1)} collective-permute-done((bf16[128,4096]{1,0:T(8,128)(2,1)}, bf16[128,4096]{1,0:T(8,128)(2,1)S(1)}, u32[]{:S(2)}, u32[]{:S(2)}) %collective-permute-start.3) | collective-permute-done | bytes 1048608 | tf_op jit(solution)/shard_map/ppermute | solution.py:263
  21.2 0.7 collective-permute-start.9
  22.0 6.0 %collective-permute-done.4.refs_2_.e3_ref = bf16[128,4096]{1,0:T(8,128)(2,1)S(1)} collective-permute-done((bf16[128,4096]{1,0:T(8,128)(2,1)S(1)}, bf16[128,4096]{1,0:T(8,128)(2,1)S(1)}, u32[]{:S(2)}, u32[]{:S(2)}) %collective-permute-start.4) | collective-permute-done | bytes 1048608 | tf_op jit(solution)/shard_map/ppermute | solution.py:263
  28.1 1.2 %collective-permute-start.8 = (bf16[128,8192]{1,0:T(8,128)(2,1)S(1)}, bf16[128,8192]{1,0:T(8,128)(2,1)S(1)}, u32[]{:S(2)}, u32[]{:S(2)}) collective-permute-start(bf16[128,8192]{1,0:T(8,128)(2,1)S(1)} %shard_map.72), channel_id=1, source_target_pairs={{0,1},{1,0},{2,3},{3,2},{4,5},{5,4},{6,7},{7,6},{8,9},{9,8},{10,11... | collective-permute-start | bytes 6291464 | tf_op jit(solution)/shard_map/ppermute | solution.py:266
  29.3 1.0 %shard_map.70 = (f32[128,128]{1,0:T(8,128)S(1)}, f32[128,128]{1,0:T(8,128)S(1)}, f32[128,128]{1,0:T(8,128)S(1)}) custom-call(bf16[128,4096]{1,0:T(8,128)(2,1)S(1)} %copy-done, bf16[128,4096]{1,0:T(8,128)(2,1)S(1)} %copy-done.1, bf16[128,4096]{1,0:T(8,128)(2,1)S(1)} %shard_map.68.refs_1_.n1_ref, bf16[128,4096]{1,0:T(8,128)(2,1)S(1)} %collective-permute-done.4.refs_2_.e3_ref), custom_call_target="tpu_custom_call" | custom-call | bytes 4390912 | tf_op jit(solution)/shard_map/pallas_call | solution.py:31
  30.3 2.4 %collective-permute-done.1.refs_2_ = bf16[272,1024]{1,0:T(8,128)(2,1)S(1)} collective-permute-done((bf16[272,1024]{1,0:T(8,128)(2,1)S(1)}, bf16[272,1024]{1,0:T(8,128)(2,1)S(1)}, u32[]{:S(2)}, u32[]{:S(2)}) %collective-permute-start.1) | collective-permute-done | bytes 557088 | tf_op jit(solution)/shard_map/ppermute | solution.py:269
  32.7 1.4 %shard_map.71 = (f32[3,128]{1,0:T(4,128)S(1)}, f32[3,128]{1,0:T(4,128)S(1)}, f32[3,128]{1,0:T(4,128)S(1)}, f32[3,128]{1,0:T(4,128)S(1)}) custom-call(bf16[272,1024]{1,0:T(8,128)(2,1)S(1)} %get-tuple-element.33.refs_0_, bf16[272,1024]{1,0:T(8,128)(2,1)S(1)} %collective-permute-done.refs_1_, bf16[272,1024]{1,0:T(8,128)(2,1)S(1)} %collective-permute-done.1.refs_2_, ...), custom_call_target="tpu_custom_call" | custom-call | flops 49999998976 | bytes 2299904 | tf_op jit(solution)/shard_map/pallas_call | solution.py:31
  34.1 1.3 %collective-permute-start.5 = (f32[3,128]{1,0:T(4,128)S(1)}, f32[3,128]{1,0:T(4,128)S(1)}, u32[]{:S(2)}, u32[]{:S(2)}) collective-permute-start(f32[3,128]{1,0:T(4,128)S(1)} %get-tuple-element.40), channel_id=1, source_target_pairs={{0,8},{8,0},{16,24},{24,16},{1,9},{9,1},{17,25},{25,17},{2,10},{10... | collective-permute-start | bytes 4616 | tf_op jit(solution)/shard_map/ppermute | solution.py:269
  35.4 0.8 collective-permute-start.6
  36.2 1.4 %collective-permute-start.7 = (f32[3,128]{1,0:T(4,128)S(1)}, f32[3,128]{1,0:T(4,128)S(1)}, u32[]{:S(2)}, u32[]{:S(2)}) collective-permute-start(f32[3,128]{1,0:T(4,128)S(1)} %get-tuple-element.42), channel_id=1, source_target_pairs={{0,24},{8,16},{16,8},{24,0},{1,25},{9,17},{17,9},{25,1},{2,26},{10... | collective-permute-start | bytes 4616 | tf_op jit(solution)/shard_map/ppermute | solution.py:269
  38.1 0.9 %collective-permute-done.6.refs_2_ = f32[3,128]{1,0:T(4,128)S(1)} collective-permute-done((f32[3,128]{1,0:T(4,128)S(1)}, f32[3,128]{1,0:T(4,128)S(1)}, u32[]{:S(2)}, u32[]{:S(2)}) %collective-permute-start.6) | collective-permute-done | bytes 1568 | tf_op jit(solution)/shard_map/ppermute | solution.py:269
  39.0 1.7 %collective-permute-done.7.refs_3_ = f32[3,128]{1,0:T(4,128)S(1)} collective-permute-done((f32[3,128]{1,0:T(4,128)S(1)}, f32[3,128]{1,0:T(4,128)S(1)}, u32[]{:S(2)}, u32[]{:S(2)}) %collective-permute-start.7) | collective-permute-done | bytes 1568 | tf_op jit(solution)/shard_map/ppermute | solution.py:269
  40.7 1.1 %shard_map.74 = (f32[1,128]{1,0:T(1,128)}, bf16[128,512]{1,0:T(8,128)(2,1)S(1)}, f32[3,128]{1,0:T(4,128)S(1)}, bf16[128,256]{1,0:T(8,128)(2,1)S(1)}, bf16[128,4096]{1,0:T(8,128)(2,1)S(1)}) custom-call(f32[3,128]{1,0:T(4,128)S(1)} %get-tuple-element.39.refs_0_, f32[3,128]{1,0:T(4,128)S(1)} %collective-permute-done.5.refs_1_, ...), custom_call_target="tpu_custom_call" | custom-call | bytes 3613184 | tf_op jit(solution)/shard_map/pallas_call | solution.py:31
  42.6 0.9 %collective-permute-start.10 = (bf16[128,256]{1,0:T(8,128)(2,1)S(1)}, bf16[128,256]{1,0:T(8,128)(2,1)S(1)}, u32[]{:S(2)}, u32[]{:S(2)}) collective-permute-start(bf16[128,256]{1,0:T(8,128)(2,1)S(1)} %get-tuple-element.47), channel_id=1, source_target_pairs={{0,1},{1,0},{2,3},{3,2},{4,5},{5,4},{6,7},{7,6},{8,9},{9,8},{10,11... | collective-permute-start | bytes 196616 | tf_op jit(solution)/shard_map/ppermute | solution.py:266
  43.5 1.4 %collective-permute-start.14 = (f32[3,128]{1,0:T(4,128)S(1)}, f32[3,128]{1,0:T(4,128)S(1)}, u32[]{:S(2)}, u32[]{:S(2)}) collective-permute-start(f32[3,128]{1,0:T(4,128)S(1)} %get-tuple-element.55.refs_4_), channel_id=1, source_target_pairs={{0,8},{8,0},{16,24},{24,16},{1,9},{9,1},{17,25},{25,17},{2,10},{10... | collective-permute-start | bytes 4616 | tf_op jit(solution)/shard_map/ppermute | solution.py:269
  44.9 1.5 %collective-permute-start.15 = (f32[3,128]{1,0:T(4,128)S(1)}, f32[3,128]{1,0:T(4,128)S(1)}, u32[]{:S(2)}, u32[]{:S(2)}) collective-permute-start(f32[3,128]{1,0:T(4,128)S(1)} %get-tuple-element.55.refs_4_), channel_id=1, source_target_pairs={{0,16},{8,24},{16,0},{24,8},{1,17},{9,25},{17,1},{25,9},{2,18},{10... | collective-permute-start | bytes 4616 | tf_op jit(solution)/shard_map/ppermute | solution.py:269
  47.5 2.4 %collective-permute-start.11 = (bf16[128,4096]{1,0:T(8,128)(2,1)S(1)}, bf16[128,4096]{1,0:T(8,128)(2,1)S(1)}, u32[]{:S(2)}, u32[]{:S(2)}) collective-permute-start(bf16[128,4096]{1,0:T(8,128)(2,1)S(1)} %get-tuple-element.48), channel_id=1, source_target_pairs={{0,3},{2,5},{4,7},{6,1},{8,11},{10,13},{12,15},{14,9},{16,19},{18,... | collective-permute-start | bytes 3145736 | tf_op jit(solution)/shard_map/ppermute | solution.py:263
  49.9 1.0 %collective-permute-done.16.refs_7_ = f32[3,128]{1,0:T(4,128)S(1)} collective-permute-done((f32[3,128]{1,0:T(4,128)S(1)}, f32[3,128]{1,0:T(4,128)S(1)}, u32[]{:S(2)}, u32[]{:S(2)}) %collective-permute-start.16) | collective-permute-done | bytes 1568 | tf_op jit(solution)/shard_map/ppermute | solution.py:269
  50.9 2.1 %shard_map.78 = (bf16[256,1024]{1,0:T(8,128)(2,1)S(1)}, bf16[256,1024]{1,0:T(8,128)(2,1)S(1)}, bf16[256,1024]{1,0:T(8,128)(2,1)S(1)}, bf16[256,1024]{1,0:T(8,128)(2,1)S(1)}, f32[8,128]{1,0:T(8,128)}) custom-call(bf16[272,1024]{1,0:T(8,128)(2,1)S(1)} %get-tuple-element.33.refs_0_, bf16[272,1024]{1,0:T(8,128)(2,1)S(1)} %collective-permute-done.refs_1_, ...), custom_call_target="tpu_custom_call" | custom-call | bytes 4339712 | tf_op jit(solution)/shard_map/pallas_call | solution.py:31
  53.5 1.4 %collective-permute-start.18 = (bf16[256,1024]{1,0:T(8,128)(2,1)S(1)}, bf16[256,1024]{1,0:T(8,128)(2,1)S(1)}, u32[]{:S(2)}, u32[]{:S(2)}) collective-permute-start(bf16[256,1024]{1,0:T(8,128)(2,1)S(1)} %get-tuple-element.59), channel_id=1, source_target_pairs={{0,16},{8,24},{16,0},{24,8},{1,17},{9,25},{17,1},{25,9},{2,18},{10... | collective-permute-start | bytes 1572872 | tf_op jit(solution)/shard_map/ppermute | solution.py:269
  54.9 1.6 %collective-permute-start.19 = (bf16[256,1024]{1,0:T(8,128)(2,1)S(1)}, bf16[256,1024]{1,0:T(8,128)(2,1)S(1)}, u32[]{:S(2)}, u32[]{:S(2)}) collective-permute-start(bf16[256,1024]{1,0:T(8,128)(2,1)S(1)} %get-tuple-element.60), channel_id=1, source_target_pairs={{0,24},{8,16},{16,8},{24,0},{1,25},{9,17},{17,9},{25,1},{2,26},{10... | collective-permute-start | bytes 1572872 | tf_op jit(solution)/shard_map/ppermute | solution.py:269
  56.7 1.3 %collective-permute-start.13 = (bf16[128,4096]{1,0:T(8,128)(2,1)S(1)}, bf16[128,4096]{1,0:T(8,128)(2,1)S(1)}, u32[]{:S(2)}, u32[]{:S(2)}) collective-permute-start(bf16[128,4096]{1,0:T(8,128)(2,1)S(1)} %get-tuple-element.54), channel_id=1, source_target_pairs={{1,2},{3,4},{5,6},{7,0},{9,10},{11,12},{13,14},{15,8},{17,18},{19,... | collective-permute-start | bytes 3145736 | tf_op jit(solution)/shard_map/ppermute | solution.py:263
  58.0 8.3 %collective-permute-done.11.own3_ref = bf16[128,4096]{1,0:T(8,128)(2,1)S(1)} collective-permute-done((bf16[128,4096]{1,0:T(8,128)(2,1)S(1)}, bf16[128,4096]{1,0:T(8,128)(2,1)S(1)}, u32[]{:S(2)}, u32[]{:S(2)}) %collective-permute-start.11) | collective-permute-done | bytes 1048608 | tf_op jit(solution)/shard_map/ppermute | solution.py:263
  66.3 1.7 %shard_map.77 = (f32[128,4096]{1,0:T(8,128)S(1)}, f32[128,4096]{1,0:T(8,128)S(1)}) custom-call(bf16[128,4096]{1,0:T(8,128)(2,1)S(1)} %copy-done, bf16[128,8192]{1,0:T(8,128)(2,1)S(1)} %collective-permute-done.8.pair_ref, bf16[128,4096]{1,0:T(8,128)(2,1)S(1)} %copy-done.1, bf16[128,4096]{1,0:T(8,128)(2,1)S(1)} %shard_map.68.refs_1_.n1_ref, ...), custom_call_target="tpu_custom_call" | custom-call | flops 49999998976 | bytes 12784128 | tf_op jit(solution)/shard_map/pallas_call | solution.py:31
  68.0 8.7 %collective-permute-done.18.refs_2_ = bf16[256,1024]{1,0:T(8,128)(2,1)S(1)} collective-permute-done((bf16[256,1024]{1,0:T(8,128)(2,1)S(1)}, bf16[256,1024]{1,0:T(8,128)(2,1)S(1)}, u32[]{:S(2)}, u32[]{:S(2)}) %collective-permute-start.18) | collective-permute-done | bytes 524320 | tf_op jit(solution)/shard_map/ppermute | solution.py:269
  76.7 5.2 %collective-permute-done.13.own1 = bf16[128,4096]{1,0:T(8,128)(2,1)S(1)} collective-permute-done((bf16[128,4096]{1,0:T(8,128)(2,1)S(1)}, bf16[128,4096]{1,0:T(8,128)(2,1)S(1)}, u32[]{:S(2)}, u32[]{:S(2)}) %collective-permute-start.13) | collective-permute-done | bytes 1048608 | tf_op jit(solution)/shard_map/ppermute | solution.py:263
  81.9 1.5 %shard_map.79 = (bf16[128,4096]{1,0:T(8,128)(2,1)}, bf16[128,4096]{1,0:T(8,128)(2,1)}) custom-call(f32[128,4096]{1,0:T(8,128)S(1)} %get-tuple-element.52.pulled, f32[128,4096]{1,0:T(8,128)S(1)} %get-tuple-element.53.base, bf16[128,4096]{1,0:T(8,128)(2,1)S(1)} %collective-permute-done.13.own1, bf16[256,1024]{1,0:T(8,128)(2,1)S(1)} %get-tuple-element.57.refs_0_, ...), custom_call_target="tpu_custom_call" | custom-call | bytes 9437184 | tf_op jit(solution)/shard_map/pallas_call | solution.py:31
  (29 shorter events, 4.4 us)
Async XLA Ops:
  0.6 10.4 %copy-start.1 = (bf16[128,4096]{1,0:T(8,128)(2,1)S(1)}, bf16[128,4096]{1,0:T(8,128)(2,1)}, u32[]{:S(2)}) copy-start(bf16[128,4096]{1,0:T(8,128)(2,1)} %p_ref.1) | copy-start | bytes 3145732
  0.6 20.5 %collective-permute-start.3 = (bf16[128,4096]{1,0:T(8,128)(2,1)}, bf16[128,4096]{1,0:T(8,128)(2,1)S(1)}, u32[]{:S(2)}, u32[]{:S(2)}) collective-permute-start(bf16[128,4096]{1,0:T(8,128)(2,1)} %p_ref.1), channel_id=1, source_target_pairs={{0,7},{1,0},{2,1},{3,2},{4,3},{5,4},{6,5},{7,6},{8,15},{9,8},{10,9... | collective-permute-start | bytes 3145736 | tf_op jit(solution)/shard_map/ppermute | solution.py:263
  5.2 0.7 copy-start.2
  7.5 22.8 %collective-permute-start = (bf16[272,1024]{1,0:T(8,128)(2,1)S(1)}, bf16[272,1024]{1,0:T(8,128)(2,1)S(1)}, u32[]{:S(2)}, u32[]{:S(2)}) collective-permute-start(bf16[272,1024]{1,0:T(8,128)(2,1)S(1)} %get-tuple-element.34), channel_id=1, source_target_pairs={{0,8},{8,0},{16,24},{24,16},{1,9},{9,1},{17,25},{25,17},{2,10},{10... | collective-permute-start | bytes 1671176 | tf_op jit(solution)/shard_map/ppermute | solution.py:269
  9.0 23.7 %collective-permute-start.1 = (bf16[272,1024]{1,0:T(8,128)(2,1)S(1)}, bf16[272,1024]{1,0:T(8,128)(2,1)S(1)}, u32[]{:S(2)}, u32[]{:S(2)}) collective-permute-start(bf16[272,1024]{1,0:T(8,128)(2,1)S(1)} %get-tuple-element.35), channel_id=1, source_target_pairs={{0,16},{8,24},{16,0},{24,8},{1,17},{9,25},{17,1},{25,9},{2,18},{10... | collective-permute-start | bytes 1671176 | tf_op jit(solution)/shard_map/ppermute | solution.py:269
  10.5 22.1 %collective-permute-start.2 = (bf16[272,1024]{1,0:T(8,128)(2,1)S(1)}, bf16[272,1024]{1,0:T(8,128)(2,1)S(1)}, u32[]{:S(2)}, u32[]{:S(2)}) collective-permute-start(bf16[272,1024]{1,0:T(8,128)(2,1)S(1)} %get-tuple-element.36), channel_id=1, source_target_pairs={{0,24},{8,16},{16,8},{24,0},{1,25},{9,17},{17,9},{25,1},{2,26},{10... | collective-permute-start | bytes 1671176 | tf_op jit(solution)/shard_map/ppermute | solution.py:269
  11.1 16.9 %copy-start = (bf16[128,4096]{1,0:T(8,128)(2,1)S(1)}, bf16[128,4096]{1,0:T(8,128)(2,1)}, u32[]{:S(2)}) copy-start(bf16[128,4096]{1,0:T(8,128)(2,1)} %q_ref.9) | copy-start | bytes 3145732
  11.1 16.8 %collective-permute-start.4 = (bf16[128,4096]{1,0:T(8,128)(2,1)S(1)}, bf16[128,4096]{1,0:T(8,128)(2,1)S(1)}, u32[]{:S(2)}, u32[]{:S(2)}) collective-permute-start(bf16[128,4096]{1,0:T(8,128)(2,1)S(1)} %shard_map.69), channel_id=1, source_target_pairs={{1,6},{3,0},{5,2},{7,4},{9,14},{11,8},{13,10},{15,12},{17,22},{19,... | collective-permute-start | bytes 3145736 | tf_op jit(solution)/shard_map/ppermute | solution.py:263
  21.2 19.5 %collective-permute-start.9 = (bf16[128,4096]{1,0:T(8,128)(2,1)S(1)}, bf16[128,4096]{1,0:T(8,128)(2,1)S(1)}, u32[]{:S(2)}, u32[]{:S(2)}) collective-permute-start(bf16[128,4096]{1,0:T(8,128)(2,1)S(1)} %shard_map.68.refs_1_.n1_ref), channel_id=1, source_target_pairs={{1,7},{3,1},{5,3},{7,5},{9,15},{11,9},{13,11},{15,13},{17,23},{19,... | collective-permute-start | bytes 3145736 | tf_op jit(solution)/shard_map/ppermute | solution.py:263
  28.1 9.6 %collective-permute-start.8 = (bf16[128,8192]{1,0:T(8,128)(2,1)S(1)}, bf16[128,8192]{1,0:T(8,128)(2,1)S(1)}, u32[]{:S(2)}, u32[]{:S(2)}) collective-permute-start(bf16[128,8192]{1,0:T(8,128)(2,1)S(1)} %shard_map.72), channel_id=1, source_target_pairs={{0,1},{1,0},{2,3},{3,2},{4,5},{5,4},{6,7},{7,6},{8,9},{9,8},{10,11... | collective-permute-start | bytes 6291464 | tf_op jit(solution)/shard_map/ppermute | solution.py:266
  34.1 6.6 %copy-start.3 = (f32[128]{0:T(128)S(1)}, f32[128]{0:T(128)}, u32[]{:S(2)}) copy-start(f32[128]{0:T(128)} %param.7) | copy-start | bytes 1540
  34.1 4.0 %collective-permute-start.5 = (f32[3,128]{1,0:T(4,128)S(1)}, f32[3,128]{1,0:T(4,128)S(1)}, u32[]{:S(2)}, u32[]{:S(2)}) collective-permute-start(f32[3,128]{1,0:T(4,128)S(1)} %get-tuple-element.40), channel_id=1, source_target_pairs={{0,8},{8,0},{16,24},{24,16},{1,9},{9,1},{17,25},{25,17},{2,10},{10... | collective-permute-start | bytes 4616 | tf_op jit(solution)/shard_map/ppermute | solution.py:269
  35.4 3.6 %collective-permute-start.6 = (f32[3,128]{1,0:T(4,128)S(1)}, f32[3,128]{1,0:T(4,128)S(1)}, u32[]{:S(2)}, u32[]{:S(2)}) collective-permute-start(f32[3,128]{1,0:T(4,128)S(1)} %get-tuple-element.41), channel_id=1, source_target_pairs={{0,16},{8,24},{16,0},{24,8},{1,17},{9,25},{17,1},{25,9},{2,18},{10... | collective-permute-start | bytes 4616 | tf_op jit(solution)/shard_map/ppermute | solution.py:269
  36.2 4.5 %collective-permute-start.7 = (f32[3,128]{1,0:T(4,128)S(1)}, f32[3,128]{1,0:T(4,128)S(1)}, u32[]{:S(2)}, u32[]{:S(2)}) collective-permute-start(f32[3,128]{1,0:T(4,128)S(1)} %get-tuple-element.42), channel_id=1, source_target_pairs={{0,24},{8,16},{16,8},{24,0},{1,25},{9,17},{17,9},{25,1},{2,26},{10... | collective-permute-start | bytes 4616 | tf_op jit(solution)/shard_map/ppermute | solution.py:269
  41.8 14.6 %collective-permute-start.12 = (bf16[128,4096]{1,0:T(8,128)(2,1)S(1)}, bf16[128,4096]{1,0:T(8,128)(2,1)S(1)}, u32[]{:S(2)}, u32[]{:S(2)}) collective-permute-start(bf16[128,4096]{1,0:T(8,128)(2,1)S(1)} %get-tuple-element.50), channel_id=1, source_target_pairs={{1,3},{3,5},{5,7},{7,1},{9,11},{11,13},{13,15},{15,9},{17,19},{19,... | collective-permute-start | bytes 3145736 | tf_op jit(solution)/shard_map/ppermute | solution.py:263
  42.6 4.4 %collective-permute-start.10 = (bf16[128,256]{1,0:T(8,128)(2,1)S(1)}, bf16[128,256]{1,0:T(8,128)(2,1)S(1)}, u32[]{:S(2)}, u32[]{:S(2)}) collective-permute-start(bf16[128,256]{1,0:T(8,128)(2,1)S(1)} %get-tuple-element.47), channel_id=1, source_target_pairs={{0,1},{1,0},{2,3},{3,2},{4,5},{5,4},{6,7},{7,6},{8,9},{9,8},{10,11... | collective-permute-start | bytes 196616 | tf_op jit(solution)/shard_map/ppermute | solution.py:266
  43.5 6.4 %collective-permute-start.14 = (f32[3,128]{1,0:T(4,128)S(1)}, f32[3,128]{1,0:T(4,128)S(1)}, u32[]{:S(2)}, u32[]{:S(2)}) collective-permute-start(f32[3,128]{1,0:T(4,128)S(1)} %get-tuple-element.55.refs_4_), channel_id=1, source_target_pairs={{0,8},{8,0},{16,24},{24,16},{1,9},{9,1},{17,25},{25,17},{2,10},{10... | collective-permute-start | bytes 4616 | tf_op jit(solution)/shard_map/ppermute | solution.py:269
  44.9 5.0 %collective-permute-start.15 = (f32[3,128]{1,0:T(4,128)S(1)}, f32[3,128]{1,0:T(4,128)S(1)}, u32[]{:S(2)}, u32[]{:S(2)}) collective-permute-start(f32[3,128]{1,0:T(4,128)S(1)} %get-tuple-element.55.refs_4_), channel_id=1, source_target_pairs={{0,16},{8,24},{16,0},{24,8},{1,17},{9,25},{17,1},{25,9},{2,18},{10... | collective-permute-start | bytes 4616 | tf_op jit(solution)/shard_map/ppermute | solution.py:269
  46.4 4.5 %collective-permute-start.16 = (f32[3,128]{1,0:T(4,128)S(1)}, f32[3,128]{1,0:T(4,128)S(1)}, u32[]{:S(2)}, u32[]{:S(2)}) collective-permute-start(f32[3,128]{1,0:T(4,128)S(1)} %get-tuple-element.55.refs_4_), channel_id=1, source_target_pairs={{0,24},{8,16},{16,8},{24,0},{1,25},{9,17},{17,9},{25,1},{2,26},{10... | collective-permute-start | bytes 4616 | tf_op jit(solution)/shard_map/ppermute | solution.py:269
  47.5 18.8 %collective-permute-start.11 = (bf16[128,4096]{1,0:T(8,128)(2,1)S(1)}, bf16[128,4096]{1,0:T(8,128)(2,1)S(1)}, u32[]{:S(2)}, u32[]{:S(2)}) collective-permute-start(bf16[128,4096]{1,0:T(8,128)(2,1)S(1)} %get-tuple-element.48), channel_id=1, source_target_pairs={{0,3},{2,5},{4,7},{6,1},{8,11},{10,13},{12,15},{14,9},{16,19},{18,... | collective-permute-start | bytes 3145736 | tf_op jit(solution)/shard_map/ppermute | solution.py:263
  53.0 15.0 %collective-permute-start.17 = (bf16[256,1024]{1,0:T(8,128)(2,1)S(1)}, bf16[256,1024]{1,0:T(8,128)(2,1)S(1)}, u32[]{:S(2)}, u32[]{:S(2)}) collective-permute-start(bf16[256,1024]{1,0:T(8,128)(2,1)S(1)} %get-tuple-element.58), channel_id=1, source_target_pairs={{0,8},{8,0},{16,24},{24,16},{1,9},{9,1},{17,25},{25,17},{2,10},{10... | collective-permute-start | bytes 1572872 | tf_op jit(solution)/shard_map/ppermute | solution.py:269
  53.5 23.2 %collective-permute-start.18 = (bf16[256,1024]{1,0:T(8,128)(2,1)S(1)}, bf16[256,1024]{1,0:T(8,128)(2,1)S(1)}, u32[]{:S(2)}, u32[]{:S(2)}) collective-permute-start(bf16[256,1024]{1,0:T(8,128)(2,1)S(1)} %get-tuple-element.59), channel_id=1, source_target_pairs={{0,16},{8,24},{16,0},{24,8},{1,17},{9,25},{17,1},{25,9},{2,18},{10... | collective-permute-start | bytes 1572872 | tf_op jit(solution)/shard_map/ppermute | solution.py:269
  54.9 21.8 %collective-permute-start.19 = (bf16[256,1024]{1,0:T(8,128)(2,1)S(1)}, bf16[256,1024]{1,0:T(8,128)(2,1)S(1)}, u32[]{:S(2)}, u32[]{:S(2)}) collective-permute-start(bf16[256,1024]{1,0:T(8,128)(2,1)S(1)} %get-tuple-element.60), channel_id=1, source_target_pairs={{0,24},{8,16},{16,8},{24,0},{1,25},{9,17},{17,9},{25,1},{2,26},{10... | collective-permute-start | bytes 1572872 | tf_op jit(solution)/shard_map/ppermute | solution.py:269
  56.7 25.2 %collective-permute-start.13 = (bf16[128,4096]{1,0:T(8,128)(2,1)S(1)}, bf16[128,4096]{1,0:T(8,128)(2,1)S(1)}, u32[]{:S(2)}, u32[]{:S(2)}) collective-permute-start(bf16[128,4096]{1,0:T(8,128)(2,1)S(1)} %get-tuple-element.54), channel_id=1, source_target_pairs={{1,2},{3,4},{5,6},{7,0},{9,10},{11,12},{13,14},{15,8},{17,18},{19,... | collective-permute-start | bytes 3145736 | tf_op jit(solution)/shard_map/ppermute | solution.py:263

commit v2 on v1

--- a/solution.py
+++ b/solution.py
@@ -13,7 +13,7 @@
 F32 = jnp.float32
 CHUNK = 512
 TAIL = 16
-LONG, SOME = 5 * 10**10, 16 * 10**9
+LONG, SOME = 5 * 10**10, 10 * 10**9
 VMEM = pl.BlockSpec(memory_space=pltpu.VMEM)
 HBM = pl.BlockSpec(memory_space=pltpu.HBM)
 TOKEN = jax.ShapeDtypeStruct((8, 128), F32)
@@ -87,7 +87,7 @@
 
 
 def hard_scores_body(groups, *refs):
-    pieces, outs = refs[:groups], refs[groups + 1 :]
+    pieces, outs = refs[:groups][::-1], refs[groups + 1 :]
     rows = outs[0].shape[1]
     ids = lax.broadcasted_iota(jnp.int32, (groups * rows, rows), 0)
     p_all = jnp.concatenate([piece[rows : 2 * rows] for piece in pieces], axis=0)
@@ -100,7 +100,7 @@
 
 
 def hard_grads_body(groups, *refs):
-    pieces, coefs, outs = refs[:groups], refs[groups : 2 * groups], refs[2 * groups + 1 : 3 * groups + 1]
+    coefs, pieces, outs = refs[:groups][::-1], refs[groups : 2 * groups][::-1], refs[2 * groups + 1 : 3 * groups + 1]
     token, matrix, matrix_t = refs[3 * groups + 1 :]
     rows = coefs[0].shape[1]
     cols = outs[0].shape[1]
@@ -165,8 +165,8 @@
     w = w_ref[...]
     s3 = INV_TEMP * (s3_ref[...] + dot(last_ref[...], q_ref[...], ((1,), (1,))))
     scores = [INV_TEMP * s0_ref[...], INV_TEMP * s1_ref[...], INV_TEMP * s2_ref[...], s3]
-    hard = parts[0][...]
-    for other in parts[1:]:
+    hard = parts[-1][...]
+    for other in parts[-2::-1]:
         hard = hard + other[...]
     hard = INV_TEMP * hard
     largest = jnp.max(hard, axis=0, keepdims=True)
@@ -234,7 +234,7 @@
 
 
 def finish_body(groups, pulled, base, own1, *refs):
-    backs = refs[:groups]
+    backs = refs[:groups][::-1]
     q_out, p_out, q_held, p_held, sems = refs[groups:]
     rows, cols = pulled.shape[0], backs[0].shape[1]
     g = lax.axis_index("grp")
@@ -301,14 +301,14 @@
 
     s0, s1, s3 = local_call(scores_body, [square] * 3, queries, passages, next1, next3_even)
     parts = local_call(
-        functools.partial(hard_scores_body, groups), [triple] * groups, *pieces, s0, flops=LONG
+        functools.partial(hard_scores_body, groups), [triple] * groups, *pieces[::-1], s0, flops=LONG
     )
     (s2,) = local_call(last_score_body, [square], queries, pair)
     parts = exchange(parts)
     loss_rows, coef, hard_coef, to_core, term3 = local_call(
         functools.partial(weigh_body, groups),
         [like(1, rows, dtype=F32), like(rows, 4 * rows), triple, like(rows, 2 * rows), block],
-        *parts, queries, s0, s1, s2, s3, next3_odd, weights[None, :],
+        *parts[::-1], queries, s0, s1, s2, s3, next3_odd, weights[None, :],
     )
 
     got3 = shift(term3, 2, (1,))
@@ -322,7 +322,7 @@
     square_all = pltpu.VMEM((groups * rows, groups * rows), BF16)
     *backs, token = local_call(
         functools.partial(hard_grads_body, groups), [back] * groups + [TOKEN],
-        *pieces, *hard_coefs, token, scratch=[square_all, square_all],
+        *hard_coefs[::-1], *pieces[::-1], token, scratch=[square_all, square_all],
     )
     backs = exchange(backs)
 
@@ -335,7 +335,7 @@
         weights[None, :], own3, token, flops=LONG, scratch=[pltpu.VMEM((rows, 5 * rows), BF16)],
     )
     grad_queries, grad_passages = local_call(
-        functools.partial(finish_body, groups), [block, block], pulled, base, own1, *backs,
+        functools.partial(finish_body, groups), [block, block], pulled, base, own1, *backs[::-1],
         out_specs=[HBM, HBM],
         scratch=[
             pltpu.VMEM((rows, width), BF16),

time: 83.6 us -> 83.6 us (level)
  waiting for transfers between devices: 42.9 us -> 41.5 us
  starting transfers between devices: 27.3 us -> 28.6 us
    ppermute x6, waiting for transfers between devices: 28.1 us -> 21.1 us  [shift(): return lax.ppermute(array, 'blk', pairs)]
    ppermute x12, waiting for transfers between devices: 14.7 us -> 19.5 us  [over_groups(): return lax.ppermute(array, 'grp', [(i, i ^ r) for i in range(groups)])]
    ppermute x6, starting transfers between devices: 11.1 us -> 12.2 us  [shift(): return lax.ppermute(array, 'blk', pairs)]
    ppermute x2, waiting for transfers between devices: 0.01 us -> 0.9 us  [swap(): return lax.ppermute(array, 'blk', [(i, i ^ 1) for i in range(loop)])]
  transfers between devices with their start and end apart: 20 -> 20, of which waited for: 9 -> 15; matrix products, arithmetic and copies ran while one was open for 0% -> 0% of each run, Pallas kernels for 11% -> 11%
where the time goes in v2:
time: 83.6 us; the launch traced here: 83.4 us
  waiting for transfers between devices  41.5 us (50%)
  starting transfers between devices  28.6 us (34%)
  Pallas kernels  11.8 us (14%)
    ppermute x6, waiting for transfers between devices, shift(): return lax.ppermute(array, 'blk', pairs)  21.1 us
    ppermute x12, waiting for transfers between devices, over_groups(): return lax.ppermute(array, 'grp', [(i, i ^ r) for i in range(groups)])  19.5 us
    ppermute x12, starting transfers between devices, over_groups(): return lax.ppermute(array, 'grp', [(i, i ^ r) for i in range(groups)])  14.1 us
    ppermute x6, starting transfers between devices, shift(): return lax.ppermute(array, 'blk', pairs)  12.2 us
    pallas_call x13, Pallas kernels, local_call(): pl.pallas_call(body, out_shape=out_shape, in_specs=in_specs or [VMEM] * l...  11.8 us
    ppermute x2, starting transfers between devices, swap(): return lax.ppermute(array, 'blk', [(i, i ^ 1) for i in range(loop)])  2.24 us
  transfers between devices with their start and end apart: 20, of which 15 were waited for; matrix products, arithmetic and copies ran while one was open for 0% of the time, Pallas kernels for 11%

profile of v2, /device:TPU:0, one launch (start us, length us, event | category | flops | bytes accessed | tf_op | source)
XLA Modules:
  0.0 83.4 jit_solution(16856865570021045914)
XLA Ops:
  0.6 4.5 %collective-permute-start.3 = (bf16[128,4096]{1,0:T(8,128)(2,1)}, bf16[128,4096]{1,0:T(8,128)(2,1)S(1)}, u32[]{:S(2)}, u32[]{:S(2)}) collective-permute-start(bf16[128,4096]{1,0:T(8,128)(2,1)} %p_ref.1), channel_id=1, source_target_pairs={{0,7},{1,0},{2,1},{3,2},{4,3},{5,4},{6,5},{7,6},{8,15},{9,8},{10,9... | collective-permute-start | bytes 3145736 | tf_op jit(solution)/shard_map/ppermute | solution.py:263
  5.9 1.6 %shard_map.67 = (bf16[272,1024]{1,0:T(8,128)(2,1)S(1)}, bf16[272,1024]{1,0:T(8,128)(2,1)S(1)}, bf16[272,1024]{1,0:T(8,128)(2,1)S(1)}, bf16[272,1024]{1,0:T(8,128)(2,1)S(1)}, f32[8,128]{1,0:T(8,128)S(1)}) custom-call(bf16[128,4096]{1,0:T(8,128)(2,1)} %q_ref.9, bf16[128,4096]{1,0:T(8,128)(2,1)} %p_ref.1, s32[3,128]{1,0:T(4,128)S(1)} %bitcast.3), custom_call_target="tpu_custom_call" | custom-call | bytes 4331008 | tf_op jit(solution)/shard_map/pallas_call | solution.py:31
  7.5 2.5 %collective-permute-start = (bf16[272,1024]{1,0:T(8,128)(2,1)S(1)}, bf16[272,1024]{1,0:T(8,128)(2,1)S(1)}, u32[]{:S(2)}, u32[]{:S(2)}) collective-permute-start(bf16[272,1024]{1,0:T(8,128)(2,1)S(1)} %get-tuple-element.33), channel_id=1, source_target_pairs={{0,24},{8,16},{16,8},{24,0},{1,25},{9,17},{17,9},{25,1},{2,26},{10... | collective-permute-start | bytes 1671176 | tf_op jit(solution)/shard_map/ppermute | solution.py:269
  11.1 1.4 %collective-permute-start.4 = (bf16[128,4096]{1,0:T(8,128)(2,1)S(1)}, bf16[128,4096]{1,0:T(8,128)(2,1)S(1)}, u32[]{:S(2)}, u32[]{:S(2)}) collective-permute-start(bf16[128,4096]{1,0:T(8,128)(2,1)S(1)} %shard_map.69), channel_id=1, source_target_pairs={{1,6},{3,0},{5,2},{7,4},{9,14},{11,8},{13,10},{15,12},{17,22},{19,... | collective-permute-start | bytes 3145736 | tf_op jit(solution)/shard_map/ppermute | solution.py:263
  12.5 8.6 %collective-permute-done.3.source = bf16[128,4096]{1,0:T(8,128)(2,1)S(1)} collective-permute-done((bf16[128,4096]{1,0:T(8,128)(2,1)}, bf16[128,4096]{1,0:T(8,128)(2,1)S(1)}, u32[]{:S(2)}, u32[]{:S(2)}) %collective-permute-start.3) | collective-permute-done | bytes 1048608 | tf_op jit(solution)/shard_map/ppermute | solution.py:263
  21.2 0.7 collective-permute-start.9
  22.0 6.0 %collective-permute-done.4.refs_2_.e3_ref = bf16[128,4096]{1,0:T(8,128)(2,1)S(1)} collective-permute-done((bf16[128,4096]{1,0:T(8,128)(2,1)S(1)}, bf16[128,4096]{1,0:T(8,128)(2,1)S(1)}, u32[]{:S(2)}, u32[]{:S(2)}) %collective-permute-start.4) | collective-permute-done | bytes 1048608 | tf_op jit(solution)/shard_map/ppermute | solution.py:263
  28.1 1.2 %collective-permute-start.8 = (bf16[128,8192]{1,0:T(8,128)(2,1)S(1)}, bf16[128,8192]{1,0:T(8,128)(2,1)S(1)}, u32[]{:S(2)}, u32[]{:S(2)}) collective-permute-start(bf16[128,8192]{1,0:T(8,128)(2,1)S(1)} %shard_map.72), channel_id=1, source_target_pairs={{0,1},{1,0},{2,3},{3,2},{4,5},{5,4},{6,7},{7,6},{8,9},{9,8},{10,11... | collective-permute-start | bytes 6291464 | tf_op jit(solution)/shard_map/ppermute | solution.py:266
  29.3 1.0 %shard_map.70 = (f32[128,128]{1,0:T(8,128)S(1)}, f32[128,128]{1,0:T(8,128)S(1)}, f32[128,128]{1,0:T(8,128)S(1)}) custom-call(bf16[128,4096]{1,0:T(8,128)(2,1)S(1)} %copy-done, bf16[128,4096]{1,0:T(8,128)(2,1)S(1)} %copy-done.1, bf16[128,4096]{1,0:T(8,128)(2,1)S(1)} %shard_map.68.refs_1_.n1_ref, bf16[128,4096]{1,0:T(8,128)(2,1)S(1)} %collective-permute-done.4.refs_2_.e3_ref), custom_call_target="tpu_custom_call" | custom-call | bytes 4390912 | tf_op jit(solution)/shard_map/pallas_call | solution.py:31
  30.3 1.9 %collective-permute-done.1.refs_1_.refs_5_ = bf16[272,1024]{1,0:T(8,128)(2,1)S(1)} collective-permute-done((bf16[272,1024]{1,0:T(8,128)(2,1)S(1)}, bf16[272,1024]{1,0:T(8,128)(2,1)S(1)}, u32[]{:S(2)}, u32[]{:S(2)}) %collective-permute-start.1) | collective-permute-done | bytes 557088 | tf_op jit(solution)/shard_map/ppermute | solution.py:269
  32.5 1.4 %shard_map.71 = (f32[3,128]{1,0:T(4,128)S(1)}, f32[3,128]{1,0:T(4,128)S(1)}, f32[3,128]{1,0:T(4,128)S(1)}, f32[3,128]{1,0:T(4,128)S(1)}) custom-call(bf16[272,1024]{1,0:T(8,128)(2,1)S(1)} %collective-permute-done.refs_0_.refs_4_, bf16[272,1024]{1,0:T(8,128)(2,1)S(1)} %collective-permute-done.1.refs_1_.refs_5_, ...), custom_call_target="tpu_custom_call" | custom-call | flops 49999998976 | bytes 2299904 | tf_op jit(solution)/shard_map/pallas_call | solution.py:31
  33.9 1.6 %collective-permute-start.5 = (f32[3,128]{1,0:T(4,128)S(1)}, f32[3,128]{1,0:T(4,128)S(1)}, u32[]{:S(2)}, u32[]{:S(2)}) collective-permute-start(f32[3,128]{1,0:T(4,128)S(1)} %get-tuple-element.39), channel_id=1, source_target_pairs={{0,24},{8,16},{16,8},{24,0},{1,25},{9,17},{17,9},{25,1},{2,26},{10... | collective-permute-start | bytes 4616 | tf_op jit(solution)/shard_map/ppermute | solution.py:269
  35.5 1.4 %collective-permute-start.6 = (f32[3,128]{1,0:T(4,128)S(1)}, f32[3,128]{1,0:T(4,128)S(1)}, u32[]{:S(2)}, u32[]{:S(2)}) collective-permute-start(f32[3,128]{1,0:T(4,128)S(1)} %get-tuple-element.40), channel_id=1, source_target_pairs={{0,16},{8,24},{16,0},{24,8},{1,17},{9,25},{17,1},{25,9},{2,18},{10... | collective-permute-start | bytes 4616 | tf_op jit(solution)/shard_map/ppermute | solution.py:269
  39.1 1.4 %collective-permute-done.7.refs_2_ = f32[3,128]{1,0:T(4,128)S(1)} collective-permute-done((f32[3,128]{1,0:T(4,128)S(1)}, f32[3,128]{1,0:T(4,128)S(1)}, u32[]{:S(2)}, u32[]{:S(2)}) %collective-permute-start.7) | collective-permute-done | bytes 1568 | tf_op jit(solution)/shard_map/ppermute | solution.py:269
  40.5 1.1 %shard_map.74 = (f32[1,128]{1,0:T(1,128)}, bf16[128,512]{1,0:T(8,128)(2,1)S(1)}, f32[3,128]{1,0:T(4,128)S(1)}, bf16[128,256]{1,0:T(8,128)(2,1)S(1)}, bf16[128,4096]{1,0:T(8,128)(2,1)S(1)}) custom-call(f32[3,128]{1,0:T(4,128)S(1)} %collective-permute-done.5.refs_0_, f32[3,128]{1,0:T(4,128)S(1)} %collective-permute-done.6.refs_1_, ...), custom_call_target="tpu_custom_call" | custom-call | bytes 3613184 | tf_op jit(solution)/shard_map/pallas_call | solution.py:31
  41.6 0.7 collective-permute-start.12
  42.3 1.1 %collective-permute-start.10 = (bf16[128,256]{1,0:T(8,128)(2,1)S(1)}, bf16[128,256]{1,0:T(8,128)(2,1)S(1)}, u32[]{:S(2)}, u32[]{:S(2)}) collective-permute-start(bf16[128,256]{1,0:T(8,128)(2,1)S(1)} %get-tuple-element.47), channel_id=1, source_target_pairs={{0,1},{1,0},{2,3},{3,2},{4,5},{5,4},{6,7},{7,6},{8,9},{9,8},{10,11... | collective-permute-start | bytes 196616 | tf_op jit(solution)/shard_map/ppermute | solution.py:266
  43.4 0.9 %collective-permute-done.10.swap_ref = bf16[128,256]{1,0:T(8,128)(2,1)S(1)} collective-permute-done((bf16[128,256]{1,0:T(8,128)(2,1)S(1)}, bf16[128,256]{1,0:T(8,128)(2,1)S(1)}, u32[]{:S(2)}, u32[]{:S(2)}) %collective-permute-start.10) | collective-permute-done | bytes 65568 | tf_op jit(solution)/shard_map/ppermute | solution.py:266
  44.8 3.5 %collective-permute-start.11 = (bf16[128,4096]{1,0:T(8,128)(2,1)S(1)}, bf16[128,4096]{1,0:T(8,128)(2,1)S(1)}, u32[]{:S(2)}, u32[]{:S(2)}) collective-permute-start(bf16[128,4096]{1,0:T(8,128)(2,1)S(1)} %get-tuple-element.48), channel_id=1, source_target_pairs={{0,3},{2,5},{4,7},{6,1},{8,11},{10,13},{12,15},{14,9},{16,19},{18,... | collective-permute-start | bytes 3145736 | tf_op jit(solution)/shard_map/ppermute | solution.py:263
  48.3 2.5 %collective-permute-start.14 = (f32[3,128]{1,0:T(4,128)S(1)}, f32[3,128]{1,0:T(4,128)S(1)}, u32[]{:S(2)}, u32[]{:S(2)}) collective-permute-start(f32[3,128]{1,0:T(4,128)S(1)} %get-tuple-element.55.refs_3_), channel_id=1, source_target_pairs={{0,24},{8,16},{16,8},{24,0},{1,25},{9,17},{17,9},{25,1},{2,26},{10... | collective-permute-start | bytes 4616 | tf_op jit(solution)/shard_map/ppermute | solution.py:269
  51.8 1.0 %collective-permute-done.14.refs_0_ = f32[3,128]{1,0:T(4,128)S(1)} collective-permute-done((f32[3,128]{1,0:T(4,128)S(1)}, f32[3,128]{1,0:T(4,128)S(1)}, u32[]{:S(2)}, u32[]{:S(2)}) %collective-permute-start.14) | collective-permute-done | bytes 1568 | tf_op jit(solution)/shard_map/ppermute | solution.py:269
  52.8 1.5 %collective-permute-done.15.refs_1_ = f32[3,128]{1,0:T(4,128)S(1)} collective-permute-done((f32[3,128]{1,0:T(4,128)S(1)}, f32[3,128]{1,0:T(4,128)S(1)}, u32[]{:S(2)}, u32[]{:S(2)}) %collective-permute-start.15) | collective-permute-done | bytes 1568 | tf_op jit(solution)/shard_map/ppermute | solution.py:269
  54.9 2.1 %shard_map.78 = (bf16[256,1024]{1,0:T(8,128)(2,1)S(1)}, bf16[256,1024]{1,0:T(8,128)(2,1)S(1)}, bf16[256,1024]{1,0:T(8,128)(2,1)S(1)}, bf16[256,1024]{1,0:T(8,128)(2,1)S(1)}, f32[8,128]{1,0:T(8,128)}) custom-call(f32[3,128]{1,0:T(4,128)S(1)} %collective-permute-done.14.refs_0_, f32[3,128]{1,0:T(4,128)S(1)} %collective-permute-done.15.refs_1_, ...), custom_call_target="tpu_custom_call" | custom-call | bytes 4339712 | tf_op jit(solution)/shard_map/pallas_call | solution.py:31
  57.0 1.5 %collective-permute-start.17 = (bf16[256,1024]{1,0:T(8,128)(2,1)S(1)}, bf16[256,1024]{1,0:T(8,128)(2,1)S(1)}, u32[]{:S(2)}, u32[]{:S(2)}) collective-permute-start(bf16[256,1024]{1,0:T(8,128)(2,1)S(1)} %get-tuple-element.57), channel_id=1, source_target_pairs={{0,24},{8,16},{16,8},{24,0},{1,25},{9,17},{17,9},{25,1},{2,26},{10... | collective-permute-start | bytes 1572872 | tf_op jit(solution)/shard_map/ppermute | solution.py:269
  58.9 1.6 %collective-permute-start.19 = (bf16[256,1024]{1,0:T(8,128)(2,1)S(1)}, bf16[256,1024]{1,0:T(8,128)(2,1)S(1)}, u32[]{:S(2)}, u32[]{:S(2)}) collective-permute-start(bf16[256,1024]{1,0:T(8,128)(2,1)S(1)} %get-tuple-element.59), channel_id=1, source_target_pairs={{0,8},{8,0},{16,24},{24,16},{1,9},{9,1},{17,25},{25,17},{2,10},{10... | collective-permute-start | bytes 1572872 | tf_op jit(solution)/shard_map/ppermute | solution.py:269
  60.8 1.3 %collective-permute-start.13 = (bf16[128,4096]{1,0:T(8,128)(2,1)S(1)}, bf16[128,4096]{1,0:T(8,128)(2,1)S(1)}, u32[]{:S(2)}, u32[]{:S(2)}) collective-permute-start(bf16[128,4096]{1,0:T(8,128)(2,1)S(1)} %get-tuple-element.54), channel_id=1, source_target_pairs={{1,2},{3,4},{5,6},{7,0},{9,10},{11,12},{13,14},{15,8},{17,18},{19,... | collective-permute-start | bytes 3145736 | tf_op jit(solution)/shard_map/ppermute | solution.py:263
  62.1 4.1 %collective-permute-done.11.own3_ref = bf16[128,4096]{1,0:T(8,128)(2,1)S(1)} collective-permute-done((bf16[128,4096]{1,0:T(8,128)(2,1)S(1)}, bf16[128,4096]{1,0:T(8,128)(2,1)S(1)}, u32[]{:S(2)}, u32[]{:S(2)}) %collective-permute-start.11) | collective-permute-done | bytes 1048608 | tf_op jit(solution)/shard_map/ppermute | solution.py:263
  66.2 1.6 %shard_map.77 = (f32[128,4096]{1,0:T(8,128)S(1)}, f32[128,4096]{1,0:T(8,128)S(1)}) custom-call(bf16[128,4096]{1,0:T(8,128)(2,1)S(1)} %copy-done, bf16[128,8192]{1,0:T(8,128)(2,1)S(1)} %collective-permute-done.8.pair_ref, bf16[128,4096]{1,0:T(8,128)(2,1)S(1)} %copy-done.1, bf16[128,4096]{1,0:T(8,128)(2,1)S(1)} %shard_map.68.refs_1_.n1_ref, ...), custom_call_target="tpu_custom_call" | custom-call | flops 49999998976 | bytes 12784128 | tf_op jit(solution)/shard_map/pallas_call | solution.py:31
  67.8 4.9 %collective-permute-done.17.refs_0_ = bf16[256,1024]{1,0:T(8,128)(2,1)S(1)} collective-permute-done((bf16[256,1024]{1,0:T(8,128)(2,1)S(1)}, bf16[256,1024]{1,0:T(8,128)(2,1)S(1)}, u32[]{:S(2)}, u32[]{:S(2)}) %collective-permute-start.17) | collective-permute-done | bytes 524320 | tf_op jit(solution)/shard_map/ppermute | solution.py:269
  72.8 6.6 %collective-permute-done.18.refs_1_ = bf16[256,1024]{1,0:T(8,128)(2,1)S(1)} collective-permute-done((bf16[256,1024]{1,0:T(8,128)(2,1)S(1)}, bf16[256,1024]{1,0:T(8,128)(2,1)S(1)}, u32[]{:S(2)}, u32[]{:S(2)}) %collective-permute-start.18) | collective-permute-done | bytes 524320 | tf_op jit(solution)/shard_map/ppermute | solution.py:269
  79.4 2.4 %collective-permute-done.13.own1 = bf16[128,4096]{1,0:T(8,128)(2,1)S(1)} collective-permute-done((bf16[128,4096]{1,0:T(8,128)(2,1)S(1)}, bf16[128,4096]{1,0:T(8,128)(2,1)S(1)}, u32[]{:S(2)}, u32[]{:S(2)}) %collective-permute-start.13) | collective-permute-done | bytes 1048608 | tf_op jit(solution)/shard_map/ppermute | solution.py:263
  81.9 1.5 %shard_map.79 = (bf16[128,4096]{1,0:T(8,128)(2,1)}, bf16[128,4096]{1,0:T(8,128)(2,1)}) custom-call(f32[128,4096]{1,0:T(8,128)S(1)} %get-tuple-element.52.pulled, f32[128,4096]{1,0:T(8,128)S(1)} %get-tuple-element.53.base, bf16[128,4096]{1,0:T(8,128)(2,1)S(1)} %collective-permute-done.13.own1, bf16[256,1024]{1,0:T(8,128)(2,1)S(1)} %collective-permute-done.17.refs_0_, ...), custom_call_target="tpu_custom_call" | custom-call | bytes 9437184 | tf_op jit(solution)/shard_map/pallas_call | solution.py:31
  (29 shorter events, 7.3 us)
Async XLA Ops:
  0.6 10.4 %copy-start.1 = (bf16[128,4096]{1,0:T(8,128)(2,1)S(1)}, bf16[128,4096]{1,0:T(8,128)(2,1)}, u32[]{:S(2)}) copy-start(bf16[128,4096]{1,0:T(8,128)(2,1)} %p_ref.1) | copy-start | bytes 3145732
  0.6 20.5 %collective-permute-start.3 = (bf16[128,4096]{1,0:T(8,128)(2,1)}, bf16[128,4096]{1,0:T(8,128)(2,1)S(1)}, u32[]{:S(2)}, u32[]{:S(2)}) collective-permute-start(bf16[128,4096]{1,0:T(8,128)(2,1)} %p_ref.1), channel_id=1, source_target_pairs={{0,7},{1,0},{2,1},{3,2},{4,3},{5,4},{6,5},{7,6},{8,15},{9,8},{10,9... | collective-permute-start | bytes 3145736 | tf_op jit(solution)/shard_map/ppermute | solution.py:263
  5.2 0.7 copy-start.2
  7.5 22.8 %collective-permute-start = (bf16[272,1024]{1,0:T(8,128)(2,1)S(1)}, bf16[272,1024]{1,0:T(8,128)(2,1)S(1)}, u32[]{:S(2)}, u32[]{:S(2)}) collective-permute-start(bf16[272,1024]{1,0:T(8,128)(2,1)S(1)} %get-tuple-element.33), channel_id=1, source_target_pairs={{0,24},{8,16},{16,8},{24,0},{1,25},{9,17},{17,9},{25,1},{2,26},{10... | collective-permute-start | bytes 1671176 | tf_op jit(solution)/shard_map/ppermute | solution.py:269
  10.0 22.2 %collective-permute-start.1 = (bf16[272,1024]{1,0:T(8,128)(2,1)S(1)}, bf16[272,1024]{1,0:T(8,128)(2,1)S(1)}, u32[]{:S(2)}, u32[]{:S(2)}) collective-permute-start(bf16[272,1024]{1,0:T(8,128)(2,1)S(1)} %get-tuple-element.34), channel_id=1, source_target_pairs={{0,16},{8,24},{16,0},{24,8},{1,17},{9,25},{17,1},{25,9},{2,18},{10... | collective-permute-start | bytes 1671176 | tf_op jit(solution)/shard_map/ppermute | solution.py:269
  10.5 22.0 %collective-permute-start.2 = (bf16[272,1024]{1,0:T(8,128)(2,1)S(1)}, bf16[272,1024]{1,0:T(8,128)(2,1)S(1)}, u32[]{:S(2)}, u32[]{:S(2)}) collective-permute-start(bf16[272,1024]{1,0:T(8,128)(2,1)S(1)} %get-tuple-element.35), channel_id=1, source_target_pairs={{0,8},{8,0},{16,24},{24,16},{1,9},{9,1},{17,25},{25,17},{2,10},{10... | collective-permute-start | bytes 1671176 | tf_op jit(solution)/shard_map/ppermute | solution.py:269
  11.1 16.9 %copy-start = (bf16[128,4096]{1,0:T(8,128)(2,1)S(1)}, bf16[128,4096]{1,0:T(8,128)(2,1)}, u32[]{:S(2)}) copy-start(bf16[128,4096]{1,0:T(8,128)(2,1)} %q_ref.9) | copy-start | bytes 3145732
  11.1 16.8 %collective-permute-start.4 = (bf16[128,4096]{1,0:T(8,128)(2,1)S(1)}, bf16[128,4096]{1,0:T(8,128)(2,1)S(1)}, u32[]{:S(2)}, u32[]{:S(2)}) collective-permute-start(bf16[128,4096]{1,0:T(8,128)(2,1)S(1)} %shard_map.69), channel_id=1, source_target_pairs={{1,6},{3,0},{5,2},{7,4},{9,14},{11,8},{13,10},{15,12},{17,22},{19,... | collective-permute-start | bytes 3145736 | tf_op jit(solution)/shard_map/ppermute | solution.py:263
  21.2 19.3 %collective-permute-start.9 = (bf16[128,4096]{1,0:T(8,128)(2,1)S(1)}, bf16[128,4096]{1,0:T(8,128)(2,1)S(1)}, u32[]{:S(2)}, u32[]{:S(2)}) collective-permute-start(bf16[128,4096]{1,0:T(8,128)(2,1)S(1)} %shard_map.68.refs_1_.n1_ref), channel_id=1, source_target_pairs={{1,7},{3,1},{5,3},{7,5},{9,15},{11,9},{13,11},{15,13},{17,23},{19,... | collective-permute-start | bytes 3145736 | tf_op jit(solution)/shard_map/ppermute | solution.py:263
  28.1 9.4 %collective-permute-start.8 = (bf16[128,8192]{1,0:T(8,128)(2,1)S(1)}, bf16[128,8192]{1,0:T(8,128)(2,1)S(1)}, u32[]{:S(2)}, u32[]{:S(2)}) collective-permute-start(bf16[128,8192]{1,0:T(8,128)(2,1)S(1)} %shard_map.72), channel_id=1, source_target_pairs={{0,1},{1,0},{2,3},{3,2},{4,5},{5,4},{6,7},{7,6},{8,9},{9,8},{10,11... | collective-permute-start | bytes 6291464 | tf_op jit(solution)/shard_map/ppermute | solution.py:266
  33.9 6.6 %copy-start.3 = (f32[128]{0:T(128)S(1)}, f32[128]{0:T(128)}, u32[]{:S(2)}) copy-start(f32[128]{0:T(128)} %param.7) | copy-start | bytes 1540
  33.9 4.5 %collective-permute-start.5 = (f32[3,128]{1,0:T(4,128)S(1)}, f32[3,128]{1,0:T(4,128)S(1)}, u32[]{:S(2)}, u32[]{:S(2)}) collective-permute-start(f32[3,128]{1,0:T(4,128)S(1)} %get-tuple-element.39), channel_id=1, source_target_pairs={{0,24},{8,16},{16,8},{24,0},{1,25},{9,17},{17,9},{25,1},{2,26},{10... | collective-permute-start | bytes 4616 | tf_op jit(solution)/shard_map/ppermute | solution.py:269
  35.5 3.6 %collective-permute-start.6 = (f32[3,128]{1,0:T(4,128)S(1)}, f32[3,128]{1,0:T(4,128)S(1)}, u32[]{:S(2)}, u32[]{:S(2)}) collective-permute-start(f32[3,128]{1,0:T(4,128)S(1)} %get-tuple-element.40), channel_id=1, source_target_pairs={{0,16},{8,24},{16,0},{24,8},{1,17},{9,25},{17,1},{25,9},{2,18},{10... | collective-permute-start | bytes 4616 | tf_op jit(solution)/shard_map/ppermute | solution.py:269
  36.9 3.6 %collective-permute-start.7 = (f32[3,128]{1,0:T(4,128)S(1)}, f32[3,128]{1,0:T(4,128)S(1)}, u32[]{:S(2)}, u32[]{:S(2)}) collective-permute-start(f32[3,128]{1,0:T(4,128)S(1)} %get-tuple-element.41), channel_id=1, source_target_pairs={{0,8},{8,0},{16,24},{24,16},{1,9},{9,1},{17,25},{25,17},{2,10},{10... | collective-permute-start | bytes 4616 | tf_op jit(solution)/shard_map/ppermute | solution.py:269
  41.6 18.9 %collective-permute-start.12 = (bf16[128,4096]{1,0:T(8,128)(2,1)S(1)}, bf16[128,4096]{1,0:T(8,128)(2,1)S(1)}, u32[]{:S(2)}, u32[]{:S(2)}) collective-permute-start(bf16[128,4096]{1,0:T(8,128)(2,1)S(1)} %get-tuple-element.50), channel_id=1, source_target_pairs={{1,3},{3,5},{5,7},{7,1},{9,11},{11,13},{13,15},{15,9},{17,19},{19,... | collective-permute-start | bytes 3145736 | tf_op jit(solution)/shard_map/ppermute | solution.py:263
  42.3 2.0 %collective-permute-start.10 = (bf16[128,256]{1,0:T(8,128)(2,1)S(1)}, bf16[128,256]{1,0:T(8,128)(2,1)S(1)}, u32[]{:S(2)}, u32[]{:S(2)}) collective-permute-start(bf16[128,256]{1,0:T(8,128)(2,1)S(1)} %get-tuple-element.47), channel_id=1, source_target_pairs={{0,1},{1,0},{2,3},{3,2},{4,5},{5,4},{6,7},{7,6},{8,9},{9,8},{10,11... | collective-permute-start | bytes 196616 | tf_op jit(solution)/shard_map/ppermute | solution.py:266
  44.8 21.4 %collective-permute-start.11 = (bf16[128,4096]{1,0:T(8,128)(2,1)S(1)}, bf16[128,4096]{1,0:T(8,128)(2,1)S(1)}, u32[]{:S(2)}, u32[]{:S(2)}) collective-permute-start(bf16[128,4096]{1,0:T(8,128)(2,1)S(1)} %get-tuple-element.48), channel_id=1, source_target_pairs={{0,3},{2,5},{4,7},{6,1},{8,11},{10,13},{12,15},{14,9},{16,19},{18,... | collective-permute-start | bytes 3145736 | tf_op jit(solution)/shard_map/ppermute | solution.py:263
  48.3 4.5 %collective-permute-start.14 = (f32[3,128]{1,0:T(4,128)S(1)}, f32[3,128]{1,0:T(4,128)S(1)}, u32[]{:S(2)}, u32[]{:S(2)}) collective-permute-start(f32[3,128]{1,0:T(4,128)S(1)} %get-tuple-element.55.refs_3_), channel_id=1, source_target_pairs={{0,24},{8,16},{16,8},{24,0},{1,25},{9,17},{17,9},{25,1},{2,26},{10... | collective-permute-start | bytes 4616 | tf_op jit(solution)/shard_map/ppermute | solution.py:269
  50.8 3.6 %collective-permute-start.15 = (f32[3,128]{1,0:T(4,128)S(1)}, f32[3,128]{1,0:T(4,128)S(1)}, u32[]{:S(2)}, u32[]{:S(2)}) collective-permute-start(f32[3,128]{1,0:T(4,128)S(1)} %get-tuple-element.55.refs_3_), channel_id=1, source_target_pairs={{0,16},{8,24},{16,0},{24,8},{1,17},{9,25},{17,1},{25,9},{2,18},{10... | collective-permute-start | bytes 4616 | tf_op jit(solution)/shard_map/ppermute | solution.py:269
  51.4 3.6 %collective-permute-start.16 = (f32[3,128]{1,0:T(4,128)S(1)}, f32[3,128]{1,0:T(4,128)S(1)}, u32[]{:S(2)}, u32[]{:S(2)}) collective-permute-start(f32[3,128]{1,0:T(4,128)S(1)} %get-tuple-element.55.refs_3_), channel_id=1, source_target_pairs={{0,8},{8,0},{16,24},{24,16},{1,9},{9,1},{17,25},{25,17},{2,10},{10... | collective-permute-start | bytes 4616 | tf_op jit(solution)/shard_map/ppermute | solution.py:269
  57.0 15.8 %collective-permute-start.17 = (bf16[256,1024]{1,0:T(8,128)(2,1)S(1)}, bf16[256,1024]{1,0:T(8,128)(2,1)S(1)}, u32[]{:S(2)}, u32[]{:S(2)}) collective-permute-start(bf16[256,1024]{1,0:T(8,128)(2,1)S(1)} %get-tuple-element.57), channel_id=1, source_target_pairs={{0,24},{8,16},{16,8},{24,0},{1,25},{9,17},{17,9},{25,1},{2,26},{10... | collective-permute-start | bytes 1572872 | tf_op jit(solution)/shard_map/ppermute | solution.py:269
  58.5 20.9 %collective-permute-start.18 = (bf16[256,1024]{1,0:T(8,128)(2,1)S(1)}, bf16[256,1024]{1,0:T(8,128)(2,1)S(1)}, u32[]{:S(2)}, u32[]{:S(2)}) collective-permute-start(bf16[256,1024]{1,0:T(8,128)(2,1)S(1)} %get-tuple-element.58), channel_id=1, source_target_pairs={{0,16},{8,24},{16,0},{24,8},{1,17},{9,25},{17,1},{25,9},{2,18},{10... | collective-permute-start | bytes 1572872 | tf_op jit(solution)/shard_map/ppermute | solution.py:269
  58.9 20.5 %collective-permute-start.19 = (bf16[256,1024]{1,0:T(8,128)(2,1)S(1)}, bf16[256,1024]{1,0:T(8,128)(2,1)S(1)}, u32[]{:S(2)}, u32[]{:S(2)}) collective-permute-start(bf16[256,1024]{1,0:T(8,128)(2,1)S(1)} %get-tuple-element.59), channel_id=1, source_target_pairs={{0,8},{8,0},{16,24},{24,16},{1,9},{9,1},{17,25},{25,17},{2,10},{10... | collective-permute-start | bytes 1572872 | tf_op jit(solution)/shard_map/ppermute | solution.py:269
  60.8 21.0 %collective-permute-start.13 = (bf16[128,4096]{1,0:T(8,128)(2,1)S(1)}, bf16[128,4096]{1,0:T(8,128)(2,1)S(1)}, u32[]{:S(2)}, u32[]{:S(2)}) collective-permute-start(bf16[128,4096]{1,0:T(8,128)(2,1)S(1)} %get-tuple-element.54), channel_id=1, source_target_pairs={{1,2},{3,4},{5,6},{7,0},{9,10},{11,12},{13,14},{15,8},{17,18},{19,... | collective-permute-start | bytes 3145736 | tf_op jit(solution)/shard_map/ppermute | solution.py:263

commit v3 on v2

--- a/solution.py
+++ b/solution.py
@@ -13,7 +13,7 @@
 F32 = jnp.float32
 CHUNK = 512
 TAIL = 16
-LONG, SOME = 5 * 10**10, 10 * 10**9
+LONG, SOME = 5 * 10**10, 16 * 10**9
 VMEM = pl.BlockSpec(memory_space=pltpu.VMEM)
 HBM = pl.BlockSpec(memory_space=pltpu.HBM)
 TOKEN = jax.ShapeDtypeStruct((8, 128), F32)

time: 83.6 us -> 83.6 us (level)
  waiting for transfers between devices: 41.5 us -> 42.8 us
  starting transfers between devices: 28.6 us -> 27.4 us
    ppermute x6, waiting for transfers between devices: 21.1 us -> 28.8 us  [shift(): return lax.ppermute(array, 'blk', pairs)]
    ppermute x12, waiting for transfers between devices: 19.5 us -> 13.9 us  [over_groups(): return lax.ppermute(array, 'grp', [(i, i ^ r) for i in range(groups)])]
    ppermute x6, starting transfers between devices: 12.2 us -> 11.1 us  [shift(): return lax.ppermute(array, 'blk', pairs)]
    ppermute x2, waiting for transfers between devices: 0.9 us -> 0.01 us  [swap(): return lax.ppermute(array, 'blk', [(i, i ^ 1) for i in range(loop)])]
  transfers between devices with their start and end apart: 20 -> 20, of which waited for: 15 -> 12; matrix products, arithmetic and copies ran while one was open for 0% -> 0% of each run, Pallas kernels for 11% -> 11%
where the time goes in v3:
time: 83.6 us; the launch traced here: 83.4 us
  waiting for transfers between devices  42.8 us (51%)
  starting transfers between devices  27.4 us (33%)
  Pallas kernels  11.7 us (14%)
    ppermute x6, waiting for transfers between devices, shift(): return lax.ppermute(array, 'blk', pairs)  28.8 us
    ppermute x12, starting transfers between devices, over_groups(): return lax.ppermute(array, 'grp', [(i, i ^ r) for i in range(groups)])  14.1 us
    ppermute x12, waiting for transfers between devices, over_groups(): return lax.ppermute(array, 'grp', [(i, i ^ r) for i in range(groups)])  13.9 us
    pallas_call x13, Pallas kernels, local_call(): pl.pallas_call(body, out_shape=out_shape, in_specs=in_specs or [VMEM] * l...  11.7 us
    ppermute x6, starting transfers between devices, shift(): return lax.ppermute(array, 'blk', pairs)  11.1 us
    ppermute x2, starting transfers between devices, swap(): return lax.ppermute(array, 'blk', [(i, i ^ 1) for i in range(loop)])  2.24 us
  transfers between devices with their start and end apart: 20, of which 12 were waited for; matrix products, arithmetic and copies ran while one was open for 0% of the time, Pallas kernels for 11%

profile of v3, /device:TPU:0, one launch (start us, length us, event | category | flops | bytes accessed | tf_op | source)
XLA Modules:
  0.0 83.4 jit_solution(9358744432512694733)
XLA Ops:
  0.6 4.5 %collective-permute-start.3 = (bf16[128,4096]{1,0:T(8,128)(2,1)}, bf16[128,4096]{1,0:T(8,128)(2,1)S(1)}, u32[]{:S(2)}, u32[]{:S(2)}) collective-permute-start(bf16[128,4096]{1,0:T(8,128)(2,1)} %p_ref.1), channel_id=1, source_target_pairs={{0,7},{1,0},{2,1},{3,2},{4,3},{5,4},{6,5},{7,6},{8,15},{9,8},{10,9... | collective-permute-start | bytes 3145736 | tf_op jit(solution)/shard_map/ppermute | solution.py:263
  5.2 0.7 copy-done.2
  5.9 1.6 %shard_map.67 = (bf16[272,1024]{1,0:T(8,128)(2,1)S(1)}, bf16[272,1024]{1,0:T(8,128)(2,1)S(1)}, bf16[272,1024]{1,0:T(8,128)(2,1)S(1)}, bf16[272,1024]{1,0:T(8,128)(2,1)S(1)}, f32[8,128]{1,0:T(8,128)S(1)}) custom-call(bf16[128,4096]{1,0:T(8,128)(2,1)} %q_ref.9, bf16[128,4096]{1,0:T(8,128)(2,1)} %p_ref.1, s32[3,128]{1,0:T(4,128)S(1)} %bitcast.3), custom_call_target="tpu_custom_call" | custom-call | bytes 4331008 | tf_op jit(solution)/shard_map/pallas_call | solution.py:31
  7.5 2.5 %collective-permute-start = (bf16[272,1024]{1,0:T(8,128)(2,1)S(1)}, bf16[272,1024]{1,0:T(8,128)(2,1)S(1)}, u32[]{:S(2)}, u32[]{:S(2)}) collective-permute-start(bf16[272,1024]{1,0:T(8,128)(2,1)S(1)} %get-tuple-element.33), channel_id=1, source_target_pairs={{0,24},{8,16},{16,8},{24,0},{1,25},{9,17},{17,9},{25,1},{2,26},{10... | collective-permute-start | bytes 1671176 | tf_op jit(solution)/shard_map/ppermute | solution.py:269
  11.1 1.4 %collective-permute-start.4 = (bf16[128,4096]{1,0:T(8,128)(2,1)S(1)}, bf16[128,4096]{1,0:T(8,128)(2,1)S(1)}, u32[]{:S(2)}, u32[]{:S(2)}) collective-permute-start(bf16[128,4096]{1,0:T(8,128)(2,1)S(1)} %shard_map.69), channel_id=1, source_target_pairs={{1,6},{3,0},{5,2},{7,4},{9,14},{11,8},{13,10},{15,12},{17,22},{19,... | collective-permute-start | bytes 3145736 | tf_op jit(solution)/shard_map/ppermute | solution.py:263
  12.5 8.6 %collective-permute-done.3.source = bf16[128,4096]{1,0:T(8,128)(2,1)S(1)} collective-permute-done((bf16[128,4096]{1,0:T(8,128)(2,1)}, bf16[128,4096]{1,0:T(8,128)(2,1)S(1)}, u32[]{:S(2)}, u32[]{:S(2)}) %collective-permute-start.3) | collective-permute-done | bytes 1048608 | tf_op jit(solution)/shard_map/ppermute | solution.py:263
  21.2 0.7 collective-permute-start.9
  22.0 6.0 %collective-permute-done.4.refs_2_.e3_ref = bf16[128,4096]{1,0:T(8,128)(2,1)S(1)} collective-permute-done((bf16[128,4096]{1,0:T(8,128)(2,1)S(1)}, bf16[128,4096]{1,0:T(8,128)(2,1)S(1)}, u32[]{:S(2)}, u32[]{:S(2)}) %collective-permute-start.4) | collective-permute-done | bytes 1048608 | tf_op jit(solution)/shard_map/ppermute | solution.py:263
  28.1 1.2 %collective-permute-start.8 = (bf16[128,8192]{1,0:T(8,128)(2,1)S(1)}, bf16[128,8192]{1,0:T(8,128)(2,1)S(1)}, u32[]{:S(2)}, u32[]{:S(2)}) collective-permute-start(bf16[128,8192]{1,0:T(8,128)(2,1)S(1)} %shard_map.72), channel_id=1, source_target_pairs={{0,1},{1,0},{2,3},{3,2},{4,5},{5,4},{6,7},{7,6},{8,9},{9,8},{10,11... | collective-permute-start | bytes 6291464 | tf_op jit(solution)/shard_map/ppermute | solution.py:266
  29.3 1.0 %shard_map.70 = (f32[128,128]{1,0:T(8,128)S(1)}, f32[128,128]{1,0:T(8,128)S(1)}, f32[128,128]{1,0:T(8,128)S(1)}) custom-call(bf16[128,4096]{1,0:T(8,128)(2,1)S(1)} %copy-done, bf16[128,4096]{1,0:T(8,128)(2,1)S(1)} %copy-done.1, bf16[128,4096]{1,0:T(8,128)(2,1)S(1)} %shard_map.68.refs_1_.n1_ref, bf16[128,4096]{1,0:T(8,128)(2,1)S(1)} %collective-permute-done.4.refs_2_.e3_ref), custom_call_target="tpu_custom_call" | custom-call | bytes 4390912 | tf_op jit(solution)/shard_map/pallas_call | solution.py:31
  30.3 1.9 %collective-permute-done.1.refs_1_.refs_5_ = bf16[272,1024]{1,0:T(8,128)(2,1)S(1)} collective-permute-done((bf16[272,1024]{1,0:T(8,128)(2,1)S(1)}, bf16[272,1024]{1,0:T(8,128)(2,1)S(1)}, u32[]{:S(2)}, u32[]{:S(2)}) %collective-permute-start.1) | collective-permute-done | bytes 557088 | tf_op jit(solution)/shard_map/ppermute | solution.py:269
  32.5 1.4 %shard_map.71 = (f32[3,128]{1,0:T(4,128)S(1)}, f32[3,128]{1,0:T(4,128)S(1)}, f32[3,128]{1,0:T(4,128)S(1)}, f32[3,128]{1,0:T(4,128)S(1)}) custom-call(bf16[272,1024]{1,0:T(8,128)(2,1)S(1)} %collective-permute-done.refs_0_.refs_4_, bf16[272,1024]{1,0:T(8,128)(2,1)S(1)} %collective-permute-done.1.refs_1_.refs_5_, ...), custom_call_target="tpu_custom_call" | custom-call | flops 49999998976 | bytes 2299904 | tf_op jit(solution)/shard_map/pallas_call | solution.py:31
  33.9 1.6 %collective-permute-start.5 = (f32[3,128]{1,0:T(4,128)S(1)}, f32[3,128]{1,0:T(4,128)S(1)}, u32[]{:S(2)}, u32[]{:S(2)}) collective-permute-start(f32[3,128]{1,0:T(4,128)S(1)} %get-tuple-element.39), channel_id=1, source_target_pairs={{0,24},{8,16},{16,8},{24,0},{1,25},{9,17},{17,9},{25,1},{2,26},{10... | collective-permute-start | bytes 4616 | tf_op jit(solution)/shard_map/ppermute | solution.py:269
  35.5 1.4 %collective-permute-start.6 = (f32[3,128]{1,0:T(4,128)S(1)}, f32[3,128]{1,0:T(4,128)S(1)}, u32[]{:S(2)}, u32[]{:S(2)}) collective-permute-start(f32[3,128]{1,0:T(4,128)S(1)} %get-tuple-element.40), channel_id=1, source_target_pairs={{0,16},{8,24},{16,0},{24,8},{1,17},{9,25},{17,1},{25,9},{2,18},{10... | collective-permute-start | bytes 4616 | tf_op jit(solution)/shard_map/ppermute | solution.py:269
  38.5 0.6 collective-permute-done.6.refs_1_
  39.1 1.4 %collective-permute-done.7.refs_2_ = f32[3,128]{1,0:T(4,128)S(1)} collective-permute-done((f32[3,128]{1,0:T(4,128)S(1)}, f32[3,128]{1,0:T(4,128)S(1)}, u32[]{:S(2)}, u32[]{:S(2)}) %collective-permute-start.7) | collective-permute-done | bytes 1568 | tf_op jit(solution)/shard_map/ppermute | solution.py:269
  40.5 1.1 %shard_map.74 = (f32[1,128]{1,0:T(1,128)}, bf16[128,512]{1,0:T(8,128)(2,1)S(1)}, f32[3,128]{1,0:T(4,128)S(1)}, bf16[128,256]{1,0:T(8,128)(2,1)S(1)}, bf16[128,4096]{1,0:T(8,128)(2,1)S(1)}) custom-call(f32[3,128]{1,0:T(4,128)S(1)} %collective-permute-done.5.refs_0_, f32[3,128]{1,0:T(4,128)S(1)} %collective-permute-done.6.refs_1_, ...), custom_call_target="tpu_custom_call" | custom-call | bytes 3613184 | tf_op jit(solution)/shard_map/pallas_call | solution.py:31
  41.6 0.7 collective-permute-start.12
  42.3 1.1 %collective-permute-start.10 = (bf16[128,256]{1,0:T(8,128)(2,1)S(1)}, bf16[128,256]{1,0:T(8,128)(2,1)S(1)}, u32[]{:S(2)}, u32[]{:S(2)}) collective-permute-start(bf16[128,256]{1,0:T(8,128)(2,1)S(1)} %get-tuple-element.47), channel_id=1, source_target_pairs={{0,1},{1,0},{2,3},{3,2},{4,5},{5,4},{6,7},{7,6},{8,9},{9,8},{10,11... | collective-permute-start | bytes 196616 | tf_op jit(solution)/shard_map/ppermute | solution.py:266
  43.4 2.4 %collective-permute-start.14 = (f32[3,128]{1,0:T(4,128)S(1)}, f32[3,128]{1,0:T(4,128)S(1)}, u32[]{:S(2)}, u32[]{:S(2)}) collective-permute-start(f32[3,128]{1,0:T(4,128)S(1)} %get-tuple-element.55.refs_3_), channel_id=1, source_target_pairs={{0,24},{8,16},{16,8},{24,0},{1,25},{9,17},{17,9},{25,1},{2,26},{10... | collective-permute-start | bytes 4616 | tf_op jit(solution)/shard_map/ppermute | solution.py:269
  45.8 0.6 collective-permute-start.15
  47.4 2.4 %collective-permute-start.11 = (bf16[128,4096]{1,0:T(8,128)(2,1)S(1)}, bf16[128,4096]{1,0:T(8,128)(2,1)S(1)}, u32[]{:S(2)}, u32[]{:S(2)}) collective-permute-start(bf16[128,4096]{1,0:T(8,128)(2,1)S(1)} %get-tuple-element.48), channel_id=1, source_target_pairs={{0,3},{2,5},{4,7},{6,1},{8,11},{10,13},{12,15},{14,9},{16,19},{18,... | collective-permute-start | bytes 3145736 | tf_op jit(solution)/shard_map/ppermute | solution.py:263
  50.0 2.1 %shard_map.78 = (bf16[256,1024]{1,0:T(8,128)(2,1)S(1)}, bf16[256,1024]{1,0:T(8,128)(2,1)S(1)}, bf16[256,1024]{1,0:T(8,128)(2,1)S(1)}, bf16[256,1024]{1,0:T(8,128)(2,1)S(1)}, f32[8,128]{1,0:T(8,128)}) custom-call(f32[3,128]{1,0:T(4,128)S(1)} %collective-permute-done.14.refs_0_, f32[3,128]{1,0:T(4,128)S(1)} %collective-permute-done.15.refs_1_, ...), custom_call_target="tpu_custom_call" | custom-call | bytes 4339712 | tf_op jit(solution)/shard_map/pallas_call | solution.py:31
  52.1 2.2 %collective-permute-start.17 = (bf16[256,1024]{1,0:T(8,128)(2,1)S(1)}, bf16[256,1024]{1,0:T(8,128)(2,1)S(1)}, u32[]{:S(2)}, u32[]{:S(2)}) collective-permute-start(bf16[256,1024]{1,0:T(8,128)(2,1)S(1)} %get-tuple-element.57), channel_id=1, source_target_pairs={{0,24},{8,16},{16,8},{24,0},{1,25},{9,17},{17,9},{25,1},{2,26},{10... | collective-permute-start | bytes 1572872 | tf_op jit(solution)/shard_map/ppermute | solution.py:269
  54.3 0.6 collective-permute-start.18
  54.9 0.7 collective-permute-start.19
  55.8 1.3 %collective-permute-start.13 = (bf16[128,4096]{1,0:T(8,128)(2,1)S(1)}, bf16[128,4096]{1,0:T(8,128)(2,1)S(1)}, u32[]{:S(2)}, u32[]{:S(2)}) collective-permute-start(bf16[128,4096]{1,0:T(8,128)(2,1)S(1)} %get-tuple-element.54), channel_id=1, source_target_pairs={{1,2},{3,4},{5,6},{7,0},{9,10},{11,12},{13,14},{15,8},{17,18},{19,... | collective-permute-start | bytes 3145736 | tf_op jit(solution)/shard_map/ppermute | solution.py:263
  57.1 9.1 %collective-permute-done.11.own3_ref = bf16[128,4096]{1,0:T(8,128)(2,1)S(1)} collective-permute-done((bf16[128,4096]{1,0:T(8,128)(2,1)S(1)}, bf16[128,4096]{1,0:T(8,128)(2,1)S(1)}, u32[]{:S(2)}, u32[]{:S(2)}) %collective-permute-start.11) | collective-permute-done | bytes 1048608 | tf_op jit(solution)/shard_map/ppermute | solution.py:263
  66.2 1.6 %shard_map.77 = (f32[128,4096]{1,0:T(8,128)S(1)}, f32[128,4096]{1,0:T(8,128)S(1)}) custom-call(bf16[128,4096]{1,0:T(8,128)(2,1)S(1)} %copy-done, bf16[128,8192]{1,0:T(8,128)(2,1)S(1)} %collective-permute-done.8.pair_ref, bf16[128,4096]{1,0:T(8,128)(2,1)S(1)} %copy-done.1, bf16[128,4096]{1,0:T(8,128)(2,1)S(1)} %shard_map.68.refs_1_.n1_ref, ...), custom_call_target="tpu_custom_call" | custom-call | flops 49999998976 | bytes 12784128 | tf_op jit(solution)/shard_map/pallas_call | solution.py:31
  67.8 8.6 %collective-permute-done.18.refs_1_ = bf16[256,1024]{1,0:T(8,128)(2,1)S(1)} collective-permute-done((bf16[256,1024]{1,0:T(8,128)(2,1)S(1)}, bf16[256,1024]{1,0:T(8,128)(2,1)S(1)}, u32[]{:S(2)}, u32[]{:S(2)}) %collective-permute-start.18) | collective-permute-done | bytes 524320 | tf_op jit(solution)/shard_map/ppermute | solution.py:269
  76.7 5.1 %collective-permute-done.13.own1 = bf16[128,4096]{1,0:T(8,128)(2,1)S(1)} collective-permute-done((bf16[128,4096]{1,0:T(8,128)(2,1)S(1)}, bf16[128,4096]{1,0:T(8,128)(2,1)S(1)}, u32[]{:S(2)}, u32[]{:S(2)}) %collective-permute-start.13) | collective-permute-done | bytes 1048608 | tf_op jit(solution)/shard_map/ppermute | solution.py:263
  81.9 1.5 %shard_map.79 = (bf16[128,4096]{1,0:T(8,128)(2,1)}, bf16[128,4096]{1,0:T(8,128)(2,1)}) custom-call(f32[128,4096]{1,0:T(8,128)S(1)} %get-tuple-element.52.pulled, f32[128,4096]{1,0:T(8,128)S(1)} %get-tuple-element.53.base, bf16[128,4096]{1,0:T(8,128)(2,1)S(1)} %collective-permute-done.13.own1, bf16[256,1024]{1,0:T(8,128)(2,1)S(1)} %collective-permute-done.17.refs_0_, ...), custom_call_target="tpu_custom_call" | custom-call | bytes 9437184 | tf_op jit(solution)/shard_map/pallas_call | solution.py:31
  (29 shorter events, 4.9 us)
Async XLA Ops:
  0.6 10.4 %copy-start.1 = (bf16[128,4096]{1,0:T(8,128)(2,1)S(1)}, bf16[128,4096]{1,0:T(8,128)(2,1)}, u32[]{:S(2)}) copy-start(bf16[128,4096]{1,0:T(8,128)(2,1)} %p_ref.1) | copy-start | bytes 3145732
  0.6 20.5 %collective-permute-start.3 = (bf16[128,4096]{1,0:T(8,128)(2,1)}, bf16[128,4096]{1,0:T(8,128)(2,1)S(1)}, u32[]{:S(2)}, u32[]{:S(2)}) collective-permute-start(bf16[128,4096]{1,0:T(8,128)(2,1)} %p_ref.1), channel_id=1, source_target_pairs={{0,7},{1,0},{2,1},{3,2},{4,3},{5,4},{6,5},{7,6},{8,15},{9,8},{10,9... | collective-permute-start | bytes 3145736 | tf_op jit(solution)/shard_map/ppermute | solution.py:263
  5.2 0.7 copy-start.2
  7.5 22.8 %collective-permute-start = (bf16[272,1024]{1,0:T(8,128)(2,1)S(1)}, bf16[272,1024]{1,0:T(8,128)(2,1)S(1)}, u32[]{:S(2)}, u32[]{:S(2)}) collective-permute-start(bf16[272,1024]{1,0:T(8,128)(2,1)S(1)} %get-tuple-element.33), channel_id=1, source_target_pairs={{0,24},{8,16},{16,8},{24,0},{1,25},{9,17},{17,9},{25,1},{2,26},{10... | collective-permute-start | bytes 1671176 | tf_op jit(solution)/shard_map/ppermute | solution.py:269
  10.0 22.2 %collective-permute-start.1 = (bf16[272,1024]{1,0:T(8,128)(2,1)S(1)}, bf16[272,1024]{1,0:T(8,128)(2,1)S(1)}, u32[]{:S(2)}, u32[]{:S(2)}) collective-permute-start(bf16[272,1024]{1,0:T(8,128)(2,1)S(1)} %get-tuple-element.34), channel_id=1, source_target_pairs={{0,16},{8,24},{16,0},{24,8},{1,17},{9,25},{17,1},{25,9},{2,18},{10... | collective-permute-start | bytes 1671176 | tf_op jit(solution)/shard_map/ppermute | solution.py:269
  10.5 22.0 %collective-permute-start.2 = (bf16[272,1024]{1,0:T(8,128)(2,1)S(1)}, bf16[272,1024]{1,0:T(8,128)(2,1)S(1)}, u32[]{:S(2)}, u32[]{:S(2)}) collective-permute-start(bf16[272,1024]{1,0:T(8,128)(2,1)S(1)} %get-tuple-element.35), channel_id=1, source_target_pairs={{0,8},{8,0},{16,24},{24,16},{1,9},{9,1},{17,25},{25,17},{2,10},{10... | collective-permute-start | bytes 1671176 | tf_op jit(solution)/shard_map/ppermute | solution.py:269
  11.1 16.9 %copy-start = (bf16[128,4096]{1,0:T(8,128)(2,1)S(1)}, bf16[128,4096]{1,0:T(8,128)(2,1)}, u32[]{:S(2)}) copy-start(bf16[128,4096]{1,0:T(8,128)(2,1)} %q_ref.9) | copy-start | bytes 3145732
  11.1 16.8 %collective-permute-start.4 = (bf16[128,4096]{1,0:T(8,128)(2,1)S(1)}, bf16[128,4096]{1,0:T(8,128)(2,1)S(1)}, u32[]{:S(2)}, u32[]{:S(2)}) collective-permute-start(bf16[128,4096]{1,0:T(8,128)(2,1)S(1)} %shard_map.69), channel_id=1, source_target_pairs={{1,6},{3,0},{5,2},{7,4},{9,14},{11,8},{13,10},{15,12},{17,22},{19,... | collective-permute-start | bytes 3145736 | tf_op jit(solution)/shard_map/ppermute | solution.py:263
  21.2 19.3 %collective-permute-start.9 = (bf16[128,4096]{1,0:T(8,128)(2,1)S(1)}, bf16[128,4096]{1,0:T(8,128)(2,1)S(1)}, u32[]{:S(2)}, u32[]{:S(2)}) collective-permute-start(bf16[128,4096]{1,0:T(8,128)(2,1)S(1)} %shard_map.68.refs_1_.n1_ref), channel_id=1, source_target_pairs={{1,7},{3,1},{5,3},{7,5},{9,15},{11,9},{13,11},{15,13},{17,23},{19,... | collective-permute-start | bytes 3145736 | tf_op jit(solution)/shard_map/ppermute | solution.py:263
  28.1 9.4 %collective-permute-start.8 = (bf16[128,8192]{1,0:T(8,128)(2,1)S(1)}, bf16[128,8192]{1,0:T(8,128)(2,1)S(1)}, u32[]{:S(2)}, u32[]{:S(2)}) collective-permute-start(bf16[128,8192]{1,0:T(8,128)(2,1)S(1)} %shard_map.72), channel_id=1, source_target_pairs={{0,1},{1,0},{2,3},{3,2},{4,5},{5,4},{6,7},{7,6},{8,9},{9,8},{10,11... | collective-permute-start | bytes 6291464 | tf_op jit(solution)/shard_map/ppermute | solution.py:266
  33.9 6.6 %copy-start.3 = (f32[128]{0:T(128)S(1)}, f32[128]{0:T(128)}, u32[]{:S(2)}) copy-start(f32[128]{0:T(128)} %param.7) | copy-start | bytes 1540
  33.9 4.5 %collective-permute-start.5 = (f32[3,128]{1,0:T(4,128)S(1)}, f32[3,128]{1,0:T(4,128)S(1)}, u32[]{:S(2)}, u32[]{:S(2)}) collective-permute-start(f32[3,128]{1,0:T(4,128)S(1)} %get-tuple-element.39), channel_id=1, source_target_pairs={{0,24},{8,16},{16,8},{24,0},{1,25},{9,17},{17,9},{25,1},{2,26},{10... | collective-permute-start | bytes 4616 | tf_op jit(solution)/shard_map/ppermute | solution.py:269
  35.5 3.6 %collective-permute-start.6 = (f32[3,128]{1,0:T(4,128)S(1)}, f32[3,128]{1,0:T(4,128)S(1)}, u32[]{:S(2)}, u32[]{:S(2)}) collective-permute-start(f32[3,128]{1,0:T(4,128)S(1)} %get-tuple-element.40), channel_id=1, source_target_pairs={{0,16},{8,24},{16,0},{24,8},{1,17},{9,25},{17,1},{25,9},{2,18},{10... | collective-permute-start | bytes 4616 | tf_op jit(solution)/shard_map/ppermute | solution.py:269
  36.9 3.6 %collective-permute-start.7 = (f32[3,128]{1,0:T(4,128)S(1)}, f32[3,128]{1,0:T(4,128)S(1)}, u32[]{:S(2)}, u32[]{:S(2)}) collective-permute-start(f32[3,128]{1,0:T(4,128)S(1)} %get-tuple-element.41), channel_id=1, source_target_pairs={{0,8},{8,0},{16,24},{24,16},{1,9},{9,1},{17,25},{25,17},{2,10},{10... | collective-permute-start | bytes 4616 | tf_op jit(solution)/shard_map/ppermute | solution.py:269
  41.6 13.9 %collective-permute-start.12 = (bf16[128,4096]{1,0:T(8,128)(2,1)S(1)}, bf16[128,4096]{1,0:T(8,128)(2,1)S(1)}, u32[]{:S(2)}, u32[]{:S(2)}) collective-permute-start(bf16[128,4096]{1,0:T(8,128)(2,1)S(1)} %get-tuple-element.50), channel_id=1, source_target_pairs={{1,3},{3,5},{5,7},{7,1},{9,11},{11,13},{13,15},{15,9},{17,19},{19,... | collective-permute-start | bytes 3145736 | tf_op jit(solution)/shard_map/ppermute | solution.py:263
  42.3 4.6 %collective-permute-start.10 = (bf16[128,256]{1,0:T(8,128)(2,1)S(1)}, bf16[128,256]{1,0:T(8,128)(2,1)S(1)}, u32[]{:S(2)}, u32[]{:S(2)}) collective-permute-start(bf16[128,256]{1,0:T(8,128)(2,1)S(1)} %get-tuple-element.47), channel_id=1, source_target_pairs={{0,1},{1,0},{2,3},{3,2},{4,5},{5,4},{6,7},{7,6},{8,9},{9,8},{10,11... | collective-permute-start | bytes 196616 | tf_op jit(solution)/shard_map/ppermute | solution.py:266
  43.4 6.3 %collective-permute-start.14 = (f32[3,128]{1,0:T(4,128)S(1)}, f32[3,128]{1,0:T(4,128)S(1)}, u32[]{:S(2)}, u32[]{:S(2)}) collective-permute-start(f32[3,128]{1,0:T(4,128)S(1)} %get-tuple-element.55.refs_3_), channel_id=1, source_target_pairs={{0,24},{8,16},{16,8},{24,0},{1,25},{9,17},{17,9},{25,1},{2,26},{10... | collective-permute-start | bytes 4616 | tf_op jit(solution)/shard_map/ppermute | solution.py:269
  45.8 3.9 %collective-permute-start.15 = (f32[3,128]{1,0:T(4,128)S(1)}, f32[3,128]{1,0:T(4,128)S(1)}, u32[]{:S(2)}, u32[]{:S(2)}) collective-permute-start(f32[3,128]{1,0:T(4,128)S(1)} %get-tuple-element.55.refs_3_), channel_id=1, source_target_pairs={{0,16},{8,24},{16,0},{24,8},{1,17},{9,25},{17,1},{25,9},{2,18},{10... | collective-permute-start | bytes 4616 | tf_op jit(solution)/shard_map/ppermute | solution.py:269
  46.4 3.6 %collective-permute-start.16 = (f32[3,128]{1,0:T(4,128)S(1)}, f32[3,128]{1,0:T(4,128)S(1)}, u32[]{:S(2)}, u32[]{:S(2)}) collective-permute-start(f32[3,128]{1,0:T(4,128)S(1)} %get-tuple-element.55.refs_3_), channel_id=1, source_target_pairs={{0,8},{8,0},{16,24},{24,16},{1,9},{9,1},{17,25},{25,17},{2,10},{10... | collective-permute-start | bytes 4616 | tf_op jit(solution)/shard_map/ppermute | solution.py:269
  47.4 18.8 %collective-permute-start.11 = (bf16[128,4096]{1,0:T(8,128)(2,1)S(1)}, bf16[128,4096]{1,0:T(8,128)(2,1)S(1)}, u32[]{:S(2)}, u32[]{:S(2)}) collective-permute-start(bf16[128,4096]{1,0:T(8,128)(2,1)S(1)} %get-tuple-element.48), channel_id=1, source_target_pairs={{0,3},{2,5},{4,7},{6,1},{8,11},{10,13},{12,15},{14,9},{16,19},{18,... | collective-permute-start | bytes 3145736 | tf_op jit(solution)/shard_map/ppermute | solution.py:263
  52.1 15.8 %collective-permute-start.17 = (bf16[256,1024]{1,0:T(8,128)(2,1)S(1)}, bf16[256,1024]{1,0:T(8,128)(2,1)S(1)}, u32[]{:S(2)}, u32[]{:S(2)}) collective-permute-start(bf16[256,1024]{1,0:T(8,128)(2,1)S(1)} %get-tuple-element.57), channel_id=1, source_target_pairs={{0,24},{8,16},{16,8},{24,0},{1,25},{9,17},{17,9},{25,1},{2,26},{10... | collective-permute-start | bytes 1572872 | tf_op jit(solution)/shard_map/ppermute | solution.py:269
  54.3 22.1 %collective-permute-start.18 = (bf16[256,1024]{1,0:T(8,128)(2,1)S(1)}, bf16[256,1024]{1,0:T(8,128)(2,1)S(1)}, u32[]{:S(2)}, u32[]{:S(2)}) collective-permute-start(bf16[256,1024]{1,0:T(8,128)(2,1)S(1)} %get-tuple-element.58), channel_id=1, source_target_pairs={{0,16},{8,24},{16,0},{24,8},{1,17},{9,25},{17,1},{25,9},{2,18},{10... | collective-permute-start | bytes 1572872 | tf_op jit(solution)/shard_map/ppermute | solution.py:269
  54.9 21.8 %collective-permute-start.19 = (bf16[256,1024]{1,0:T(8,128)(2,1)S(1)}, bf16[256,1024]{1,0:T(8,128)(2,1)S(1)}, u32[]{:S(2)}, u32[]{:S(2)}) collective-permute-start(bf16[256,1024]{1,0:T(8,128)(2,1)S(1)} %get-tuple-element.59), channel_id=1, source_target_pairs={{0,8},{8,0},{16,24},{24,16},{1,9},{9,1},{17,25},{25,17},{2,10},{10... | collective-permute-start | bytes 1572872 | tf_op jit(solution)/shard_map/ppermute | solution.py:269
  55.8 26.1 %collective-permute-start.13 = (bf16[128,4096]{1,0:T(8,128)(2,1)S(1)}, bf16[128,4096]{1,0:T(8,128)(2,1)S(1)}, u32[]{:S(2)}, u32[]{:S(2)}) collective-permute-start(bf16[128,4096]{1,0:T(8,128)(2,1)S(1)} %get-tuple-element.54), channel_id=1, source_target_pairs={{1,2},{3,4},{5,6},{7,0},{9,10},{11,12},{13,14},{15,8},{17,18},{19,... | collective-permute-start | bytes 3145736 | tf_op jit(solution)/shard_map/ppermute | solution.py:263

commit v4 on v3

--- a/solution.py
+++ b/solution.py
@@ -127,18 +127,21 @@
             outs[r][rows:, at] = grad_p[mine]
 
 
-def pass_body(source, token, out):
-    out[...] = source[...]
-
-
-def choose_body(n1_ref, e3_ref, q_ref, out):
+def pass_body(source, token, *outs):
+    width = outs[0].shape[1]
+    for n, out in enumerate(outs):
+        out[...] = source[:, n * width : (n + 1) * width]
+
+
+def choose_body(n1_a, n1_b, e3_ref, q_ref, out):
     width = q_ref.shape[1]
     odd = lax.axis_index("blk") % 2 == 1
     out[:, width:] = q_ref[...]
 
     @pl.when(odd)
     def _():
-        out[:, :width] = n1_ref[...]
+        out[:, : width // 2] = n1_a[...]
+        out[:, width // 2 : width] = n1_b[...]
 
     @pl.when(jnp.logical_not(odd))
     def _():
@@ -159,11 +162,13 @@
     groups, *refs
 ):
     parts, refs = refs[:groups], refs[groups:]
-    q_ref, s0_ref, s1_ref, s2_ref, s3_ref, last_ref, w_ref, *refs = refs
+    q_ref, s0_ref, s1_ref, s2_ref, s3_ref, last_a, last_b, w_ref, *refs = refs
     loss_ref, coef_ref, hard_out, swap_ref, term3_ref = refs
     rows, width = q_ref.shape
     w = w_ref[...]
-    s3 = INV_TEMP * (s3_ref[...] + dot(last_ref[...], q_ref[...], ((1,), (1,))))
+    half = width // 2
+    last = dot(last_a[...], q_ref[:, :half], ((1,), (1,)))
+    s3 = INV_TEMP * (s3_ref[...] + last + dot(last_b[...], q_ref[:, half:], ((1,), (1,))))
     scores = [INV_TEMP * s0_ref[...], INV_TEMP * s1_ref[...], INV_TEMP * s2_ref[...], s3]
     hard = parts[-1][...]
     for other in parts[-2::-1]:
@@ -212,13 +217,13 @@
 
 
 def base_body(
-    q_ref, pair_ref, p_ref, n1_ref, e3_ref, o3_ref, coef_ref, swap_ref, w_ref, own3_ref,
+    q_ref, pair_ref, p_ref, n1_ref, e3_ref, o3_a, o3_b, coef_ref, swap_ref, w_ref, own3_ref,
     token, pulled, base, coef_t,
 ):
     rows, width = q_ref.shape
     w = jnp.broadcast_to(w_ref[...], (rows, rows)).T[:, :1]
     odd = lax.axis_index("blk") % 2 == 1
-    blocks = (p_ref, n1_ref, pair_ref, e3_ref, o3_ref)
+    blocks = (p_ref, n1_ref, pair_ref, e3_ref)
     for s in range(5):
         k = min(s, 3) * rows
         coef_t[:, s * rows : (s + 1) * rows] = coef_ref[:, k : k + rows].astype(F32).T.astype(BF16)
@@ -226,7 +231,8 @@
     coef = jnp.concatenate(coef, axis=1)
     for c in range(0, width, CHUNK):
         at = slice(c, c + CHUNK)
-        held = jnp.concatenate([block[:, at] for block in blocks], axis=0)
+        late = o3_a[:, at] if c < width // 2 else o3_b[:, c - width // 2 : c - width // 2 + CHUNK]
+        held = jnp.concatenate([block[:, at] for block in blocks] + [late], axis=0)
         pulled[:, at] = dot(coef_t[...], held, ((1,), (0,))) - w * p_ref[:, at].astype(F32)
         held = jnp.concatenate([q_ref[:, at], pair_ref[:, width + c : width + c + CHUNK]], axis=0)
         own = dot(coef, held, ((1,), (0,))) + own3_ref[:, at].astype(F32)
@@ -277,6 +283,7 @@
     def like(*shape, dtype=BF16):
         return jax.ShapeDtypeStruct(shape, dtype)
 
+    half = like(rows, width // 2)
     block, block32 = like(rows, width), like(rows, width, dtype=F32)
     square, triple = like(rows, rows, dtype=F32), like(3, rows, dtype=F32)
     piece, back = like(2 * rows + TAIL, cols), like(2 * rows, cols)
@@ -293,10 +300,10 @@
 
     (later_p,) = local_call(pass_body, [block], passages, token)
     next3_even = shift(later_p, -3, (1,))
-    (next1,) = local_call(pass_body, [block], next1, token, flops=LONG)
-    next3_odd = shift(next1, -2, (1,))
+    halves = local_call(pass_body, [half] * 2, next1, token, flops=LONG)
+    next3_odd = [shift(part, -2, (1,)) for part in halves]
     pair = swap(
-        local_call(choose_body, [like(rows, 2 * width)], next1, next3_even, queries, flops=LONG)[0]
+        local_call(choose_body, [like(rows, 2 * width)], *halves, next3_even, queries, flops=LONG)[0]
     )
 
     s0, s1, s3 = local_call(scores_body, [square] * 3, queries, passages, next1, next3_even)
@@ -308,7 +315,7 @@
     loss_rows, coef, hard_coef, to_core, term3 = local_call(
         functools.partial(weigh_body, groups),
         [like(1, rows, dtype=F32), like(rows, 4 * rows), triple, like(rows, 2 * rows), block],
-        *parts[::-1], queries, s0, s1, s2, s3, next3_odd, weights[None, :],
+        *parts[::-1], queries, s0, s1, s2, s3, *next3_odd, weights[None, :],
     )
 
     got3 = shift(term3, 2, (1,))
@@ -331,7 +338,7 @@
 
     pulled, base = local_call(
         base_body, [block32, block32],
-        queries, pair, passages, next1, next3_even, next3_odd, coef, from_core,
+        queries, pair, passages, next1, next3_even, *next3_odd, coef, from_core,
         weights[None, :], own3, token, flops=LONG, scratch=[pltpu.VMEM((rows, 5 * rows), BF16)],
     )
     grad_queries, grad_passages = local_call(

time: 83.6 us -> 84 us (level)
  waiting for transfers between devices: 42.8 us -> 40.3 us
  starting transfers between devices: 27.4 us -> 29.8 us
    ppermute x12, waiting for transfers between devices: 13.9 us -> 11.5 us  [over_groups(): return lax.ppermute(array, 'grp', [(i, i ^ r) for i in range(groups)])]
    ppermute x2, starting transfers between devices: 2.24 us -> 3.69 us  [swap(): return lax.ppermute(array, 'blk', [(i, i ^ 1) for i in range(loop)])]
    ppermute x6 -> x7, starting transfers between devices: 11.1 us -> 11.7 us  [shift(): return lax.ppermute(array, 'blk', pairs)]
    ppermute x6 -> x7, waiting for transfers between devices: 28.8 us -> 28.8 us  [shift(): return lax.ppermute(array, 'blk', pairs)]
  transfers between devices with their start and end apart: 20 -> 21, of which waited for: 12 -> 10; matrix products, arithmetic and copies ran while one was open for 0% -> 0% of each run, Pallas kernels for 11% -> 11%
where the time goes in v4:
time: 84 us; the launch traced here: 83.8 us
  waiting for transfers between devices  40.3 us (48%)
  starting transfers between devices  29.8 us (35%)
  Pallas kernels  12.1 us (14%)
    ppermute x7, waiting for transfers between devices, shift(): return lax.ppermute(array, 'blk', pairs)  28.8 us
    ppermute x12, starting transfers between devices, over_groups(): return lax.ppermute(array, 'grp', [(i, i ^ r) for i in range(groups)])  14.4 us
    pallas_call x13, Pallas kernels, local_call(): pl.pallas_call(body, out_shape=out_shape, in_specs=in_specs or [VMEM] * l...  12.1 us
    ppermute x7, starting transfers between devices, shift(): return lax.ppermute(array, 'blk', pairs)  11.7 us
    ppermute x12, waiting for transfers between devices, over_groups(): return lax.ppermute(array, 'grp', [(i, i ^ r) for i in range(groups)])  11.5 us
    ppermute x2, starting transfers between devices, swap(): return lax.ppermute(array, 'blk', [(i, i ^ 1) for i in range(loop)])  3.69 us
  transfers between devices with their start and end apart: 21, of which 10 were waited for; matrix products, arithmetic and copies ran while one was open for 0% of the time, Pallas kernels for 11%

profile of v4, /device:TPU:0, one launch (start us, length us, event | category | flops | bytes accessed | tf_op | source)
XLA Modules:
  0.0 83.8 jit_solution(7748093927283942595)
XLA Ops:
  0.6 4.5 %collective-permute-start.3 = (bf16[128,4096]{1,0:T(8,128)(2,1)}, bf16[128,4096]{1,0:T(8,128)(2,1)S(1)}, u32[]{:S(2)}, u32[]{:S(2)}) collective-permute-start(bf16[128,4096]{1,0:T(8,128)(2,1)} %p_ref.1), channel_id=1, source_target_pairs={{0,7},{1,0},{2,1},{3,2},{4,3},{5,4},{6,5},{7,6},{8,15},{9,8},{10,9... | collective-permute-start | bytes 3145736 | tf_op jit(solution)/shard_map/ppermute | solution.py:269
  5.2 0.7 copy-done.2
  5.9 1.6 %shard_map.67 = (bf16[272,1024]{1,0:T(8,128)(2,1)S(1)}, bf16[272,1024]{1,0:T(8,128)(2,1)S(1)}, bf16[272,1024]{1,0:T(8,128)(2,1)S(1)}, bf16[272,1024]{1,0:T(8,128)(2,1)S(1)}, f32[8,128]{1,0:T(8,128)S(1)}) custom-call(bf16[128,4096]{1,0:T(8,128)(2,1)} %q_ref.9, bf16[128,4096]{1,0:T(8,128)(2,1)} %p_ref.1, s32[3,128]{1,0:T(4,128)S(1)} %bitcast.3), custom_call_target="tpu_custom_call" | custom-call | bytes 4331008 | tf_op jit(solution)/shard_map/pallas_call | solution.py:31
  7.5 2.5 %collective-permute-start = (bf16[272,1024]{1,0:T(8,128)(2,1)S(1)}, bf16[272,1024]{1,0:T(8,128)(2,1)S(1)}, u32[]{:S(2)}, u32[]{:S(2)}) collective-permute-start(bf16[272,1024]{1,0:T(8,128)(2,1)S(1)} %get-tuple-element.35), channel_id=1, source_target_pairs={{0,24},{8,16},{16,8},{24,0},{1,25},{9,17},{17,9},{25,1},{2,26},{10... | collective-permute-start | bytes 1671176 | tf_op jit(solution)/shard_map/ppermute | solution.py:275
  10.5 0.5 collective-permute-start.2
  11.1 1.4 %collective-permute-start.4 = (bf16[128,4096]{1,0:T(8,128)(2,1)S(1)}, bf16[128,4096]{1,0:T(8,128)(2,1)S(1)}, u32[]{:S(2)}, u32[]{:S(2)}) collective-permute-start(bf16[128,4096]{1,0:T(8,128)(2,1)S(1)} %shard_map.68), channel_id=1, source_target_pairs={{1,6},{3,0},{5,2},{7,4},{9,14},{11,8},{13,10},{15,12},{17,22},{19,... | collective-permute-start | bytes 3145736 | tf_op jit(solution)/shard_map/ppermute | solution.py:269
  12.5 8.6 %collective-permute-done.3.refs_1_.source.n1_ref = bf16[128,4096]{1,0:T(8,128)(2,1)S(1)} collective-permute-done((bf16[128,4096]{1,0:T(8,128)(2,1)}, bf16[128,4096]{1,0:T(8,128)(2,1)S(1)}, u32[]{:S(2)}, u32[]{:S(2)}) %collective-permute-start.3) | collective-permute-done | bytes 1048608 | tf_op jit(solution)/shard_map/ppermute | solution.py:269
  21.2 0.7 collective-permute-start.9
  21.9 6.0 %collective-permute-done.4.refs_2_.e3_ref = bf16[128,4096]{1,0:T(8,128)(2,1)S(1)} collective-permute-done((bf16[128,4096]{1,0:T(8,128)(2,1)S(1)}, bf16[128,4096]{1,0:T(8,128)(2,1)S(1)}, u32[]{:S(2)}, u32[]{:S(2)}) %collective-permute-start.4) | collective-permute-done | bytes 1048608 | tf_op jit(solution)/shard_map/ppermute | solution.py:269
  27.9 0.7 collective-permute-start.10
  28.8 1.0 %shard_map.69 = (f32[128,128]{1,0:T(8,128)S(1)}, f32[128,128]{1,0:T(8,128)S(1)}, f32[128,128]{1,0:T(8,128)S(1)}) custom-call(bf16[128,4096]{1,0:T(8,128)(2,1)S(1)} %copy-done, bf16[128,4096]{1,0:T(8,128)(2,1)S(1)} %copy-done.1, bf16[128,4096]{1,0:T(8,128)(2,1)S(1)} %collective-permute-done.3.refs_1_.source.n1_ref, ...), custom_call_target="tpu_custom_call" | custom-call | bytes 4390912 | tf_op jit(solution)/shard_map/pallas_call | solution.py:31
  29.8 2.7 %collective-permute-start.8 = (bf16[128,8192]{1,0:T(8,128)(2,1)S(1)}, bf16[128,8192]{1,0:T(8,128)(2,1)S(1)}, u32[]{:S(2)}, u32[]{:S(2)}) collective-permute-start(bf16[128,8192]{1,0:T(8,128)(2,1)S(1)} %shard_map.72), channel_id=1, source_target_pairs={{0,1},{1,0},{2,3},{3,2},{4,5},{5,4},{6,7},{7,6},{8,9},{9,8},{10,11... | collective-permute-start | bytes 6291464 | tf_op jit(solution)/shard_map/ppermute | solution.py:272
  32.5 1.4 %shard_map.70 = (f32[3,128]{1,0:T(4,128)S(1)}, f32[3,128]{1,0:T(4,128)S(1)}, f32[3,128]{1,0:T(4,128)S(1)}, f32[3,128]{1,0:T(4,128)S(1)}) custom-call(bf16[272,1024]{1,0:T(8,128)(2,1)S(1)} %collective-permute-done.refs_0_.refs_4_, bf16[272,1024]{1,0:T(8,128)(2,1)S(1)} %collective-permute-done.1.refs_1_.refs_5_, ...), custom_call_target="tpu_custom_call" | custom-call | flops 49999998976 | bytes 2299904 | tf_op jit(solution)/shard_map/pallas_call | solution.py:31
  33.9 2.5 %collective-permute-start.5 = (f32[3,128]{1,0:T(4,128)S(1)}, f32[3,128]{1,0:T(4,128)S(1)}, u32[]{:S(2)}, u32[]{:S(2)}) collective-permute-start(f32[3,128]{1,0:T(4,128)S(1)} %get-tuple-element.41), channel_id=1, source_target_pairs={{0,24},{8,16},{16,8},{24,0},{1,25},{9,17},{17,9},{25,1},{2,26},{10... | collective-permute-start | bytes 4616 | tf_op jit(solution)/shard_map/ppermute | solution.py:275
  36.9 0.8 collective-permute-start.7
  38.5 1.6 %collective-permute-done.6.refs_1_ = f32[3,128]{1,0:T(4,128)S(1)} collective-permute-done((f32[3,128]{1,0:T(4,128)S(1)}, f32[3,128]{1,0:T(4,128)S(1)}, u32[]{:S(2)}, u32[]{:S(2)}) %collective-permute-start.6) | collective-permute-done | bytes 1568 | tf_op jit(solution)/shard_map/ppermute | solution.py:275
  40.5 1.5 %shard_map.74 = (f32[1,128]{1,0:T(1,128)}, bf16[128,512]{1,0:T(8,128)(2,1)S(1)}, f32[3,128]{1,0:T(4,128)S(1)}, bf16[128,256]{1,0:T(8,128)(2,1)S(1)}, bf16[128,4096]{1,0:T(8,128)(2,1)S(1)}) custom-call(f32[3,128]{1,0:T(4,128)S(1)} %collective-permute-done.5.refs_0_, f32[3,128]{1,0:T(4,128)S(1)} %collective-permute-done.6.refs_1_, ...), custom_call_target="tpu_custom_call" | custom-call | bytes 3613184 | tf_op jit(solution)/shard_map/pallas_call | solution.py:31
  42.0 0.7 collective-permute-start.13
  42.8 1.0 %collective-permute-start.11 = (bf16[128,256]{1,0:T(8,128)(2,1)S(1)}, bf16[128,256]{1,0:T(8,128)(2,1)S(1)}, u32[]{:S(2)}, u32[]{:S(2)}) collective-permute-start(bf16[128,256]{1,0:T(8,128)(2,1)S(1)} %get-tuple-element.51), channel_id=1, source_target_pairs={{0,1},{1,0},{2,3},{3,2},{4,5},{5,4},{6,7},{7,6},{8,9},{9,8},{10,11... | collective-permute-start | bytes 196616 | tf_op jit(solution)/shard_map/ppermute | solution.py:272
  43.8 2.4 %collective-permute-start.15 = (f32[3,128]{1,0:T(4,128)S(1)}, f32[3,128]{1,0:T(4,128)S(1)}, u32[]{:S(2)}, u32[]{:S(2)}) collective-permute-start(f32[3,128]{1,0:T(4,128)S(1)} %get-tuple-element.59.refs_3_), channel_id=1, source_target_pairs={{0,24},{8,16},{16,8},{24,0},{1,25},{9,17},{17,9},{25,1},{2,26},{10... | collective-permute-start | bytes 4616 | tf_op jit(solution)/shard_map/ppermute | solution.py:275
  46.2 0.6 collective-permute-start.16
  47.7 2.4 %collective-permute-start.12 = (bf16[128,4096]{1,0:T(8,128)(2,1)S(1)}, bf16[128,4096]{1,0:T(8,128)(2,1)S(1)}, u32[]{:S(2)}, u32[]{:S(2)}) collective-permute-start(bf16[128,4096]{1,0:T(8,128)(2,1)S(1)} %get-tuple-element.52), channel_id=1, source_target_pairs={{0,3},{2,5},{4,7},{6,1},{8,11},{10,13},{12,15},{14,9},{16,19},{18,... | collective-permute-start | bytes 3145736 | tf_op jit(solution)/shard_map/ppermute | solution.py:269
  50.4 2.1 %shard_map.78 = (bf16[256,1024]{1,0:T(8,128)(2,1)S(1)}, bf16[256,1024]{1,0:T(8,128)(2,1)S(1)}, bf16[256,1024]{1,0:T(8,128)(2,1)S(1)}, bf16[256,1024]{1,0:T(8,128)(2,1)S(1)}, f32[8,128]{1,0:T(8,128)}) custom-call(f32[3,128]{1,0:T(4,128)S(1)} %collective-permute-done.15.refs_0_, f32[3,128]{1,0:T(4,128)S(1)} %collective-permute-done.16.refs_1_, ...), custom_call_target="tpu_custom_call" | custom-call | bytes 4339712 | tf_op jit(solution)/shard_map/pallas_call | solution.py:31
  52.5 2.2 %collective-permute-start.18 = (bf16[256,1024]{1,0:T(8,128)(2,1)S(1)}, bf16[256,1024]{1,0:T(8,128)(2,1)S(1)}, u32[]{:S(2)}, u32[]{:S(2)}) collective-permute-start(bf16[256,1024]{1,0:T(8,128)(2,1)S(1)} %get-tuple-element.61), channel_id=1, source_target_pairs={{0,24},{8,16},{16,8},{24,0},{1,25},{9,17},{17,9},{25,1},{2,26},{10... | collective-permute-start | bytes 1572872 | tf_op jit(solution)/shard_map/ppermute | solution.py:275
  54.7 0.6 collective-permute-start.19
  55.3 0.7 collective-permute-start.20
  56.2 1.3 %collective-permute-start.14 = (bf16[128,4096]{1,0:T(8,128)(2,1)S(1)}, bf16[128,4096]{1,0:T(8,128)(2,1)S(1)}, u32[]{:S(2)}, u32[]{:S(2)}) collective-permute-start(bf16[128,4096]{1,0:T(8,128)(2,1)S(1)} %get-tuple-element.58), channel_id=1, source_target_pairs={{1,2},{3,4},{5,6},{7,0},{9,10},{11,12},{13,14},{15,8},{17,18},{19,... | collective-permute-start | bytes 3145736 | tf_op jit(solution)/shard_map/ppermute | solution.py:269
  57.5 9.1 %collective-permute-done.12.own3_ref = bf16[128,4096]{1,0:T(8,128)(2,1)S(1)} collective-permute-done((bf16[128,4096]{1,0:T(8,128)(2,1)S(1)}, bf16[128,4096]{1,0:T(8,128)(2,1)S(1)}, u32[]{:S(2)}, u32[]{:S(2)}) %collective-permute-start.12) | collective-permute-done | bytes 1048608 | tf_op jit(solution)/shard_map/ppermute | solution.py:269
  66.6 1.6 %shard_map.77 = (f32[128,4096]{1,0:T(8,128)S(1)}, f32[128,4096]{1,0:T(8,128)S(1)}) custom-call(bf16[128,4096]{1,0:T(8,128)(2,1)S(1)} %copy-done, bf16[128,8192]{1,0:T(8,128)(2,1)S(1)} %collective-permute-done.8.pair_ref, bf16[128,4096]{1,0:T(8,128)(2,1)S(1)} %copy-done.1, bf16[128,4096]{1,0:T(8,128)(2,1)S(1)} %collective-permute-done.3.refs_1_.source.n1_ref, ...), custom_call_target="tpu_custom_call" | custom-call | flops 49999998976 | bytes 12784128 | tf_op jit(solution)/shard_map/pallas_call | solution.py:31
  68.2 8.6 %collective-permute-done.19.refs_1_ = bf16[256,1024]{1,0:T(8,128)(2,1)S(1)} collective-permute-done((bf16[256,1024]{1,0:T(8,128)(2,1)S(1)}, bf16[256,1024]{1,0:T(8,128)(2,1)S(1)}, u32[]{:S(2)}, u32[]{:S(2)}) %collective-permute-start.19) | collective-permute-done | bytes 524320 | tf_op jit(solution)/shard_map/ppermute | solution.py:275
  77.1 5.1 %collective-permute-done.14.own1 = bf16[128,4096]{1,0:T(8,128)(2,1)S(1)} collective-permute-done((bf16[128,4096]{1,0:T(8,128)(2,1)S(1)}, bf16[128,4096]{1,0:T(8,128)(2,1)S(1)}, u32[]{:S(2)}, u32[]{:S(2)}) %collective-permute-start.14) | collective-permute-done | bytes 1048608 | tf_op jit(solution)/shard_map/ppermute | solution.py:269
  82.2 1.5 %shard_map.79 = (bf16[128,4096]{1,0:T(8,128)(2,1)}, bf16[128,4096]{1,0:T(8,128)(2,1)}) custom-call(f32[128,4096]{1,0:T(8,128)S(1)} %get-tuple-element.56.pulled, f32[128,4096]{1,0:T(8,128)S(1)} %get-tuple-element.57.base, bf16[128,4096]{1,0:T(8,128)(2,1)S(1)} %collective-permute-done.14.own1, bf16[256,1024]{1,0:T(8,128)(2,1)S(1)} %collective-permute-done.18.refs_0_, ...), custom_call_target="tpu_custom_call" | custom-call | bytes 9437184 | tf_op jit(solution)/shard_map/pallas_call | solution.py:31
  (31 shorter events, 4.3 us)
Async XLA Ops:
  0.6 10.4 %copy-start.1 = (bf16[128,4096]{1,0:T(8,128)(2,1)S(1)}, bf16[128,4096]{1,0:T(8,128)(2,1)}, u32[]{:S(2)}) copy-start(bf16[128,4096]{1,0:T(8,128)(2,1)} %p_ref.1) | copy-start | bytes 3145732
  0.6 20.5 %collective-permute-start.3 = (bf16[128,4096]{1,0:T(8,128)(2,1)}, bf16[128,4096]{1,0:T(8,128)(2,1)S(1)}, u32[]{:S(2)}, u32[]{:S(2)}) collective-permute-start(bf16[128,4096]{1,0:T(8,128)(2,1)} %p_ref.1), channel_id=1, source_target_pairs={{0,7},{1,0},{2,1},{3,2},{4,3},{5,4},{6,5},{7,6},{8,15},{9,8},{10,9... | collective-permute-start | bytes 3145736 | tf_op jit(solution)/shard_map/ppermute | solution.py:269
  5.2 0.7 copy-start.2
  7.5 22.3 %collective-permute-start = (bf16[272,1024]{1,0:T(8,128)(2,1)S(1)}, bf16[272,1024]{1,0:T(8,128)(2,1)S(1)}, u32[]{:S(2)}, u32[]{:S(2)}) collective-permute-start(bf16[272,1024]{1,0:T(8,128)(2,1)S(1)} %get-tuple-element.35), channel_id=1, source_target_pairs={{0,24},{8,16},{16,8},{24,0},{1,25},{9,17},{17,9},{25,1},{2,26},{10... | collective-permute-start | bytes 1671176 | tf_op jit(solution)/shard_map/ppermute | solution.py:275
  10.0 22.5 %collective-permute-start.1 = (bf16[272,1024]{1,0:T(8,128)(2,1)S(1)}, bf16[272,1024]{1,0:T(8,128)(2,1)S(1)}, u32[]{:S(2)}, u32[]{:S(2)}) collective-permute-start(bf16[272,1024]{1,0:T(8,128)(2,1)S(1)} %get-tuple-element.36), channel_id=1, source_target_pairs={{0,16},{8,24},{16,0},{24,8},{1,17},{9,25},{17,1},{25,9},{2,18},{10... | collective-permute-start | bytes 1671176 | tf_op jit(solution)/shard_map/ppermute | solution.py:275
  10.5 22.0 %collective-permute-start.2 = (bf16[272,1024]{1,0:T(8,128)(2,1)S(1)}, bf16[272,1024]{1,0:T(8,128)(2,1)S(1)}, u32[]{:S(2)}, u32[]{:S(2)}) collective-permute-start(bf16[272,1024]{1,0:T(8,128)(2,1)S(1)} %get-tuple-element.37), channel_id=1, source_target_pairs={{0,8},{8,0},{16,24},{24,16},{1,9},{9,1},{17,25},{25,17},{2,10},{10... | collective-permute-start | bytes 1671176 | tf_op jit(solution)/shard_map/ppermute | solution.py:275
  11.1 17.6 %copy-start = (bf16[128,4096]{1,0:T(8,128)(2,1)S(1)}, bf16[128,4096]{1,0:T(8,128)(2,1)}, u32[]{:S(2)}) copy-start(bf16[128,4096]{1,0:T(8,128)(2,1)} %q_ref.9) | copy-start | bytes 3145732
  11.1 16.8 %collective-permute-start.4 = (bf16[128,4096]{1,0:T(8,128)(2,1)S(1)}, bf16[128,4096]{1,0:T(8,128)(2,1)S(1)}, u32[]{:S(2)}, u32[]{:S(2)}) collective-permute-start(bf16[128,4096]{1,0:T(8,128)(2,1)S(1)} %shard_map.68), channel_id=1, source_target_pairs={{1,6},{3,0},{5,2},{7,4},{9,14},{11,8},{13,10},{15,12},{17,22},{19,... | collective-permute-start | bytes 3145736 | tf_op jit(solution)/shard_map/ppermute | solution.py:269
  21.2 19.3 %collective-permute-start.9 = (bf16[128,2048]{1,0:T(8,128)(2,1)S(1)}, bf16[128,2048]{1,0:T(8,128)(2,1)S(1)}, u32[]{:S(2)}, u32[]{:S(2)}) collective-permute-start(bf16[128,2048]{1,0:T(8,128)(2,1)S(1)} %get-tuple-element.46.n1_a), channel_id=1, source_target_pairs={{1,7},{3,1},{5,3},{7,5},{9,15},{11,9},{13,11},{15,13},{17,23},{19,... | collective-permute-start | bytes 1572872 | tf_op jit(solution)/shard_map/ppermute | solution.py:269
  27.9 12.6 %collective-permute-start.10 = (bf16[128,2048]{1,0:T(8,128)(2,1)S(1)}, bf16[128,2048]{1,0:T(8,128)(2,1)S(1)}, u32[]{:S(2)}, u32[]{:S(2)}) collective-permute-start(bf16[128,2048]{1,0:T(8,128)(2,1)S(1)} %get-tuple-element.47.n1_b), channel_id=1, source_target_pairs={{1,7},{3,1},{5,3},{7,5},{9,15},{11,9},{13,11},{15,13},{17,23},{19,... | collective-permute-start | bytes 1572872 | tf_op jit(solution)/shard_map/ppermute | solution.py:269
  29.8 7.2 %collective-permute-start.8 = (bf16[128,8192]{1,0:T(8,128)(2,1)S(1)}, bf16[128,8192]{1,0:T(8,128)(2,1)S(1)}, u32[]{:S(2)}, u32[]{:S(2)}) collective-permute-start(bf16[128,8192]{1,0:T(8,128)(2,1)S(1)} %shard_map.72), channel_id=1, source_target_pairs={{0,1},{1,0},{2,3},{3,2},{4,5},{5,4},{6,7},{7,6},{8,9},{9,8},{10,11... | collective-permute-start | bytes 6291464 | tf_op jit(solution)/shard_map/ppermute | solution.py:272
  33.9 6.6 %copy-start.3 = (f32[128]{0:T(128)S(1)}, f32[128]{0:T(128)}, u32[]{:S(2)}) copy-start(f32[128]{0:T(128)} %param.7) | copy-start | bytes 1540
  33.9 4.5 %collective-permute-start.5 = (f32[3,128]{1,0:T(4,128)S(1)}, f32[3,128]{1,0:T(4,128)S(1)}, u32[]{:S(2)}, u32[]{:S(2)}) collective-permute-start(f32[3,128]{1,0:T(4,128)S(1)} %get-tuple-element.41), channel_id=1, source_target_pairs={{0,24},{8,16},{16,8},{24,0},{1,25},{9,17},{17,9},{25,1},{2,26},{10... | collective-permute-start | bytes 4616 | tf_op jit(solution)/shard_map/ppermute | solution.py:275
  36.4 3.6 %collective-permute-start.6 = (f32[3,128]{1,0:T(4,128)S(1)}, f32[3,128]{1,0:T(4,128)S(1)}, u32[]{:S(2)}, u32[]{:S(2)}) collective-permute-start(f32[3,128]{1,0:T(4,128)S(1)} %get-tuple-element.42), channel_id=1, source_target_pairs={{0,16},{8,24},{16,0},{24,8},{1,17},{9,25},{17,1},{25,9},{2,18},{10... | collective-permute-start | bytes 4616 | tf_op jit(solution)/shard_map/ppermute | solution.py:275
  36.9 3.6 %collective-permute-start.7 = (f32[3,128]{1,0:T(4,128)S(1)}, f32[3,128]{1,0:T(4,128)S(1)}, u32[]{:S(2)}, u32[]{:S(2)}) collective-permute-start(f32[3,128]{1,0:T(4,128)S(1)} %get-tuple-element.43), channel_id=1, source_target_pairs={{0,8},{8,0},{16,24},{24,16},{1,9},{9,1},{17,25},{25,17},{2,10},{10... | collective-permute-start | bytes 4616 | tf_op jit(solution)/shard_map/ppermute | solution.py:275
  42.0 13.9 %collective-permute-start.13 = (bf16[128,4096]{1,0:T(8,128)(2,1)S(1)}, bf16[128,4096]{1,0:T(8,128)(2,1)S(1)}, u32[]{:S(2)}, u32[]{:S(2)}) collective-permute-start(bf16[128,4096]{1,0:T(8,128)(2,1)S(1)} %get-tuple-element.54), channel_id=1, source_target_pairs={{1,3},{3,5},{5,7},{7,1},{9,11},{11,13},{13,15},{15,9},{17,19},{19,... | collective-permute-start | bytes 3145736 | tf_op jit(solution)/shard_map/ppermute | solution.py:269
  42.8 4.5 %collective-permute-start.11 = (bf16[128,256]{1,0:T(8,128)(2,1)S(1)}, bf16[128,256]{1,0:T(8,128)(2,1)S(1)}, u32[]{:S(2)}, u32[]{:S(2)}) collective-permute-start(bf16[128,256]{1,0:T(8,128)(2,1)S(1)} %get-tuple-element.51), channel_id=1, source_target_pairs={{0,1},{1,0},{2,3},{3,2},{4,5},{5,4},{6,7},{7,6},{8,9},{9,8},{10,11... | collective-permute-start | bytes 196616 | tf_op jit(solution)/shard_map/ppermute | solution.py:272
  43.8 6.3 %collective-permute-start.15 = (f32[3,128]{1,0:T(4,128)S(1)}, f32[3,128]{1,0:T(4,128)S(1)}, u32[]{:S(2)}, u32[]{:S(2)}) collective-permute-start(f32[3,128]{1,0:T(4,128)S(1)} %get-tuple-element.59.refs_3_), channel_id=1, source_target_pairs={{0,24},{8,16},{16,8},{24,0},{1,25},{9,17},{17,9},{25,1},{2,26},{10... | collective-permute-start | bytes 4616 | tf_op jit(solution)/shard_map/ppermute | solution.py:275
  46.2 3.9 %collective-permute-start.16 = (f32[3,128]{1,0:T(4,128)S(1)}, f32[3,128]{1,0:T(4,128)S(1)}, u32[]{:S(2)}, u32[]{:S(2)}) collective-permute-start(f32[3,128]{1,0:T(4,128)S(1)} %get-tuple-element.59.refs_3_), channel_id=1, source_target_pairs={{0,16},{8,24},{16,0},{24,8},{1,17},{9,25},{17,1},{25,9},{2,18},{10... | collective-permute-start | bytes 4616 | tf_op jit(solution)/shard_map/ppermute | solution.py:275
  46.8 3.6 %collective-permute-start.17 = (f32[3,128]{1,0:T(4,128)S(1)}, f32[3,128]{1,0:T(4,128)S(1)}, u32[]{:S(2)}, u32[]{:S(2)}) collective-permute-start(f32[3,128]{1,0:T(4,128)S(1)} %get-tuple-element.59.refs_3_), channel_id=1, source_target_pairs={{0,8},{8,0},{16,24},{24,16},{1,9},{9,1},{17,25},{25,17},{2,10},{10... | collective-permute-start | bytes 4616 | tf_op jit(solution)/shard_map/ppermute | solution.py:275
  47.7 18.8 %collective-permute-start.12 = (bf16[128,4096]{1,0:T(8,128)(2,1)S(1)}, bf16[128,4096]{1,0:T(8,128)(2,1)S(1)}, u32[]{:S(2)}, u32[]{:S(2)}) collective-permute-start(bf16[128,4096]{1,0:T(8,128)(2,1)S(1)} %get-tuple-element.52), channel_id=1, source_target_pairs={{0,3},{2,5},{4,7},{6,1},{8,11},{10,13},{12,15},{14,9},{16,19},{18,... | collective-permute-start | bytes 3145736 | tf_op jit(solution)/shard_map/ppermute | solution.py:269
  52.5 15.8 %collective-permute-start.18 = (bf16[256,1024]{1,0:T(8,128)(2,1)S(1)}, bf16[256,1024]{1,0:T(8,128)(2,1)S(1)}, u32[]{:S(2)}, u32[]{:S(2)}) collective-permute-start(bf16[256,1024]{1,0:T(8,128)(2,1)S(1)} %get-tuple-element.61), channel_id=1, source_target_pairs={{0,24},{8,16},{16,8},{24,0},{1,25},{9,17},{17,9},{25,1},{2,26},{10... | collective-permute-start | bytes 1572872 | tf_op jit(solution)/shard_map/ppermute | solution.py:275
  54.7 22.1 %collective-permute-start.19 = (bf16[256,1024]{1,0:T(8,128)(2,1)S(1)}, bf16[256,1024]{1,0:T(8,128)(2,1)S(1)}, u32[]{:S(2)}, u32[]{:S(2)}) collective-permute-start(bf16[256,1024]{1,0:T(8,128)(2,1)S(1)} %get-tuple-element.62), channel_id=1, source_target_pairs={{0,16},{8,24},{16,0},{24,8},{1,17},{9,25},{17,1},{25,9},{2,18},{10... | collective-permute-start | bytes 1572872 | tf_op jit(solution)/shard_map/ppermute | solution.py:275
  55.3 21.9 %collective-permute-start.20 = (bf16[256,1024]{1,0:T(8,128)(2,1)S(1)}, bf16[256,1024]{1,0:T(8,128)(2,1)S(1)}, u32[]{:S(2)}, u32[]{:S(2)}) collective-permute-start(bf16[256,1024]{1,0:T(8,128)(2,1)S(1)} %get-tuple-element.63), channel_id=1, source_target_pairs={{0,8},{8,0},{16,24},{24,16},{1,9},{9,1},{17,25},{25,17},{2,10},{10... | collective-permute-start | bytes 1572872 | tf_op jit(solution)/shard_map/ppermute | solution.py:275
  56.2 26.0 %collective-permute-start.14 = (bf16[128,4096]{1,0:T(8,128)(2,1)S(1)}, bf16[128,4096]{1,0:T(8,128)(2,1)S(1)}, u32[]{:S(2)}, u32[]{:S(2)}) collective-permute-start(bf16[128,4096]{1,0:T(8,128)(2,1)S(1)} %get-tuple-element.58), channel_id=1, source_target_pairs={{1,2},{3,4},{5,6},{7,0},{9,10},{11,12},{13,14},{15,8},{17,18},{19,... | collective-permute-start | bytes 3145736 | tf_op jit(solution)/shard_map/ppermute | solution.py:269

commit v5 on v3

--- a/solution.py
+++ b/solution.py
@@ -89,14 +89,19 @@
 def hard_scores_body(groups, *refs):
     pieces, outs = refs[:groups][::-1], refs[groups + 1 :]
     rows = outs[0].shape[1]
-    ids = lax.broadcasted_iota(jnp.int32, (groups * rows, rows), 0)
-    p_all = jnp.concatenate([piece[rows : 2 * rows] for piece in pieces], axis=0)
+    ids = lax.broadcasted_iota(jnp.int32, (rows, rows), 0)
     for r in range(groups):
+        others = [other for other in range(groups) if other != r]
         places = places_of(pieces[r], rows)
-        dots = dot(p_all, pieces[r][:rows], ((1,), (1,)))
-        for k in range(3):
-            hit = jnp.where(ids == places[k], dots, 0.0)
-            outs[r][k : k + 1] = jnp.sum(hit, axis=0, keepdims=True)
+        held = jnp.concatenate([pieces[other][rows : 2 * rows] for other in others], axis=0)
+        dots = dot(held, pieces[r][:rows], ((1,), (1,)))
+        sums = [jnp.zeros((1, rows), F32) for _ in places]
+        for n, other in enumerate(others):
+            block = dots[n * rows : (n + 1) * rows]
+            for k, place in enumerate(places):
+                hit = jnp.where(ids == place - other * rows, block, 0.0)
+                sums[k] += jnp.sum(hit, axis=0, keepdims=True)
+        outs[r][...] = jnp.concatenate(sums, axis=0)
 
 
 def hard_grads_body(groups, *refs):
@@ -233,20 +238,28 @@
         base[:, at] = own - w * q_ref[:, at].astype(F32)
 
 
-def finish_body(groups, pulled, base, own1, *refs):
-    backs = refs[:groups][::-1]
-    q_out, p_out, q_held, p_held, sems = refs[groups:]
+def gather_body(groups, pulled, base, *refs):
+    backs, (out, almost, held, sems) = refs[:groups][::-1], refs[groups:]
     rows, cols = pulled.shape[0], backs[0].shape[1]
     g = lax.axis_index("grp")
     copies = []
     for r, back in enumerate(backs):
         at = pl.ds(pl.multiple_of((g ^ r) * cols, 128), cols)
-        q_held[:, at] = (INV_TEMP * (pulled[:, at] + back[:rows].astype(F32))).astype(BF16)
-        copies.append(pltpu.make_async_copy(q_held.at[:, at], q_out.at[:, at], sems.at[2 * r]))
+        held[:, at] = (INV_TEMP * (pulled[:, at] + back[:rows].astype(F32))).astype(BF16)
+        copies.append(pltpu.make_async_copy(held.at[:, at], out.at[:, at], sems.at[r]))
         copies[-1].start()
-        total = base[:, at] + back[rows:].astype(F32) + own1[:, at].astype(F32)
-        p_held[:, at] = (INV_TEMP * total).astype(BF16)
-        copies.append(pltpu.make_async_copy(p_held.at[:, at], p_out.at[:, at], sems.at[2 * r + 1]))
+        almost[:, at] = base[:, at] + back[rows:].astype(F32)
+    for copy in copies:
+        copy.wait()
+
+
+def finish_body(almost, own1, out, held, sems):
+    width = almost.shape[1]
+    copies = []
+    for n, c in enumerate(range(0, width, CHUNK)):
+        at = slice(c, c + CHUNK)
+        held[:, at] = (INV_TEMP * (almost[:, at] + own1[:, at].astype(F32))).astype(BF16)
+        copies.append(pltpu.make_async_copy(held.at[:, at], out.at[:, at], sems.at[n]))
         copies[-1].start()
     for copy in copies:
         copy.wait()
@@ -334,14 +347,14 @@
         queries, pair, passages, next1, next3_even, next3_odd, coef, from_core,
         weights[None, :], own3, token, flops=LONG, scratch=[pltpu.VMEM((rows, 5 * rows), BF16)],
     )
-    grad_queries, grad_passages = local_call(
-        functools.partial(finish_body, groups), [block, block], pulled, base, own1, *backs[::-1],
-        out_specs=[HBM, HBM],
-        scratch=[
-            pltpu.VMEM((rows, width), BF16),
-            pltpu.VMEM((rows, width), BF16),
-            pltpu.SemaphoreType.DMA((2 * groups,)),
-        ],
+    held = pltpu.VMEM((rows, width), BF16)
+    grad_queries, almost = local_call(
+        functools.partial(gather_body, groups), [block, block32], pulled, base, *backs[::-1],
+        out_specs=[HBM, VMEM], scratch=[held, pltpu.SemaphoreType.DMA((groups,))],
+    )
+    (grad_passages,) = local_call(
+        finish_body, [block], almost, own1, out_specs=[HBM],
+        scratch=[held, pltpu.SemaphoreType.DMA((width // CHUNK,))],
     )
     return loss_rows.reshape(rows), grad_queries, grad_passages
 

time: 83.6 us -> 83.2 us (level)
  waiting for transfers between devices: 42.8 us -> 41.4 us
    ppermute x6, waiting for transfers between devices: 28.8 us -> 27.7 us  [shift(): return lax.ppermute(array, 'blk', pairs)]
    pallas_call x13 -> x14, Pallas kernels: 11.7 us -> 12.2 us  [local_call(): pl.pallas_call(body, out_shape=out_shape, in_specs=in_specs or [VMEM] * l...]
  transfers between devices with their start and end apart: 20 -> 20, of which waited for: 12 -> 11; matrix products, arithmetic and copies ran while one was open for 0% -> 0% of each run, Pallas kernels for 11% -> 12%
where the time goes in v5:
time: 83.2 us; the launch traced here: 82.9 us
  waiting for transfers between devices  41.4 us (50%)
  starting transfers between devices  27.8 us (33%)
  Pallas kernels  12.2 us (15%)
    ppermute x6, waiting for transfers between devices, shift(): return lax.ppermute(array, 'blk', pairs)  27.7 us
    ppermute x12, starting transfers between devices, over_groups(): return lax.ppermute(array, 'grp', [(i, i ^ r) for i in range(groups)])  14.1 us
    ppermute x12, waiting for transfers between devices, over_groups(): return lax.ppermute(array, 'grp', [(i, i ^ r) for i in range(groups)])  13.7 us
    pallas_call x14, Pallas kernels, local_call(): pl.pallas_call(body, out_shape=out_shape, in_specs=in_specs or [VMEM] * l...  12.2 us
    ppermute x6, starting transfers between devices, shift(): return lax.ppermute(array, 'blk', pairs)  11.2 us
    ppermute x2, starting transfers between devices, swap(): return lax.ppermute(array, 'blk', [(i, i ^ 1) for i in range(loop)])  2.54 us
  transfers between devices with their start and end apart: 20, of which 11 were waited for; matrix products, arithmetic and copies ran while one was open for 0% of the time, Pallas kernels for 12%

profile of v5, /device:TPU:0, one launch (start us, length us, event | category | flops | bytes accessed | tf_op | source)
XLA Modules:
  0.0 82.9 jit_solution(13164893493313586257)
XLA Ops:
  0.6 4.5 %collective-permute-start.3 = (bf16[128,4096]{1,0:T(8,128)(2,1)}, bf16[128,4096]{1,0:T(8,128)(2,1)S(1)}, u32[]{:S(2)}, u32[]{:S(2)}) collective-permute-start(bf16[128,4096]{1,0:T(8,128)(2,1)} %p_ref.1), channel_id=1, source_target_pairs={{0,7},{1,0},{2,1},{3,2},{4,3},{5,4},{6,5},{7,6},{8,15},{9,8},{10,9... | collective-permute-start | bytes 3145736 | tf_op jit(solution)/shard_map/ppermute | solution.py:276
  5.2 0.7 copy-done.2
  5.9 1.6 %shard_map.67 = (bf16[272,1024]{1,0:T(8,128)(2,1)S(1)}, bf16[272,1024]{1,0:T(8,128)(2,1)S(1)}, bf16[272,1024]{1,0:T(8,128)(2,1)S(1)}, bf16[272,1024]{1,0:T(8,128)(2,1)S(1)}, f32[8,128]{1,0:T(8,128)S(1)}) custom-call(bf16[128,4096]{1,0:T(8,128)(2,1)} %q_ref.9, bf16[128,4096]{1,0:T(8,128)(2,1)} %p_ref.1, s32[3,128]{1,0:T(4,128)S(1)} %bitcast.3), custom_call_target="tpu_custom_call" | custom-call | bytes 4331008 | tf_op jit(solution)/shard_map/pallas_call | solution.py:31
  7.5 2.5 %collective-permute-start = (bf16[272,1024]{1,0:T(8,128)(2,1)S(1)}, bf16[272,1024]{1,0:T(8,128)(2,1)S(1)}, u32[]{:S(2)}, u32[]{:S(2)}) collective-permute-start(bf16[272,1024]{1,0:T(8,128)(2,1)S(1)} %get-tuple-element.33), channel_id=1, source_target_pairs={{0,24},{8,16},{16,8},{24,0},{1,25},{9,17},{17,9},{25,1},{2,26},{10... | collective-permute-start | bytes 1671176 | tf_op jit(solution)/shard_map/ppermute | solution.py:282
  11.1 1.4 %collective-permute-start.4 = (bf16[128,4096]{1,0:T(8,128)(2,1)S(1)}, bf16[128,4096]{1,0:T(8,128)(2,1)S(1)}, u32[]{:S(2)}, u32[]{:S(2)}) collective-permute-start(bf16[128,4096]{1,0:T(8,128)(2,1)S(1)} %shard_map.69), channel_id=1, source_target_pairs={{1,6},{3,0},{5,2},{7,4},{9,14},{11,8},{13,10},{15,12},{17,22},{19,... | collective-permute-start | bytes 3145736 | tf_op jit(solution)/shard_map/ppermute | solution.py:276
  12.5 8.6 %collective-permute-done.3.source = bf16[128,4096]{1,0:T(8,128)(2,1)S(1)} collective-permute-done((bf16[128,4096]{1,0:T(8,128)(2,1)}, bf16[128,4096]{1,0:T(8,128)(2,1)S(1)}, u32[]{:S(2)}, u32[]{:S(2)}) %collective-permute-start.3) | collective-permute-done | bytes 1048608 | tf_op jit(solution)/shard_map/ppermute | solution.py:276
  21.2 0.7 collective-permute-start.9
  22.0 6.0 %collective-permute-done.4.refs_2_.e3_ref = bf16[128,4096]{1,0:T(8,128)(2,1)S(1)} collective-permute-done((bf16[128,4096]{1,0:T(8,128)(2,1)S(1)}, bf16[128,4096]{1,0:T(8,128)(2,1)S(1)}, u32[]{:S(2)}, u32[]{:S(2)}) %collective-permute-start.4) | collective-permute-done | bytes 1048608 | tf_op jit(solution)/shard_map/ppermute | solution.py:276
  28.1 1.2 %collective-permute-start.8 = (bf16[128,8192]{1,0:T(8,128)(2,1)S(1)}, bf16[128,8192]{1,0:T(8,128)(2,1)S(1)}, u32[]{:S(2)}, u32[]{:S(2)}) collective-permute-start(bf16[128,8192]{1,0:T(8,128)(2,1)S(1)} %shard_map.72), channel_id=1, source_target_pairs={{0,1},{1,0},{2,3},{3,2},{4,5},{5,4},{6,7},{7,6},{8,9},{9,8},{10,11... | collective-permute-start | bytes 6291464 | tf_op jit(solution)/shard_map/ppermute | solution.py:279
  29.3 1.0 %shard_map.70 = (f32[128,128]{1,0:T(8,128)S(1)}, f32[128,128]{1,0:T(8,128)S(1)}, f32[128,128]{1,0:T(8,128)S(1)}) custom-call(bf16[128,4096]{1,0:T(8,128)(2,1)S(1)} %copy-done, bf16[128,4096]{1,0:T(8,128)(2,1)S(1)} %copy-done.1, bf16[128,4096]{1,0:T(8,128)(2,1)S(1)} %shard_map.68.refs_1_.n1_ref, bf16[128,4096]{1,0:T(8,128)(2,1)S(1)} %collective-permute-done.4.refs_2_.e3_ref), custom_call_target="tpu_custom_call" | custom-call | bytes 4390912 | tf_op jit(solution)/shard_map/pallas_call | solution.py:31
  30.3 1.9 %collective-permute-done.1.refs_1_.refs_5_ = bf16[272,1024]{1,0:T(8,128)(2,1)S(1)} collective-permute-done((bf16[272,1024]{1,0:T(8,128)(2,1)S(1)}, bf16[272,1024]{1,0:T(8,128)(2,1)S(1)}, u32[]{:S(2)}, u32[]{:S(2)}) %collective-permute-start.1) | collective-permute-done | bytes 557088 | tf_op jit(solution)/shard_map/ppermute | solution.py:282
  32.5 1.2 %shard_map.71 = (f32[3,128]{1,0:T(4,128)S(1)}, f32[3,128]{1,0:T(4,128)S(1)}, f32[3,128]{1,0:T(4,128)S(1)}, f32[3,128]{1,0:T(4,128)S(1)}) custom-call(bf16[272,1024]{1,0:T(8,128)(2,1)S(1)} %collective-permute-done.refs_0_.refs_4_, bf16[272,1024]{1,0:T(8,128)(2,1)S(1)} %collective-permute-done.1.refs_1_.refs_5_, ...), custom_call_target="tpu_custom_call" | custom-call | flops 49999998976 | bytes 2299904 | tf_op jit(solution)/shard_map/pallas_call | solution.py:31
  33.6 1.6 %collective-permute-start.5 = (f32[3,128]{1,0:T(4,128)S(1)}, f32[3,128]{1,0:T(4,128)S(1)}, u32[]{:S(2)}, u32[]{:S(2)}) collective-permute-start(f32[3,128]{1,0:T(4,128)S(1)} %get-tuple-element.39), channel_id=1, source_target_pairs={{0,24},{8,16},{16,8},{24,0},{1,25},{9,17},{17,9},{25,1},{2,26},{10... | collective-permute-start | bytes 4616 | tf_op jit(solution)/shard_map/ppermute | solution.py:282
  35.2 1.4 %collective-permute-start.6 = (f32[3,128]{1,0:T(4,128)S(1)}, f32[3,128]{1,0:T(4,128)S(1)}, u32[]{:S(2)}, u32[]{:S(2)}) collective-permute-start(f32[3,128]{1,0:T(4,128)S(1)} %get-tuple-element.40), channel_id=1, source_target_pairs={{0,16},{8,24},{16,0},{24,8},{1,17},{9,25},{17,1},{25,9},{2,18},{10... | collective-permute-start | bytes 4616 | tf_op jit(solution)/shard_map/ppermute | solution.py:282
  38.2 0.6 collective-permute-done.6.refs_1_
  38.8 1.4 %collective-permute-done.7.refs_2_ = f32[3,128]{1,0:T(4,128)S(1)} collective-permute-done((f32[3,128]{1,0:T(4,128)S(1)}, f32[3,128]{1,0:T(4,128)S(1)}, u32[]{:S(2)}, u32[]{:S(2)}) %collective-permute-start.7) | collective-permute-done | bytes 1568 | tf_op jit(solution)/shard_map/ppermute | solution.py:282
  40.2 1.1 %shard_map.74 = (f32[1,128]{1,0:T(1,128)}, bf16[128,512]{1,0:T(8,128)(2,1)S(1)}, f32[3,128]{1,0:T(4,128)S(1)}, bf16[128,256]{1,0:T(8,128)(2,1)S(1)}, bf16[128,4096]{1,0:T(8,128)(2,1)S(1)}) custom-call(f32[3,128]{1,0:T(4,128)S(1)} %collective-permute-done.5.refs_0_, f32[3,128]{1,0:T(4,128)S(1)} %collective-permute-done.6.refs_1_, ...), custom_call_target="tpu_custom_call" | custom-call | bytes 3613184 | tf_op jit(solution)/shard_map/pallas_call | solution.py:31
  41.4 0.7 collective-permute-start.12
  42.1 1.4 %collective-permute-start.10 = (bf16[128,256]{1,0:T(8,128)(2,1)S(1)}, bf16[128,256]{1,0:T(8,128)(2,1)S(1)}, u32[]{:S(2)}, u32[]{:S(2)}) collective-permute-start(bf16[128,256]{1,0:T(8,128)(2,1)S(1)} %get-tuple-element.47), channel_id=1, source_target_pairs={{0,1},{1,0},{2,3},{3,2},{4,5},{5,4},{6,7},{7,6},{8,9},{9,8},{10,11... | collective-permute-start | bytes 196616 | tf_op jit(solution)/shard_map/ppermute | solution.py:279
  43.4 2.7 %collective-permute-start.13 = (f32[3,128]{1,0:T(4,128)S(1)}, f32[3,128]{1,0:T(4,128)S(1)}, u32[]{:S(2)}, u32[]{:S(2)}) collective-permute-start(f32[3,128]{1,0:T(4,128)S(1)} %get-tuple-element.54.refs_3_), channel_id=1, source_target_pairs={{0,24},{8,16},{16,8},{24,0},{1,25},{9,17},{17,9},{25,1},{2,26},{10... | collective-permute-start | bytes 4616 | tf_op jit(solution)/shard_map/ppermute | solution.py:282
  46.3 0.6 collective-permute-start.15
  47.4 2.5 %collective-permute-start.11 = (bf16[128,4096]{1,0:T(8,128)(2,1)S(1)}, bf16[128,4096]{1,0:T(8,128)(2,1)S(1)}, u32[]{:S(2)}, u32[]{:S(2)}) collective-permute-start(bf16[128,4096]{1,0:T(8,128)(2,1)S(1)} %get-tuple-element.48), channel_id=1, source_target_pairs={{0,3},{2,5},{4,7},{6,1},{8,11},{10,13},{12,15},{14,9},{16,19},{18,... | collective-permute-start | bytes 3145736 | tf_op jit(solution)/shard_map/ppermute | solution.py:276
  49.9 2.1 %shard_map.78 = (bf16[256,1024]{1,0:T(8,128)(2,1)S(1)}, bf16[256,1024]{1,0:T(8,128)(2,1)S(1)}, bf16[256,1024]{1,0:T(8,128)(2,1)S(1)}, bf16[256,1024]{1,0:T(8,128)(2,1)S(1)}, f32[8,128]{1,0:T(8,128)}) custom-call(f32[3,128]{1,0:T(4,128)S(1)} %collective-permute-done.13.refs_0_, f32[3,128]{1,0:T(4,128)S(1)} %collective-permute-done.14.refs_1_, ...), custom_call_target="tpu_custom_call" | custom-call | bytes 4339712 | tf_op jit(solution)/shard_map/pallas_call | solution.py:31
  52.0 2.6 %collective-permute-start.16 = (bf16[256,1024]{1,0:T(8,128)(2,1)S(1)}, bf16[256,1024]{1,0:T(8,128)(2,1)S(1)}, u32[]{:S(2)}, u32[]{:S(2)}) collective-permute-start(bf16[256,1024]{1,0:T(8,128)(2,1)S(1)} %get-tuple-element.56), channel_id=1, source_target_pairs={{0,24},{8,16},{16,8},{24,0},{1,25},{9,17},{17,9},{25,1},{2,26},{10... | collective-permute-start | bytes 1572872 | tf_op jit(solution)/shard_map/ppermute | solution.py:282
  54.9 0.6 collective-permute-start.18
  55.7 1.3 %collective-permute-start.19 = (bf16[128,4096]{1,0:T(8,128)(2,1)S(1)}, bf16[128,4096]{1,0:T(8,128)(2,1)S(1)}, u32[]{:S(2)}, u32[]{:S(2)}) collective-permute-start(bf16[128,4096]{1,0:T(8,128)(2,1)S(1)} %get-tuple-element.62), channel_id=1, source_target_pairs={{1,2},{3,4},{5,6},{7,0},{9,10},{11,12},{13,14},{15,8},{17,18},{19,... | collective-permute-start | bytes 3145736 | tf_op jit(solution)/shard_map/ppermute | solution.py:276
  57.0 9.2 %collective-permute-done.11.own3_ref = bf16[128,4096]{1,0:T(8,128)(2,1)S(1)} collective-permute-done((bf16[128,4096]{1,0:T(8,128)(2,1)S(1)}, bf16[128,4096]{1,0:T(8,128)(2,1)S(1)}, u32[]{:S(2)}, u32[]{:S(2)}) %collective-permute-start.11) | collective-permute-done | bytes 1048608 | tf_op jit(solution)/shard_map/ppermute | solution.py:276
  66.2 1.6 %shard_map.77 = (f32[128,4096]{1,0:T(8,128)S(1)}, f32[128,4096]{1,0:T(8,128)S(1)}) custom-call(bf16[128,4096]{1,0:T(8,128)(2,1)S(1)} %copy-done, bf16[128,8192]{1,0:T(8,128)(2,1)S(1)} %collective-permute-done.8.pair_ref, bf16[128,4096]{1,0:T(8,128)(2,1)S(1)} %copy-done.1, bf16[128,4096]{1,0:T(8,128)(2,1)S(1)} %shard_map.68.refs_1_.n1_ref, ...), custom_call_target="tpu_custom_call" | custom-call | flops 49999998976 | bytes 12784128 | tf_op jit(solution)/shard_map/pallas_call | solution.py:31
  67.9 8.5 %collective-permute-done.17.refs_1_ = bf16[256,1024]{1,0:T(8,128)(2,1)S(1)} collective-permute-done((bf16[256,1024]{1,0:T(8,128)(2,1)S(1)}, bf16[256,1024]{1,0:T(8,128)(2,1)S(1)}, u32[]{:S(2)}, u32[]{:S(2)}) %collective-permute-start.17) | collective-permute-done | bytes 524320 | tf_op jit(solution)/shard_map/ppermute | solution.py:282
  76.7 1.2 %shard_map.79 = (bf16[128,4096]{1,0:T(8,128)(2,1)}, f32[128,4096]{1,0:T(8,128)S(1)}) custom-call(f32[128,4096]{1,0:T(8,128)S(1)} %get-tuple-element.52.pulled, f32[128,4096]{1,0:T(8,128)S(1)} %get-tuple-element.53.base, bf16[256,1024]{1,0:T(8,128)(2,1)S(1)} %collective-permute-done.16.refs_0_, bf16[256,1024]{1,0:T(8,128)(2,1)S(1)} %collective-permute-done.17.refs_1_, ...), custom_call_target="tpu_custom_call" | custom-call | bytes 9437184 | tf_op jit(solution)/shard_map/pallas_call | solution.py:31
  77.9 3.9 %collective-permute-done.19.own1 = bf16[128,4096]{1,0:T(8,128)(2,1)S(1)} collective-permute-done((bf16[128,4096]{1,0:T(8,128)(2,1)S(1)}, bf16[128,4096]{1,0:T(8,128)(2,1)S(1)}, u32[]{:S(2)}, u32[]{:S(2)}) %collective-permute-start.19) | collective-permute-done | bytes 1048608 | tf_op jit(solution)/shard_map/ppermute | solution.py:276
  81.9 1.1 %shard_map.80 = bf16[128,4096]{1,0:T(8,128)(2,1)} custom-call(f32[128,4096]{1,0:T(8,128)S(1)} %get-tuple-element.61.almost, bf16[128,4096]{1,0:T(8,128)(2,1)S(1)} %collective-permute-done.19.own1), custom_call_target="tpu_custom_call" | custom-call | bytes 4194304 | tf_op jit(solution)/shard_map/pallas_call | solution.py:31
  (30 shorter events, 4.7 us)
Async XLA Ops:
  0.6 10.4 %copy-start.1 = (bf16[128,4096]{1,0:T(8,128)(2,1)S(1)}, bf16[128,4096]{1,0:T(8,128)(2,1)}, u32[]{:S(2)}) copy-start(bf16[128,4096]{1,0:T(8,128)(2,1)} %p_ref.1) | copy-start | bytes 3145732
  0.6 20.5 %collective-permute-start.3 = (bf16[128,4096]{1,0:T(8,128)(2,1)}, bf16[128,4096]{1,0:T(8,128)(2,1)S(1)}, u32[]{:S(2)}, u32[]{:S(2)}) collective-permute-start(bf16[128,4096]{1,0:T(8,128)(2,1)} %p_ref.1), channel_id=1, source_target_pairs={{0,7},{1,0},{2,1},{3,2},{4,3},{5,4},{6,5},{7,6},{8,15},{9,8},{10,9... | collective-permute-start | bytes 3145736 | tf_op jit(solution)/shard_map/ppermute | solution.py:276
  5.2 0.7 copy-start.2
  7.5 22.8 %collective-permute-start = (bf16[272,1024]{1,0:T(8,128)(2,1)S(1)}, bf16[272,1024]{1,0:T(8,128)(2,1)S(1)}, u32[]{:S(2)}, u32[]{:S(2)}) collective-permute-start(bf16[272,1024]{1,0:T(8,128)(2,1)S(1)} %get-tuple-element.33), channel_id=1, source_target_pairs={{0,24},{8,16},{16,8},{24,0},{1,25},{9,17},{17,9},{25,1},{2,26},{10... | collective-permute-start | bytes 1671176 | tf_op jit(solution)/shard_map/ppermute | solution.py:282
  10.0 22.2 %collective-permute-start.1 = (bf16[272,1024]{1,0:T(8,128)(2,1)S(1)}, bf16[272,1024]{1,0:T(8,128)(2,1)S(1)}, u32[]{:S(2)}, u32[]{:S(2)}) collective-permute-start(bf16[272,1024]{1,0:T(8,128)(2,1)S(1)} %get-tuple-element.34), channel_id=1, source_target_pairs={{0,16},{8,24},{16,0},{24,8},{1,17},{9,25},{17,1},{25,9},{2,18},{10... | collective-permute-start | bytes 1671176 | tf_op jit(solution)/shard_map/ppermute | solution.py:282
  10.5 22.0 %collective-permute-start.2 = (bf16[272,1024]{1,0:T(8,128)(2,1)S(1)}, bf16[272,1024]{1,0:T(8,128)(2,1)S(1)}, u32[]{:S(2)}, u32[]{:S(2)}) collective-permute-start(bf16[272,1024]{1,0:T(8,128)(2,1)S(1)} %get-tuple-element.35), channel_id=1, source_target_pairs={{0,8},{8,0},{16,24},{24,16},{1,9},{9,1},{17,25},{25,17},{2,10},{10... | collective-permute-start | bytes 1671176 | tf_op jit(solution)/shard_map/ppermute | solution.py:282
  11.1 16.9 %copy-start = (bf16[128,4096]{1,0:T(8,128)(2,1)S(1)}, bf16[128,4096]{1,0:T(8,128)(2,1)}, u32[]{:S(2)}) copy-start(bf16[128,4096]{1,0:T(8,128)(2,1)} %q_ref.9) | copy-start | bytes 3145732
  11.1 16.8 %collective-permute-start.4 = (bf16[128,4096]{1,0:T(8,128)(2,1)S(1)}, bf16[128,4096]{1,0:T(8,128)(2,1)S(1)}, u32[]{:S(2)}, u32[]{:S(2)}) collective-permute-start(bf16[128,4096]{1,0:T(8,128)(2,1)S(1)} %shard_map.69), channel_id=1, source_target_pairs={{1,6},{3,0},{5,2},{7,4},{9,14},{11,8},{13,10},{15,12},{17,22},{19,... | collective-permute-start | bytes 3145736 | tf_op jit(solution)/shard_map/ppermute | solution.py:276
  21.2 19.0 %collective-permute-start.9 = (bf16[128,4096]{1,0:T(8,128)(2,1)S(1)}, bf16[128,4096]{1,0:T(8,128)(2,1)S(1)}, u32[]{:S(2)}, u32[]{:S(2)}) collective-permute-start(bf16[128,4096]{1,0:T(8,128)(2,1)S(1)} %shard_map.68.refs_1_.n1_ref), channel_id=1, source_target_pairs={{1,7},{3,1},{5,3},{7,5},{9,15},{11,9},{13,11},{15,13},{17,23},{19,... | collective-permute-start | bytes 3145736 | tf_op jit(solution)/shard_map/ppermute | solution.py:276
  28.1 9.1 %collective-permute-start.8 = (bf16[128,8192]{1,0:T(8,128)(2,1)S(1)}, bf16[128,8192]{1,0:T(8,128)(2,1)S(1)}, u32[]{:S(2)}, u32[]{:S(2)}) collective-permute-start(bf16[128,8192]{1,0:T(8,128)(2,1)S(1)} %shard_map.72), channel_id=1, source_target_pairs={{0,1},{1,0},{2,3},{3,2},{4,5},{5,4},{6,7},{7,6},{8,9},{9,8},{10,11... | collective-permute-start | bytes 6291464 | tf_op jit(solution)/shard_map/ppermute | solution.py:279
  33.6 6.6 %copy-start.3 = (f32[128]{0:T(128)S(1)}, f32[128]{0:T(128)}, u32[]{:S(2)}) copy-start(f32[128]{0:T(128)} %param.7) | copy-start | bytes 1540
  33.6 4.5 %collective-permute-start.5 = (f32[3,128]{1,0:T(4,128)S(1)}, f32[3,128]{1,0:T(4,128)S(1)}, u32[]{:S(2)}, u32[]{:S(2)}) collective-permute-start(f32[3,128]{1,0:T(4,128)S(1)} %get-tuple-element.39), channel_id=1, source_target_pairs={{0,24},{8,16},{16,8},{24,0},{1,25},{9,17},{17,9},{25,1},{2,26},{10... | collective-permute-start | bytes 4616 | tf_op jit(solution)/shard_map/ppermute | solution.py:282
  35.2 3.6 %collective-permute-start.6 = (f32[3,128]{1,0:T(4,128)S(1)}, f32[3,128]{1,0:T(4,128)S(1)}, u32[]{:S(2)}, u32[]{:S(2)}) collective-permute-start(f32[3,128]{1,0:T(4,128)S(1)} %get-tuple-element.40), channel_id=1, source_target_pairs={{0,16},{8,24},{16,0},{24,8},{1,17},{9,25},{17,1},{25,9},{2,18},{10... | collective-permute-start | bytes 4616 | tf_op jit(solution)/shard_map/ppermute | solution.py:282
  36.7 3.6 %collective-permute-start.7 = (f32[3,128]{1,0:T(4,128)S(1)}, f32[3,128]{1,0:T(4,128)S(1)}, u32[]{:S(2)}, u32[]{:S(2)}) collective-permute-start(f32[3,128]{1,0:T(4,128)S(1)} %get-tuple-element.41), channel_id=1, source_target_pairs={{0,8},{8,0},{16,24},{24,16},{1,9},{9,1},{17,25},{25,17},{2,10},{10... | collective-permute-start | bytes 4616 | tf_op jit(solution)/shard_map/ppermute | solution.py:282
  41.4 14.1 %collective-permute-start.12 = (bf16[128,4096]{1,0:T(8,128)(2,1)S(1)}, bf16[128,4096]{1,0:T(8,128)(2,1)S(1)}, u32[]{:S(2)}, u32[]{:S(2)}) collective-permute-start(bf16[128,4096]{1,0:T(8,128)(2,1)S(1)} %get-tuple-element.50), channel_id=1, source_target_pairs={{1,3},{3,5},{5,7},{7,1},{9,11},{11,13},{13,15},{15,9},{17,19},{19,... | collective-permute-start | bytes 3145736 | tf_op jit(solution)/shard_map/ppermute | solution.py:276
  42.1 4.9 %collective-permute-start.10 = (bf16[128,256]{1,0:T(8,128)(2,1)S(1)}, bf16[128,256]{1,0:T(8,128)(2,1)S(1)}, u32[]{:S(2)}, u32[]{:S(2)}) collective-permute-start(bf16[128,256]{1,0:T(8,128)(2,1)S(1)} %get-tuple-element.47), channel_id=1, source_target_pairs={{0,1},{1,0},{2,3},{3,2},{4,5},{5,4},{6,7},{7,6},{8,9},{9,8},{10,11... | collective-permute-start | bytes 196616 | tf_op jit(solution)/shard_map/ppermute | solution.py:279
  43.4 6.5 %collective-permute-start.13 = (f32[3,128]{1,0:T(4,128)S(1)}, f32[3,128]{1,0:T(4,128)S(1)}, u32[]{:S(2)}, u32[]{:S(2)}) collective-permute-start(f32[3,128]{1,0:T(4,128)S(1)} %get-tuple-element.54.refs_3_), channel_id=1, source_target_pairs={{0,24},{8,16},{16,8},{24,0},{1,25},{9,17},{17,9},{25,1},{2,26},{10... | collective-permute-start | bytes 4616 | tf_op jit(solution)/shard_map/ppermute | solution.py:282
  46.1 3.8 %collective-permute-start.14 = (f32[3,128]{1,0:T(4,128)S(1)}, f32[3,128]{1,0:T(4,128)S(1)}, u32[]{:S(2)}, u32[]{:S(2)}) collective-permute-start(f32[3,128]{1,0:T(4,128)S(1)} %get-tuple-element.54.refs_3_), channel_id=1, source_target_pairs={{0,16},{8,24},{16,0},{24,8},{1,17},{9,25},{17,1},{25,9},{2,18},{10... | collective-permute-start | bytes 4616 | tf_op jit(solution)/shard_map/ppermute | solution.py:282
  46.3 3.6 %collective-permute-start.15 = (f32[3,128]{1,0:T(4,128)S(1)}, f32[3,128]{1,0:T(4,128)S(1)}, u32[]{:S(2)}, u32[]{:S(2)}) collective-permute-start(f32[3,128]{1,0:T(4,128)S(1)} %get-tuple-element.54.refs_3_), channel_id=1, source_target_pairs={{0,8},{8,0},{16,24},{24,16},{1,9},{9,1},{17,25},{25,17},{2,10},{10... | collective-permute-start | bytes 4616 | tf_op jit(solution)/shard_map/ppermute | solution.py:282
  47.4 18.8 %collective-permute-start.11 = (bf16[128,4096]{1,0:T(8,128)(2,1)S(1)}, bf16[128,4096]{1,0:T(8,128)(2,1)S(1)}, u32[]{:S(2)}, u32[]{:S(2)}) collective-permute-start(bf16[128,4096]{1,0:T(8,128)(2,1)S(1)} %get-tuple-element.48), channel_id=1, source_target_pairs={{0,3},{2,5},{4,7},{6,1},{8,11},{10,13},{12,15},{14,9},{16,19},{18,... | collective-permute-start | bytes 3145736 | tf_op jit(solution)/shard_map/ppermute | solution.py:276
  52.0 15.9 %collective-permute-start.16 = (bf16[256,1024]{1,0:T(8,128)(2,1)S(1)}, bf16[256,1024]{1,0:T(8,128)(2,1)S(1)}, u32[]{:S(2)}, u32[]{:S(2)}) collective-permute-start(bf16[256,1024]{1,0:T(8,128)(2,1)S(1)} %get-tuple-element.56), channel_id=1, source_target_pairs={{0,24},{8,16},{16,8},{24,0},{1,25},{9,17},{17,9},{25,1},{2,26},{10... | collective-permute-start | bytes 1572872 | tf_op jit(solution)/shard_map/ppermute | solution.py:282
  54.6 21.8 %collective-permute-start.17 = (bf16[256,1024]{1,0:T(8,128)(2,1)S(1)}, bf16[256,1024]{1,0:T(8,128)(2,1)S(1)}, u32[]{:S(2)}, u32[]{:S(2)}) collective-permute-start(bf16[256,1024]{1,0:T(8,128)(2,1)S(1)} %get-tuple-element.57), channel_id=1, source_target_pairs={{0,16},{8,24},{16,0},{24,8},{1,17},{9,25},{17,1},{25,9},{2,18},{10... | collective-permute-start | bytes 1572872 | tf_op jit(solution)/shard_map/ppermute | solution.py:282
  54.9 21.8 %collective-permute-start.18 = (bf16[256,1024]{1,0:T(8,128)(2,1)S(1)}, bf16[256,1024]{1,0:T(8,128)(2,1)S(1)}, u32[]{:S(2)}, u32[]{:S(2)}) collective-permute-start(bf16[256,1024]{1,0:T(8,128)(2,1)S(1)} %get-tuple-element.58), channel_id=1, source_target_pairs={{0,8},{8,0},{16,24},{24,16},{1,9},{9,1},{17,25},{25,17},{2,10},{10... | collective-permute-start | bytes 1572872 | tf_op jit(solution)/shard_map/ppermute | solution.py:282
  55.7 26.1 %collective-permute-start.19 = (bf16[128,4096]{1,0:T(8,128)(2,1)S(1)}, bf16[128,4096]{1,0:T(8,128)(2,1)S(1)}, u32[]{:S(2)}, u32[]{:S(2)}) collective-permute-start(bf16[128,4096]{1,0:T(8,128)(2,1)S(1)} %get-tuple-element.62), channel_id=1, source_target_pairs={{1,2},{3,4},{5,6},{7,0},{9,10},{11,12},{13,14},{15,8},{17,18},{19,... | collective-permute-start | bytes 3145736 | tf_op jit(solution)/shard_map/ppermute | solution.py:276

commit v6 on v5

--- a/solution.py
+++ b/solution.py
@@ -105,17 +105,19 @@
 
 
 def hard_grads_body(groups, *refs):
-    coefs, pieces, outs = refs[:groups][::-1], refs[groups : 2 * groups][::-1], refs[2 * groups + 1 : 3 * groups + 1]
-    token, matrix, matrix_t = refs[3 * groups + 1 :]
-    rows = coefs[0].shape[1]
+    coefs, pieces, outs = refs[0], refs[1 : groups + 1], refs[groups + 2 : 2 * groups + 2]
+    token, matrix, matrix_t = refs[2 * groups + 2 :]
+    g = lax.axis_index("grp")
+    rows = coefs.shape[2]
     cols = outs[0].shape[1]
     signal(token)
     ids = lax.broadcasted_iota(jnp.int32, (groups * rows, rows), 0)
     for r in range(groups):
         places = places_of(pieces[r], rows)
+        coef = coefs[g ^ r]
         total = jnp.zeros(ids.shape, F32)
         for k in range(3):
-            total += jnp.where(ids == places[k], coefs[r][k : k + 1], 0.0)
+            total += jnp.where(ids == places[k], coef[k : k + 1], 0.0)
         mine = slice(r * rows, (r + 1) * rows)
         matrix[:, mine] = total.astype(BF16)
         matrix_t[mine] = total.T.astype(BF16)
@@ -190,7 +192,8 @@
     for c in range(0, width, CHUNK):
         at = slice(c, c + CHUNK)
         term3_ref[:, at] = dot(coef3, q_ref[:, at], ((1,), (0,))).astype(BF16)
-    hard_out[...] = (w * jnp.exp(hard - log_total)).astype(BF16).astype(F32)
+    hard_out[...] = jnp.zeros(hard_out.shape, F32)
+    hard_out[:3] = (w * jnp.exp(hard - log_total)).astype(BF16).astype(F32)
     eye = lax.broadcasted_iota(jnp.int32, (rows, rows), 0) == lax.broadcasted_iota(
         jnp.int32, (rows, rows), 1
     )
@@ -320,7 +323,7 @@
     parts = exchange(parts)
     loss_rows, coef, hard_coef, to_core, term3 = local_call(
         functools.partial(weigh_body, groups),
-        [like(1, rows, dtype=F32), like(rows, 4 * rows), triple, like(rows, 2 * rows), block],
+        [like(1, rows, dtype=F32), like(rows, 4 * rows), like(8, rows, dtype=F32), like(rows, 2 * rows), block],
         *parts[::-1], queries, s0, s1, s2, s3, next3_odd, weights[None, :],
     )
 
@@ -331,11 +334,11 @@
     )
     own3 = shift(sent3, 3, (0,))
 
-    hard_coefs = exchange([hard_coef] * groups)
+    hard_coefs = lax.all_gather(hard_coef, "grp")
     square_all = pltpu.VMEM((groups * rows, groups * rows), BF16)
     *backs, token = local_call(
         functools.partial(hard_grads_body, groups), [back] * groups + [TOKEN],
-        *hard_coefs[::-1], *pieces[::-1], token, scratch=[square_all, square_all],
+        hard_coefs, *pieces, token, scratch=[square_all, square_all],
     )
     backs = exchange(backs)
 

time: 83.2 us -> 83.2 us (level)
  blocking collectives: 0 us -> 8.11 us
  starting transfers between devices: 27.8 us -> 23.2 us
  waiting for transfers between devices: 41.4 us -> 37.9 us
    all_gather x0 -> x1, blocking collectives: none -> 8.11 us  [per_device(): hard_coefs = lax.all_gather(hard_coef, 'grp')]
    ppermute x6, waiting for transfers between devices: 27.7 us -> 22.9 us  [shift(): return lax.ppermute(array, 'blk', pairs)]
    ppermute x12 -> x9, starting transfers between devices: 14.1 us -> 10.6 us  [over_groups(): return lax.ppermute(array, 'grp', [(i, i ^ r) for i in range(groups)])]
    ppermute x12 -> x9, waiting for transfers between devices: 13.7 us -> 15.1 us  [over_groups(): return lax.ppermute(array, 'grp', [(i, i ^ r) for i in range(groups)])]
    ppermute x6, starting transfers between devices: 11.2 us -> 10.1 us  [shift(): return lax.ppermute(array, 'blk', pairs)]
  transfers between devices with their start and end apart: 20 -> 17, of which waited for: 11 -> 12; matrix products, arithmetic and copies ran while one was open for 0% -> 0% of each run, Pallas kernels for 12% -> 12%
where the time goes in v6:
time: 83.2 us; the launch traced here: 82.9 us
  waiting for transfers between devices  37.9 us (46%)
  starting transfers between devices  23.2 us (28%)
  Pallas kernels  12.2 us (15%)
  blocking collectives  8.11 us (10%)
    ppermute x6, waiting for transfers between devices, shift(): return lax.ppermute(array, 'blk', pairs)  22.9 us
    ppermute x9, waiting for transfers between devices, over_groups(): return lax.ppermute(array, 'grp', [(i, i ^ r) for i in range(groups)])  15.1 us
    pallas_call x14, Pallas kernels, local_call(): pl.pallas_call(body, out_shape=out_shape, in_specs=in_specs or [VMEM] * l...  12.2 us
    ppermute x9, starting transfers between devices, over_groups(): return lax.ppermute(array, 'grp', [(i, i ^ r) for i in range(groups)])  10.6 us
    ppermute x6, starting transfers between devices, shift(): return lax.ppermute(array, 'blk', pairs)  10.1 us
    all_gather x1, blocking collectives, per_device(): hard_coefs = lax.all_gather(hard_coef, 'grp')  8.11 us
    ppermute x2, starting transfers between devices, swap(): return lax.ppermute(array, 'blk', [(i, i ^ 1) for i in range(loop)])  2.54 us
  transfers between devices with their start and end apart: 17, of which 12 were waited for; matrix products, arithmetic and copies ran while one was open for 0% of the time, Pallas kernels for 12%

profile of v6, /device:TPU:0, one launch (start us, length us, event | category | flops | bytes accessed | tf_op | source)
XLA Modules:
  0.0 82.9 jit_solution(5302787461760131622)
XLA Ops:
  0.6 4.5 %collective-permute-start.3 = (bf16[128,4096]{1,0:T(8,128)(2,1)}, bf16[128,4096]{1,0:T(8,128)(2,1)S(1)}, u32[]{:S(2)}, u32[]{:S(2)}) collective-permute-start(bf16[128,4096]{1,0:T(8,128)(2,1)} %p_ref.1), channel_id=1, source_target_pairs={{0,7},{1,0},{2,1},{3,2},{4,3},{5,4},{6,5},{7,6},{8,15},{9,8},{10,9... | collective-permute-start | bytes 3145736 | tf_op jit(solution)/shard_map/ppermute | solution.py:279
  5.2 0.7 copy-done.2
  5.9 1.6 %shard_map.67 = (bf16[272,1024]{1,0:T(8,128)(2,1)S(1)}, bf16[272,1024]{1,0:T(8,128)(2,1)S(1)}, bf16[272,1024]{1,0:T(8,128)(2,1)S(1)}, bf16[272,1024]{1,0:T(8,128)(2,1)S(1)}, f32[8,128]{1,0:T(8,128)S(1)}) custom-call(bf16[128,4096]{1,0:T(8,128)(2,1)} %q_ref.9, bf16[128,4096]{1,0:T(8,128)(2,1)} %p_ref.1, s32[3,128]{1,0:T(4,128)S(1)} %bitcast.5), custom_call_target="tpu_custom_call" | custom-call | bytes 4331008 | tf_op jit(solution)/shard_map/pallas_call | solution.py:31
  7.5 2.5 %collective-permute-start = (bf16[272,1024]{1,0:T(8,128)(2,1)S(1)}, bf16[272,1024]{1,0:T(8,128)(2,1)S(1)}, u32[]{:S(2)}, u32[]{:S(2)}) collective-permute-start(bf16[272,1024]{1,0:T(8,128)(2,1)S(1)} %get-tuple-element.33), channel_id=1, source_target_pairs={{0,24},{8,16},{16,8},{24,0},{1,25},{9,17},{17,9},{25,1},{2,26},{10... | collective-permute-start | bytes 1671176 | tf_op jit(solution)/shard_map/ppermute | solution.py:285
  11.1 1.4 %collective-permute-start.4 = (bf16[128,4096]{1,0:T(8,128)(2,1)S(1)}, bf16[128,4096]{1,0:T(8,128)(2,1)S(1)}, u32[]{:S(2)}, u32[]{:S(2)}) collective-permute-start(bf16[128,4096]{1,0:T(8,128)(2,1)S(1)} %shard_map.69), channel_id=1, source_target_pairs={{1,6},{3,0},{5,2},{7,4},{9,14},{11,8},{13,10},{15,12},{17,22},{19,... | collective-permute-start | bytes 3145736 | tf_op jit(solution)/shard_map/ppermute | solution.py:279
  12.5 8.6 %collective-permute-done.3.source = bf16[128,4096]{1,0:T(8,128)(2,1)S(1)} collective-permute-done((bf16[128,4096]{1,0:T(8,128)(2,1)}, bf16[128,4096]{1,0:T(8,128)(2,1)S(1)}, u32[]{:S(2)}, u32[]{:S(2)}) %collective-permute-start.3) | collective-permute-done | bytes 1048608 | tf_op jit(solution)/shard_map/ppermute | solution.py:279
  21.2 0.7 collective-permute-start.9
  22.0 6.0 %collective-permute-done.4.refs_2_.e3_ref = bf16[128,4096]{1,0:T(8,128)(2,1)S(1)} collective-permute-done((bf16[128,4096]{1,0:T(8,128)(2,1)S(1)}, bf16[128,4096]{1,0:T(8,128)(2,1)S(1)}, u32[]{:S(2)}, u32[]{:S(2)}) %collective-permute-start.4) | collective-permute-done | bytes 1048608 | tf_op jit(solution)/shard_map/ppermute | solution.py:279
  28.1 1.2 %collective-permute-start.8 = (bf16[128,8192]{1,0:T(8,128)(2,1)S(1)}, bf16[128,8192]{1,0:T(8,128)(2,1)S(1)}, u32[]{:S(2)}, u32[]{:S(2)}) collective-permute-start(bf16[128,8192]{1,0:T(8,128)(2,1)S(1)} %shard_map.72), channel_id=1, source_target_pairs={{0,1},{1,0},{2,3},{3,2},{4,5},{5,4},{6,7},{7,6},{8,9},{9,8},{10,11... | collective-permute-start | bytes 6291464 | tf_op jit(solution)/shard_map/ppermute | solution.py:282
  29.3 1.0 %shard_map.70 = (f32[128,128]{1,0:T(8,128)S(1)}, f32[128,128]{1,0:T(8,128)S(1)}, f32[128,128]{1,0:T(8,128)S(1)}) custom-call(bf16[128,4096]{1,0:T(8,128)(2,1)S(1)} %copy-done, bf16[128,4096]{1,0:T(8,128)(2,1)S(1)} %copy-done.1, bf16[128,4096]{1,0:T(8,128)(2,1)S(1)} %shard_map.68.refs_1_.n1_ref, bf16[128,4096]{1,0:T(8,128)(2,1)S(1)} %collective-permute-done.4.refs_2_.e3_ref), custom_call_target="tpu_custom_call" | custom-call | bytes 4390912 | tf_op jit(solution)/shard_map/pallas_call | solution.py:31
  30.3 1.9 %collective-permute-done.1.refs_1_.refs_3_ = bf16[272,1024]{1,0:T(8,128)(2,1)S(1)} collective-permute-done((bf16[272,1024]{1,0:T(8,128)(2,1)S(1)}, bf16[272,1024]{1,0:T(8,128)(2,1)S(1)}, u32[]{:S(2)}, u32[]{:S(2)}) %collective-permute-start.1) | collective-permute-done | bytes 557088 | tf_op jit(solution)/shard_map/ppermute | solution.py:285
  32.5 1.2 %shard_map.71 = (f32[3,128]{1,0:T(4,128)S(1)}, f32[3,128]{1,0:T(4,128)S(1)}, f32[3,128]{1,0:T(4,128)S(1)}, f32[3,128]{1,0:T(4,128)S(1)}) custom-call(bf16[272,1024]{1,0:T(8,128)(2,1)S(1)} %collective-permute-done.refs_0_.refs_4_, bf16[272,1024]{1,0:T(8,128)(2,1)S(1)} %collective-permute-done.1.refs_1_.refs_3_, ...), custom_call_target="tpu_custom_call" | custom-call | flops 49999998976 | bytes 2299904 | tf_op jit(solution)/shard_map/pallas_call | solution.py:31
  33.6 1.6 %collective-permute-start.5 = (f32[3,128]{1,0:T(4,128)S(1)}, f32[3,128]{1,0:T(4,128)S(1)}, u32[]{:S(2)}, u32[]{:S(2)}) collective-permute-start(f32[3,128]{1,0:T(4,128)S(1)} %get-tuple-element.39), channel_id=1, source_target_pairs={{0,24},{8,16},{16,8},{24,0},{1,25},{9,17},{17,9},{25,1},{2,26},{10... | collective-permute-start | bytes 4616 | tf_op jit(solution)/shard_map/ppermute | solution.py:285
  35.2 1.4 %collective-permute-start.6 = (f32[3,128]{1,0:T(4,128)S(1)}, f32[3,128]{1,0:T(4,128)S(1)}, u32[]{:S(2)}, u32[]{:S(2)}) collective-permute-start(f32[3,128]{1,0:T(4,128)S(1)} %get-tuple-element.40), channel_id=1, source_target_pairs={{0,16},{8,24},{16,0},{24,8},{1,17},{9,25},{17,1},{25,9},{2,18},{10... | collective-permute-start | bytes 4616 | tf_op jit(solution)/shard_map/ppermute | solution.py:285
  38.2 0.6 collective-permute-done.6.refs_1_
  38.8 1.4 %collective-permute-done.7.refs_2_ = f32[3,128]{1,0:T(4,128)S(1)} collective-permute-done((f32[3,128]{1,0:T(4,128)S(1)}, f32[3,128]{1,0:T(4,128)S(1)}, u32[]{:S(2)}, u32[]{:S(2)}) %collective-permute-start.7) | collective-permute-done | bytes 1568 | tf_op jit(solution)/shard_map/ppermute | solution.py:285
  40.2 1.1 %shard_map.74 = (f32[1,128]{1,0:T(1,128)}, bf16[128,512]{1,0:T(8,128)(2,1)S(1)}, f32[8,128]{1,0:T(8,128)S(1)}, bf16[128,256]{1,0:T(8,128)(2,1)S(1)}, bf16[128,4096]{1,0:T(8,128)(2,1)S(1)}) custom-call(f32[3,128]{1,0:T(4,128)S(1)} %collective-permute-done.5.refs_0_, f32[3,128]{1,0:T(4,128)S(1)} %collective-permute-done.6.refs_1_, ...), custom_call_target="tpu_custom_call" | custom-call | bytes 3615744 | tf_op jit(solution)/shard_map/pallas_call | solution.py:31
  41.4 0.7 collective-permute-start.12
  42.1 1.4 %collective-permute-start.10 = (bf16[128,256]{1,0:T(8,128)(2,1)S(1)}, bf16[128,256]{1,0:T(8,128)(2,1)S(1)}, u32[]{:S(2)}, u32[]{:S(2)}) collective-permute-start(bf16[128,256]{1,0:T(8,128)(2,1)S(1)} %get-tuple-element.47), channel_id=1, source_target_pairs={{0,1},{1,0},{2,3},{3,2},{4,5},{5,4},{6,7},{7,6},{8,9},{9,8},{10,11... | collective-permute-start | bytes 196616 | tf_op jit(solution)/shard_map/ppermute | solution.py:282
  43.4 8.1 %all-gather = f32[32,128]{1,0:T(8,128)S(1)} all-gather(f32[8,128]{1,0:T(8,128)S(1)} %get-tuple-element.54), channel_id=2, replica_groups=mesh['grp'=4,'blk'=8] {'grp'}, dimensions={0}, use_global_device_ids=true | all-gather | bytes 20480 | tf_op jit(solution)/shard_map/all_gather | solution.py:337
  52.0 1.4 %collective-permute-start.11 = (bf16[128,4096]{1,0:T(8,128)(2,1)S(1)}, bf16[128,4096]{1,0:T(8,128)(2,1)S(1)}, u32[]{:S(2)}, u32[]{:S(2)}) collective-permute-start(bf16[128,4096]{1,0:T(8,128)(2,1)S(1)} %get-tuple-element.48), channel_id=1, source_target_pairs={{0,3},{2,5},{4,7},{6,1},{8,11},{10,13},{12,15},{14,9},{16,19},{18,... | collective-permute-start | bytes 3145736 | tf_op jit(solution)/shard_map/ppermute | solution.py:279
  53.4 2.1 %shard_map.78 = (bf16[256,1024]{1,0:T(8,128)(2,1)S(1)}, bf16[256,1024]{1,0:T(8,128)(2,1)S(1)}, bf16[256,1024]{1,0:T(8,128)(2,1)S(1)}, bf16[256,1024]{1,0:T(8,128)(2,1)S(1)}, f32[8,128]{1,0:T(8,128)}) custom-call(f32[4,8,128]{2,1,0:T(8,128)S(1)} %bitcast.4, bf16[272,1024]{1,0:T(8,128)(2,1)S(1)} %get-tuple-element.36.refs_3_.refs_1_, ...), custom_call_target="tpu_custom_call" | custom-call | bytes 4349952 | tf_op jit(solution)/shard_map/pallas_call | solution.py:31
  55.4 1.5 %collective-permute-start.13 = (bf16[256,1024]{1,0:T(8,128)(2,1)S(1)}, bf16[256,1024]{1,0:T(8,128)(2,1)S(1)}, u32[]{:S(2)}, u32[]{:S(2)}) collective-permute-start(bf16[256,1024]{1,0:T(8,128)(2,1)S(1)} %get-tuple-element.56), channel_id=1, source_target_pairs={{0,24},{8,16},{16,8},{24,0},{1,25},{9,17},{17,9},{25,1},{2,26},{10... | collective-permute-start | bytes 1572872 | tf_op jit(solution)/shard_map/ppermute | solution.py:285
  56.9 1.8 %collective-permute-start.14 = (bf16[256,1024]{1,0:T(8,128)(2,1)S(1)}, bf16[256,1024]{1,0:T(8,128)(2,1)S(1)}, u32[]{:S(2)}, u32[]{:S(2)}) collective-permute-start(bf16[256,1024]{1,0:T(8,128)(2,1)S(1)} %get-tuple-element.57), channel_id=1, source_target_pairs={{0,16},{8,24},{16,0},{24,8},{1,17},{9,25},{17,1},{25,9},{2,18},{10... | collective-permute-start | bytes 1572872 | tf_op jit(solution)/shard_map/ppermute | solution.py:285
  59.2 1.3 %collective-permute-start.16 = (bf16[128,4096]{1,0:T(8,128)(2,1)S(1)}, bf16[128,4096]{1,0:T(8,128)(2,1)S(1)}, u32[]{:S(2)}, u32[]{:S(2)}) collective-permute-start(bf16[128,4096]{1,0:T(8,128)(2,1)S(1)} %get-tuple-element.62), channel_id=1, source_target_pairs={{1,2},{3,4},{5,6},{7,0},{9,10},{11,12},{13,14},{15,8},{17,18},{19,... | collective-permute-start | bytes 3145736 | tf_op jit(solution)/shard_map/ppermute | solution.py:279
  60.5 7.3 %collective-permute-done.11.own3_ref = bf16[128,4096]{1,0:T(8,128)(2,1)S(1)} collective-permute-done((bf16[128,4096]{1,0:T(8,128)(2,1)S(1)}, bf16[128,4096]{1,0:T(8,128)(2,1)S(1)}, u32[]{:S(2)}, u32[]{:S(2)}) %collective-permute-start.11) | collective-permute-done | bytes 1048608 | tf_op jit(solution)/shard_map/ppermute | solution.py:279
  67.8 1.7 %shard_map.77 = (f32[128,4096]{1,0:T(8,128)S(1)}, f32[128,4096]{1,0:T(8,128)S(1)}) custom-call(bf16[128,4096]{1,0:T(8,128)(2,1)S(1)} %copy-done, bf16[128,8192]{1,0:T(8,128)(2,1)S(1)} %collective-permute-done.8.pair_ref, bf16[128,4096]{1,0:T(8,128)(2,1)S(1)} %copy-done.1, bf16[128,4096]{1,0:T(8,128)(2,1)S(1)} %shard_map.68.refs_1_.n1_ref, ...), custom_call_target="tpu_custom_call" | custom-call | flops 49999998976 | bytes 12784128 | tf_op jit(solution)/shard_map/pallas_call | solution.py:31
  69.4 1.8 %collective-permute-done.13.refs_0_ = bf16[256,1024]{1,0:T(8,128)(2,1)S(1)} collective-permute-done((bf16[256,1024]{1,0:T(8,128)(2,1)S(1)}, bf16[256,1024]{1,0:T(8,128)(2,1)S(1)}, u32[]{:S(2)}, u32[]{:S(2)}) %collective-permute-start.13) | collective-permute-done | bytes 524320 | tf_op jit(solution)/shard_map/ppermute | solution.py:285
  71.2 8.2 %collective-permute-done.14.refs_1_ = bf16[256,1024]{1,0:T(8,128)(2,1)S(1)} collective-permute-done((bf16[256,1024]{1,0:T(8,128)(2,1)S(1)}, bf16[256,1024]{1,0:T(8,128)(2,1)S(1)}, u32[]{:S(2)}, u32[]{:S(2)}) %collective-permute-start.14) | collective-permute-done | bytes 524320 | tf_op jit(solution)/shard_map/ppermute | solution.py:285
  79.7 1.2 %shard_map.79 = (bf16[128,4096]{1,0:T(8,128)(2,1)}, f32[128,4096]{1,0:T(8,128)S(1)}) custom-call(f32[128,4096]{1,0:T(8,128)S(1)} %get-tuple-element.52.pulled, f32[128,4096]{1,0:T(8,128)S(1)} %get-tuple-element.53.base, bf16[256,1024]{1,0:T(8,128)(2,1)S(1)} %collective-permute-done.13.refs_0_, bf16[256,1024]{1,0:T(8,128)(2,1)S(1)} %collective-permute-done.14.refs_1_, ...), custom_call_target="tpu_custom_call" | custom-call | bytes 9437184 | tf_op jit(solution)/shard_map/pallas_call | solution.py:31
  80.9 0.9 %collective-permute-done.16.own1 = bf16[128,4096]{1,0:T(8,128)(2,1)S(1)} collective-permute-done((bf16[128,4096]{1,0:T(8,128)(2,1)S(1)}, bf16[128,4096]{1,0:T(8,128)(2,1)S(1)}, u32[]{:S(2)}, u32[]{:S(2)}) %collective-permute-start.16) | collective-permute-done | bytes 1048608 | tf_op jit(solution)/shard_map/ppermute | solution.py:279
  81.8 1.1 %shard_map.80 = bf16[128,4096]{1,0:T(8,128)(2,1)} custom-call(f32[128,4096]{1,0:T(8,128)S(1)} %get-tuple-element.61.almost, bf16[128,4096]{1,0:T(8,128)(2,1)S(1)} %collective-permute-done.16.own1), custom_call_target="tpu_custom_call" | custom-call | bytes 4194304 | tf_op jit(solution)/shard_map/pallas_call | solution.py:31
  (25 shorter events, 4.4 us)
Async XLA Ops:
  0.6 10.4 %copy-start.1 = (bf16[128,4096]{1,0:T(8,128)(2,1)S(1)}, bf16[128,4096]{1,0:T(8,128)(2,1)}, u32[]{:S(2)}) copy-start(bf16[128,4096]{1,0:T(8,128)(2,1)} %p_ref.1) | copy-start | bytes 3145732
  0.6 20.5 %collective-permute-start.3 = (bf16[128,4096]{1,0:T(8,128)(2,1)}, bf16[128,4096]{1,0:T(8,128)(2,1)S(1)}, u32[]{:S(2)}, u32[]{:S(2)}) collective-permute-start(bf16[128,4096]{1,0:T(8,128)(2,1)} %p_ref.1), channel_id=1, source_target_pairs={{0,7},{1,0},{2,1},{3,2},{4,3},{5,4},{6,5},{7,6},{8,15},{9,8},{10,9... | collective-permute-start | bytes 3145736 | tf_op jit(solution)/shard_map/ppermute | solution.py:279
  5.2 0.7 copy-start.2
  7.5 22.8 %collective-permute-start = (bf16[272,1024]{1,0:T(8,128)(2,1)S(1)}, bf16[272,1024]{1,0:T(8,128)(2,1)S(1)}, u32[]{:S(2)}, u32[]{:S(2)}) collective-permute-start(bf16[272,1024]{1,0:T(8,128)(2,1)S(1)} %get-tuple-element.33), channel_id=1, source_target_pairs={{0,24},{8,16},{16,8},{24,0},{1,25},{9,17},{17,9},{25,1},{2,26},{10... | collective-permute-start | bytes 1671176 | tf_op jit(solution)/shard_map/ppermute | solution.py:285
  10.0 22.2 %collective-permute-start.1 = (bf16[272,1024]{1,0:T(8,128)(2,1)S(1)}, bf16[272,1024]{1,0:T(8,128)(2,1)S(1)}, u32[]{:S(2)}, u32[]{:S(2)}) collective-permute-start(bf16[272,1024]{1,0:T(8,128)(2,1)S(1)} %get-tuple-element.34), channel_id=1, source_target_pairs={{0,16},{8,24},{16,0},{24,8},{1,17},{9,25},{17,1},{25,9},{2,18},{10... | collective-permute-start | bytes 1671176 | tf_op jit(solution)/shard_map/ppermute | solution.py:285
  10.5 22.0 %collective-permute-start.2 = (bf16[272,1024]{1,0:T(8,128)(2,1)S(1)}, bf16[272,1024]{1,0:T(8,128)(2,1)S(1)}, u32[]{:S(2)}, u32[]{:S(2)}) collective-permute-start(bf16[272,1024]{1,0:T(8,128)(2,1)S(1)} %get-tuple-element.35), channel_id=1, source_target_pairs={{0,8},{8,0},{16,24},{24,16},{1,9},{9,1},{17,25},{25,17},{2,10},{10... | collective-permute-start | bytes 1671176 | tf_op jit(solution)/shard_map/ppermute | solution.py:285
  11.1 16.9 %copy-start = (bf16[128,4096]{1,0:T(8,128)(2,1)S(1)}, bf16[128,4096]{1,0:T(8,128)(2,1)}, u32[]{:S(2)}) copy-start(bf16[128,4096]{1,0:T(8,128)(2,1)} %q_ref.9) | copy-start | bytes 3145732
  11.1 16.8 %collective-permute-start.4 = (bf16[128,4096]{1,0:T(8,128)(2,1)S(1)}, bf16[128,4096]{1,0:T(8,128)(2,1)S(1)}, u32[]{:S(2)}, u32[]{:S(2)}) collective-permute-start(bf16[128,4096]{1,0:T(8,128)(2,1)S(1)} %shard_map.69), channel_id=1, source_target_pairs={{1,6},{3,0},{5,2},{7,4},{9,14},{11,8},{13,10},{15,12},{17,22},{19,... | collective-permute-start | bytes 3145736 | tf_op jit(solution)/shard_map/ppermute | solution.py:279
  21.2 19.0 %collective-permute-start.9 = (bf16[128,4096]{1,0:T(8,128)(2,1)S(1)}, bf16[128,4096]{1,0:T(8,128)(2,1)S(1)}, u32[]{:S(2)}, u32[]{:S(2)}) collective-permute-start(bf16[128,4096]{1,0:T(8,128)(2,1)S(1)} %shard_map.68.refs_1_.n1_ref), channel_id=1, source_target_pairs={{1,7},{3,1},{5,3},{7,5},{9,15},{11,9},{13,11},{15,13},{17,23},{19,... | collective-permute-start | bytes 3145736 | tf_op jit(solution)/shard_map/ppermute | solution.py:279
  28.1 9.1 %collective-permute-start.8 = (bf16[128,8192]{1,0:T(8,128)(2,1)S(1)}, bf16[128,8192]{1,0:T(8,128)(2,1)S(1)}, u32[]{:S(2)}, u32[]{:S(2)}) collective-permute-start(bf16[128,8192]{1,0:T(8,128)(2,1)S(1)} %shard_map.72), channel_id=1, source_target_pairs={{0,1},{1,0},{2,3},{3,2},{4,5},{5,4},{6,7},{7,6},{8,9},{9,8},{10,11... | collective-permute-start | bytes 6291464 | tf_op jit(solution)/shard_map/ppermute | solution.py:282
  33.6 6.6 %copy-start.3 = (f32[128]{0:T(128)S(1)}, f32[128]{0:T(128)}, u32[]{:S(2)}) copy-start(f32[128]{0:T(128)} %param.7) | copy-start | bytes 1540
  33.6 4.5 %collective-permute-start.5 = (f32[3,128]{1,0:T(4,128)S(1)}, f32[3,128]{1,0:T(4,128)S(1)}, u32[]{:S(2)}, u32[]{:S(2)}) collective-permute-start(f32[3,128]{1,0:T(4,128)S(1)} %get-tuple-element.39), channel_id=1, source_target_pairs={{0,24},{8,16},{16,8},{24,0},{1,25},{9,17},{17,9},{25,1},{2,26},{10... | collective-permute-start | bytes 4616 | tf_op jit(solution)/shard_map/ppermute | solution.py:285
  35.2 3.6 %collective-permute-start.6 = (f32[3,128]{1,0:T(4,128)S(1)}, f32[3,128]{1,0:T(4,128)S(1)}, u32[]{:S(2)}, u32[]{:S(2)}) collective-permute-start(f32[3,128]{1,0:T(4,128)S(1)} %get-tuple-element.40), channel_id=1, source_target_pairs={{0,16},{8,24},{16,0},{24,8},{1,17},{9,25},{17,1},{25,9},{2,18},{10... | collective-permute-start | bytes 4616 | tf_op jit(solution)/shard_map/ppermute | solution.py:285
  36.7 3.6 %collective-permute-start.7 = (f32[3,128]{1,0:T(4,128)S(1)}, f32[3,128]{1,0:T(4,128)S(1)}, u32[]{:S(2)}, u32[]{:S(2)}) collective-permute-start(f32[3,128]{1,0:T(4,128)S(1)} %get-tuple-element.41), channel_id=1, source_target_pairs={{0,8},{8,0},{16,24},{24,16},{1,9},{9,1},{17,25},{25,17},{2,10},{10... | collective-permute-start | bytes 4616 | tf_op jit(solution)/shard_map/ppermute | solution.py:285
  41.4 17.6 %collective-permute-start.12 = (bf16[128,4096]{1,0:T(8,128)(2,1)S(1)}, bf16[128,4096]{1,0:T(8,128)(2,1)S(1)}, u32[]{:S(2)}, u32[]{:S(2)}) collective-permute-start(bf16[128,4096]{1,0:T(8,128)(2,1)S(1)} %get-tuple-element.50), channel_id=1, source_target_pairs={{1,3},{3,5},{5,7},{7,1},{9,11},{11,13},{13,15},{15,9},{17,19},{19,... | collective-permute-start | bytes 3145736 | tf_op jit(solution)/shard_map/ppermute | solution.py:279
  42.1 9.5 %collective-permute-start.10 = (bf16[128,256]{1,0:T(8,128)(2,1)S(1)}, bf16[128,256]{1,0:T(8,128)(2,1)S(1)}, u32[]{:S(2)}, u32[]{:S(2)}) collective-permute-start(bf16[128,256]{1,0:T(8,128)(2,1)S(1)} %get-tuple-element.47), channel_id=1, source_target_pairs={{0,1},{1,0},{2,3},{3,2},{4,5},{5,4},{6,7},{7,6},{8,9},{9,8},{10,11... | collective-permute-start | bytes 196616 | tf_op jit(solution)/shard_map/ppermute | solution.py:282
  52.0 15.8 %collective-permute-start.11 = (bf16[128,4096]{1,0:T(8,128)(2,1)S(1)}, bf16[128,4096]{1,0:T(8,128)(2,1)S(1)}, u32[]{:S(2)}, u32[]{:S(2)}) collective-permute-start(bf16[128,4096]{1,0:T(8,128)(2,1)S(1)} %get-tuple-element.48), channel_id=1, source_target_pairs={{0,3},{2,5},{4,7},{6,1},{8,11},{10,13},{12,15},{14,9},{16,19},{18,... | collective-permute-start | bytes 3145736 | tf_op jit(solution)/shard_map/ppermute | solution.py:279
  55.4 15.8 %collective-permute-start.13 = (bf16[256,1024]{1,0:T(8,128)(2,1)S(1)}, bf16[256,1024]{1,0:T(8,128)(2,1)S(1)}, u32[]{:S(2)}, u32[]{:S(2)}) collective-permute-start(bf16[256,1024]{1,0:T(8,128)(2,1)S(1)} %get-tuple-element.56), channel_id=1, source_target_pairs={{0,24},{8,16},{16,8},{24,0},{1,25},{9,17},{17,9},{25,1},{2,26},{10... | collective-permute-start | bytes 1572872 | tf_op jit(solution)/shard_map/ppermute | solution.py:285
  56.9 22.5 %collective-permute-start.14 = (bf16[256,1024]{1,0:T(8,128)(2,1)S(1)}, bf16[256,1024]{1,0:T(8,128)(2,1)S(1)}, u32[]{:S(2)}, u32[]{:S(2)}) collective-permute-start(bf16[256,1024]{1,0:T(8,128)(2,1)S(1)} %get-tuple-element.57), channel_id=1, source_target_pairs={{0,16},{8,24},{16,0},{24,8},{1,17},{9,25},{17,1},{25,9},{2,18},{10... | collective-permute-start | bytes 1572872 | tf_op jit(solution)/shard_map/ppermute | solution.py:285
  58.7 21.0 %collective-permute-start.15 = (bf16[256,1024]{1,0:T(8,128)(2,1)S(1)}, bf16[256,1024]{1,0:T(8,128)(2,1)S(1)}, u32[]{:S(2)}, u32[]{:S(2)}) collective-permute-start(bf16[256,1024]{1,0:T(8,128)(2,1)S(1)} %get-tuple-element.58), channel_id=1, source_target_pairs={{0,8},{8,0},{16,24},{24,16},{1,9},{9,1},{17,25},{25,17},{2,10},{10... | collective-permute-start | bytes 1572872 | tf_op jit(solution)/shard_map/ppermute | solution.py:285
  59.2 22.7 %collective-permute-start.16 = (bf16[128,4096]{1,0:T(8,128)(2,1)S(1)}, bf16[128,4096]{1,0:T(8,128)(2,1)S(1)}, u32[]{:S(2)}, u32[]{:S(2)}) collective-permute-start(bf16[128,4096]{1,0:T(8,128)(2,1)S(1)} %get-tuple-element.62), channel_id=1, source_target_pairs={{1,2},{3,4},{5,6},{7,0},{9,10},{11,12},{13,14},{15,8},{17,18},{19,... | collective-permute-start | bytes 3145736 | tf_op jit(solution)/shard_map/ppermute | solution.py:279

commit v7 on v5

--- a/solution.py
+++ b/solution.py
@@ -271,9 +271,11 @@
     loop = lax.axis_size("blk")
     cols = width // groups
 
+    def pairs_of(by, which=(0, 1)):
+        return [(i, (i + by) % loop) for i in range(loop) if i % 2 in which]
+
     def shift(array, by, which=(0, 1)):
-        pairs = [(i, (i + by) % loop) for i in range(loop) if i % 2 in which]
-        return lax.ppermute(array, "blk", pairs)
+        return lax.ppermute(array, "blk", pairs_of(by, which))
 
     def swap(array):
         return lax.ppermute(array, "blk", [(i, i ^ 1) for i in range(loop)])
@@ -329,7 +331,8 @@
     sent3, partial1, token = local_call(
         sums_body, [block, block32, TOKEN], queries, pair, coef, from_core
     )
-    own3 = shift(sent3, 3, (0,))
+    late = (loop - 4, loop - 1)
+    own3 = lax.ppermute(sent3, "blk", [pair for pair in pairs_of(3, (0,)) if pair != late])
 
     hard_coefs = exchange([hard_coef] * groups)
     square_all = pltpu.VMEM((groups * rows, groups * rows), BF16)
@@ -340,7 +343,7 @@
     backs = exchange(backs)
 
     sent1, token = local_call(relay_body, [block, TOKEN], partial1, got3, flops=SOME)
-    own1 = shift(sent1, 1, (1,))
+    own1 = lax.ppermute(sent1, "blk", pairs_of(1, (1,)) + [late])
 
     pulled, base = local_call(
         base_body, [block32, block32],

time: 83.2 us -> 84.1 us (1.011); the launches traced: 82.9 us -> 82.9 us
  no operation moved by 1% of the time
where the time goes in v7:
time: 84.1 us; the launch traced here: 82.9 us
  waiting for transfers between devices  41.4 us (49%)
  starting transfers between devices  27.8 us (33%)
  Pallas kernels  12.2 us (15%)
    ppermute x4, waiting for transfers between devices, shift(): return lax.ppermute(array, 'blk', pairs_of(by, which))  14.6 us
    ppermute x12, starting transfers between devices, over_groups(): return lax.ppermute(array, 'grp', [(i, i ^ r) for i in range(groups)])  14.1 us
    ppermute x12, waiting for transfers between devices, over_groups(): return lax.ppermute(array, 'grp', [(i, i ^ r) for i in range(groups)])  13.7 us
    pallas_call x14, Pallas kernels, local_call(): pl.pallas_call(body, out_shape=out_shape, in_specs=in_specs or [VMEM] * l...  12.2 us
    ppermute x1, waiting for transfers between devices, per_device(): lax.ppermute(sent3, 'blk', [pair for pair in pairs_of(3, (0,)) if pair !=...  9.19 us
    ppermute x4, starting transfers between devices, shift(): return lax.ppermute(array, 'blk', pairs_of(by, which))  7.41 us
    ppermute x1, waiting for transfers between devices, per_device(): own1 = lax.ppermute(sent1, 'blk', pairs_of(1, (1,)) + [late])  3.91 us
    ppermute x2, starting transfers between devices, swap(): return lax.ppermute(array, 'blk', [(i, i ^ 1) for i in range(loop)])  2.54 us
  transfers between devices with their start and end apart: 20, of which 11 were waited for; matrix products, arithmetic and copies ran while one was open for 0% of the time, Pallas kernels for 12%

profile of v7, /device:TPU:0, one launch (start us, length us, event | category | flops | bytes accessed | tf_op | source)
XLA Modules:
  0.0 82.9 jit_solution(13386284120969751253)
XLA Ops:
  0.6 4.5 %collective-permute-start.3 = (bf16[128,4096]{1,0:T(8,128)(2,1)}, bf16[128,4096]{1,0:T(8,128)(2,1)S(1)}, u32[]{:S(2)}, u32[]{:S(2)}) collective-permute-start(bf16[128,4096]{1,0:T(8,128)(2,1)} %p_ref.1), channel_id=1, source_target_pairs={{0,7},{1,0},{2,1},{3,2},{4,3},{5,4},{6,5},{7,6},{8,15},{9,8},{10,9... | collective-permute-start | bytes 3145736 | tf_op jit(solution)/shard_map/ppermute | solution.py:278
  5.2 0.7 copy-done.2
  5.9 1.6 %shard_map.67 = (bf16[272,1024]{1,0:T(8,128)(2,1)S(1)}, bf16[272,1024]{1,0:T(8,128)(2,1)S(1)}, bf16[272,1024]{1,0:T(8,128)(2,1)S(1)}, bf16[272,1024]{1,0:T(8,128)(2,1)S(1)}, f32[8,128]{1,0:T(8,128)S(1)}) custom-call(bf16[128,4096]{1,0:T(8,128)(2,1)} %q_ref.9, bf16[128,4096]{1,0:T(8,128)(2,1)} %p_ref.1, s32[3,128]{1,0:T(4,128)S(1)} %bitcast.3), custom_call_target="tpu_custom_call" | custom-call | bytes 4331008 | tf_op jit(solution)/shard_map/pallas_call | solution.py:31
  7.5 2.5 %collective-permute-start = (bf16[272,1024]{1,0:T(8,128)(2,1)S(1)}, bf16[272,1024]{1,0:T(8,128)(2,1)S(1)}, u32[]{:S(2)}, u32[]{:S(2)}) collective-permute-start(bf16[272,1024]{1,0:T(8,128)(2,1)S(1)} %get-tuple-element.33), channel_id=1, source_target_pairs={{0,24},{8,16},{16,8},{24,0},{1,25},{9,17},{17,9},{25,1},{2,26},{10... | collective-permute-start | bytes 1671176 | tf_op jit(solution)/shard_map/ppermute | solution.py:284
  11.1 1.4 %collective-permute-start.4 = (bf16[128,4096]{1,0:T(8,128)(2,1)S(1)}, bf16[128,4096]{1,0:T(8,128)(2,1)S(1)}, u32[]{:S(2)}, u32[]{:S(2)}) collective-permute-start(bf16[128,4096]{1,0:T(8,128)(2,1)S(1)} %shard_map.69), channel_id=1, source_target_pairs={{1,6},{3,0},{5,2},{7,4},{9,14},{11,8},{13,10},{15,12},{17,22},{19,... | collective-permute-start | bytes 3145736 | tf_op jit(solution)/shard_map/ppermute | solution.py:278
  12.5 8.6 %collective-permute-done.3.source = bf16[128,4096]{1,0:T(8,128)(2,1)S(1)} collective-permute-done((bf16[128,4096]{1,0:T(8,128)(2,1)}, bf16[128,4096]{1,0:T(8,128)(2,1)S(1)}, u32[]{:S(2)}, u32[]{:S(2)}) %collective-permute-start.3) | collective-permute-done | bytes 1048608 | tf_op jit(solution)/shard_map/ppermute | solution.py:278
  21.2 0.7 collective-permute-start.9
  22.0 6.0 %collective-permute-done.4.refs_2_.e3_ref = bf16[128,4096]{1,0:T(8,128)(2,1)S(1)} collective-permute-done((bf16[128,4096]{1,0:T(8,128)(2,1)S(1)}, bf16[128,4096]{1,0:T(8,128)(2,1)S(1)}, u32[]{:S(2)}, u32[]{:S(2)}) %collective-permute-start.4) | collective-permute-done | bytes 1048608 | tf_op jit(solution)/shard_map/ppermute | solution.py:278
  28.1 1.2 %collective-permute-start.8 = (bf16[128,8192]{1,0:T(8,128)(2,1)S(1)}, bf16[128,8192]{1,0:T(8,128)(2,1)S(1)}, u32[]{:S(2)}, u32[]{:S(2)}) collective-permute-start(bf16[128,8192]{1,0:T(8,128)(2,1)S(1)} %shard_map.72), channel_id=1, source_target_pairs={{0,1},{1,0},{2,3},{3,2},{4,5},{5,4},{6,7},{7,6},{8,9},{9,8},{10,11... | collective-permute-start | bytes 6291464 | tf_op jit(solution)/shard_map/ppermute | solution.py:281
  29.3 1.0 %shard_map.70 = (f32[128,128]{1,0:T(8,128)S(1)}, f32[128,128]{1,0:T(8,128)S(1)}, f32[128,128]{1,0:T(8,128)S(1)}) custom-call(bf16[128,4096]{1,0:T(8,128)(2,1)S(1)} %copy-done, bf16[128,4096]{1,0:T(8,128)(2,1)S(1)} %copy-done.1, bf16[128,4096]{1,0:T(8,128)(2,1)S(1)} %shard_map.68.refs_1_.n1_ref, bf16[128,4096]{1,0:T(8,128)(2,1)S(1)} %collective-permute-done.4.refs_2_.e3_ref), custom_call_target="tpu_custom_call" | custom-call | bytes 4390912 | tf_op jit(solution)/shard_map/pallas_call | solution.py:31
  30.3 1.9 %collective-permute-done.1.refs_1_.refs_5_ = bf16[272,1024]{1,0:T(8,128)(2,1)S(1)} collective-permute-done((bf16[272,1024]{1,0:T(8,128)(2,1)S(1)}, bf16[272,1024]{1,0:T(8,128)(2,1)S(1)}, u32[]{:S(2)}, u32[]{:S(2)}) %collective-permute-start.1) | collective-permute-done | bytes 557088 | tf_op jit(solution)/shard_map/ppermute | solution.py:284
  32.5 1.2 %shard_map.71 = (f32[3,128]{1,0:T(4,128)S(1)}, f32[3,128]{1,0:T(4,128)S(1)}, f32[3,128]{1,0:T(4,128)S(1)}, f32[3,128]{1,0:T(4,128)S(1)}) custom-call(bf16[272,1024]{1,0:T(8,128)(2,1)S(1)} %collective-permute-done.refs_0_.refs_4_, bf16[272,1024]{1,0:T(8,128)(2,1)S(1)} %collective-permute-done.1.refs_1_.refs_5_, ...), custom_call_target="tpu_custom_call" | custom-call | flops 49999998976 | bytes 2299904 | tf_op jit(solution)/shard_map/pallas_call | solution.py:31
  33.6 1.6 %collective-permute-start.5 = (f32[3,128]{1,0:T(4,128)S(1)}, f32[3,128]{1,0:T(4,128)S(1)}, u32[]{:S(2)}, u32[]{:S(2)}) collective-permute-start(f32[3,128]{1,0:T(4,128)S(1)} %get-tuple-element.39), channel_id=1, source_target_pairs={{0,24},{8,16},{16,8},{24,0},{1,25},{9,17},{17,9},{25,1},{2,26},{10... | collective-permute-start | bytes 4616 | tf_op jit(solution)/shard_map/ppermute | solution.py:284
  35.2 1.4 %collective-permute-start.6 = (f32[3,128]{1,0:T(4,128)S(1)}, f32[3,128]{1,0:T(4,128)S(1)}, u32[]{:S(2)}, u32[]{:S(2)}) collective-permute-start(f32[3,128]{1,0:T(4,128)S(1)} %get-tuple-element.40), channel_id=1, source_target_pairs={{0,16},{8,24},{16,0},{24,8},{1,17},{9,25},{17,1},{25,9},{2,18},{10... | collective-permute-start | bytes 4616 | tf_op jit(solution)/shard_map/ppermute | solution.py:284
  38.2 0.6 collective-permute-done.6.refs_1_
  38.8 1.4 %collective-permute-done.7.refs_2_ = f32[3,128]{1,0:T(4,128)S(1)} collective-permute-done((f32[3,128]{1,0:T(4,128)S(1)}, f32[3,128]{1,0:T(4,128)S(1)}, u32[]{:S(2)}, u32[]{:S(2)}) %collective-permute-start.7) | collective-permute-done | bytes 1568 | tf_op jit(solution)/shard_map/ppermute | solution.py:284
  40.2 1.1 %shard_map.74 = (f32[1,128]{1,0:T(1,128)}, bf16[128,512]{1,0:T(8,128)(2,1)S(1)}, f32[3,128]{1,0:T(4,128)S(1)}, bf16[128,256]{1,0:T(8,128)(2,1)S(1)}, bf16[128,4096]{1,0:T(8,128)(2,1)S(1)}) custom-call(f32[3,128]{1,0:T(4,128)S(1)} %collective-permute-done.5.refs_0_, f32[3,128]{1,0:T(4,128)S(1)} %collective-permute-done.6.refs_1_, ...), custom_call_target="tpu_custom_call" | custom-call | bytes 3613184 | tf_op jit(solution)/shard_map/pallas_call | solution.py:31
  41.4 0.7 collective-permute-start.12
  42.1 1.4 %collective-permute-start.10 = (bf16[128,256]{1,0:T(8,128)(2,1)S(1)}, bf16[128,256]{1,0:T(8,128)(2,1)S(1)}, u32[]{:S(2)}, u32[]{:S(2)}) collective-permute-start(bf16[128,256]{1,0:T(8,128)(2,1)S(1)} %get-tuple-element.47), channel_id=1, source_target_pairs={{0,1},{1,0},{2,3},{3,2},{4,5},{5,4},{6,7},{7,6},{8,9},{9,8},{10,11... | collective-permute-start | bytes 196616 | tf_op jit(solution)/shard_map/ppermute | solution.py:281
  43.4 2.7 %collective-permute-start.13 = (f32[3,128]{1,0:T(4,128)S(1)}, f32[3,128]{1,0:T(4,128)S(1)}, u32[]{:S(2)}, u32[]{:S(2)}) collective-permute-start(f32[3,128]{1,0:T(4,128)S(1)} %get-tuple-element.54.refs_3_), channel_id=1, source_target_pairs={{0,24},{8,16},{16,8},{24,0},{1,25},{9,17},{17,9},{25,1},{2,26},{10... | collective-permute-start | bytes 4616 | tf_op jit(solution)/shard_map/ppermute | solution.py:284
  46.3 0.6 collective-permute-start.15
  47.4 2.5 %collective-permute-start.11 = (bf16[128,4096]{1,0:T(8,128)(2,1)S(1)}, bf16[128,4096]{1,0:T(8,128)(2,1)S(1)}, u32[]{:S(2)}, u32[]{:S(2)}) collective-permute-start(bf16[128,4096]{1,0:T(8,128)(2,1)S(1)} %get-tuple-element.48), channel_id=1, source_target_pairs={{0,3},{2,5},{6,1},{8,11},{10,13},{14,9},{16,19},{18,21},{22,17},{2... | collective-permute-start | bytes 3145736 | tf_op jit(solution)/shard_map/ppermute | solution.py:335
  49.9 2.1 %shard_map.78 = (bf16[256,1024]{1,0:T(8,128)(2,1)S(1)}, bf16[256,1024]{1,0:T(8,128)(2,1)S(1)}, bf16[256,1024]{1,0:T(8,128)(2,1)S(1)}, bf16[256,1024]{1,0:T(8,128)(2,1)S(1)}, f32[8,128]{1,0:T(8,128)}) custom-call(f32[3,128]{1,0:T(4,128)S(1)} %collective-permute-done.13.refs_0_, f32[3,128]{1,0:T(4,128)S(1)} %collective-permute-done.14.refs_1_, ...), custom_call_target="tpu_custom_call" | custom-call | bytes 4339712 | tf_op jit(solution)/shard_map/pallas_call | solution.py:31
  52.0 2.6 %collective-permute-start.16 = (bf16[256,1024]{1,0:T(8,128)(2,1)S(1)}, bf16[256,1024]{1,0:T(8,128)(2,1)S(1)}, u32[]{:S(2)}, u32[]{:S(2)}) collective-permute-start(bf16[256,1024]{1,0:T(8,128)(2,1)S(1)} %get-tuple-element.56), channel_id=1, source_target_pairs={{0,24},{8,16},{16,8},{24,0},{1,25},{9,17},{17,9},{25,1},{2,26},{10... | collective-permute-start | bytes 1572872 | tf_op jit(solution)/shard_map/ppermute | solution.py:284
  54.9 0.6 collective-permute-start.18
  55.7 1.3 %collective-permute-start.19 = (bf16[128,4096]{1,0:T(8,128)(2,1)S(1)}, bf16[128,4096]{1,0:T(8,128)(2,1)S(1)}, u32[]{:S(2)}, u32[]{:S(2)}) collective-permute-start(bf16[128,4096]{1,0:T(8,128)(2,1)S(1)} %get-tuple-element.62), channel_id=1, source_target_pairs={{1,2},{3,4},{5,6},{7,0},{4,7},{9,10},{11,12},{13,14},{15,8},{12,15... | collective-permute-start | bytes 3145736 | tf_op jit(solution)/shard_map/ppermute | solution.py:346
  57.0 9.2 %collective-permute-done.11.own3_ref = bf16[128,4096]{1,0:T(8,128)(2,1)S(1)} collective-permute-done((bf16[128,4096]{1,0:T(8,128)(2,1)S(1)}, bf16[128,4096]{1,0:T(8,128)(2,1)S(1)}, u32[]{:S(2)}, u32[]{:S(2)}) %collective-permute-start.11) | collective-permute-done | bytes 1048608 | tf_op jit(solution)/shard_map/ppermute | solution.py:335
  66.2 1.6 %shard_map.77 = (f32[128,4096]{1,0:T(8,128)S(1)}, f32[128,4096]{1,0:T(8,128)S(1)}) custom-call(bf16[128,4096]{1,0:T(8,128)(2,1)S(1)} %copy-done, bf16[128,8192]{1,0:T(8,128)(2,1)S(1)} %collective-permute-done.8.pair_ref, bf16[128,4096]{1,0:T(8,128)(2,1)S(1)} %copy-done.1, bf16[128,4096]{1,0:T(8,128)(2,1)S(1)} %shard_map.68.refs_1_.n1_ref, ...), custom_call_target="tpu_custom_call" | custom-call | flops 49999998976 | bytes 12784128 | tf_op jit(solution)/shard_map/pallas_call | solution.py:31
  67.9 8.5 %collective-permute-done.17.refs_1_ = bf16[256,1024]{1,0:T(8,128)(2,1)S(1)} collective-permute-done((bf16[256,1024]{1,0:T(8,128)(2,1)S(1)}, bf16[256,1024]{1,0:T(8,128)(2,1)S(1)}, u32[]{:S(2)}, u32[]{:S(2)}) %collective-permute-start.17) | collective-permute-done | bytes 524320 | tf_op jit(solution)/shard_map/ppermute | solution.py:284
  76.7 1.2 %shard_map.79 = (bf16[128,4096]{1,0:T(8,128)(2,1)}, f32[128,4096]{1,0:T(8,128)S(1)}) custom-call(f32[128,4096]{1,0:T(8,128)S(1)} %get-tuple-element.52.pulled, f32[128,4096]{1,0:T(8,128)S(1)} %get-tuple-element.53.base, bf16[256,1024]{1,0:T(8,128)(2,1)S(1)} %collective-permute-done.16.refs_0_, bf16[256,1024]{1,0:T(8,128)(2,1)S(1)} %collective-permute-done.17.refs_1_, ...), custom_call_target="tpu_custom_call" | custom-call | bytes 9437184 | tf_op jit(solution)/shard_map/pallas_call | solution.py:31
  77.9 3.9 %collective-permute-done.19.own1 = bf16[128,4096]{1,0:T(8,128)(2,1)S(1)} collective-permute-done((bf16[128,4096]{1,0:T(8,128)(2,1)S(1)}, bf16[128,4096]{1,0:T(8,128)(2,1)S(1)}, u32[]{:S(2)}, u32[]{:S(2)}) %collective-permute-start.19) | collective-permute-done | bytes 1048608 | tf_op jit(solution)/shard_map/ppermute | solution.py:346
  81.9 1.1 %shard_map.80 = bf16[128,4096]{1,0:T(8,128)(2,1)} custom-call(f32[128,4096]{1,0:T(8,128)S(1)} %get-tuple-element.61.almost, bf16[128,4096]{1,0:T(8,128)(2,1)S(1)} %collective-permute-done.19.own1), custom_call_target="tpu_custom_call" | custom-call | bytes 4194304 | tf_op jit(solution)/shard_map/pallas_call | solution.py:31
  (30 shorter events, 4.7 us)
Async XLA Ops:
  0.6 10.4 %copy-start.1 = (bf16[128,4096]{1,0:T(8,128)(2,1)S(1)}, bf16[128,4096]{1,0:T(8,128)(2,1)}, u32[]{:S(2)}) copy-start(bf16[128,4096]{1,0:T(8,128)(2,1)} %p_ref.1) | copy-start | bytes 3145732
  0.6 20.5 %collective-permute-start.3 = (bf16[128,4096]{1,0:T(8,128)(2,1)}, bf16[128,4096]{1,0:T(8,128)(2,1)S(1)}, u32[]{:S(2)}, u32[]{:S(2)}) collective-permute-start(bf16[128,4096]{1,0:T(8,128)(2,1)} %p_ref.1), channel_id=1, source_target_pairs={{0,7},{1,0},{2,1},{3,2},{4,3},{5,4},{6,5},{7,6},{8,15},{9,8},{10,9... | collective-permute-start | bytes 3145736 | tf_op jit(solution)/shard_map/ppermute | solution.py:278
  5.2 0.7 copy-start.2
  7.5 22.8 %collective-permute-start = (bf16[272,1024]{1,0:T(8,128)(2,1)S(1)}, bf16[272,1024]{1,0:T(8,128)(2,1)S(1)}, u32[]{:S(2)}, u32[]{:S(2)}) collective-permute-start(bf16[272,1024]{1,0:T(8,128)(2,1)S(1)} %get-tuple-element.33), channel_id=1, source_target_pairs={{0,24},{8,16},{16,8},{24,0},{1,25},{9,17},{17,9},{25,1},{2,26},{10... | collective-permute-start | bytes 1671176 | tf_op jit(solution)/shard_map/ppermute | solution.py:284
  10.0 22.2 %collective-permute-start.1 = (bf16[272,1024]{1,0:T(8,128)(2,1)S(1)}, bf16[272,1024]{1,0:T(8,128)(2,1)S(1)}, u32[]{:S(2)}, u32[]{:S(2)}) collective-permute-start(bf16[272,1024]{1,0:T(8,128)(2,1)S(1)} %get-tuple-element.34), channel_id=1, source_target_pairs={{0,16},{8,24},{16,0},{24,8},{1,17},{9,25},{17,1},{25,9},{2,18},{10... | collective-permute-start | bytes 1671176 | tf_op jit(solution)/shard_map/ppermute | solution.py:284
  10.5 22.0 %collective-permute-start.2 = (bf16[272,1024]{1,0:T(8,128)(2,1)S(1)}, bf16[272,1024]{1,0:T(8,128)(2,1)S(1)}, u32[]{:S(2)}, u32[]{:S(2)}) collective-permute-start(bf16[272,1024]{1,0:T(8,128)(2,1)S(1)} %get-tuple-element.35), channel_id=1, source_target_pairs={{0,8},{8,0},{16,24},{24,16},{1,9},{9,1},{17,25},{25,17},{2,10},{10... | collective-permute-start | bytes 1671176 | tf_op jit(solution)/shard_map/ppermute | solution.py:284
  11.1 16.9 %copy-start = (bf16[128,4096]{1,0:T(8,128)(2,1)S(1)}, bf16[128,4096]{1,0:T(8,128)(2,1)}, u32[]{:S(2)}) copy-start(bf16[128,4096]{1,0:T(8,128)(2,1)} %q_ref.9) | copy-start | bytes 3145732
  11.1 16.8 %collective-permute-start.4 = (bf16[128,4096]{1,0:T(8,128)(2,1)S(1)}, bf16[128,4096]{1,0:T(8,128)(2,1)S(1)}, u32[]{:S(2)}, u32[]{:S(2)}) collective-permute-start(bf16[128,4096]{1,0:T(8,128)(2,1)S(1)} %shard_map.69), channel_id=1, source_target_pairs={{1,6},{3,0},{5,2},{7,4},{9,14},{11,8},{13,10},{15,12},{17,22},{19,... | collective-permute-start | bytes 3145736 | tf_op jit(solution)/shard_map/ppermute | solution.py:278
  21.2 19.0 %collective-permute-start.9 = (bf16[128,4096]{1,0:T(8,128)(2,1)S(1)}, bf16[128,4096]{1,0:T(8,128)(2,1)S(1)}, u32[]{:S(2)}, u32[]{:S(2)}) collective-permute-start(bf16[128,4096]{1,0:T(8,128)(2,1)S(1)} %shard_map.68.refs_1_.n1_ref), channel_id=1, source_target_pairs={{1,7},{3,1},{5,3},{7,5},{9,15},{11,9},{13,11},{15,13},{17,23},{19,... | collective-permute-start | bytes 3145736 | tf_op jit(solution)/shard_map/ppermute | solution.py:278
  28.1 9.1 %collective-permute-start.8 = (bf16[128,8192]{1,0:T(8,128)(2,1)S(1)}, bf16[128,8192]{1,0:T(8,128)(2,1)S(1)}, u32[]{:S(2)}, u32[]{:S(2)}) collective-permute-start(bf16[128,8192]{1,0:T(8,128)(2,1)S(1)} %shard_map.72), channel_id=1, source_target_pairs={{0,1},{1,0},{2,3},{3,2},{4,5},{5,4},{6,7},{7,6},{8,9},{9,8},{10,11... | collective-permute-start | bytes 6291464 | tf_op jit(solution)/shard_map/ppermute | solution.py:281
  33.6 6.6 %copy-start.3 = (f32[128]{0:T(128)S(1)}, f32[128]{0:T(128)}, u32[]{:S(2)}) copy-start(f32[128]{0:T(128)} %param.7) | copy-start | bytes 1540
  33.6 4.5 %collective-permute-start.5 = (f32[3,128]{1,0:T(4,128)S(1)}, f32[3,128]{1,0:T(4,128)S(1)}, u32[]{:S(2)}, u32[]{:S(2)}) collective-permute-start(f32[3,128]{1,0:T(4,128)S(1)} %get-tuple-element.39), channel_id=1, source_target_pairs={{0,24},{8,16},{16,8},{24,0},{1,25},{9,17},{17,9},{25,1},{2,26},{10... | collective-permute-start | bytes 4616 | tf_op jit(solution)/shard_map/ppermute | solution.py:284
  35.2 3.6 %collective-permute-start.6 = (f32[3,128]{1,0:T(4,128)S(1)}, f32[3,128]{1,0:T(4,128)S(1)}, u32[]{:S(2)}, u32[]{:S(2)}) collective-permute-start(f32[3,128]{1,0:T(4,128)S(1)} %get-tuple-element.40), channel_id=1, source_target_pairs={{0,16},{8,24},{16,0},{24,8},{1,17},{9,25},{17,1},{25,9},{2,18},{10... | collective-permute-start | bytes 4616 | tf_op jit(solution)/shard_map/ppermute | solution.py:284
  36.7 3.6 %collective-permute-start.7 = (f32[3,128]{1,0:T(4,128)S(1)}, f32[3,128]{1,0:T(4,128)S(1)}, u32[]{:S(2)}, u32[]{:S(2)}) collective-permute-start(f32[3,128]{1,0:T(4,128)S(1)} %get-tuple-element.41), channel_id=1, source_target_pairs={{0,8},{8,0},{16,24},{24,16},{1,9},{9,1},{17,25},{25,17},{2,10},{10... | collective-permute-start | bytes 4616 | tf_op jit(solution)/shard_map/ppermute | solution.py:284
  41.4 14.1 %collective-permute-start.12 = (bf16[128,4096]{1,0:T(8,128)(2,1)S(1)}, bf16[128,4096]{1,0:T(8,128)(2,1)S(1)}, u32[]{:S(2)}, u32[]{:S(2)}) collective-permute-start(bf16[128,4096]{1,0:T(8,128)(2,1)S(1)} %get-tuple-element.50), channel_id=1, source_target_pairs={{1,3},{3,5},{5,7},{7,1},{9,11},{11,13},{13,15},{15,9},{17,19},{19,... | collective-permute-start | bytes 3145736 | tf_op jit(solution)/shard_map/ppermute | solution.py:278
  42.1 4.9 %collective-permute-start.10 = (bf16[128,256]{1,0:T(8,128)(2,1)S(1)}, bf16[128,256]{1,0:T(8,128)(2,1)S(1)}, u32[]{:S(2)}, u32[]{:S(2)}) collective-permute-start(bf16[128,256]{1,0:T(8,128)(2,1)S(1)} %get-tuple-element.47), channel_id=1, source_target_pairs={{0,1},{1,0},{2,3},{3,2},{4,5},{5,4},{6,7},{7,6},{8,9},{9,8},{10,11... | collective-permute-start | bytes 196616 | tf_op jit(solution)/shard_map/ppermute | solution.py:281
  43.4 6.5 %collective-permute-start.13 = (f32[3,128]{1,0:T(4,128)S(1)}, f32[3,128]{1,0:T(4,128)S(1)}, u32[]{:S(2)}, u32[]{:S(2)}) collective-permute-start(f32[3,128]{1,0:T(4,128)S(1)} %get-tuple-element.54.refs_3_), channel_id=1, source_target_pairs={{0,24},{8,16},{16,8},{24,0},{1,25},{9,17},{17,9},{25,1},{2,26},{10... | collective-permute-start | bytes 4616 | tf_op jit(solution)/shard_map/ppermute | solution.py:284
  46.1 3.8 %collective-permute-start.14 = (f32[3,128]{1,0:T(4,128)S(1)}, f32[3,128]{1,0:T(4,128)S(1)}, u32[]{:S(2)}, u32[]{:S(2)}) collective-permute-start(f32[3,128]{1,0:T(4,128)S(1)} %get-tuple-element.54.refs_3_), channel_id=1, source_target_pairs={{0,16},{8,24},{16,0},{24,8},{1,17},{9,25},{17,1},{25,9},{2,18},{10... | collective-permute-start | bytes 4616 | tf_op jit(solution)/shard_map/ppermute | solution.py:284
  46.3 3.6 %collective-permute-start.15 = (f32[3,128]{1,0:T(4,128)S(1)}, f32[3,128]{1,0:T(4,128)S(1)}, u32[]{:S(2)}, u32[]{:S(2)}) collective-permute-start(f32[3,128]{1,0:T(4,128)S(1)} %get-tuple-element.54.refs_3_), channel_id=1, source_target_pairs={{0,8},{8,0},{16,24},{24,16},{1,9},{9,1},{17,25},{25,17},{2,10},{10... | collective-permute-start | bytes 4616 | tf_op jit(solution)/shard_map/ppermute | solution.py:284
  47.4 18.8 %collective-permute-start.11 = (bf16[128,4096]{1,0:T(8,128)(2,1)S(1)}, bf16[128,4096]{1,0:T(8,128)(2,1)S(1)}, u32[]{:S(2)}, u32[]{:S(2)}) collective-permute-start(bf16[128,4096]{1,0:T(8,128)(2,1)S(1)} %get-tuple-element.48), channel_id=1, source_target_pairs={{0,3},{2,5},{6,1},{8,11},{10,13},{14,9},{16,19},{18,21},{22,17},{2... | collective-permute-start | bytes 3145736 | tf_op jit(solution)/shard_map/ppermute | solution.py:335
  52.0 15.9 %collective-permute-start.16 = (bf16[256,1024]{1,0:T(8,128)(2,1)S(1)}, bf16[256,1024]{1,0:T(8,128)(2,1)S(1)}, u32[]{:S(2)}, u32[]{:S(2)}) collective-permute-start(bf16[256,1024]{1,0:T(8,128)(2,1)S(1)} %get-tuple-element.56), channel_id=1, source_target_pairs={{0,24},{8,16},{16,8},{24,0},{1,25},{9,17},{17,9},{25,1},{2,26},{10... | collective-permute-start | bytes 1572872 | tf_op jit(solution)/shard_map/ppermute | solution.py:284
  54.6 21.8 %collective-permute-start.17 = (bf16[256,1024]{1,0:T(8,128)(2,1)S(1)}, bf16[256,1024]{1,0:T(8,128)(2,1)S(1)}, u32[]{:S(2)}, u32[]{:S(2)}) collective-permute-start(bf16[256,1024]{1,0:T(8,128)(2,1)S(1)} %get-tuple-element.57), channel_id=1, source_target_pairs={{0,16},{8,24},{16,0},{24,8},{1,17},{9,25},{17,1},{25,9},{2,18},{10... | collective-permute-start | bytes 1572872 | tf_op jit(solution)/shard_map/ppermute | solution.py:284
  54.9 21.8 %collective-permute-start.18 = (bf16[256,1024]{1,0:T(8,128)(2,1)S(1)}, bf16[256,1024]{1,0:T(8,128)(2,1)S(1)}, u32[]{:S(2)}, u32[]{:S(2)}) collective-permute-start(bf16[256,1024]{1,0:T(8,128)(2,1)S(1)} %get-tuple-element.58), channel_id=1, source_target_pairs={{0,8},{8,0},{16,24},{24,16},{1,9},{9,1},{17,25},{25,17},{2,10},{10... | collective-permute-start | bytes 1572872 | tf_op jit(solution)/shard_map/ppermute | solution.py:284
  55.7 26.1 %collective-permute-start.19 = (bf16[128,4096]{1,0:T(8,128)(2,1)S(1)}, bf16[128,4096]{1,0:T(8,128)(2,1)S(1)}, u32[]{:S(2)}, u32[]{:S(2)}) collective-permute-start(bf16[128,4096]{1,0:T(8,128)(2,1)S(1)} %get-tuple-element.62), channel_id=1, source_target_pairs={{1,2},{3,4},{5,6},{7,0},{4,7},{9,10},{11,12},{13,14},{15,8},{12,15... | collective-permute-start | bytes 3145736 | tf_op jit(solution)/shard_map/ppermute | solution.py:346

commit v8 on v7

--- a/solution.py
+++ b/solution.py
@@ -136,6 +136,19 @@
     out[...] = source[...]
 
 
+def relay_passages_body(next_ref, p_ref, token, out, relay):
+    out[...] = next_ref[...]
+    own = lax.axis_index("blk") == 2
+
+    @pl.when(own)
+    def _():
+        relay[...] = p_ref[...]
+
+    @pl.when(jnp.logical_not(own))
+    def _():
+        relay[...] = next_ref[...]
+
+
 def choose_body(n1_ref, e3_ref, q_ref, out):
     width = q_ref.shape[1]
     odd = lax.axis_index("blk") % 2 == 1
@@ -164,7 +177,7 @@
     groups, *refs
 ):
     parts, refs = refs[:groups], refs[groups:]
-    q_ref, s0_ref, s1_ref, s2_ref, s3_ref, last_ref, w_ref, *refs = refs
+    last_ref, q_ref, s0_ref, s1_ref, s2_ref, s3_ref, w_ref, *refs = refs
     loss_ref, coef_ref, hard_out, swap_ref, term3_ref = refs
     rows, width = q_ref.shape
     w = w_ref[...]
@@ -308,8 +321,12 @@
 
     (later_p,) = local_call(pass_body, [block], passages, token)
     next3_even = shift(later_p, -3, (1,))
-    (next1,) = local_call(pass_body, [block], next1, token, flops=LONG)
-    next3_odd = shift(next1, -2, (1,))
+    next1, relay = local_call(
+        relay_passages_body, [block] * 2, next1, passages, token, flops=LONG
+    )
+    round_pair = (1, loop - 1)
+    pairs = [pair for pair in pairs_of(-2, (1,)) if pair != round_pair] + [(2, loop - 1)]
+    next3_odd = lax.ppermute(relay, "blk", pairs)
     pair = swap(
         local_call(choose_body, [like(rows, 2 * width)], next1, next3_even, queries, flops=LONG)[0]
     )
@@ -323,7 +340,7 @@
     loss_rows, coef, hard_coef, to_core, term3 = local_call(
         functools.partial(weigh_body, groups),
         [like(1, rows, dtype=F32), like(rows, 4 * rows), triple, like(rows, 2 * rows), block],
-        *parts[::-1], queries, s0, s1, s2, s3, next3_odd, weights[None, :],
+        *parts[::-1], next3_odd, queries, s0, s1, s2, s3, weights[None, :],
     )
 
     got3 = shift(term3, 2, (1,))
@@ -331,8 +348,7 @@
     sent3, partial1, token = local_call(
         sums_body, [block, block32, TOKEN], queries, pair, coef, from_core
     )
-    late = (loop - 4, loop - 1)
-    own3 = lax.ppermute(sent3, "blk", [pair for pair in pairs_of(3, (0,)) if pair != late])
+    own3 = shift(sent3, 3, (0,))
 
     hard_coefs = exchange([hard_coef] * groups)
     square_all = pltpu.VMEM((groups * rows, groups * rows), BF16)
@@ -343,7 +359,7 @@
     backs = exchange(backs)
 
     sent1, token = local_call(relay_body, [block, TOKEN], partial1, got3, flops=SOME)
-    own1 = lax.ppermute(sent1, "blk", pairs_of(1, (1,)) + [late])
+    own1 = shift(sent1, 1, (1,))
 
     pulled, base = local_call(
         base_body, [block32, block32],

time: 84.1 us -> 83.2 us (0.989); the launches traced: 82.9 us -> 82.9 us
    ppermute x2 -> x1, waiting for transfers between devices: 13.1 us -> 0.01 us  [per_device(): next3_odd = lax.ppermute(relay, 'blk', pairs)]
    ppermute x4 -> x5, waiting for transfers between devices: 14.6 us -> 27.6 us  [shift(): return lax.ppermute(array, 'blk', pairs_of(by, which))]
    ppermute x2 -> x1, starting transfers between devices: 3.8 us -> 0.73 us  [per_device(): next3_odd = lax.ppermute(relay, 'blk', pairs)]
    ppermute x4 -> x5, starting transfers between devices: 7.41 us -> 10.5 us  [shift(): return lax.ppermute(array, 'blk', pairs_of(by, which))]
where the time goes in v8:
time: 83.2 us; the launch traced here: 82.9 us
  waiting for transfers between devices  41.3 us (50%)
  starting transfers between devices  27.8 us (33%)
  Pallas kernels  12.2 us (15%)
    ppermute x5, waiting for transfers between devices, shift(): return lax.ppermute(array, 'blk', pairs_of(by, which))  27.6 us
    ppermute x12, starting transfers between devices, over_groups(): return lax.ppermute(array, 'grp', [(i, i ^ r) for i in range(groups)])  14.1 us
    ppermute x12, waiting for transfers between devices, over_groups(): return lax.ppermute(array, 'grp', [(i, i ^ r) for i in range(groups)])  13.7 us
    pallas_call x14, Pallas kernels, local_call(): pl.pallas_call(body, out_shape=out_shape, in_specs=in_specs or [VMEM] * l...  12.2 us
    ppermute x5, starting transfers between devices, shift(): return lax.ppermute(array, 'blk', pairs_of(by, which))  10.5 us
    ppermute x2, starting transfers between devices, swap(): return lax.ppermute(array, 'blk', [(i, i ^ 1) for i in range(loop)])  2.54 us
  transfers between devices with their start and end apart: 20, of which 11 were waited for; matrix products, arithmetic and copies ran while one was open for 0% of the time, Pallas kernels for 12%

profile of v8, /device:TPU:0, one launch (start us, length us, event | category | flops | bytes accessed | tf_op | source)
XLA Modules:
  0.0 82.9 jit_solution(9253525278458089187)
XLA Ops:
  0.6 4.5 %collective-permute-start.3 = (bf16[128,4096]{1,0:T(8,128)(2,1)}, bf16[128,4096]{1,0:T(8,128)(2,1)S(1)}, u32[]{:S(2)}, u32[]{:S(2)}) collective-permute-start(bf16[128,4096]{1,0:T(8,128)(2,1)} %p_ref.3), channel_id=1, source_target_pairs={{0,7},{1,0},{2,1},{3,2},{4,3},{5,4},{6,5},{7,6},{8,15},{9,8},{10,9... | collective-permute-start | bytes 3145736 | tf_op jit(solution)/shard_map/ppermute | solution.py:291
  5.2 0.7 copy-done.2
  5.9 1.6 %shard_map.67 = (bf16[272,1024]{1,0:T(8,128)(2,1)S(1)}, bf16[272,1024]{1,0:T(8,128)(2,1)S(1)}, bf16[272,1024]{1,0:T(8,128)(2,1)S(1)}, bf16[272,1024]{1,0:T(8,128)(2,1)S(1)}, f32[8,128]{1,0:T(8,128)S(1)}) custom-call(bf16[128,4096]{1,0:T(8,128)(2,1)} %q_ref.9, bf16[128,4096]{1,0:T(8,128)(2,1)} %p_ref.3, s32[3,128]{1,0:T(4,128)S(1)} %bitcast.3), custom_call_target="tpu_custom_call" | custom-call | bytes 4331008 | tf_op jit(solution)/shard_map/pallas_call | solution.py:31
  7.5 2.5 %collective-permute-start = (bf16[272,1024]{1,0:T(8,128)(2,1)S(1)}, bf16[272,1024]{1,0:T(8,128)(2,1)S(1)}, u32[]{:S(2)}, u32[]{:S(2)}) collective-permute-start(bf16[272,1024]{1,0:T(8,128)(2,1)S(1)} %get-tuple-element.35), channel_id=1, source_target_pairs={{0,24},{8,16},{16,8},{24,0},{1,25},{9,17},{17,9},{25,1},{2,26},{10... | collective-permute-start | bytes 1671176 | tf_op jit(solution)/shard_map/ppermute | solution.py:297
  11.1 1.4 %collective-permute-start.4 = (bf16[128,4096]{1,0:T(8,128)(2,1)S(1)}, bf16[128,4096]{1,0:T(8,128)(2,1)S(1)}, u32[]{:S(2)}, u32[]{:S(2)}) collective-permute-start(bf16[128,4096]{1,0:T(8,128)(2,1)S(1)} %shard_map.69), channel_id=1, source_target_pairs={{1,6},{3,0},{5,2},{7,4},{9,14},{11,8},{13,10},{15,12},{17,22},{19,... | collective-permute-start | bytes 3145736 | tf_op jit(solution)/shard_map/ppermute | solution.py:291
  12.5 8.6 %collective-permute-done.3.next_ref = bf16[128,4096]{1,0:T(8,128)(2,1)S(1)} collective-permute-done((bf16[128,4096]{1,0:T(8,128)(2,1)}, bf16[128,4096]{1,0:T(8,128)(2,1)S(1)}, u32[]{:S(2)}, u32[]{:S(2)}) %collective-permute-start.3) | collective-permute-done | bytes 1048608 | tf_op jit(solution)/shard_map/ppermute | solution.py:291
  21.3 0.7 collective-permute-start.8
  22.0 5.9 %collective-permute-done.4.refs_2_.e3_ref = bf16[128,4096]{1,0:T(8,128)(2,1)S(1)} collective-permute-done((bf16[128,4096]{1,0:T(8,128)(2,1)S(1)}, bf16[128,4096]{1,0:T(8,128)(2,1)S(1)}, u32[]{:S(2)}, u32[]{:S(2)}) %collective-permute-start.4) | collective-permute-done | bytes 1048608 | tf_op jit(solution)/shard_map/ppermute | solution.py:291
  28.1 1.2 %collective-permute-start.9 = (bf16[128,8192]{1,0:T(8,128)(2,1)S(1)}, bf16[128,8192]{1,0:T(8,128)(2,1)S(1)}, u32[]{:S(2)}, u32[]{:S(2)}) collective-permute-start(bf16[128,8192]{1,0:T(8,128)(2,1)S(1)} %shard_map.72), channel_id=1, source_target_pairs={{0,1},{1,0},{2,3},{3,2},{4,5},{5,4},{6,7},{7,6},{8,9},{9,8},{10,11... | collective-permute-start | bytes 6291464 | tf_op jit(solution)/shard_map/ppermute | solution.py:294
  29.3 1.0 %shard_map.70 = (f32[128,128]{1,0:T(8,128)S(1)}, f32[128,128]{1,0:T(8,128)S(1)}, f32[128,128]{1,0:T(8,128)S(1)}) custom-call(bf16[128,4096]{1,0:T(8,128)(2,1)S(1)} %copy-done, bf16[128,4096]{1,0:T(8,128)(2,1)S(1)} %copy-done.1, bf16[128,4096]{1,0:T(8,128)(2,1)S(1)} %get-tuple-element.40.refs_1_.n1_ref, ...), custom_call_target="tpu_custom_call" | custom-call | bytes 4390912 | tf_op jit(solution)/shard_map/pallas_call | solution.py:31
  30.3 1.9 %collective-permute-done.1.refs_1_.refs_5_ = bf16[272,1024]{1,0:T(8,128)(2,1)S(1)} collective-permute-done((bf16[272,1024]{1,0:T(8,128)(2,1)S(1)}, bf16[272,1024]{1,0:T(8,128)(2,1)S(1)}, u32[]{:S(2)}, u32[]{:S(2)}) %collective-permute-start.1) | collective-permute-done | bytes 557088 | tf_op jit(solution)/shard_map/ppermute | solution.py:297
  32.5 1.2 %shard_map.71 = (f32[3,128]{1,0:T(4,128)S(1)}, f32[3,128]{1,0:T(4,128)S(1)}, f32[3,128]{1,0:T(4,128)S(1)}, f32[3,128]{1,0:T(4,128)S(1)}) custom-call(bf16[272,1024]{1,0:T(8,128)(2,1)S(1)} %collective-permute-done.refs_0_.refs_4_, bf16[272,1024]{1,0:T(8,128)(2,1)S(1)} %collective-permute-done.1.refs_1_.refs_5_, ...), custom_call_target="tpu_custom_call" | custom-call | flops 49999998976 | bytes 2299904 | tf_op jit(solution)/shard_map/pallas_call | solution.py:31
  33.6 1.6 %collective-permute-start.5 = (f32[3,128]{1,0:T(4,128)S(1)}, f32[3,128]{1,0:T(4,128)S(1)}, u32[]{:S(2)}, u32[]{:S(2)}) collective-permute-start(f32[3,128]{1,0:T(4,128)S(1)} %get-tuple-element.42), channel_id=1, source_target_pairs={{0,24},{8,16},{16,8},{24,0},{1,25},{9,17},{17,9},{25,1},{2,26},{10... | collective-permute-start | bytes 4616 | tf_op jit(solution)/shard_map/ppermute | solution.py:297
  35.2 1.4 %collective-permute-start.6 = (f32[3,128]{1,0:T(4,128)S(1)}, f32[3,128]{1,0:T(4,128)S(1)}, u32[]{:S(2)}, u32[]{:S(2)}) collective-permute-start(f32[3,128]{1,0:T(4,128)S(1)} %get-tuple-element.43), channel_id=1, source_target_pairs={{0,16},{8,24},{16,0},{24,8},{1,17},{9,25},{17,1},{25,9},{2,18},{10... | collective-permute-start | bytes 4616 | tf_op jit(solution)/shard_map/ppermute | solution.py:297
  38.2 0.6 collective-permute-done.6.refs_1_
  38.8 1.4 %collective-permute-done.7.refs_2_ = f32[3,128]{1,0:T(4,128)S(1)} collective-permute-done((f32[3,128]{1,0:T(4,128)S(1)}, f32[3,128]{1,0:T(4,128)S(1)}, u32[]{:S(2)}, u32[]{:S(2)}) %collective-permute-start.7) | collective-permute-done | bytes 1568 | tf_op jit(solution)/shard_map/ppermute | solution.py:297
  40.2 1.1 %shard_map.74 = (f32[1,128]{1,0:T(1,128)}, bf16[128,512]{1,0:T(8,128)(2,1)S(1)}, f32[3,128]{1,0:T(4,128)S(1)}, bf16[128,256]{1,0:T(8,128)(2,1)S(1)}, bf16[128,4096]{1,0:T(8,128)(2,1)S(1)}) custom-call(f32[3,128]{1,0:T(4,128)S(1)} %collective-permute-done.5.refs_0_, f32[3,128]{1,0:T(4,128)S(1)} %collective-permute-done.6.refs_1_, ...), custom_call_target="tpu_custom_call" | custom-call | bytes 3613184 | tf_op jit(solution)/shard_map/pallas_call | solution.py:31
  41.4 0.7 collective-permute-start.12
  42.1 1.4 %collective-permute-start.10 = (bf16[128,256]{1,0:T(8,128)(2,1)S(1)}, bf16[128,256]{1,0:T(8,128)(2,1)S(1)}, u32[]{:S(2)}, u32[]{:S(2)}) collective-permute-start(bf16[128,256]{1,0:T(8,128)(2,1)S(1)} %get-tuple-element.51), channel_id=1, source_target_pairs={{0,1},{1,0},{2,3},{3,2},{4,5},{5,4},{6,7},{7,6},{8,9},{9,8},{10,11... | collective-permute-start | bytes 196616 | tf_op jit(solution)/shard_map/ppermute | solution.py:294
  43.4 2.7 %collective-permute-start.13 = (f32[3,128]{1,0:T(4,128)S(1)}, f32[3,128]{1,0:T(4,128)S(1)}, u32[]{:S(2)}, u32[]{:S(2)}) collective-permute-start(f32[3,128]{1,0:T(4,128)S(1)} %get-tuple-element.58.refs_3_), channel_id=1, source_target_pairs={{0,24},{8,16},{16,8},{24,0},{1,25},{9,17},{17,9},{25,1},{2,26},{10... | collective-permute-start | bytes 4616 | tf_op jit(solution)/shard_map/ppermute | solution.py:297
  46.3 0.6 collective-permute-start.15
  47.4 2.5 %collective-permute-start.11 = (bf16[128,4096]{1,0:T(8,128)(2,1)S(1)}, bf16[128,4096]{1,0:T(8,128)(2,1)S(1)}, u32[]{:S(2)}, u32[]{:S(2)}) collective-permute-start(bf16[128,4096]{1,0:T(8,128)(2,1)S(1)} %get-tuple-element.52), channel_id=1, source_target_pairs={{0,3},{2,5},{4,7},{6,1},{8,11},{10,13},{12,15},{14,9},{16,19},{18,... | collective-permute-start | bytes 3145736 | tf_op jit(solution)/shard_map/ppermute | solution.py:291
  49.9 2.1 %shard_map.78 = (bf16[256,1024]{1,0:T(8,128)(2,1)S(1)}, bf16[256,1024]{1,0:T(8,128)(2,1)S(1)}, bf16[256,1024]{1,0:T(8,128)(2,1)S(1)}, bf16[256,1024]{1,0:T(8,128)(2,1)S(1)}, f32[8,128]{1,0:T(8,128)}) custom-call(f32[3,128]{1,0:T(4,128)S(1)} %collective-permute-done.13.refs_0_, f32[3,128]{1,0:T(4,128)S(1)} %collective-permute-done.14.refs_1_, ...), custom_call_target="tpu_custom_call" | custom-call | bytes 4339712 | tf_op jit(solution)/shard_map/pallas_call | solution.py:31
  52.0 2.6 %collective-permute-start.16 = (bf16[256,1024]{1,0:T(8,128)(2,1)S(1)}, bf16[256,1024]{1,0:T(8,128)(2,1)S(1)}, u32[]{:S(2)}, u32[]{:S(2)}) collective-permute-start(bf16[256,1024]{1,0:T(8,128)(2,1)S(1)} %get-tuple-element.60), channel_id=1, source_target_pairs={{0,24},{8,16},{16,8},{24,0},{1,25},{9,17},{17,9},{25,1},{2,26},{10... | collective-permute-start | bytes 1572872 | tf_op jit(solution)/shard_map/ppermute | solution.py:297
  54.9 0.6 collective-permute-start.18
  55.7 1.3 %collective-permute-start.19 = (bf16[128,4096]{1,0:T(8,128)(2,1)S(1)}, bf16[128,4096]{1,0:T(8,128)(2,1)S(1)}, u32[]{:S(2)}, u32[]{:S(2)}) collective-permute-start(bf16[128,4096]{1,0:T(8,128)(2,1)S(1)} %get-tuple-element.66), channel_id=1, source_target_pairs={{1,2},{3,4},{5,6},{7,0},{9,10},{11,12},{13,14},{15,8},{17,18},{19,... | collective-permute-start | bytes 3145736 | tf_op jit(solution)/shard_map/ppermute | solution.py:291
  57.0 9.2 %collective-permute-done.11.own3_ref = bf16[128,4096]{1,0:T(8,128)(2,1)S(1)} collective-permute-done((bf16[128,4096]{1,0:T(8,128)(2,1)S(1)}, bf16[128,4096]{1,0:T(8,128)(2,1)S(1)}, u32[]{:S(2)}, u32[]{:S(2)}) %collective-permute-start.11) | collective-permute-done | bytes 1048608 | tf_op jit(solution)/shard_map/ppermute | solution.py:291
  66.2 1.6 %shard_map.77 = (f32[128,4096]{1,0:T(8,128)S(1)}, f32[128,4096]{1,0:T(8,128)S(1)}) custom-call(bf16[128,4096]{1,0:T(8,128)(2,1)S(1)} %copy-done, bf16[128,8192]{1,0:T(8,128)(2,1)S(1)} %collective-permute-done.9.pair_ref, bf16[128,4096]{1,0:T(8,128)(2,1)S(1)} %copy-done.1, bf16[128,4096]{1,0:T(8,128)(2,1)S(1)} %get-tuple-element.40.refs_1_.n1_ref, ...), custom_call_target="tpu_custom_call" | custom-call | flops 49999998976 | bytes 12784128 | tf_op jit(solution)/shard_map/pallas_call | solution.py:31
  67.9 8.5 %collective-permute-done.17.refs_1_ = bf16[256,1024]{1,0:T(8,128)(2,1)S(1)} collective-permute-done((bf16[256,1024]{1,0:T(8,128)(2,1)S(1)}, bf16[256,1024]{1,0:T(8,128)(2,1)S(1)}, u32[]{:S(2)}, u32[]{:S(2)}) %collective-permute-start.17) | collective-permute-done | bytes 524320 | tf_op jit(solution)/shard_map/ppermute | solution.py:297
  76.7 1.2 %shard_map.79 = (bf16[128,4096]{1,0:T(8,128)(2,1)}, f32[128,4096]{1,0:T(8,128)S(1)}) custom-call(f32[128,4096]{1,0:T(8,128)S(1)} %get-tuple-element.56.pulled, f32[128,4096]{1,0:T(8,128)S(1)} %get-tuple-element.57.base, bf16[256,1024]{1,0:T(8,128)(2,1)S(1)} %collective-permute-done.16.refs_0_, bf16[256,1024]{1,0:T(8,128)(2,1)S(1)} %collective-permute-done.17.refs_1_, ...), custom_call_target="tpu_custom_call" | custom-call | bytes 9437184 | tf_op jit(solution)/shard_map/pallas_call | solution.py:31
  77.9 3.9 %collective-permute-done.19.own1 = bf16[128,4096]{1,0:T(8,128)(2,1)S(1)} collective-permute-done((bf16[128,4096]{1,0:T(8,128)(2,1)S(1)}, bf16[128,4096]{1,0:T(8,128)(2,1)S(1)}, u32[]{:S(2)}, u32[]{:S(2)}) %collective-permute-start.19) | collective-permute-done | bytes 1048608 | tf_op jit(solution)/shard_map/ppermute | solution.py:291
  81.9 1.1 %shard_map.80 = bf16[128,4096]{1,0:T(8,128)(2,1)} custom-call(f32[128,4096]{1,0:T(8,128)S(1)} %get-tuple-element.65.almost, bf16[128,4096]{1,0:T(8,128)(2,1)S(1)} %collective-permute-done.19.own1), custom_call_target="tpu_custom_call" | custom-call | bytes 4194304 | tf_op jit(solution)/shard_map/pallas_call | solution.py:31
  (30 shorter events, 4.7 us)
Async XLA Ops:
  0.6 10.4 %copy-start.1 = (bf16[128,4096]{1,0:T(8,128)(2,1)S(1)}, bf16[128,4096]{1,0:T(8,128)(2,1)}, u32[]{:S(2)}) copy-start(bf16[128,4096]{1,0:T(8,128)(2,1)} %p_ref.3) | copy-start | bytes 3145732
  0.6 20.5 %collective-permute-start.3 = (bf16[128,4096]{1,0:T(8,128)(2,1)}, bf16[128,4096]{1,0:T(8,128)(2,1)S(1)}, u32[]{:S(2)}, u32[]{:S(2)}) collective-permute-start(bf16[128,4096]{1,0:T(8,128)(2,1)} %p_ref.3), channel_id=1, source_target_pairs={{0,7},{1,0},{2,1},{3,2},{4,3},{5,4},{6,5},{7,6},{8,15},{9,8},{10,9... | collective-permute-start | bytes 3145736 | tf_op jit(solution)/shard_map/ppermute | solution.py:291
  5.2 0.7 copy-start.2
  7.5 22.8 %collective-permute-start = (bf16[272,1024]{1,0:T(8,128)(2,1)S(1)}, bf16[272,1024]{1,0:T(8,128)(2,1)S(1)}, u32[]{:S(2)}, u32[]{:S(2)}) collective-permute-start(bf16[272,1024]{1,0:T(8,128)(2,1)S(1)} %get-tuple-element.35), channel_id=1, source_target_pairs={{0,24},{8,16},{16,8},{24,0},{1,25},{9,17},{17,9},{25,1},{2,26},{10... | collective-permute-start | bytes 1671176 | tf_op jit(solution)/shard_map/ppermute | solution.py:297
  10.0 22.2 %collective-permute-start.1 = (bf16[272,1024]{1,0:T(8,128)(2,1)S(1)}, bf16[272,1024]{1,0:T(8,128)(2,1)S(1)}, u32[]{:S(2)}, u32[]{:S(2)}) collective-permute-start(bf16[272,1024]{1,0:T(8,128)(2,1)S(1)} %get-tuple-element.36), channel_id=1, source_target_pairs={{0,16},{8,24},{16,0},{24,8},{1,17},{9,25},{17,1},{25,9},{2,18},{10... | collective-permute-start | bytes 1671176 | tf_op jit(solution)/shard_map/ppermute | solution.py:297
  10.5 22.0 %collective-permute-start.2 = (bf16[272,1024]{1,0:T(8,128)(2,1)S(1)}, bf16[272,1024]{1,0:T(8,128)(2,1)S(1)}, u32[]{:S(2)}, u32[]{:S(2)}) collective-permute-start(bf16[272,1024]{1,0:T(8,128)(2,1)S(1)} %get-tuple-element.37), channel_id=1, source_target_pairs={{0,8},{8,0},{16,24},{24,16},{1,9},{9,1},{17,25},{25,17},{2,10},{10... | collective-permute-start | bytes 1671176 | tf_op jit(solution)/shard_map/ppermute | solution.py:297
  11.1 16.9 %copy-start = (bf16[128,4096]{1,0:T(8,128)(2,1)S(1)}, bf16[128,4096]{1,0:T(8,128)(2,1)}, u32[]{:S(2)}) copy-start(bf16[128,4096]{1,0:T(8,128)(2,1)} %q_ref.9) | copy-start | bytes 3145732
  11.1 16.8 %collective-permute-start.4 = (bf16[128,4096]{1,0:T(8,128)(2,1)S(1)}, bf16[128,4096]{1,0:T(8,128)(2,1)S(1)}, u32[]{:S(2)}, u32[]{:S(2)}) collective-permute-start(bf16[128,4096]{1,0:T(8,128)(2,1)S(1)} %shard_map.69), channel_id=1, source_target_pairs={{1,6},{3,0},{5,2},{7,4},{9,14},{11,8},{13,10},{15,12},{17,22},{19,... | collective-permute-start | bytes 3145736 | tf_op jit(solution)/shard_map/ppermute | solution.py:291
  21.3 18.9 %collective-permute-start.8 = (bf16[128,4096]{1,0:T(8,128)(2,1)S(1)}, bf16[128,4096]{1,0:T(8,128)(2,1)S(1)}, u32[]{:S(2)}, u32[]{:S(2)}) collective-permute-start(bf16[128,4096]{1,0:T(8,128)(2,1)S(1)} %get-tuple-element.46), channel_id=1, source_target_pairs={{3,1},{5,3},{7,5},{2,7},{11,9},{13,11},{15,13},{10,15},{19,17},{21... | collective-permute-start | bytes 3145736 | tf_op jit(solution)/shard_map/ppermute | solution.py:329
  28.1 9.1 %collective-permute-start.9 = (bf16[128,8192]{1,0:T(8,128)(2,1)S(1)}, bf16[128,8192]{1,0:T(8,128)(2,1)S(1)}, u32[]{:S(2)}, u32[]{:S(2)}) collective-permute-start(bf16[128,8192]{1,0:T(8,128)(2,1)S(1)} %shard_map.72), channel_id=1, source_target_pairs={{0,1},{1,0},{2,3},{3,2},{4,5},{5,4},{6,7},{7,6},{8,9},{9,8},{10,11... | collective-permute-start | bytes 6291464 | tf_op jit(solution)/shard_map/ppermute | solution.py:294
  33.6 6.6 %copy-start.3 = (f32[128]{0:T(128)S(1)}, f32[128]{0:T(128)}, u32[]{:S(2)}) copy-start(f32[128]{0:T(128)} %param.7) | copy-start | bytes 1540
  33.6 4.5 %collective-permute-start.5 = (f32[3,128]{1,0:T(4,128)S(1)}, f32[3,128]{1,0:T(4,128)S(1)}, u32[]{:S(2)}, u32[]{:S(2)}) collective-permute-start(f32[3,128]{1,0:T(4,128)S(1)} %get-tuple-element.42), channel_id=1, source_target_pairs={{0,24},{8,16},{16,8},{24,0},{1,25},{9,17},{17,9},{25,1},{2,26},{10... | collective-permute-start | bytes 4616 | tf_op jit(solution)/shard_map/ppermute | solution.py:297
  35.2 3.6 %collective-permute-start.6 = (f32[3,128]{1,0:T(4,128)S(1)}, f32[3,128]{1,0:T(4,128)S(1)}, u32[]{:S(2)}, u32[]{:S(2)}) collective-permute-start(f32[3,128]{1,0:T(4,128)S(1)} %get-tuple-element.43), channel_id=1, source_target_pairs={{0,16},{8,24},{16,0},{24,8},{1,17},{9,25},{17,1},{25,9},{2,18},{10... | collective-permute-start | bytes 4616 | tf_op jit(solution)/shard_map/ppermute | solution.py:297
  36.7 3.6 %collective-permute-start.7 = (f32[3,128]{1,0:T(4,128)S(1)}, f32[3,128]{1,0:T(4,128)S(1)}, u32[]{:S(2)}, u32[]{:S(2)}) collective-permute-start(f32[3,128]{1,0:T(4,128)S(1)} %get-tuple-element.44), channel_id=1, source_target_pairs={{0,8},{8,0},{16,24},{24,16},{1,9},{9,1},{17,25},{25,17},{2,10},{10... | collective-permute-start | bytes 4616 | tf_op jit(solution)/shard_map/ppermute | solution.py:297
  41.4 14.1 %collective-permute-start.12 = (bf16[128,4096]{1,0:T(8,128)(2,1)S(1)}, bf16[128,4096]{1,0:T(8,128)(2,1)S(1)}, u32[]{:S(2)}, u32[]{:S(2)}) collective-permute-start(bf16[128,4096]{1,0:T(8,128)(2,1)S(1)} %get-tuple-element.54), channel_id=1, source_target_pairs={{1,3},{3,5},{5,7},{7,1},{9,11},{11,13},{13,15},{15,9},{17,19},{19,... | collective-permute-start | bytes 3145736 | tf_op jit(solution)/shard_map/ppermute | solution.py:291
  42.1 4.9 %collective-permute-start.10 = (bf16[128,256]{1,0:T(8,128)(2,1)S(1)}, bf16[128,256]{1,0:T(8,128)(2,1)S(1)}, u32[]{:S(2)}, u32[]{:S(2)}) collective-permute-start(bf16[128,256]{1,0:T(8,128)(2,1)S(1)} %get-tuple-element.51), channel_id=1, source_target_pairs={{0,1},{1,0},{2,3},{3,2},{4,5},{5,4},{6,7},{7,6},{8,9},{9,8},{10,11... | collective-permute-start | bytes 196616 | tf_op jit(solution)/shard_map/ppermute | solution.py:294
  43.4 6.5 %collective-permute-start.13 = (f32[3,128]{1,0:T(4,128)S(1)}, f32[3,128]{1,0:T(4,128)S(1)}, u32[]{:S(2)}, u32[]{:S(2)}) collective-permute-start(f32[3,128]{1,0:T(4,128)S(1)} %get-tuple-element.58.refs_3_), channel_id=1, source_target_pairs={{0,24},{8,16},{16,8},{24,0},{1,25},{9,17},{17,9},{25,1},{2,26},{10... | collective-permute-start | bytes 4616 | tf_op jit(solution)/shard_map/ppermute | solution.py:297
  46.1 3.8 %collective-permute-start.14 = (f32[3,128]{1,0:T(4,128)S(1)}, f32[3,128]{1,0:T(4,128)S(1)}, u32[]{:S(2)}, u32[]{:S(2)}) collective-permute-start(f32[3,128]{1,0:T(4,128)S(1)} %get-tuple-element.58.refs_3_), channel_id=1, source_target_pairs={{0,16},{8,24},{16,0},{24,8},{1,17},{9,25},{17,1},{25,9},{2,18},{10... | collective-permute-start | bytes 4616 | tf_op jit(solution)/shard_map/ppermute | solution.py:297
  46.3 3.6 %collective-permute-start.15 = (f32[3,128]{1,0:T(4,128)S(1)}, f32[3,128]{1,0:T(4,128)S(1)}, u32[]{:S(2)}, u32[]{:S(2)}) collective-permute-start(f32[3,128]{1,0:T(4,128)S(1)} %get-tuple-element.58.refs_3_), channel_id=1, source_target_pairs={{0,8},{8,0},{16,24},{24,16},{1,9},{9,1},{17,25},{25,17},{2,10},{10... | collective-permute-start | bytes 4616 | tf_op jit(solution)/shard_map/ppermute | solution.py:297
  47.4 18.8 %collective-permute-start.11 = (bf16[128,4096]{1,0:T(8,128)(2,1)S(1)}, bf16[128,4096]{1,0:T(8,128)(2,1)S(1)}, u32[]{:S(2)}, u32[]{:S(2)}) collective-permute-start(bf16[128,4096]{1,0:T(8,128)(2,1)S(1)} %get-tuple-element.52), channel_id=1, source_target_pairs={{0,3},{2,5},{4,7},{6,1},{8,11},{10,13},{12,15},{14,9},{16,19},{18,... | collective-permute-start | bytes 3145736 | tf_op jit(solution)/shard_map/ppermute | solution.py:291
  52.0 15.9 %collective-permute-start.16 = (bf16[256,1024]{1,0:T(8,128)(2,1)S(1)}, bf16[256,1024]{1,0:T(8,128)(2,1)S(1)}, u32[]{:S(2)}, u32[]{:S(2)}) collective-permute-start(bf16[256,1024]{1,0:T(8,128)(2,1)S(1)} %get-tuple-element.60), channel_id=1, source_target_pairs={{0,24},{8,16},{16,8},{24,0},{1,25},{9,17},{17,9},{25,1},{2,26},{10... | collective-permute-start | bytes 1572872 | tf_op jit(solution)/shard_map/ppermute | solution.py:297
  54.6 21.8 %collective-permute-start.17 = (bf16[256,1024]{1,0:T(8,128)(2,1)S(1)}, bf16[256,1024]{1,0:T(8,128)(2,1)S(1)}, u32[]{:S(2)}, u32[]{:S(2)}) collective-permute-start(bf16[256,1024]{1,0:T(8,128)(2,1)S(1)} %get-tuple-element.61), channel_id=1, source_target_pairs={{0,16},{8,24},{16,0},{24,8},{1,17},{9,25},{17,1},{25,9},{2,18},{10... | collective-permute-start | bytes 1572872 | tf_op jit(solution)/shard_map/ppermute | solution.py:297
  54.9 21.8 %collective-permute-start.18 = (bf16[256,1024]{1,0:T(8,128)(2,1)S(1)}, bf16[256,1024]{1,0:T(8,128)(2,1)S(1)}, u32[]{:S(2)}, u32[]{:S(2)}) collective-permute-start(bf16[256,1024]{1,0:T(8,128)(2,1)S(1)} %get-tuple-element.62), channel_id=1, source_target_pairs={{0,8},{8,0},{16,24},{24,16},{1,9},{9,1},{17,25},{25,17},{2,10},{10... | collective-permute-start | bytes 1572872 | tf_op jit(solution)/shard_map/ppermute | solution.py:297
  55.7 26.1 %collective-permute-start.19 = (bf16[128,4096]{1,0:T(8,128)(2,1)S(1)}, bf16[128,4096]{1,0:T(8,128)(2,1)S(1)}, u32[]{:S(2)}, u32[]{:S(2)}) collective-permute-start(bf16[128,4096]{1,0:T(8,128)(2,1)S(1)} %get-tuple-element.66), channel_id=1, source_target_pairs={{1,2},{3,4},{5,6},{7,0},{9,10},{11,12},{13,14},{15,8},{17,18},{19,... | collective-permute-start | bytes 3145736 | tf_op jit(solution)/shard_map/ppermute | solution.py:291

commit v9 on v5

--- a/solution.py
+++ b/solution.py
@@ -87,7 +87,7 @@
 
 
 def hard_scores_body(groups, *refs):
-    pieces, outs = refs[:groups][::-1], refs[groups + 1 :]
+    pieces, outs = [*refs[2 : groups + 1][::-1], refs[0]], refs[groups + 1 :]
     rows = outs[0].shape[1]
     ids = lax.broadcasted_iota(jnp.int32, (rows, rows), 0)
     for r in range(groups):
@@ -314,7 +314,7 @@
 
     s0, s1, s3 = local_call(scores_body, [square] * 3, queries, passages, next1, next3_even)
     parts = local_call(
-        functools.partial(hard_scores_body, groups), [triple] * groups, *pieces[::-1], s0, flops=LONG
+        functools.partial(hard_scores_body, groups), [triple] * groups, pieces[-1], s0, *pieces[-2::-1], flops=LONG
     )
     (s2,) = local_call(last_score_body, [square], queries, pair)
     parts = exchange(parts)

time: 83.2 us -> 83.4 us (level)
  waiting for transfers between devices: 41.4 us -> 40.3 us
  starting transfers between devices: 27.8 us -> 28.9 us
    ppermute x6, waiting for transfers between devices: 27.7 us -> 26.2 us  [shift(): return lax.ppermute(array, 'blk', pairs)]
    ppermute x12, starting transfers between devices: 14.1 us -> 15.4 us  [over_groups(): return lax.ppermute(array, 'grp', [(i, i ^ r) for i in range(groups)])]
  transfers between devices with their start and end apart: 20 -> 20, of which waited for: 11 -> 13; matrix products, arithmetic and copies ran while one was open for 0% -> 0% of each run, Pallas kernels for 12% -> 12%
where the time goes in v9:
time: 83.4 us; the launch traced here: 82.9 us
  waiting for transfers between devices  40.3 us (48%)
  starting transfers between devices  28.9 us (35%)
  Pallas kernels  12.2 us (15%)
    ppermute x6, waiting for transfers between devices, shift(): return lax.ppermute(array, 'blk', pairs)  26.2 us
    ppermute x12, starting transfers between devices, over_groups(): return lax.ppermute(array, 'grp', [(i, i ^ r) for i in range(groups)])  15.4 us
    ppermute x12, waiting for transfers between devices, over_groups(): return lax.ppermute(array, 'grp', [(i, i ^ r) for i in range(groups)])  14.1 us
    pallas_call x14, Pallas kernels, local_call(): pl.pallas_call(body, out_shape=out_shape, in_specs=in_specs or [VMEM] * l...  12.2 us
    ppermute x6, starting transfers between devices, shift(): return lax.ppermute(array, 'blk', pairs)  11 us
    ppermute x2, starting transfers between devices, swap(): return lax.ppermute(array, 'blk', [(i, i ^ 1) for i in range(loop)])  2.5 us
  transfers between devices with their start and end apart: 20, of which 13 were waited for; matrix products, arithmetic and copies ran while one was open for 0% of the time, Pallas kernels for 12%

profile of v9, /device:TPU:0, one launch (start us, length us, event | category | flops | bytes accessed | tf_op | source)
XLA Modules:
  0.0 82.9 jit_solution(10284753861583368816)
XLA Ops:
  0.6 4.5 %collective-permute-start.1 = (bf16[128,4096]{1,0:T(8,128)(2,1)}, bf16[128,4096]{1,0:T(8,128)(2,1)S(1)}, u32[]{:S(2)}, u32[]{:S(2)}) collective-permute-start(bf16[128,4096]{1,0:T(8,128)(2,1)} %p_ref.1), channel_id=1, source_target_pairs={{0,7},{1,0},{2,1},{3,2},{4,3},{5,4},{6,5},{7,6},{8,15},{9,8},{10,9... | collective-permute-start | bytes 3145736 | tf_op jit(solution)/shard_map/ppermute | solution.py:276
  5.2 0.7 copy-done.2
  5.9 1.6 %shard_map.67 = (bf16[272,1024]{1,0:T(8,128)(2,1)S(1)}, bf16[272,1024]{1,0:T(8,128)(2,1)S(1)}, bf16[272,1024]{1,0:T(8,128)(2,1)S(1)}, bf16[272,1024]{1,0:T(8,128)(2,1)S(1)}, f32[8,128]{1,0:T(8,128)S(1)}) custom-call(bf16[128,4096]{1,0:T(8,128)(2,1)} %q_ref.9, bf16[128,4096]{1,0:T(8,128)(2,1)} %p_ref.1, s32[3,128]{1,0:T(4,128)S(1)} %bitcast.3), custom_call_target="tpu_custom_call" | custom-call | bytes 4331008 | tf_op jit(solution)/shard_map/pallas_call | solution.py:31
  7.5 2.5 %collective-permute-start = (bf16[272,1024]{1,0:T(8,128)(2,1)S(1)}, bf16[272,1024]{1,0:T(8,128)(2,1)S(1)}, u32[]{:S(2)}, u32[]{:S(2)}) collective-permute-start(bf16[272,1024]{1,0:T(8,128)(2,1)S(1)} %get-tuple-element.33), channel_id=1, source_target_pairs={{0,24},{8,16},{16,8},{24,0},{1,25},{9,17},{17,9},{25,1},{2,26},{10... | collective-permute-start | bytes 1671176 | tf_op jit(solution)/shard_map/ppermute | solution.py:282
  10.0 1.3 %collective-permute-start.2 = (bf16[128,4096]{1,0:T(8,128)(2,1)S(1)}, bf16[128,4096]{1,0:T(8,128)(2,1)S(1)}, u32[]{:S(2)}, u32[]{:S(2)}) collective-permute-start(bf16[128,4096]{1,0:T(8,128)(2,1)S(1)} %shard_map.69), channel_id=1, source_target_pairs={{1,6},{3,0},{5,2},{7,4},{9,14},{11,8},{13,10},{15,12},{17,22},{19,... | collective-permute-start | bytes 3145736 | tf_op jit(solution)/shard_map/ppermute | solution.py:276
  11.3 0.6 collective-permute-start.3
  12.5 9.9 %collective-permute-done.1.source = bf16[128,4096]{1,0:T(8,128)(2,1)S(1)} collective-permute-done((bf16[128,4096]{1,0:T(8,128)(2,1)}, bf16[128,4096]{1,0:T(8,128)(2,1)S(1)}, u32[]{:S(2)}, u32[]{:S(2)}) %collective-permute-start.1) | collective-permute-done | bytes 1048608 | tf_op jit(solution)/shard_map/ppermute | solution.py:276
  22.4 0.7 collective-permute-start.9
  23.2 4.8 %collective-permute-done.2.refs_2_.e3_ref = bf16[128,4096]{1,0:T(8,128)(2,1)S(1)} collective-permute-done((bf16[128,4096]{1,0:T(8,128)(2,1)S(1)}, bf16[128,4096]{1,0:T(8,128)(2,1)S(1)}, u32[]{:S(2)}, u32[]{:S(2)}) %collective-permute-start.2) | collective-permute-done | bytes 1048608 | tf_op jit(solution)/shard_map/ppermute | solution.py:276
  28.1 1.2 %collective-permute-start.8 = (bf16[128,8192]{1,0:T(8,128)(2,1)S(1)}, bf16[128,8192]{1,0:T(8,128)(2,1)S(1)}, u32[]{:S(2)}, u32[]{:S(2)}) collective-permute-start(bf16[128,8192]{1,0:T(8,128)(2,1)S(1)} %shard_map.72), channel_id=1, source_target_pairs={{0,1},{1,0},{2,3},{3,2},{4,5},{5,4},{6,7},{7,6},{8,9},{9,8},{10,11... | collective-permute-start | bytes 6291464 | tf_op jit(solution)/shard_map/ppermute | solution.py:279
  29.3 1.0 %shard_map.70 = (f32[128,128]{1,0:T(8,128)S(1)}, f32[128,128]{1,0:T(8,128)S(1)}, f32[128,128]{1,0:T(8,128)S(1)}) custom-call(bf16[128,4096]{1,0:T(8,128)(2,1)S(1)} %copy-done, bf16[128,4096]{1,0:T(8,128)(2,1)S(1)} %copy-done.1, bf16[128,4096]{1,0:T(8,128)(2,1)S(1)} %shard_map.68.refs_1_.n1_ref, bf16[128,4096]{1,0:T(8,128)(2,1)S(1)} %collective-permute-done.2.refs_2_.e3_ref), custom_call_target="tpu_custom_call" | custom-call | bytes 4390912 | tf_op jit(solution)/shard_map/pallas_call | solution.py:31
  30.3 1.9 %collective-permute-done.3.refs_2_.refs_5_ = bf16[272,1024]{1,0:T(8,128)(2,1)S(1)} collective-permute-done((bf16[272,1024]{1,0:T(8,128)(2,1)S(1)}, bf16[272,1024]{1,0:T(8,128)(2,1)S(1)}, u32[]{:S(2)}, u32[]{:S(2)}) %collective-permute-start.3) | collective-permute-done | bytes 557088 | tf_op jit(solution)/shard_map/ppermute | solution.py:282
  32.5 1.2 %shard_map.71 = (f32[3,128]{1,0:T(4,128)S(1)}, f32[3,128]{1,0:T(4,128)S(1)}, f32[3,128]{1,0:T(4,128)S(1)}, f32[3,128]{1,0:T(4,128)S(1)}) custom-call(bf16[272,1024]{1,0:T(8,128)(2,1)S(1)} %collective-permute-done.refs_0_.refs_4_, f32[128,128]{1,0:T(8,128)S(1)} %get-tuple-element.35.refs_1_.refs_5_, ...), custom_call_target="tpu_custom_call" | custom-call | flops 49999998976 | bytes 2299904 | tf_op jit(solution)/shard_map/pallas_call | solution.py:31
  33.6 2.4 %collective-permute-start.5 = (f32[3,128]{1,0:T(4,128)S(1)}, f32[3,128]{1,0:T(4,128)S(1)}, u32[]{:S(2)}, u32[]{:S(2)}) collective-permute-start(f32[3,128]{1,0:T(4,128)S(1)} %get-tuple-element.39), channel_id=1, source_target_pairs={{0,24},{8,16},{16,8},{24,0},{1,25},{9,17},{17,9},{25,1},{2,26},{10... | collective-permute-start | bytes 4616 | tf_op jit(solution)/shard_map/ppermute | solution.py:282
  36.0 0.6 collective-permute-start.6
  38.2 1.4 %collective-permute-done.6.refs_1_ = f32[3,128]{1,0:T(4,128)S(1)} collective-permute-done((f32[3,128]{1,0:T(4,128)S(1)}, f32[3,128]{1,0:T(4,128)S(1)}, u32[]{:S(2)}, u32[]{:S(2)}) %collective-permute-start.6) | collective-permute-done | bytes 1568 | tf_op jit(solution)/shard_map/ppermute | solution.py:282
  39.6 0.6 collective-permute-done.7.refs_2_
  40.2 1.1 %shard_map.74 = (f32[1,128]{1,0:T(1,128)}, bf16[128,512]{1,0:T(8,128)(2,1)S(1)}, f32[3,128]{1,0:T(4,128)S(1)}, bf16[128,256]{1,0:T(8,128)(2,1)S(1)}, bf16[128,4096]{1,0:T(8,128)(2,1)S(1)}) custom-call(f32[3,128]{1,0:T(4,128)S(1)} %collective-permute-done.5.refs_0_, f32[3,128]{1,0:T(4,128)S(1)} %collective-permute-done.6.refs_1_, ...), custom_call_target="tpu_custom_call" | custom-call | bytes 3613184 | tf_op jit(solution)/shard_map/pallas_call | solution.py:31
  41.4 0.7 collective-permute-start.12
  42.1 1.3 %collective-permute-start.10 = (bf16[128,256]{1,0:T(8,128)(2,1)S(1)}, bf16[128,256]{1,0:T(8,128)(2,1)S(1)}, u32[]{:S(2)}, u32[]{:S(2)}) collective-permute-start(bf16[128,256]{1,0:T(8,128)(2,1)S(1)} %get-tuple-element.47), channel_id=1, source_target_pairs={{0,1},{1,0},{2,3},{3,2},{4,5},{5,4},{6,7},{7,6},{8,9},{9,8},{10,11... | collective-permute-start | bytes 196616 | tf_op jit(solution)/shard_map/ppermute | solution.py:279
  43.4 4.2 %collective-permute-start.13 = (f32[3,128]{1,0:T(4,128)S(1)}, f32[3,128]{1,0:T(4,128)S(1)}, u32[]{:S(2)}, u32[]{:S(2)}) collective-permute-start(f32[3,128]{1,0:T(4,128)S(1)} %get-tuple-element.54.refs_3_), channel_id=1, source_target_pairs={{0,24},{8,16},{16,8},{24,0},{1,25},{9,17},{17,9},{25,1},{2,26},{10... | collective-permute-start | bytes 4616 | tf_op jit(solution)/shard_map/ppermute | solution.py:282
  48.6 2.5 %collective-permute-start.11 = (bf16[128,4096]{1,0:T(8,128)(2,1)S(1)}, bf16[128,4096]{1,0:T(8,128)(2,1)S(1)}, u32[]{:S(2)}, u32[]{:S(2)}) collective-permute-start(bf16[128,4096]{1,0:T(8,128)(2,1)S(1)} %get-tuple-element.48), channel_id=1, source_target_pairs={{0,3},{2,5},{4,7},{6,1},{8,11},{10,13},{12,15},{14,9},{16,19},{18,... | collective-permute-start | bytes 3145736 | tf_op jit(solution)/shard_map/ppermute | solution.py:276
  51.2 2.1 %shard_map.78 = (bf16[256,1024]{1,0:T(8,128)(2,1)S(1)}, bf16[256,1024]{1,0:T(8,128)(2,1)S(1)}, bf16[256,1024]{1,0:T(8,128)(2,1)S(1)}, bf16[256,1024]{1,0:T(8,128)(2,1)S(1)}, f32[8,128]{1,0:T(8,128)}) custom-call(f32[3,128]{1,0:T(4,128)S(1)} %collective-permute-done.13.refs_0_, f32[3,128]{1,0:T(4,128)S(1)} %collective-permute-done.14.refs_1_, ...), custom_call_target="tpu_custom_call" | custom-call | bytes 4339712 | tf_op jit(solution)/shard_map/pallas_call | solution.py:31
  53.3 2.5 %collective-permute-start.16 = (bf16[256,1024]{1,0:T(8,128)(2,1)S(1)}, bf16[256,1024]{1,0:T(8,128)(2,1)S(1)}, u32[]{:S(2)}, u32[]{:S(2)}) collective-permute-start(bf16[256,1024]{1,0:T(8,128)(2,1)S(1)} %get-tuple-element.56), channel_id=1, source_target_pairs={{0,24},{8,16},{16,8},{24,0},{1,25},{9,17},{17,9},{25,1},{2,26},{10... | collective-permute-start | bytes 1572872 | tf_op jit(solution)/shard_map/ppermute | solution.py:282
  56.0 0.7 collective-permute-start.18
  57.0 1.3 %collective-permute-start.19 = (bf16[128,4096]{1,0:T(8,128)(2,1)S(1)}, bf16[128,4096]{1,0:T(8,128)(2,1)S(1)}, u32[]{:S(2)}, u32[]{:S(2)}) collective-permute-start(bf16[128,4096]{1,0:T(8,128)(2,1)S(1)} %get-tuple-element.62), channel_id=1, source_target_pairs={{1,2},{3,4},{5,6},{7,0},{9,10},{11,12},{13,14},{15,8},{17,18},{19,... | collective-permute-start | bytes 3145736 | tf_op jit(solution)/shard_map/ppermute | solution.py:276
  58.3 9.0 %collective-permute-done.11.own3_ref = bf16[128,4096]{1,0:T(8,128)(2,1)S(1)} collective-permute-done((bf16[128,4096]{1,0:T(8,128)(2,1)S(1)}, bf16[128,4096]{1,0:T(8,128)(2,1)S(1)}, u32[]{:S(2)}, u32[]{:S(2)}) %collective-permute-start.11) | collective-permute-done | bytes 1048608 | tf_op jit(solution)/shard_map/ppermute | solution.py:276
  67.3 1.7 %shard_map.77 = (f32[128,4096]{1,0:T(8,128)S(1)}, f32[128,4096]{1,0:T(8,128)S(1)}) custom-call(bf16[128,4096]{1,0:T(8,128)(2,1)S(1)} %copy-done, bf16[128,8192]{1,0:T(8,128)(2,1)S(1)} %collective-permute-done.8.pair_ref, bf16[128,4096]{1,0:T(8,128)(2,1)S(1)} %copy-done.1, bf16[128,4096]{1,0:T(8,128)(2,1)S(1)} %shard_map.68.refs_1_.n1_ref, ...), custom_call_target="tpu_custom_call" | custom-call | flops 49999998976 | bytes 12784128 | tf_op jit(solution)/shard_map/pallas_call | solution.py:31
  69.1 8.8 %collective-permute-done.17.refs_1_ = bf16[256,1024]{1,0:T(8,128)(2,1)S(1)} collective-permute-done((bf16[256,1024]{1,0:T(8,128)(2,1)S(1)}, bf16[256,1024]{1,0:T(8,128)(2,1)S(1)}, u32[]{:S(2)}, u32[]{:S(2)}) %collective-permute-start.17) | collective-permute-done | bytes 524320 | tf_op jit(solution)/shard_map/ppermute | solution.py:282
  78.2 1.2 %shard_map.79 = (bf16[128,4096]{1,0:T(8,128)(2,1)}, f32[128,4096]{1,0:T(8,128)S(1)}) custom-call(f32[128,4096]{1,0:T(8,128)S(1)} %get-tuple-element.52.pulled, f32[128,4096]{1,0:T(8,128)S(1)} %get-tuple-element.53.base, bf16[256,1024]{1,0:T(8,128)(2,1)S(1)} %collective-permute-done.16.refs_0_, bf16[256,1024]{1,0:T(8,128)(2,1)S(1)} %collective-permute-done.17.refs_1_, ...), custom_call_target="tpu_custom_call" | custom-call | bytes 9437184 | tf_op jit(solution)/shard_map/pallas_call | solution.py:31
  79.4 2.5 %collective-permute-done.19.own1 = bf16[128,4096]{1,0:T(8,128)(2,1)S(1)} collective-permute-done((bf16[128,4096]{1,0:T(8,128)(2,1)S(1)}, bf16[128,4096]{1,0:T(8,128)(2,1)S(1)}, u32[]{:S(2)}, u32[]{:S(2)}) %collective-permute-start.19) | collective-permute-done | bytes 1048608 | tf_op jit(solution)/shard_map/ppermute | solution.py:276
  81.9 1.1 %shard_map.80 = bf16[128,4096]{1,0:T(8,128)(2,1)} custom-call(f32[128,4096]{1,0:T(8,128)S(1)} %get-tuple-element.61.almost, bf16[128,4096]{1,0:T(8,128)(2,1)S(1)} %collective-permute-done.19.own1), custom_call_target="tpu_custom_call" | custom-call | bytes 4194304 | tf_op jit(solution)/shard_map/pallas_call | solution.py:31
  (30 shorter events, 4.7 us)
Async XLA Ops:
  0.6 9.3 %copy-start.1 = (bf16[128,4096]{1,0:T(8,128)(2,1)S(1)}, bf16[128,4096]{1,0:T(8,128)(2,1)}, u32[]{:S(2)}) copy-start(bf16[128,4096]{1,0:T(8,128)(2,1)} %p_ref.1) | copy-start | bytes 3145732
  0.6 21.7 %collective-permute-start.1 = (bf16[128,4096]{1,0:T(8,128)(2,1)}, bf16[128,4096]{1,0:T(8,128)(2,1)S(1)}, u32[]{:S(2)}, u32[]{:S(2)}) collective-permute-start(bf16[128,4096]{1,0:T(8,128)(2,1)} %p_ref.1), channel_id=1, source_target_pairs={{0,7},{1,0},{2,1},{3,2},{4,3},{5,4},{6,5},{7,6},{8,15},{9,8},{10,9... | collective-permute-start | bytes 3145736 | tf_op jit(solution)/shard_map/ppermute | solution.py:276
  5.2 0.7 copy-start.2
  7.5 22.8 %collective-permute-start = (bf16[272,1024]{1,0:T(8,128)(2,1)S(1)}, bf16[272,1024]{1,0:T(8,128)(2,1)S(1)}, u32[]{:S(2)}, u32[]{:S(2)}) collective-permute-start(bf16[272,1024]{1,0:T(8,128)(2,1)S(1)} %get-tuple-element.33), channel_id=1, source_target_pairs={{0,24},{8,16},{16,8},{24,0},{1,25},{9,17},{17,9},{25,1},{2,26},{10... | collective-permute-start | bytes 1671176 | tf_op jit(solution)/shard_map/ppermute | solution.py:282
  10.0 17.9 %collective-permute-start.2 = (bf16[128,4096]{1,0:T(8,128)(2,1)S(1)}, bf16[128,4096]{1,0:T(8,128)(2,1)S(1)}, u32[]{:S(2)}, u32[]{:S(2)}) collective-permute-start(bf16[128,4096]{1,0:T(8,128)(2,1)S(1)} %shard_map.69), channel_id=1, source_target_pairs={{1,6},{3,0},{5,2},{7,4},{9,14},{11,8},{13,10},{15,12},{17,22},{19,... | collective-permute-start | bytes 3145736 | tf_op jit(solution)/shard_map/ppermute | solution.py:276
  11.3 20.8 %collective-permute-start.3 = (bf16[272,1024]{1,0:T(8,128)(2,1)S(1)}, bf16[272,1024]{1,0:T(8,128)(2,1)S(1)}, u32[]{:S(2)}, u32[]{:S(2)}) collective-permute-start(bf16[272,1024]{1,0:T(8,128)(2,1)S(1)} %get-tuple-element.36), channel_id=1, source_target_pairs={{0,16},{8,24},{16,0},{24,8},{1,17},{9,25},{17,1},{25,9},{2,18},{10... | collective-permute-start | bytes 1671176 | tf_op jit(solution)/shard_map/ppermute | solution.py:282
  11.9 16.0 %copy-start = (bf16[128,4096]{1,0:T(8,128)(2,1)S(1)}, bf16[128,4096]{1,0:T(8,128)(2,1)}, u32[]{:S(2)}) copy-start(bf16[128,4096]{1,0:T(8,128)(2,1)} %q_ref.9) | copy-start | bytes 3145732
  11.9 20.5 %collective-permute-start.4 = (bf16[272,1024]{1,0:T(8,128)(2,1)S(1)}, bf16[272,1024]{1,0:T(8,128)(2,1)S(1)}, u32[]{:S(2)}, u32[]{:S(2)}) collective-permute-start(bf16[272,1024]{1,0:T(8,128)(2,1)S(1)} %get-tuple-element.37), channel_id=1, source_target_pairs={{0,8},{8,0},{16,24},{24,16},{1,9},{9,1},{17,25},{25,17},{2,10},{10... | collective-permute-start | bytes 1671176 | tf_op jit(solution)/shard_map/ppermute | solution.py:282
  22.4 17.8 %collective-permute-start.9 = (bf16[128,4096]{1,0:T(8,128)(2,1)S(1)}, bf16[128,4096]{1,0:T(8,128)(2,1)S(1)}, u32[]{:S(2)}, u32[]{:S(2)}) collective-permute-start(bf16[128,4096]{1,0:T(8,128)(2,1)S(1)} %shard_map.68.refs_1_.n1_ref), channel_id=1, source_target_pairs={{1,7},{3,1},{5,3},{7,5},{9,15},{11,9},{13,11},{15,13},{17,23},{19,... | collective-permute-start | bytes 3145736 | tf_op jit(solution)/shard_map/ppermute | solution.py:276
  28.1 9.1 %collective-permute-start.8 = (bf16[128,8192]{1,0:T(8,128)(2,1)S(1)}, bf16[128,8192]{1,0:T(8,128)(2,1)S(1)}, u32[]{:S(2)}, u32[]{:S(2)}) collective-permute-start(bf16[128,8192]{1,0:T(8,128)(2,1)S(1)} %shard_map.72), channel_id=1, source_target_pairs={{0,1},{1,0},{2,3},{3,2},{4,5},{5,4},{6,7},{7,6},{8,9},{9,8},{10,11... | collective-permute-start | bytes 6291464 | tf_op jit(solution)/shard_map/ppermute | solution.py:279
  33.6 6.6 %copy-start.3 = (f32[128]{0:T(128)S(1)}, f32[128]{0:T(128)}, u32[]{:S(2)}) copy-start(f32[128]{0:T(128)} %param.7) | copy-start | bytes 1540
  33.6 4.5 %collective-permute-start.5 = (f32[3,128]{1,0:T(4,128)S(1)}, f32[3,128]{1,0:T(4,128)S(1)}, u32[]{:S(2)}, u32[]{:S(2)}) collective-permute-start(f32[3,128]{1,0:T(4,128)S(1)} %get-tuple-element.39), channel_id=1, source_target_pairs={{0,24},{8,16},{16,8},{24,0},{1,25},{9,17},{17,9},{25,1},{2,26},{10... | collective-permute-start | bytes 4616 | tf_op jit(solution)/shard_map/ppermute | solution.py:282
  36.0 3.6 %collective-permute-start.6 = (f32[3,128]{1,0:T(4,128)S(1)}, f32[3,128]{1,0:T(4,128)S(1)}, u32[]{:S(2)}, u32[]{:S(2)}) collective-permute-start(f32[3,128]{1,0:T(4,128)S(1)} %get-tuple-element.40), channel_id=1, source_target_pairs={{0,16},{8,24},{16,0},{24,8},{1,17},{9,25},{17,1},{25,9},{2,18},{10... | collective-permute-start | bytes 4616 | tf_op jit(solution)/shard_map/ppermute | solution.py:282
  36.7 3.6 %collective-permute-start.7 = (f32[3,128]{1,0:T(4,128)S(1)}, f32[3,128]{1,0:T(4,128)S(1)}, u32[]{:S(2)}, u32[]{:S(2)}) collective-permute-start(f32[3,128]{1,0:T(4,128)S(1)} %get-tuple-element.41), channel_id=1, source_target_pairs={{0,8},{8,0},{16,24},{24,16},{1,9},{9,1},{17,25},{25,17},{2,10},{10... | collective-permute-start | bytes 4616 | tf_op jit(solution)/shard_map/ppermute | solution.py:282
  41.4 15.4 %collective-permute-start.12 = (bf16[128,4096]{1,0:T(8,128)(2,1)S(1)}, bf16[128,4096]{1,0:T(8,128)(2,1)S(1)}, u32[]{:S(2)}, u32[]{:S(2)}) collective-permute-start(bf16[128,4096]{1,0:T(8,128)(2,1)S(1)} %get-tuple-element.50), channel_id=1, source_target_pairs={{1,3},{3,5},{5,7},{7,1},{9,11},{11,13},{13,15},{15,9},{17,19},{19,... | collective-permute-start | bytes 3145736 | tf_op jit(solution)/shard_map/ppermute | solution.py:276
  42.1 6.1 %collective-permute-start.10 = (bf16[128,256]{1,0:T(8,128)(2,1)S(1)}, bf16[128,256]{1,0:T(8,128)(2,1)S(1)}, u32[]{:S(2)}, u32[]{:S(2)}) collective-permute-start(bf16[128,256]{1,0:T(8,128)(2,1)S(1)} %get-tuple-element.47), channel_id=1, source_target_pairs={{0,1},{1,0},{2,3},{3,2},{4,5},{5,4},{6,7},{7,6},{8,9},{9,8},{10,11... | collective-permute-start | bytes 196616 | tf_op jit(solution)/shard_map/ppermute | solution.py:279
  43.4 7.7 %collective-permute-start.13 = (f32[3,128]{1,0:T(4,128)S(1)}, f32[3,128]{1,0:T(4,128)S(1)}, u32[]{:S(2)}, u32[]{:S(2)}) collective-permute-start(f32[3,128]{1,0:T(4,128)S(1)} %get-tuple-element.54.refs_3_), channel_id=1, source_target_pairs={{0,24},{8,16},{16,8},{24,0},{1,25},{9,17},{17,9},{25,1},{2,26},{10... | collective-permute-start | bytes 4616 | tf_op jit(solution)/shard_map/ppermute | solution.py:282
  47.6 3.6 %collective-permute-start.14 = (f32[3,128]{1,0:T(4,128)S(1)}, f32[3,128]{1,0:T(4,128)S(1)}, u32[]{:S(2)}, u32[]{:S(2)}) collective-permute-start(f32[3,128]{1,0:T(4,128)S(1)} %get-tuple-element.54.refs_3_), channel_id=1, source_target_pairs={{0,16},{8,24},{16,0},{24,8},{1,17},{9,25},{17,1},{25,9},{2,18},{10... | collective-permute-start | bytes 4616 | tf_op jit(solution)/shard_map/ppermute | solution.py:282
  47.6 3.6 %collective-permute-start.15 = (f32[3,128]{1,0:T(4,128)S(1)}, f32[3,128]{1,0:T(4,128)S(1)}, u32[]{:S(2)}, u32[]{:S(2)}) collective-permute-start(f32[3,128]{1,0:T(4,128)S(1)} %get-tuple-element.54.refs_3_), channel_id=1, source_target_pairs={{0,8},{8,0},{16,24},{24,16},{1,9},{9,1},{17,25},{25,17},{2,10},{10... | collective-permute-start | bytes 4616 | tf_op jit(solution)/shard_map/ppermute | solution.py:282
  48.6 18.7 %collective-permute-start.11 = (bf16[128,4096]{1,0:T(8,128)(2,1)S(1)}, bf16[128,4096]{1,0:T(8,128)(2,1)S(1)}, u32[]{:S(2)}, u32[]{:S(2)}) collective-permute-start(bf16[128,4096]{1,0:T(8,128)(2,1)S(1)} %get-tuple-element.48), channel_id=1, source_target_pairs={{0,3},{2,5},{4,7},{6,1},{8,11},{10,13},{12,15},{14,9},{16,19},{18,... | collective-permute-start | bytes 3145736 | tf_op jit(solution)/shard_map/ppermute | solution.py:276
  53.3 15.8 %collective-permute-start.16 = (bf16[256,1024]{1,0:T(8,128)(2,1)S(1)}, bf16[256,1024]{1,0:T(8,128)(2,1)S(1)}, u32[]{:S(2)}, u32[]{:S(2)}) collective-permute-start(bf16[256,1024]{1,0:T(8,128)(2,1)S(1)} %get-tuple-element.56), channel_id=1, source_target_pairs={{0,24},{8,16},{16,8},{24,0},{1,25},{9,17},{17,9},{25,1},{2,26},{10... | collective-permute-start | bytes 1572872 | tf_op jit(solution)/shard_map/ppermute | solution.py:282
  55.8 22.1 %collective-permute-start.17 = (bf16[256,1024]{1,0:T(8,128)(2,1)S(1)}, bf16[256,1024]{1,0:T(8,128)(2,1)S(1)}, u32[]{:S(2)}, u32[]{:S(2)}) collective-permute-start(bf16[256,1024]{1,0:T(8,128)(2,1)S(1)} %get-tuple-element.57), channel_id=1, source_target_pairs={{0,16},{8,24},{16,0},{24,8},{1,17},{9,25},{17,1},{25,9},{2,18},{10... | collective-permute-start | bytes 1572872 | tf_op jit(solution)/shard_map/ppermute | solution.py:282
  56.0 22.1 %collective-permute-start.18 = (bf16[256,1024]{1,0:T(8,128)(2,1)S(1)}, bf16[256,1024]{1,0:T(8,128)(2,1)S(1)}, u32[]{:S(2)}, u32[]{:S(2)}) collective-permute-start(bf16[256,1024]{1,0:T(8,128)(2,1)S(1)} %get-tuple-element.58), channel_id=1, source_target_pairs={{0,8},{8,0},{16,24},{24,16},{1,9},{9,1},{17,25},{25,17},{2,10},{10... | collective-permute-start | bytes 1572872 | tf_op jit(solution)/shard_map/ppermute | solution.py:282
  57.0 24.9 %collective-permute-start.19 = (bf16[128,4096]{1,0:T(8,128)(2,1)S(1)}, bf16[128,4096]{1,0:T(8,128)(2,1)S(1)}, u32[]{:S(2)}, u32[]{:S(2)}) collective-permute-start(bf16[128,4096]{1,0:T(8,128)(2,1)S(1)} %get-tuple-element.62), channel_id=1, source_target_pairs={{1,2},{3,4},{5,6},{7,0},{9,10},{11,12},{13,14},{15,8},{17,18},{19,... | collective-permute-start | bytes 3145736 | tf_op jit(solution)/shard_map/ppermute | solution.py:276

commit v10 on v5

--- a/solution.py
+++ b/solution.py
@@ -160,20 +160,20 @@
     out[...] = dot(pair_ref[:, : q_ref.shape[1]], q_ref[...], ((1,), (1,)))
 
 
-def weigh_body(
-    groups, *refs
-):
+def hard_total(parts):
+    total = parts[-1][...]
+    for other in parts[-2::-1]:
+        total = total + other[...]
+    return INV_TEMP * total
+
+
+def first_sum_body(groups, *refs):
     parts, refs = refs[:groups], refs[groups:]
-    q_ref, s0_ref, s1_ref, s2_ref, s3_ref, last_ref, w_ref, *refs = refs
-    loss_ref, coef_ref, hard_out, swap_ref, term3_ref = refs
-    rows, width = q_ref.shape
-    w = w_ref[...]
+    q_ref, s0_ref, s1_ref, s2_ref, s3_ref, last_ref, w_ref, total_ref, whole3_ref, term3_ref = refs
+    width = q_ref.shape[1]
     s3 = INV_TEMP * (s3_ref[...] + dot(last_ref[...], q_ref[...], ((1,), (1,))))
     scores = [INV_TEMP * s0_ref[...], INV_TEMP * s1_ref[...], INV_TEMP * s2_ref[...], s3]
-    hard = parts[-1][...]
-    for other in parts[-2::-1]:
-        hard = hard + other[...]
-    hard = INV_TEMP * hard
+    hard = hard_total(parts)
     largest = jnp.max(hard, axis=0, keepdims=True)
     for block in scores:
         largest = jnp.maximum(largest, jnp.max(block, axis=0, keepdims=True))
@@ -181,16 +181,27 @@
     for block in scores:
         summed = summed + jnp.sum(jnp.exp(block - largest), axis=0, keepdims=True)
     log_total = largest + jnp.log(summed)
-    for s, block in enumerate(scores):
+    total_ref[...] = log_total
+    whole3_ref[...] = s3
+    coef3 = (w_ref[...] * jnp.exp(s3 - log_total)).astype(BF16)
+    for c in range(0, width, CHUNK):
+        at = slice(c, c + CHUNK)
+        term3_ref[:, at] = dot(coef3, q_ref[:, at], ((1,), (0,))).astype(BF16)
+
+
+def weigh_body(groups, *refs):
+    parts, refs = refs[:groups], refs[groups:]
+    s0_ref, s1_ref, s2_ref, whole3_ref, total_ref, w_ref, *refs = refs
+    loss_ref, coef_ref, hard_out, swap_ref = refs
+    rows = s0_ref.shape[0]
+    w, log_total = w_ref[...], total_ref[...]
+    hard_out[...] = (w * jnp.exp(hard_total(parts) - log_total)).astype(BF16).astype(F32)
+    scores = [INV_TEMP * s0_ref[...], INV_TEMP * s1_ref[...], INV_TEMP * s2_ref[...]]
+    for s, block in enumerate(scores + [whole3_ref[...]]):
         coef = (w * jnp.exp(block - log_total)).astype(BF16)
         coef_ref[:, s * rows : (s + 1) * rows] = coef
         if s in (1, 2):
             swap_ref[:, (s - 1) * rows : s * rows] = coef
-    coef3 = coef_ref[:, 3 * rows :]
-    for c in range(0, width, CHUNK):
-        at = slice(c, c + CHUNK)
-        term3_ref[:, at] = dot(coef3, q_ref[:, at], ((1,), (0,))).astype(BF16)
-    hard_out[...] = (w * jnp.exp(hard - log_total)).astype(BF16).astype(F32)
     eye = lax.broadcasted_iota(jnp.int32, (rows, rows), 0) == lax.broadcasted_iota(
         jnp.int32, (rows, rows), 1
     )
@@ -318,10 +329,15 @@
     )
     (s2,) = local_call(last_score_body, [square], queries, pair)
     parts = exchange(parts)
-    loss_rows, coef, hard_coef, to_core, term3 = local_call(
+    one_row = like(1, rows, dtype=F32)
+    log_total, whole3, term3 = local_call(
+        functools.partial(first_sum_body, groups), [one_row, square, block],
+        *parts[::-1], queries, s0, s1, s2, s3, next3_odd, weights[None, :],
+    )
+    loss_rows, coef, hard_coef, to_core = local_call(
         functools.partial(weigh_body, groups),
-        [like(1, rows, dtype=F32), like(rows, 4 * rows), triple, like(rows, 2 * rows), block],
-        *parts[::-1], queries, s0, s1, s2, s3, next3_odd, weights[None, :],
+        [one_row, like(rows, 4 * rows), triple, like(rows, 2 * rows)],
+        *parts[::-1], s0, s1, s2, whole3, log_total, weights[None, :],
     )
 
     got3 = shift(term3, 2, (1,))

time: 83.2 us -> 83 us (level)
    pallas_call x14 -> x15, Pallas kernels: 12.2 us -> 12.5 us  [local_call(): pl.pallas_call(body, out_shape=out_shape, in_specs=in_specs or [VMEM] * l...]
  transfers between devices with their start and end apart: 20 -> 20, of which waited for: 11 -> 12; matrix products, arithmetic and copies ran while one was open for 0% -> 0% of each run, Pallas kernels for 12% -> 13%
where the time goes in v10:
time: 83 us; the launch traced here: 82.7 us
  waiting for transfers between devices  41.1 us (50%)
  starting transfers between devices  27.6 us (33%)
  Pallas kernels  12.5 us (15%)
    ppermute x6, waiting for transfers between devices, shift(): return lax.ppermute(array, 'blk', pairs)  27.3 us
    ppermute x12, starting transfers between devices, over_groups(): return lax.ppermute(array, 'grp', [(i, i ^ r) for i in range(groups)])  14.1 us
    ppermute x12, waiting for transfers between devices, over_groups(): return lax.ppermute(array, 'grp', [(i, i ^ r) for i in range(groups)])  13.8 us
    pallas_call x15, Pallas kernels, local_call(): pl.pallas_call(body, out_shape=out_shape, in_specs=in_specs or [VMEM] * l...  12.5 us
    ppermute x6, starting transfers between devices, shift(): return lax.ppermute(array, 'blk', pairs)  11.1 us
    ppermute x2, starting transfers between devices, swap(): return lax.ppermute(array, 'blk', [(i, i ^ 1) for i in range(loop)])  2.46 us
  transfers between devices with their start and end apart: 20, of which 12 were waited for; matrix products, arithmetic and copies ran while one was open for 0% of the time, Pallas kernels for 13%

profile of v10, /device:TPU:0, one launch (start us, length us, event | category | flops | bytes accessed | tf_op | source)
XLA Modules:
  0.0 82.7 jit_solution(8782596087562885970)
XLA Ops:
  0.6 4.5 %collective-permute-start.3 = (bf16[128,4096]{1,0:T(8,128)(2,1)}, bf16[128,4096]{1,0:T(8,128)(2,1)S(1)}, u32[]{:S(2)}, u32[]{:S(2)}) collective-permute-start(bf16[128,4096]{1,0:T(8,128)(2,1)} %p_ref.1), channel_id=1, source_target_pairs={{0,7},{1,0},{2,1},{3,2},{4,3},{5,4},{6,5},{7,6},{8,15},{9,8},{10,9... | collective-permute-start | bytes 3145736 | tf_op jit(solution)/shard_map/ppermute | solution.py:287
  5.2 0.7 copy-done.2
  5.9 1.6 %shard_map.67 = (bf16[272,1024]{1,0:T(8,128)(2,1)S(1)}, bf16[272,1024]{1,0:T(8,128)(2,1)S(1)}, bf16[272,1024]{1,0:T(8,128)(2,1)S(1)}, bf16[272,1024]{1,0:T(8,128)(2,1)S(1)}, f32[8,128]{1,0:T(8,128)S(1)}) custom-call(bf16[128,4096]{1,0:T(8,128)(2,1)} %q_ref.9, bf16[128,4096]{1,0:T(8,128)(2,1)} %p_ref.1, s32[3,128]{1,0:T(4,128)S(1)} %bitcast.3), custom_call_target="tpu_custom_call" | custom-call | bytes 4331008 | tf_op jit(solution)/shard_map/pallas_call | solution.py:31
  7.5 2.5 %collective-permute-start = (bf16[272,1024]{1,0:T(8,128)(2,1)S(1)}, bf16[272,1024]{1,0:T(8,128)(2,1)S(1)}, u32[]{:S(2)}, u32[]{:S(2)}) collective-permute-start(bf16[272,1024]{1,0:T(8,128)(2,1)S(1)} %get-tuple-element.35), channel_id=1, source_target_pairs={{0,24},{8,16},{16,8},{24,0},{1,25},{9,17},{17,9},{25,1},{2,26},{10... | collective-permute-start | bytes 1671176 | tf_op jit(solution)/shard_map/ppermute | solution.py:293
  11.1 1.4 %collective-permute-start.4 = (bf16[128,4096]{1,0:T(8,128)(2,1)S(1)}, bf16[128,4096]{1,0:T(8,128)(2,1)S(1)}, u32[]{:S(2)}, u32[]{:S(2)}) collective-permute-start(bf16[128,4096]{1,0:T(8,128)(2,1)S(1)} %shard_map.69), channel_id=1, source_target_pairs={{1,6},{3,0},{5,2},{7,4},{9,14},{11,8},{13,10},{15,12},{17,22},{19,... | collective-permute-start | bytes 3145736 | tf_op jit(solution)/shard_map/ppermute | solution.py:287
  12.5 8.6 %collective-permute-done.3.source = bf16[128,4096]{1,0:T(8,128)(2,1)S(1)} collective-permute-done((bf16[128,4096]{1,0:T(8,128)(2,1)}, bf16[128,4096]{1,0:T(8,128)(2,1)S(1)}, u32[]{:S(2)}, u32[]{:S(2)}) %collective-permute-start.3) | collective-permute-done | bytes 1048608 | tf_op jit(solution)/shard_map/ppermute | solution.py:287
  21.2 0.7 collective-permute-start.9
  22.0 6.0 %collective-permute-done.4.refs_2_.e3_ref = bf16[128,4096]{1,0:T(8,128)(2,1)S(1)} collective-permute-done((bf16[128,4096]{1,0:T(8,128)(2,1)S(1)}, bf16[128,4096]{1,0:T(8,128)(2,1)S(1)}, u32[]{:S(2)}, u32[]{:S(2)}) %collective-permute-start.4) | collective-permute-done | bytes 1048608 | tf_op jit(solution)/shard_map/ppermute | solution.py:287
  28.1 1.2 %collective-permute-start.8 = (bf16[128,8192]{1,0:T(8,128)(2,1)S(1)}, bf16[128,8192]{1,0:T(8,128)(2,1)S(1)}, u32[]{:S(2)}, u32[]{:S(2)}) collective-permute-start(bf16[128,8192]{1,0:T(8,128)(2,1)S(1)} %shard_map.72), channel_id=1, source_target_pairs={{0,1},{1,0},{2,3},{3,2},{4,5},{5,4},{6,7},{7,6},{8,9},{9,8},{10,11... | collective-permute-start | bytes 6291464 | tf_op jit(solution)/shard_map/ppermute | solution.py:290
  29.3 1.0 %shard_map.70 = (f32[128,128]{1,0:T(8,128)S(1)}, f32[128,128]{1,0:T(8,128)S(1)}, f32[128,128]{1,0:T(8,128)S(1)}) custom-call(bf16[128,4096]{1,0:T(8,128)(2,1)S(1)} %copy-done, bf16[128,4096]{1,0:T(8,128)(2,1)S(1)} %copy-done.1, bf16[128,4096]{1,0:T(8,128)(2,1)S(1)} %shard_map.68.refs_1_.n1_ref, bf16[128,4096]{1,0:T(8,128)(2,1)S(1)} %collective-permute-done.4.refs_2_.e3_ref), custom_call_target="tpu_custom_call" | custom-call | bytes 4390912 | tf_op jit(solution)/shard_map/pallas_call | solution.py:31
  30.3 1.9 %collective-permute-done.1.refs_1_.refs_5_ = bf16[272,1024]{1,0:T(8,128)(2,1)S(1)} collective-permute-done((bf16[272,1024]{1,0:T(8,128)(2,1)S(1)}, bf16[272,1024]{1,0:T(8,128)(2,1)S(1)}, u32[]{:S(2)}, u32[]{:S(2)}) %collective-permute-start.1) | collective-permute-done | bytes 557088 | tf_op jit(solution)/shard_map/ppermute | solution.py:293
  32.5 1.2 %shard_map.71 = (f32[3,128]{1,0:T(4,128)S(1)}, f32[3,128]{1,0:T(4,128)S(1)}, f32[3,128]{1,0:T(4,128)S(1)}, f32[3,128]{1,0:T(4,128)S(1)}) custom-call(bf16[272,1024]{1,0:T(8,128)(2,1)S(1)} %collective-permute-done.refs_0_.refs_4_, bf16[272,1024]{1,0:T(8,128)(2,1)S(1)} %collective-permute-done.1.refs_1_.refs_5_, ...), custom_call_target="tpu_custom_call" | custom-call | flops 49999998976 | bytes 2299904 | tf_op jit(solution)/shard_map/pallas_call | solution.py:31
  33.6 1.6 %collective-permute-start.5 = (f32[3,128]{1,0:T(4,128)S(1)}, f32[3,128]{1,0:T(4,128)S(1)}, u32[]{:S(2)}, u32[]{:S(2)}) collective-permute-start(f32[3,128]{1,0:T(4,128)S(1)} %get-tuple-element.41), channel_id=1, source_target_pairs={{0,24},{8,16},{16,8},{24,0},{1,25},{9,17},{17,9},{25,1},{2,26},{10... | collective-permute-start | bytes 4616 | tf_op jit(solution)/shard_map/ppermute | solution.py:293
  35.2 1.4 %collective-permute-start.6 = (f32[3,128]{1,0:T(4,128)S(1)}, f32[3,128]{1,0:T(4,128)S(1)}, u32[]{:S(2)}, u32[]{:S(2)}) collective-permute-start(f32[3,128]{1,0:T(4,128)S(1)} %get-tuple-element.42), channel_id=1, source_target_pairs={{0,16},{8,24},{16,0},{24,8},{1,17},{9,25},{17,1},{25,9},{2,18},{10... | collective-permute-start | bytes 4616 | tf_op jit(solution)/shard_map/ppermute | solution.py:293
  38.2 0.6 collective-permute-done.6.refs_1_
  38.8 1.4 %collective-permute-done.7.refs_2_ = f32[3,128]{1,0:T(4,128)S(1)} collective-permute-done((f32[3,128]{1,0:T(4,128)S(1)}, f32[3,128]{1,0:T(4,128)S(1)}, u32[]{:S(2)}, u32[]{:S(2)}) %collective-permute-start.7) | collective-permute-done | bytes 1568 | tf_op jit(solution)/shard_map/ppermute | solution.py:293
  40.2 0.9 %shard_map.74 = (f32[1,128]{1,0:T(1,128)S(1)}, f32[128,128]{1,0:T(8,128)S(1)}, bf16[128,4096]{1,0:T(8,128)(2,1)S(1)}) custom-call(f32[3,128]{1,0:T(4,128)S(1)} %collective-permute-done.5.refs_0_, f32[3,128]{1,0:T(4,128)S(1)} %collective-permute-done.6.refs_1_, f32[3,128]{1,0:T(4,128)S(1)} %collective-permute-done.7.refs_2_, ...), custom_call_target="tpu_custom_call" | custom-call | bytes 3480576 | tf_op jit(solution)/shard_map/pallas_call | solution.py:31
  41.2 0.7 collective-permute-start.12
  42.5 1.3 %collective-permute-start.10 = (bf16[128,256]{1,0:T(8,128)(2,1)S(1)}, bf16[128,256]{1,0:T(8,128)(2,1)S(1)}, u32[]{:S(2)}, u32[]{:S(2)}) collective-permute-start(bf16[128,256]{1,0:T(8,128)(2,1)S(1)} %get-tuple-element.51), channel_id=1, source_target_pairs={{0,1},{1,0},{2,3},{3,2},{4,5},{5,4},{6,7},{7,6},{8,9},{9,8},{10,11... | collective-permute-start | bytes 196616 | tf_op jit(solution)/shard_map/ppermute | solution.py:290
  43.8 2.7 %collective-permute-start.13 = (f32[3,128]{1,0:T(4,128)S(1)}, f32[3,128]{1,0:T(4,128)S(1)}, u32[]{:S(2)}, u32[]{:S(2)}) collective-permute-start(f32[3,128]{1,0:T(4,128)S(1)} %get-tuple-element.58.refs_3_), channel_id=1, source_target_pairs={{0,24},{8,16},{16,8},{24,0},{1,25},{9,17},{17,9},{25,1},{2,26},{10... | collective-permute-start | bytes 4616 | tf_op jit(solution)/shard_map/ppermute | solution.py:293
  46.7 0.6 collective-permute-start.15
  47.7 2.4 %collective-permute-start.11 = (bf16[128,4096]{1,0:T(8,128)(2,1)S(1)}, bf16[128,4096]{1,0:T(8,128)(2,1)S(1)}, u32[]{:S(2)}, u32[]{:S(2)}) collective-permute-start(bf16[128,4096]{1,0:T(8,128)(2,1)S(1)} %get-tuple-element.52), channel_id=1, source_target_pairs={{0,3},{2,5},{4,7},{6,1},{8,11},{10,13},{12,15},{14,9},{16,19},{18,... | collective-permute-start | bytes 3145736 | tf_op jit(solution)/shard_map/ppermute | solution.py:287
  50.3 2.1 %shard_map.79 = (bf16[256,1024]{1,0:T(8,128)(2,1)S(1)}, bf16[256,1024]{1,0:T(8,128)(2,1)S(1)}, bf16[256,1024]{1,0:T(8,128)(2,1)S(1)}, bf16[256,1024]{1,0:T(8,128)(2,1)S(1)}, f32[8,128]{1,0:T(8,128)}) custom-call(f32[3,128]{1,0:T(4,128)S(1)} %collective-permute-done.13.refs_0_, f32[3,128]{1,0:T(4,128)S(1)} %collective-permute-done.14.refs_1_, ...), custom_call_target="tpu_custom_call" | custom-call | bytes 4339712 | tf_op jit(solution)/shard_map/pallas_call | solution.py:31
  52.3 2.5 %collective-permute-start.16 = (bf16[256,1024]{1,0:T(8,128)(2,1)S(1)}, bf16[256,1024]{1,0:T(8,128)(2,1)S(1)}, u32[]{:S(2)}, u32[]{:S(2)}) collective-permute-start(bf16[256,1024]{1,0:T(8,128)(2,1)S(1)} %get-tuple-element.60), channel_id=1, source_target_pairs={{0,24},{8,16},{16,8},{24,0},{1,25},{9,17},{17,9},{25,1},{2,26},{10... | collective-permute-start | bytes 1572872 | tf_op jit(solution)/shard_map/ppermute | solution.py:293
  55.1 0.7 collective-permute-start.18
  56.0 1.3 %collective-permute-start.19 = (bf16[128,4096]{1,0:T(8,128)(2,1)S(1)}, bf16[128,4096]{1,0:T(8,128)(2,1)S(1)}, u32[]{:S(2)}, u32[]{:S(2)}) collective-permute-start(bf16[128,4096]{1,0:T(8,128)(2,1)S(1)} %get-tuple-element.66), channel_id=1, source_target_pairs={{1,2},{3,4},{5,6},{7,0},{9,10},{11,12},{13,14},{15,8},{17,18},{19,... | collective-permute-start | bytes 3145736 | tf_op jit(solution)/shard_map/ppermute | solution.py:287
  57.3 9.2 %collective-permute-done.11.own3_ref = bf16[128,4096]{1,0:T(8,128)(2,1)S(1)} collective-permute-done((bf16[128,4096]{1,0:T(8,128)(2,1)S(1)}, bf16[128,4096]{1,0:T(8,128)(2,1)S(1)}, u32[]{:S(2)}, u32[]{:S(2)}) %collective-permute-start.11) | collective-permute-done | bytes 1048608 | tf_op jit(solution)/shard_map/ppermute | solution.py:287
  66.5 1.7 %shard_map.78 = (f32[128,4096]{1,0:T(8,128)S(1)}, f32[128,4096]{1,0:T(8,128)S(1)}) custom-call(bf16[128,4096]{1,0:T(8,128)(2,1)S(1)} %copy-done, bf16[128,8192]{1,0:T(8,128)(2,1)S(1)} %collective-permute-done.8.pair_ref, bf16[128,4096]{1,0:T(8,128)(2,1)S(1)} %copy-done.1, bf16[128,4096]{1,0:T(8,128)(2,1)S(1)} %shard_map.68.refs_1_.n1_ref, ...), custom_call_target="tpu_custom_call" | custom-call | flops 49999998976 | bytes 12784128 | tf_op jit(solution)/shard_map/pallas_call | solution.py:31
  68.2 8.5 %collective-permute-done.17.refs_1_ = bf16[256,1024]{1,0:T(8,128)(2,1)S(1)} collective-permute-done((bf16[256,1024]{1,0:T(8,128)(2,1)S(1)}, bf16[256,1024]{1,0:T(8,128)(2,1)S(1)}, u32[]{:S(2)}, u32[]{:S(2)}) %collective-permute-start.17) | collective-permute-done | bytes 524320 | tf_op jit(solution)/shard_map/ppermute | solution.py:293
  77.0 1.2 %shard_map.80 = (bf16[128,4096]{1,0:T(8,128)(2,1)}, f32[128,4096]{1,0:T(8,128)S(1)}) custom-call(f32[128,4096]{1,0:T(8,128)S(1)} %get-tuple-element.56.pulled, f32[128,4096]{1,0:T(8,128)S(1)} %get-tuple-element.57.base, bf16[256,1024]{1,0:T(8,128)(2,1)S(1)} %collective-permute-done.16.refs_0_, bf16[256,1024]{1,0:T(8,128)(2,1)S(1)} %collective-permute-done.17.refs_1_, ...), custom_call_target="tpu_custom_call" | custom-call | bytes 9437184 | tf_op jit(solution)/shard_map/pallas_call | solution.py:31
  78.2 3.5 %collective-permute-done.19.own1 = bf16[128,4096]{1,0:T(8,128)(2,1)S(1)} collective-permute-done((bf16[128,4096]{1,0:T(8,128)(2,1)S(1)}, bf16[128,4096]{1,0:T(8,128)(2,1)S(1)}, u32[]{:S(2)}, u32[]{:S(2)}) %collective-permute-start.19) | collective-permute-done | bytes 1048608 | tf_op jit(solution)/shard_map/ppermute | solution.py:287
  81.7 1.1 %shard_map.81 = bf16[128,4096]{1,0:T(8,128)(2,1)} custom-call(f32[128,4096]{1,0:T(8,128)S(1)} %get-tuple-element.65.almost, bf16[128,4096]{1,0:T(8,128)(2,1)S(1)} %collective-permute-done.19.own1), custom_call_target="tpu_custom_call" | custom-call | bytes 4194304 | tf_op jit(solution)/shard_map/pallas_call | solution.py:31
  (31 shorter events, 5.3 us)
Async XLA Ops:
  0.6 10.4 %copy-start.1 = (bf16[128,4096]{1,0:T(8,128)(2,1)S(1)}, bf16[128,4096]{1,0:T(8,128)(2,1)}, u32[]{:S(2)}) copy-start(bf16[128,4096]{1,0:T(8,128)(2,1)} %p_ref.1) | copy-start | bytes 3145732
  0.6 20.5 %collective-permute-start.3 = (bf16[128,4096]{1,0:T(8,128)(2,1)}, bf16[128,4096]{1,0:T(8,128)(2,1)S(1)}, u32[]{:S(2)}, u32[]{:S(2)}) collective-permute-start(bf16[128,4096]{1,0:T(8,128)(2,1)} %p_ref.1), channel_id=1, source_target_pairs={{0,7},{1,0},{2,1},{3,2},{4,3},{5,4},{6,5},{7,6},{8,15},{9,8},{10,9... | collective-permute-start | bytes 3145736 | tf_op jit(solution)/shard_map/ppermute | solution.py:287
  5.2 0.7 copy-start.2
  7.5 22.8 %collective-permute-start = (bf16[272,1024]{1,0:T(8,128)(2,1)S(1)}, bf16[272,1024]{1,0:T(8,128)(2,1)S(1)}, u32[]{:S(2)}, u32[]{:S(2)}) collective-permute-start(bf16[272,1024]{1,0:T(8,128)(2,1)S(1)} %get-tuple-element.35), channel_id=1, source_target_pairs={{0,24},{8,16},{16,8},{24,0},{1,25},{9,17},{17,9},{25,1},{2,26},{10... | collective-permute-start | bytes 1671176 | tf_op jit(solution)/shard_map/ppermute | solution.py:293
  10.0 22.2 %collective-permute-start.1 = (bf16[272,1024]{1,0:T(8,128)(2,1)S(1)}, bf16[272,1024]{1,0:T(8,128)(2,1)S(1)}, u32[]{:S(2)}, u32[]{:S(2)}) collective-permute-start(bf16[272,1024]{1,0:T(8,128)(2,1)S(1)} %get-tuple-element.36), channel_id=1, source_target_pairs={{0,16},{8,24},{16,0},{24,8},{1,17},{9,25},{17,1},{25,9},{2,18},{10... | collective-permute-start | bytes 1671176 | tf_op jit(solution)/shard_map/ppermute | solution.py:293
  10.5 22.0 %collective-permute-start.2 = (bf16[272,1024]{1,0:T(8,128)(2,1)S(1)}, bf16[272,1024]{1,0:T(8,128)(2,1)S(1)}, u32[]{:S(2)}, u32[]{:S(2)}) collective-permute-start(bf16[272,1024]{1,0:T(8,128)(2,1)S(1)} %get-tuple-element.37), channel_id=1, source_target_pairs={{0,8},{8,0},{16,24},{24,16},{1,9},{9,1},{17,25},{25,17},{2,10},{10... | collective-permute-start | bytes 1671176 | tf_op jit(solution)/shard_map/ppermute | solution.py:293
  11.1 16.9 %copy-start = (bf16[128,4096]{1,0:T(8,128)(2,1)S(1)}, bf16[128,4096]{1,0:T(8,128)(2,1)}, u32[]{:S(2)}) copy-start(bf16[128,4096]{1,0:T(8,128)(2,1)} %q_ref.9) | copy-start | bytes 3145732
  11.1 16.8 %collective-permute-start.4 = (bf16[128,4096]{1,0:T(8,128)(2,1)S(1)}, bf16[128,4096]{1,0:T(8,128)(2,1)S(1)}, u32[]{:S(2)}, u32[]{:S(2)}) collective-permute-start(bf16[128,4096]{1,0:T(8,128)(2,1)S(1)} %shard_map.69), channel_id=1, source_target_pairs={{1,6},{3,0},{5,2},{7,4},{9,14},{11,8},{13,10},{15,12},{17,22},{19,... | collective-permute-start | bytes 3145736 | tf_op jit(solution)/shard_map/ppermute | solution.py:287
  21.2 19.0 %collective-permute-start.9 = (bf16[128,4096]{1,0:T(8,128)(2,1)S(1)}, bf16[128,4096]{1,0:T(8,128)(2,1)S(1)}, u32[]{:S(2)}, u32[]{:S(2)}) collective-permute-start(bf16[128,4096]{1,0:T(8,128)(2,1)S(1)} %shard_map.68.refs_1_.n1_ref), channel_id=1, source_target_pairs={{1,7},{3,1},{5,3},{7,5},{9,15},{11,9},{13,11},{15,13},{17,23},{19,... | collective-permute-start | bytes 3145736 | tf_op jit(solution)/shard_map/ppermute | solution.py:287
  28.1 9.1 %collective-permute-start.8 = (bf16[128,8192]{1,0:T(8,128)(2,1)S(1)}, bf16[128,8192]{1,0:T(8,128)(2,1)S(1)}, u32[]{:S(2)}, u32[]{:S(2)}) collective-permute-start(bf16[128,8192]{1,0:T(8,128)(2,1)S(1)} %shard_map.72), channel_id=1, source_target_pairs={{0,1},{1,0},{2,3},{3,2},{4,5},{5,4},{6,7},{7,6},{8,9},{9,8},{10,11... | collective-permute-start | bytes 6291464 | tf_op jit(solution)/shard_map/ppermute | solution.py:290
  33.6 6.6 %copy-start.3 = (f32[128]{0:T(128)S(1)}, f32[128]{0:T(128)}, u32[]{:S(2)}) copy-start(f32[128]{0:T(128)} %param.7) | copy-start | bytes 1540
  33.6 4.5 %collective-permute-start.5 = (f32[3,128]{1,0:T(4,128)S(1)}, f32[3,128]{1,0:T(4,128)S(1)}, u32[]{:S(2)}, u32[]{:S(2)}) collective-permute-start(f32[3,128]{1,0:T(4,128)S(1)} %get-tuple-element.41), channel_id=1, source_target_pairs={{0,24},{8,16},{16,8},{24,0},{1,25},{9,17},{17,9},{25,1},{2,26},{10... | collective-permute-start | bytes 4616 | tf_op jit(solution)/shard_map/ppermute | solution.py:293
  35.2 3.6 %collective-permute-start.6 = (f32[3,128]{1,0:T(4,128)S(1)}, f32[3,128]{1,0:T(4,128)S(1)}, u32[]{:S(2)}, u32[]{:S(2)}) collective-permute-start(f32[3,128]{1,0:T(4,128)S(1)} %get-tuple-element.42), channel_id=1, source_target_pairs={{0,16},{8,24},{16,0},{24,8},{1,17},{9,25},{17,1},{25,9},{2,18},{10... | collective-permute-start | bytes 4616 | tf_op jit(solution)/shard_map/ppermute | solution.py:293
  36.7 3.6 %collective-permute-start.7 = (f32[3,128]{1,0:T(4,128)S(1)}, f32[3,128]{1,0:T(4,128)S(1)}, u32[]{:S(2)}, u32[]{:S(2)}) collective-permute-start(f32[3,128]{1,0:T(4,128)S(1)} %get-tuple-element.43), channel_id=1, source_target_pairs={{0,8},{8,0},{16,24},{24,16},{1,9},{9,1},{17,25},{25,17},{2,10},{10... | collective-permute-start | bytes 4616 | tf_op jit(solution)/shard_map/ppermute | solution.py:293
  41.2 14.6 %collective-permute-start.12 = (bf16[128,4096]{1,0:T(8,128)(2,1)S(1)}, bf16[128,4096]{1,0:T(8,128)(2,1)S(1)}, u32[]{:S(2)}, u32[]{:S(2)}) collective-permute-start(bf16[128,4096]{1,0:T(8,128)(2,1)S(1)} %get-tuple-element.54), channel_id=1, source_target_pairs={{1,3},{3,5},{5,7},{7,1},{9,11},{11,13},{13,15},{15,9},{17,19},{19,... | collective-permute-start | bytes 3145736 | tf_op jit(solution)/shard_map/ppermute | solution.py:287
  42.5 4.8 %collective-permute-start.10 = (bf16[128,256]{1,0:T(8,128)(2,1)S(1)}, bf16[128,256]{1,0:T(8,128)(2,1)S(1)}, u32[]{:S(2)}, u32[]{:S(2)}) collective-permute-start(bf16[128,256]{1,0:T(8,128)(2,1)S(1)} %get-tuple-element.51), channel_id=1, source_target_pairs={{0,1},{1,0},{2,3},{3,2},{4,5},{5,4},{6,7},{7,6},{8,9},{9,8},{10,11... | collective-permute-start | bytes 196616 | tf_op jit(solution)/shard_map/ppermute | solution.py:290
  43.8 6.3 %collective-permute-start.13 = (f32[3,128]{1,0:T(4,128)S(1)}, f32[3,128]{1,0:T(4,128)S(1)}, u32[]{:S(2)}, u32[]{:S(2)}) collective-permute-start(f32[3,128]{1,0:T(4,128)S(1)} %get-tuple-element.58.refs_3_), channel_id=1, source_target_pairs={{0,24},{8,16},{16,8},{24,0},{1,25},{9,17},{17,9},{25,1},{2,26},{10... | collective-permute-start | bytes 4616 | tf_op jit(solution)/shard_map/ppermute | solution.py:293
  46.5 3.6 %collective-permute-start.14 = (f32[3,128]{1,0:T(4,128)S(1)}, f32[3,128]{1,0:T(4,128)S(1)}, u32[]{:S(2)}, u32[]{:S(2)}) collective-permute-start(f32[3,128]{1,0:T(4,128)S(1)} %get-tuple-element.58.refs_3_), channel_id=1, source_target_pairs={{0,16},{8,24},{16,0},{24,8},{1,17},{9,25},{17,1},{25,9},{2,18},{10... | collective-permute-start | bytes 4616 | tf_op jit(solution)/shard_map/ppermute | solution.py:293
  46.7 3.6 %collective-permute-start.15 = (f32[3,128]{1,0:T(4,128)S(1)}, f32[3,128]{1,0:T(4,128)S(1)}, u32[]{:S(2)}, u32[]{:S(2)}) collective-permute-start(f32[3,128]{1,0:T(4,128)S(1)} %get-tuple-element.58.refs_3_), channel_id=1, source_target_pairs={{0,8},{8,0},{16,24},{24,16},{1,9},{9,1},{17,25},{25,17},{2,10},{10... | collective-permute-start | bytes 4616 | tf_op jit(solution)/shard_map/ppermute | solution.py:293
  47.7 18.8 %collective-permute-start.11 = (bf16[128,4096]{1,0:T(8,128)(2,1)S(1)}, bf16[128,4096]{1,0:T(8,128)(2,1)S(1)}, u32[]{:S(2)}, u32[]{:S(2)}) collective-permute-start(bf16[128,4096]{1,0:T(8,128)(2,1)S(1)} %get-tuple-element.52), channel_id=1, source_target_pairs={{0,3},{2,5},{4,7},{6,1},{8,11},{10,13},{12,15},{14,9},{16,19},{18,... | collective-permute-start | bytes 3145736 | tf_op jit(solution)/shard_map/ppermute | solution.py:287
  52.3 15.8 %collective-permute-start.16 = (bf16[256,1024]{1,0:T(8,128)(2,1)S(1)}, bf16[256,1024]{1,0:T(8,128)(2,1)S(1)}, u32[]{:S(2)}, u32[]{:S(2)}) collective-permute-start(bf16[256,1024]{1,0:T(8,128)(2,1)S(1)} %get-tuple-element.60), channel_id=1, source_target_pairs={{0,24},{8,16},{16,8},{24,0},{1,25},{9,17},{17,9},{25,1},{2,26},{10... | collective-permute-start | bytes 1572872 | tf_op jit(solution)/shard_map/ppermute | solution.py:293
  54.8 21.8 %collective-permute-start.17 = (bf16[256,1024]{1,0:T(8,128)(2,1)S(1)}, bf16[256,1024]{1,0:T(8,128)(2,1)S(1)}, u32[]{:S(2)}, u32[]{:S(2)}) collective-permute-start(bf16[256,1024]{1,0:T(8,128)(2,1)S(1)} %get-tuple-element.61), channel_id=1, source_target_pairs={{0,16},{8,24},{16,0},{24,8},{1,17},{9,25},{17,1},{25,9},{2,18},{10... | collective-permute-start | bytes 1572872 | tf_op jit(solution)/shard_map/ppermute | solution.py:293
  55.1 21.9 %collective-permute-start.18 = (bf16[256,1024]{1,0:T(8,128)(2,1)S(1)}, bf16[256,1024]{1,0:T(8,128)(2,1)S(1)}, u32[]{:S(2)}, u32[]{:S(2)}) collective-permute-start(bf16[256,1024]{1,0:T(8,128)(2,1)S(1)} %get-tuple-element.62), channel_id=1, source_target_pairs={{0,8},{8,0},{16,24},{24,16},{1,9},{9,1},{17,25},{25,17},{2,10},{10... | collective-permute-start | bytes 1572872 | tf_op jit(solution)/shard_map/ppermute | solution.py:293
  56.0 25.7 %collective-permute-start.19 = (bf16[128,4096]{1,0:T(8,128)(2,1)S(1)}, bf16[128,4096]{1,0:T(8,128)(2,1)S(1)}, u32[]{:S(2)}, u32[]{:S(2)}) collective-permute-start(bf16[128,4096]{1,0:T(8,128)(2,1)S(1)} %get-tuple-element.66), channel_id=1, source_target_pairs={{1,2},{3,4},{5,6},{7,0},{9,10},{11,12},{13,14},{15,8},{17,18},{19,... | collective-permute-start | bytes 3145736 | tf_op jit(solution)/shard_map/ppermute | solution.py:287

commit v11 on v7

--- a/solution.py
+++ b/solution.py
@@ -13,7 +13,7 @@
 F32 = jnp.float32
 CHUNK = 512
 TAIL = 16
-LONG, SOME = 5 * 10**10, 16 * 10**9
+LONG, SOME = 5 * 10**10, 10 * 10**9
 VMEM = pl.BlockSpec(memory_space=pltpu.VMEM)
 HBM = pl.BlockSpec(memory_space=pltpu.HBM)
 TOKEN = jax.ShapeDtypeStruct((8, 128), F32)
@@ -218,7 +218,7 @@
 
 def base_body(
     q_ref, pair_ref, p_ref, n1_ref, e3_ref, o3_ref, coef_ref, swap_ref, w_ref, own3_ref,
-    token, pulled, base, coef_t,
+    token, got3_ref, pulled, base, coef_t,
 ):
     rows, width = q_ref.shape
     w = jnp.broadcast_to(w_ref[...], (rows, rows)).T[:, :1]
@@ -234,7 +234,8 @@
         held = jnp.concatenate([block[:, at] for block in blocks], axis=0)
         pulled[:, at] = dot(coef_t[...], held, ((1,), (0,))) - w * p_ref[:, at].astype(F32)
         held = jnp.concatenate([q_ref[:, at], pair_ref[:, width + c : width + c + CHUNK]], axis=0)
-        own = dot(coef, held, ((1,), (0,))) + own3_ref[:, at].astype(F32)
+        came = jnp.where(odd, 0.0, got3_ref[:, at].astype(F32)) + own3_ref[:, at].astype(F32)
+        own = dot(coef, held, ((1,), (0,))) + came
         base[:, at] = own - w * q_ref[:, at].astype(F32)
 
 
@@ -326,13 +327,12 @@
         *parts[::-1], queries, s0, s1, s2, s3, next3_odd, weights[None, :],
     )
 
-    got3 = shift(term3, 2, (1,))
+    got3 = lax.ppermute(term3, "blk", pairs_of(2, (1,))[:-1] + [(loop - 1, 2)])
     from_core = swap(to_core)
     sent3, partial1, token = local_call(
         sums_body, [block, block32, TOKEN], queries, pair, coef, from_core
     )
-    late = (loop - 4, loop - 1)
-    own3 = lax.ppermute(sent3, "blk", [pair for pair in pairs_of(3, (0,)) if pair != late])
+    own3 = shift(sent3, 3, (0,))
 
     hard_coefs = exchange([hard_coef] * groups)
     square_all = pltpu.VMEM((groups * rows, groups * rows), BF16)
@@ -343,12 +343,12 @@
     backs = exchange(backs)
 
     sent1, token = local_call(relay_body, [block, TOKEN], partial1, got3, flops=SOME)
-    own1 = lax.ppermute(sent1, "blk", pairs_of(1, (1,)) + [late])
+    own1 = shift(sent1, 1, (1,))
 
     pulled, base = local_call(
         base_body, [block32, block32],
         queries, pair, passages, next1, next3_even, next3_odd, coef, from_core,
-        weights[None, :], own3, token, flops=LONG, scratch=[pltpu.VMEM((rows, 5 * rows), BF16)],
+        weights[None, :], own3, token, got3, flops=LONG, scratch=[pltpu.VMEM((rows, 5 * rows), BF16)],
     )
     held = pltpu.VMEM((rows, width), BF16)
     grad_queries, almost = local_call(

time: 84.1 us -> 83.2 us (0.989); the launches traced: 82.9 us -> 82.9 us
  waiting for transfers between devices: 41.4 us -> 40.1 us
  starting transfers between devices: 27.8 us -> 28.9 us
    ppermute x2 -> x1, waiting for transfers between devices: 13.1 us -> 0.01 us  [per_device(): got3 = lax.ppermute(term3, 'blk', pairs_of(2, (1,))[:-1] + [(loop - 1, 2)])]
    ppermute x12, waiting for transfers between devices: 13.7 us -> 20.7 us  [over_groups(): return lax.ppermute(array, 'grp', [(i, i ^ r) for i in range(groups)])]
    ppermute x4 -> x5, starting transfers between devices: 7.41 us -> 11.4 us  [shift(): return lax.ppermute(array, 'blk', pairs_of(by, which))]
    ppermute x4 -> x5, waiting for transfers between devices: 14.6 us -> 18.4 us  [shift(): return lax.ppermute(array, 'blk', pairs_of(by, which))]
    ppermute x2 -> x1, starting transfers between devices: 3.8 us -> 0.72 us  [per_device(): got3 = lax.ppermute(term3, 'blk', pairs_of(2, (1,))[:-1] + [(loop - 1, 2)])]
    ppermute x2, waiting for transfers between devices: 0.01 us -> 0.9 us  [swap(): return lax.ppermute(array, 'blk', [(i, i ^ 1) for i in range(loop)])]
  transfers between devices with their start and end apart: 20 -> 20, of which waited for: 11 -> 15; matrix products, arithmetic and copies ran while one was open for 0% -> 0% of each run, Pallas kernels for 12% -> 12%
where the time goes in v11:
time: 83.2 us; the launch traced here: 82.9 us
  waiting for transfers between devices  40.1 us (48%)
  starting transfers between devices  28.9 us (35%)
  Pallas kernels  12.5 us (15%)
    ppermute x12, waiting for transfers between devices, over_groups(): return lax.ppermute(array, 'grp', [(i, i ^ r) for i in range(groups)])  20.7 us
    ppermute x5, waiting for transfers between devices, shift(): return lax.ppermute(array, 'blk', pairs_of(by, which))  18.4 us
    ppermute x12, starting transfers between devices, over_groups(): return lax.ppermute(array, 'grp', [(i, i ^ r) for i in range(groups)])  14.1 us
    pallas_call x14, Pallas kernels, local_call(): pl.pallas_call(body, out_shape=out_shape, in_specs=in_specs or [VMEM] * l...  12.5 us
    ppermute x5, starting transfers between devices, shift(): return lax.ppermute(array, 'blk', pairs_of(by, which))  11.4 us
    ppermute x2, starting transfers between devices, swap(): return lax.ppermute(array, 'blk', [(i, i ^ 1) for i in range(loop)])  2.6 us
  transfers between devices with their start and end apart: 20, of which 15 were waited for; matrix products, arithmetic and copies ran while one was open for 0% of the time, Pallas kernels for 12%

profile of v11, /device:TPU:0, one launch (start us, length us, event | category | flops | bytes accessed | tf_op | source)
XLA Modules:
  0.0 82.9 jit_solution(11478184257540316305)
XLA Ops:
  0.6 4.5 %collective-permute-start.3 = (bf16[128,4096]{1,0:T(8,128)(2,1)}, bf16[128,4096]{1,0:T(8,128)(2,1)S(1)}, u32[]{:S(2)}, u32[]{:S(2)}) collective-permute-start(bf16[128,4096]{1,0:T(8,128)(2,1)} %p_ref.1), channel_id=1, source_target_pairs={{0,7},{1,0},{2,1},{3,2},{4,3},{5,4},{6,5},{7,6},{8,15},{9,8},{10,9... | collective-permute-start | bytes 3145736 | tf_op jit(solution)/shard_map/ppermute | solution.py:279
  5.9 1.6 %shard_map.67 = (bf16[272,1024]{1,0:T(8,128)(2,1)S(1)}, bf16[272,1024]{1,0:T(8,128)(2,1)S(1)}, bf16[272,1024]{1,0:T(8,128)(2,1)S(1)}, bf16[272,1024]{1,0:T(8,128)(2,1)S(1)}, f32[8,128]{1,0:T(8,128)S(1)}) custom-call(bf16[128,4096]{1,0:T(8,128)(2,1)} %q_ref.9, bf16[128,4096]{1,0:T(8,128)(2,1)} %p_ref.1, s32[3,128]{1,0:T(4,128)S(1)} %bitcast.3), custom_call_target="tpu_custom_call" | custom-call | bytes 4331008 | tf_op jit(solution)/shard_map/pallas_call | solution.py:31
  7.5 2.5 %collective-permute-start = (bf16[272,1024]{1,0:T(8,128)(2,1)S(1)}, bf16[272,1024]{1,0:T(8,128)(2,1)S(1)}, u32[]{:S(2)}, u32[]{:S(2)}) collective-permute-start(bf16[272,1024]{1,0:T(8,128)(2,1)S(1)} %get-tuple-element.33), channel_id=1, source_target_pairs={{0,24},{8,16},{16,8},{24,0},{1,25},{9,17},{17,9},{25,1},{2,26},{10... | collective-permute-start | bytes 1671176 | tf_op jit(solution)/shard_map/ppermute | solution.py:285
  11.1 1.4 %collective-permute-start.4 = (bf16[128,4096]{1,0:T(8,128)(2,1)S(1)}, bf16[128,4096]{1,0:T(8,128)(2,1)S(1)}, u32[]{:S(2)}, u32[]{:S(2)}) collective-permute-start(bf16[128,4096]{1,0:T(8,128)(2,1)S(1)} %shard_map.69), channel_id=1, source_target_pairs={{1,6},{3,0},{5,2},{7,4},{9,14},{11,8},{13,10},{15,12},{17,22},{19,... | collective-permute-start | bytes 3145736 | tf_op jit(solution)/shard_map/ppermute | solution.py:279
  12.5 8.6 %collective-permute-done.3.source = bf16[128,4096]{1,0:T(8,128)(2,1)S(1)} collective-permute-done((bf16[128,4096]{1,0:T(8,128)(2,1)}, bf16[128,4096]{1,0:T(8,128)(2,1)S(1)}, u32[]{:S(2)}, u32[]{:S(2)}) %collective-permute-start.3) | collective-permute-done | bytes 1048608 | tf_op jit(solution)/shard_map/ppermute | solution.py:279
  22.0 6.0 %collective-permute-done.4.refs_2_.e3_ref = bf16[128,4096]{1,0:T(8,128)(2,1)S(1)} collective-permute-done((bf16[128,4096]{1,0:T(8,128)(2,1)S(1)}, bf16[128,4096]{1,0:T(8,128)(2,1)S(1)}, u32[]{:S(2)}, u32[]{:S(2)}) %collective-permute-start.4) | collective-permute-done | bytes 1048608 | tf_op jit(solution)/shard_map/ppermute | solution.py:279
  28.1 1.2 %collective-permute-start.8 = (bf16[128,8192]{1,0:T(8,128)(2,1)S(1)}, bf16[128,8192]{1,0:T(8,128)(2,1)S(1)}, u32[]{:S(2)}, u32[]{:S(2)}) collective-permute-start(bf16[128,8192]{1,0:T(8,128)(2,1)S(1)} %shard_map.72), channel_id=1, source_target_pairs={{0,1},{1,0},{2,3},{3,2},{4,5},{5,4},{6,7},{7,6},{8,9},{9,8},{10,11... | collective-permute-start | bytes 6291464 | tf_op jit(solution)/shard_map/ppermute | solution.py:282
  29.3 1.0 %shard_map.70 = (f32[128,128]{1,0:T(8,128)S(1)}, f32[128,128]{1,0:T(8,128)S(1)}, f32[128,128]{1,0:T(8,128)S(1)}) custom-call(bf16[128,4096]{1,0:T(8,128)(2,1)S(1)} %copy-done, bf16[128,4096]{1,0:T(8,128)(2,1)S(1)} %copy-done.1, bf16[128,4096]{1,0:T(8,128)(2,1)S(1)} %shard_map.68.refs_1_.n1_ref, bf16[128,4096]{1,0:T(8,128)(2,1)S(1)} %collective-permute-done.4.refs_2_.e3_ref), custom_call_target="tpu_custom_call" | custom-call | bytes 4390912 | tf_op jit(solution)/shard_map/pallas_call | solution.py:31
  30.3 1.9 %collective-permute-done.1.refs_1_.refs_5_ = bf16[272,1024]{1,0:T(8,128)(2,1)S(1)} collective-permute-done((bf16[272,1024]{1,0:T(8,128)(2,1)S(1)}, bf16[272,1024]{1,0:T(8,128)(2,1)S(1)}, u32[]{:S(2)}, u32[]{:S(2)}) %collective-permute-start.1) | collective-permute-done | bytes 557088 | tf_op jit(solution)/shard_map/ppermute | solution.py:285
  32.5 1.2 %shard_map.71 = (f32[3,128]{1,0:T(4,128)S(1)}, f32[3,128]{1,0:T(4,128)S(1)}, f32[3,128]{1,0:T(4,128)S(1)}, f32[3,128]{1,0:T(4,128)S(1)}) custom-call(bf16[272,1024]{1,0:T(8,128)(2,1)S(1)} %collective-permute-done.refs_0_.refs_4_, bf16[272,1024]{1,0:T(8,128)(2,1)S(1)} %collective-permute-done.1.refs_1_.refs_5_, ...), custom_call_target="tpu_custom_call" | custom-call | flops 49999998976 | bytes 2299904 | tf_op jit(solution)/shard_map/pallas_call | solution.py:31
  33.6 1.6 %collective-permute-start.5 = (f32[3,128]{1,0:T(4,128)S(1)}, f32[3,128]{1,0:T(4,128)S(1)}, u32[]{:S(2)}, u32[]{:S(2)}) collective-permute-start(f32[3,128]{1,0:T(4,128)S(1)} %get-tuple-element.39), channel_id=1, source_target_pairs={{0,24},{8,16},{16,8},{24,0},{1,25},{9,17},{17,9},{25,1},{2,26},{10... | collective-permute-start | bytes 4616 | tf_op jit(solution)/shard_map/ppermute | solution.py:285
  35.2 1.4 %collective-permute-start.6 = (f32[3,128]{1,0:T(4,128)S(1)}, f32[3,128]{1,0:T(4,128)S(1)}, u32[]{:S(2)}, u32[]{:S(2)}) collective-permute-start(f32[3,128]{1,0:T(4,128)S(1)} %get-tuple-element.40), channel_id=1, source_target_pairs={{0,16},{8,24},{16,0},{24,8},{1,17},{9,25},{17,1},{25,9},{2,18},{10... | collective-permute-start | bytes 4616 | tf_op jit(solution)/shard_map/ppermute | solution.py:285
  38.8 1.4 %collective-permute-done.7.refs_2_ = f32[3,128]{1,0:T(4,128)S(1)} collective-permute-done((f32[3,128]{1,0:T(4,128)S(1)}, f32[3,128]{1,0:T(4,128)S(1)}, u32[]{:S(2)}, u32[]{:S(2)}) %collective-permute-start.7) | collective-permute-done | bytes 1568 | tf_op jit(solution)/shard_map/ppermute | solution.py:285
  40.2 1.1 %shard_map.74 = (f32[1,128]{1,0:T(1,128)}, bf16[128,512]{1,0:T(8,128)(2,1)S(1)}, f32[3,128]{1,0:T(4,128)S(1)}, bf16[128,256]{1,0:T(8,128)(2,1)S(1)}, bf16[128,4096]{1,0:T(8,128)(2,1)S(1)}) custom-call(f32[3,128]{1,0:T(4,128)S(1)} %collective-permute-done.5.refs_0_, f32[3,128]{1,0:T(4,128)S(1)} %collective-permute-done.6.refs_1_, ...), custom_call_target="tpu_custom_call" | custom-call | bytes 3613184 | tf_op jit(solution)/shard_map/pallas_call | solution.py:31
  42.1 1.4 %collective-permute-start.10 = (bf16[128,256]{1,0:T(8,128)(2,1)S(1)}, bf16[128,256]{1,0:T(8,128)(2,1)S(1)}, u32[]{:S(2)}, u32[]{:S(2)}) collective-permute-start(bf16[128,256]{1,0:T(8,128)(2,1)S(1)} %get-tuple-element.47), channel_id=1, source_target_pairs={{0,1},{1,0},{2,3},{3,2},{4,5},{5,4},{6,7},{7,6},{8,9},{9,8},{10,11... | collective-permute-start | bytes 196616 | tf_op jit(solution)/shard_map/ppermute | solution.py:282
  43.5 0.9 %collective-permute-done.10.swap_ref = bf16[128,256]{1,0:T(8,128)(2,1)S(1)} collective-permute-done((bf16[128,256]{1,0:T(8,128)(2,1)S(1)}, bf16[128,256]{1,0:T(8,128)(2,1)S(1)}, u32[]{:S(2)}, u32[]{:S(2)}) %collective-permute-start.10) | collective-permute-done | bytes 65568 | tf_op jit(solution)/shard_map/ppermute | solution.py:282
  44.9 3.4 %collective-permute-start.11 = (bf16[128,4096]{1,0:T(8,128)(2,1)S(1)}, bf16[128,4096]{1,0:T(8,128)(2,1)S(1)}, u32[]{:S(2)}, u32[]{:S(2)}) collective-permute-start(bf16[128,4096]{1,0:T(8,128)(2,1)S(1)} %get-tuple-element.48), channel_id=1, source_target_pairs={{0,3},{2,5},{4,7},{6,1},{8,11},{10,13},{12,15},{14,9},{16,19},{18,... | collective-permute-start | bytes 3145736 | tf_op jit(solution)/shard_map/ppermute | solution.py:279
  48.3 1.5 %collective-permute-start.15 = (f32[3,128]{1,0:T(4,128)S(1)}, f32[3,128]{1,0:T(4,128)S(1)}, u32[]{:S(2)}, u32[]{:S(2)}) collective-permute-start(f32[3,128]{1,0:T(4,128)S(1)} %get-tuple-element.54.refs_3_), channel_id=1, source_target_pairs={{0,8},{8,0},{16,24},{24,16},{1,9},{9,1},{17,25},{25,17},{2,10},{10... | collective-permute-start | bytes 4616 | tf_op jit(solution)/shard_map/ppermute | solution.py:285
  49.8 1.8 %collective-permute-start.14 = (f32[3,128]{1,0:T(4,128)S(1)}, f32[3,128]{1,0:T(4,128)S(1)}, u32[]{:S(2)}, u32[]{:S(2)}) collective-permute-start(f32[3,128]{1,0:T(4,128)S(1)} %get-tuple-element.54.refs_3_), channel_id=1, source_target_pairs={{0,16},{8,24},{16,0},{24,8},{1,17},{9,25},{17,1},{25,9},{2,18},{10... | collective-permute-start | bytes 4616 | tf_op jit(solution)/shard_map/ppermute | solution.py:285
  52.0 1.4 %collective-permute-done.14.refs_1_ = f32[3,128]{1,0:T(4,128)S(1)} collective-permute-done((f32[3,128]{1,0:T(4,128)S(1)}, f32[3,128]{1,0:T(4,128)S(1)}, u32[]{:S(2)}, u32[]{:S(2)}) %collective-permute-start.14) | collective-permute-done | bytes 1568 | tf_op jit(solution)/shard_map/ppermute | solution.py:285
  53.4 2.7 %collective-permute-done.13.refs_0_ = f32[3,128]{1,0:T(4,128)S(1)} collective-permute-done((f32[3,128]{1,0:T(4,128)S(1)}, f32[3,128]{1,0:T(4,128)S(1)}, u32[]{:S(2)}, u32[]{:S(2)}) %collective-permute-start.13) | collective-permute-done | bytes 1568 | tf_op jit(solution)/shard_map/ppermute | solution.py:285
  56.1 2.1 %shard_map.78 = (bf16[256,1024]{1,0:T(8,128)(2,1)S(1)}, bf16[256,1024]{1,0:T(8,128)(2,1)S(1)}, bf16[256,1024]{1,0:T(8,128)(2,1)S(1)}, bf16[256,1024]{1,0:T(8,128)(2,1)S(1)}, f32[8,128]{1,0:T(8,128)}) custom-call(f32[3,128]{1,0:T(4,128)S(1)} %collective-permute-done.13.refs_0_, f32[3,128]{1,0:T(4,128)S(1)} %collective-permute-done.14.refs_1_, ...), custom_call_target="tpu_custom_call" | custom-call | bytes 4339712 | tf_op jit(solution)/shard_map/pallas_call | solution.py:31
  58.4 1.4 %collective-permute-start.17 = (bf16[256,1024]{1,0:T(8,128)(2,1)S(1)}, bf16[256,1024]{1,0:T(8,128)(2,1)S(1)}, u32[]{:S(2)}, u32[]{:S(2)}) collective-permute-start(bf16[256,1024]{1,0:T(8,128)(2,1)S(1)} %get-tuple-element.57), channel_id=1, source_target_pairs={{0,16},{8,24},{16,0},{24,8},{1,17},{9,25},{17,1},{25,9},{2,18},{10... | collective-permute-start | bytes 1572872 | tf_op jit(solution)/shard_map/ppermute | solution.py:285
  59.9 1.8 %collective-permute-start.18 = (bf16[256,1024]{1,0:T(8,128)(2,1)S(1)}, bf16[256,1024]{1,0:T(8,128)(2,1)S(1)}, u32[]{:S(2)}, u32[]{:S(2)}) collective-permute-start(bf16[256,1024]{1,0:T(8,128)(2,1)S(1)} %get-tuple-element.58), channel_id=1, source_target_pairs={{0,8},{8,0},{16,24},{24,16},{1,9},{9,1},{17,25},{25,17},{2,10},{10... | collective-permute-start | bytes 1572872 | tf_op jit(solution)/shard_map/ppermute | solution.py:285
  62.0 1.3 %collective-permute-start.19 = (bf16[128,4096]{1,0:T(8,128)(2,1)S(1)}, bf16[128,4096]{1,0:T(8,128)(2,1)S(1)}, u32[]{:S(2)}, u32[]{:S(2)}) collective-permute-start(bf16[128,4096]{1,0:T(8,128)(2,1)S(1)} %get-tuple-element.62), channel_id=1, source_target_pairs={{1,2},{3,4},{5,6},{7,0},{9,10},{11,12},{13,14},{15,8},{17,18},{19,... | collective-permute-start | bytes 3145736 | tf_op jit(solution)/shard_map/ppermute | solution.py:279
  63.3 2.9 %collective-permute-done.11.own3_ref = bf16[128,4096]{1,0:T(8,128)(2,1)S(1)} collective-permute-done((bf16[128,4096]{1,0:T(8,128)(2,1)S(1)}, bf16[128,4096]{1,0:T(8,128)(2,1)S(1)}, u32[]{:S(2)}, u32[]{:S(2)}) %collective-permute-start.11) | collective-permute-done | bytes 1048608 | tf_op jit(solution)/shard_map/ppermute | solution.py:279
  66.2 1.8 %shard_map.77 = (f32[128,4096]{1,0:T(8,128)S(1)}, f32[128,4096]{1,0:T(8,128)S(1)}) custom-call(bf16[128,4096]{1,0:T(8,128)(2,1)S(1)} %copy-done, bf16[128,8192]{1,0:T(8,128)(2,1)S(1)} %collective-permute-done.8.pair_ref, bf16[128,4096]{1,0:T(8,128)(2,1)S(1)} %copy-done.1, bf16[128,4096]{1,0:T(8,128)(2,1)S(1)} %shard_map.68.refs_1_.n1_ref, ...), custom_call_target="tpu_custom_call" | custom-call | flops 49999998976 | bytes 13832704 | tf_op jit(solution)/shard_map/pallas_call | solution.py:31
  68.1 5.9 %collective-permute-done.16.refs_0_ = bf16[256,1024]{1,0:T(8,128)(2,1)S(1)} collective-permute-done((bf16[256,1024]{1,0:T(8,128)(2,1)S(1)}, bf16[256,1024]{1,0:T(8,128)(2,1)S(1)}, u32[]{:S(2)}, u32[]{:S(2)}) %collective-permute-start.16) | collective-permute-done | bytes 524320 | tf_op jit(solution)/shard_map/ppermute | solution.py:285
  74.0 5.8 %collective-permute-done.17.refs_1_ = bf16[256,1024]{1,0:T(8,128)(2,1)S(1)} collective-permute-done((bf16[256,1024]{1,0:T(8,128)(2,1)S(1)}, bf16[256,1024]{1,0:T(8,128)(2,1)S(1)}, u32[]{:S(2)}, u32[]{:S(2)}) %collective-permute-start.17) | collective-permute-done | bytes 524320 | tf_op jit(solution)/shard_map/ppermute | solution.py:285
  79.8 1.2 %shard_map.79 = (bf16[128,4096]{1,0:T(8,128)(2,1)}, f32[128,4096]{1,0:T(8,128)S(1)}) custom-call(f32[128,4096]{1,0:T(8,128)S(1)} %get-tuple-element.52.pulled, f32[128,4096]{1,0:T(8,128)S(1)} %get-tuple-element.53.base, bf16[256,1024]{1,0:T(8,128)(2,1)S(1)} %collective-permute-done.16.refs_0_, bf16[256,1024]{1,0:T(8,128)(2,1)S(1)} %collective-permute-done.17.refs_1_, ...), custom_call_target="tpu_custom_call" | custom-call | bytes 9437184 | tf_op jit(solution)/shard_map/pallas_call | solution.py:31
  81.0 0.9 %collective-permute-done.19.own1 = bf16[128,4096]{1,0:T(8,128)(2,1)S(1)} collective-permute-done((bf16[128,4096]{1,0:T(8,128)(2,1)S(1)}, bf16[128,4096]{1,0:T(8,128)(2,1)S(1)}, u32[]{:S(2)}, u32[]{:S(2)}) %collective-permute-start.19) | collective-permute-done | bytes 1048608 | tf_op jit(solution)/shard_map/ppermute | solution.py:279
  81.9 1.1 %shard_map.80 = bf16[128,4096]{1,0:T(8,128)(2,1)} custom-call(f32[128,4096]{1,0:T(8,128)S(1)} %get-tuple-element.61.almost, bf16[128,4096]{1,0:T(8,128)(2,1)S(1)} %collective-permute-done.19.own1), custom_call_target="tpu_custom_call" | custom-call | bytes 4194304 | tf_op jit(solution)/shard_map/pallas_call | solution.py:31
  (30 shorter events, 7.3 us)
Async XLA Ops:
  0.6 10.4 %copy-start.1 = (bf16[128,4096]{1,0:T(8,128)(2,1)S(1)}, bf16[128,4096]{1,0:T(8,128)(2,1)}, u32[]{:S(2)}) copy-start(bf16[128,4096]{1,0:T(8,128)(2,1)} %p_ref.1) | copy-start | bytes 3145732
  0.6 20.5 %collective-permute-start.3 = (bf16[128,4096]{1,0:T(8,128)(2,1)}, bf16[128,4096]{1,0:T(8,128)(2,1)S(1)}, u32[]{:S(2)}, u32[]{:S(2)}) collective-permute-start(bf16[128,4096]{1,0:T(8,128)(2,1)} %p_ref.1), channel_id=1, source_target_pairs={{0,7},{1,0},{2,1},{3,2},{4,3},{5,4},{6,5},{7,6},{8,15},{9,8},{10,9... | collective-permute-start | bytes 3145736 | tf_op jit(solution)/shard_map/ppermute | solution.py:279
  5.2 0.7 copy-start.2
  7.5 22.8 %collective-permute-start = (bf16[272,1024]{1,0:T(8,128)(2,1)S(1)}, bf16[272,1024]{1,0:T(8,128)(2,1)S(1)}, u32[]{:S(2)}, u32[]{:S(2)}) collective-permute-start(bf16[272,1024]{1,0:T(8,128)(2,1)S(1)} %get-tuple-element.33), channel_id=1, source_target_pairs={{0,24},{8,16},{16,8},{24,0},{1,25},{9,17},{17,9},{25,1},{2,26},{10... | collective-permute-start | bytes 1671176 | tf_op jit(solution)/shard_map/ppermute | solution.py:285
  10.0 22.2 %collective-permute-start.1 = (bf16[272,1024]{1,0:T(8,128)(2,1)S(1)}, bf16[272,1024]{1,0:T(8,128)(2,1)S(1)}, u32[]{:S(2)}, u32[]{:S(2)}) collective-permute-start(bf16[272,1024]{1,0:T(8,128)(2,1)S(1)} %get-tuple-element.34), channel_id=1, source_target_pairs={{0,16},{8,24},{16,0},{24,8},{1,17},{9,25},{17,1},{25,9},{2,18},{10... | collective-permute-start | bytes 1671176 | tf_op jit(solution)/shard_map/ppermute | solution.py:285
  10.5 22.0 %collective-permute-start.2 = (bf16[272,1024]{1,0:T(8,128)(2,1)S(1)}, bf16[272,1024]{1,0:T(8,128)(2,1)S(1)}, u32[]{:S(2)}, u32[]{:S(2)}) collective-permute-start(bf16[272,1024]{1,0:T(8,128)(2,1)S(1)} %get-tuple-element.35), channel_id=1, source_target_pairs={{0,8},{8,0},{16,24},{24,16},{1,9},{9,1},{17,25},{25,17},{2,10},{10... | collective-permute-start | bytes 1671176 | tf_op jit(solution)/shard_map/ppermute | solution.py:285
  11.1 16.9 %copy-start = (bf16[128,4096]{1,0:T(8,128)(2,1)S(1)}, bf16[128,4096]{1,0:T(8,128)(2,1)}, u32[]{:S(2)}) copy-start(bf16[128,4096]{1,0:T(8,128)(2,1)} %q_ref.9) | copy-start | bytes 3145732
  11.1 16.8 %collective-permute-start.4 = (bf16[128,4096]{1,0:T(8,128)(2,1)S(1)}, bf16[128,4096]{1,0:T(8,128)(2,1)S(1)}, u32[]{:S(2)}, u32[]{:S(2)}) collective-permute-start(bf16[128,4096]{1,0:T(8,128)(2,1)S(1)} %shard_map.69), channel_id=1, source_target_pairs={{1,6},{3,0},{5,2},{7,4},{9,14},{11,8},{13,10},{15,12},{17,22},{19,... | collective-permute-start | bytes 3145736 | tf_op jit(solution)/shard_map/ppermute | solution.py:279
  21.2 19.0 %collective-permute-start.9 = (bf16[128,4096]{1,0:T(8,128)(2,1)S(1)}, bf16[128,4096]{1,0:T(8,128)(2,1)S(1)}, u32[]{:S(2)}, u32[]{:S(2)}) collective-permute-start(bf16[128,4096]{1,0:T(8,128)(2,1)S(1)} %shard_map.68.refs_1_.n1_ref), channel_id=1, source_target_pairs={{1,7},{3,1},{5,3},{7,5},{9,15},{11,9},{13,11},{15,13},{17,23},{19,... | collective-permute-start | bytes 3145736 | tf_op jit(solution)/shard_map/ppermute | solution.py:279
  28.1 9.1 %collective-permute-start.8 = (bf16[128,8192]{1,0:T(8,128)(2,1)S(1)}, bf16[128,8192]{1,0:T(8,128)(2,1)S(1)}, u32[]{:S(2)}, u32[]{:S(2)}) collective-permute-start(bf16[128,8192]{1,0:T(8,128)(2,1)S(1)} %shard_map.72), channel_id=1, source_target_pairs={{0,1},{1,0},{2,3},{3,2},{4,5},{5,4},{6,7},{7,6},{8,9},{9,8},{10,11... | collective-permute-start | bytes 6291464 | tf_op jit(solution)/shard_map/ppermute | solution.py:282
  33.6 6.6 %copy-start.3 = (f32[128]{0:T(128)S(1)}, f32[128]{0:T(128)}, u32[]{:S(2)}) copy-start(f32[128]{0:T(128)} %param.7) | copy-start | bytes 1540
  33.6 4.5 %collective-permute-start.5 = (f32[3,128]{1,0:T(4,128)S(1)}, f32[3,128]{1,0:T(4,128)S(1)}, u32[]{:S(2)}, u32[]{:S(2)}) collective-permute-start(f32[3,128]{1,0:T(4,128)S(1)} %get-tuple-element.39), channel_id=1, source_target_pairs={{0,24},{8,16},{16,8},{24,0},{1,25},{9,17},{17,9},{25,1},{2,26},{10... | collective-permute-start | bytes 4616 | tf_op jit(solution)/shard_map/ppermute | solution.py:285
  35.2 3.6 %collective-permute-start.6 = (f32[3,128]{1,0:T(4,128)S(1)}, f32[3,128]{1,0:T(4,128)S(1)}, u32[]{:S(2)}, u32[]{:S(2)}) collective-permute-start(f32[3,128]{1,0:T(4,128)S(1)} %get-tuple-element.40), channel_id=1, source_target_pairs={{0,16},{8,24},{16,0},{24,8},{1,17},{9,25},{17,1},{25,9},{2,18},{10... | collective-permute-start | bytes 4616 | tf_op jit(solution)/shard_map/ppermute | solution.py:285
  36.7 3.6 %collective-permute-start.7 = (f32[3,128]{1,0:T(4,128)S(1)}, f32[3,128]{1,0:T(4,128)S(1)}, u32[]{:S(2)}, u32[]{:S(2)}) collective-permute-start(f32[3,128]{1,0:T(4,128)S(1)} %get-tuple-element.41), channel_id=1, source_target_pairs={{0,8},{8,0},{16,24},{24,16},{1,9},{9,1},{17,25},{25,17},{2,10},{10... | collective-permute-start | bytes 4616 | tf_op jit(solution)/shard_map/ppermute | solution.py:285
  41.4 20.3 %collective-permute-start.12 = (bf16[128,4096]{1,0:T(8,128)(2,1)S(1)}, bf16[128,4096]{1,0:T(8,128)(2,1)S(1)}, u32[]{:S(2)}, u32[]{:S(2)}) collective-permute-start(bf16[128,4096]{1,0:T(8,128)(2,1)S(1)} %get-tuple-element.50), channel_id=1, source_target_pairs={{1,3},{3,5},{5,7},{7,2},{9,11},{11,13},{13,15},{15,10},{17,19},{19... | collective-permute-start | bytes 3145736 | tf_op jit(solution)/shard_map/ppermute | solution.py:330
  42.1 2.3 %collective-permute-start.10 = (bf16[128,256]{1,0:T(8,128)(2,1)S(1)}, bf16[128,256]{1,0:T(8,128)(2,1)S(1)}, u32[]{:S(2)}, u32[]{:S(2)}) collective-permute-start(bf16[128,256]{1,0:T(8,128)(2,1)S(1)} %get-tuple-element.47), channel_id=1, source_target_pairs={{0,1},{1,0},{2,3},{3,2},{4,5},{5,4},{6,7},{7,6},{8,9},{9,8},{10,11... | collective-permute-start | bytes 196616 | tf_op jit(solution)/shard_map/ppermute | solution.py:282
  44.9 21.3 %collective-permute-start.11 = (bf16[128,4096]{1,0:T(8,128)(2,1)S(1)}, bf16[128,4096]{1,0:T(8,128)(2,1)S(1)}, u32[]{:S(2)}, u32[]{:S(2)}) collective-permute-start(bf16[128,4096]{1,0:T(8,128)(2,1)S(1)} %get-tuple-element.48), channel_id=1, source_target_pairs={{0,3},{2,5},{4,7},{6,1},{8,11},{10,13},{12,15},{14,9},{16,19},{18,... | collective-permute-start | bytes 3145736 | tf_op jit(solution)/shard_map/ppermute | solution.py:279
  48.3 3.7 %collective-permute-start.15 = (f32[3,128]{1,0:T(4,128)S(1)}, f32[3,128]{1,0:T(4,128)S(1)}, u32[]{:S(2)}, u32[]{:S(2)}) collective-permute-start(f32[3,128]{1,0:T(4,128)S(1)} %get-tuple-element.54.refs_3_), channel_id=1, source_target_pairs={{0,8},{8,0},{16,24},{24,16},{1,9},{9,1},{17,25},{25,17},{2,10},{10... | collective-permute-start | bytes 4616 | tf_op jit(solution)/shard_map/ppermute | solution.py:285
  49.8 3.6 %collective-permute-start.14 = (f32[3,128]{1,0:T(4,128)S(1)}, f32[3,128]{1,0:T(4,128)S(1)}, u32[]{:S(2)}, u32[]{:S(2)}) collective-permute-start(f32[3,128]{1,0:T(4,128)S(1)} %get-tuple-element.54.refs_3_), channel_id=1, source_target_pairs={{0,16},{8,24},{16,0},{24,8},{1,17},{9,25},{17,1},{25,9},{2,18},{10... | collective-permute-start | bytes 4616 | tf_op jit(solution)/shard_map/ppermute | solution.py:285
  51.6 4.5 %collective-permute-start.13 = (f32[3,128]{1,0:T(4,128)S(1)}, f32[3,128]{1,0:T(4,128)S(1)}, u32[]{:S(2)}, u32[]{:S(2)}) collective-permute-start(f32[3,128]{1,0:T(4,128)S(1)} %get-tuple-element.54.refs_3_), channel_id=1, source_target_pairs={{0,24},{8,16},{16,8},{24,0},{1,25},{9,17},{17,9},{25,1},{2,26},{10... | collective-permute-start | bytes 4616 | tf_op jit(solution)/shard_map/ppermute | solution.py:285
  58.2 15.8 %collective-permute-start.16 = (bf16[256,1024]{1,0:T(8,128)(2,1)S(1)}, bf16[256,1024]{1,0:T(8,128)(2,1)S(1)}, u32[]{:S(2)}, u32[]{:S(2)}) collective-permute-start(bf16[256,1024]{1,0:T(8,128)(2,1)S(1)} %get-tuple-element.56), channel_id=1, source_target_pairs={{0,24},{8,16},{16,8},{24,0},{1,25},{9,17},{17,9},{25,1},{2,26},{10... | collective-permute-start | bytes 1572872 | tf_op jit(solution)/shard_map/ppermute | solution.py:285
  58.4 21.3 %collective-permute-start.17 = (bf16[256,1024]{1,0:T(8,128)(2,1)S(1)}, bf16[256,1024]{1,0:T(8,128)(2,1)S(1)}, u32[]{:S(2)}, u32[]{:S(2)}) collective-permute-start(bf16[256,1024]{1,0:T(8,128)(2,1)S(1)} %get-tuple-element.57), channel_id=1, source_target_pairs={{0,16},{8,24},{16,0},{24,8},{1,17},{9,25},{17,1},{25,9},{2,18},{10... | collective-permute-start | bytes 1572872 | tf_op jit(solution)/shard_map/ppermute | solution.py:285
  59.9 19.9 %collective-permute-start.18 = (bf16[256,1024]{1,0:T(8,128)(2,1)S(1)}, bf16[256,1024]{1,0:T(8,128)(2,1)S(1)}, u32[]{:S(2)}, u32[]{:S(2)}) collective-permute-start(bf16[256,1024]{1,0:T(8,128)(2,1)S(1)} %get-tuple-element.58), channel_id=1, source_target_pairs={{0,8},{8,0},{16,24},{24,16},{1,9},{9,1},{17,25},{25,17},{2,10},{10... | collective-permute-start | bytes 1572872 | tf_op jit(solution)/shard_map/ppermute | solution.py:285
  62.0 19.9 %collective-permute-start.19 = (bf16[128,4096]{1,0:T(8,128)(2,1)S(1)}, bf16[128,4096]{1,0:T(8,128)(2,1)S(1)}, u32[]{:S(2)}, u32[]{:S(2)}) collective-permute-start(bf16[128,4096]{1,0:T(8,128)(2,1)S(1)} %get-tuple-element.62), channel_id=1, source_target_pairs={{1,2},{3,4},{5,6},{7,0},{9,10},{11,12},{13,14},{15,8},{17,18},{19,... | collective-permute-start | bytes 3145736 | tf_op jit(solution)/shard_map/ppermute | solution.py:279

commit v12 on v10

--- a/solution.py
+++ b/solution.py
@@ -13,7 +13,7 @@
 F32 = jnp.float32
 CHUNK = 512
 TAIL = 16
-LONG, SOME = 5 * 10**10, 16 * 10**9
+LONG, SOME = 5 * 10**10, 10 * 10**9
 VMEM = pl.BlockSpec(memory_space=pltpu.VMEM)
 HBM = pl.BlockSpec(memory_space=pltpu.HBM)
 TOKEN = jax.ShapeDtypeStruct((8, 128), F32)
@@ -105,7 +105,7 @@
 
 
 def hard_grads_body(groups, *refs):
-    coefs, pieces, outs = refs[:groups][::-1], refs[groups : 2 * groups][::-1], refs[2 * groups + 1 : 3 * groups + 1]
+    coefs, pieces, outs = refs[:groups], refs[groups : 2 * groups][::-1], refs[2 * groups + 1 : 3 * groups + 1]
     token, matrix, matrix_t = refs[3 * groups + 1 :]
     rows = coefs[0].shape[1]
     cols = outs[0].shape[1]
@@ -229,7 +229,7 @@
 
 def base_body(
     q_ref, pair_ref, p_ref, n1_ref, e3_ref, o3_ref, coef_ref, swap_ref, w_ref, own3_ref,
-    token, pulled, base, coef_t,
+    token, got3_ref, pulled, base, coef_t,
 ):
     rows, width = q_ref.shape
     w = jnp.broadcast_to(w_ref[...], (rows, rows)).T[:, :1]
@@ -245,7 +245,8 @@
         held = jnp.concatenate([block[:, at] for block in blocks], axis=0)
         pulled[:, at] = dot(coef_t[...], held, ((1,), (0,))) - w * p_ref[:, at].astype(F32)
         held = jnp.concatenate([q_ref[:, at], pair_ref[:, width + c : width + c + CHUNK]], axis=0)
-        own = dot(coef, held, ((1,), (0,))) + own3_ref[:, at].astype(F32)
+        came = jnp.where(odd, 0.0, got3_ref[:, at].astype(F32)) + own3_ref[:, at].astype(F32)
+        own = dot(coef, held, ((1,), (0,))) + came
         base[:, at] = own - w * q_ref[:, at].astype(F32)
 
 
@@ -282,9 +283,11 @@
     loop = lax.axis_size("blk")
     cols = width // groups
 
+    def pairs_of(by, which=(0, 1)):
+        return [(i, (i + by) % loop) for i in range(loop) if i % 2 in which]
+
     def shift(array, by, which=(0, 1)):
-        pairs = [(i, (i + by) % loop) for i in range(loop) if i % 2 in which]
-        return lax.ppermute(array, "blk", pairs)
+        return lax.ppermute(array, "blk", pairs_of(by, which))
 
     def swap(array):
         return lax.ppermute(array, "blk", [(i, i ^ 1) for i in range(loop)])
@@ -340,7 +343,7 @@
         *parts[::-1], s0, s1, s2, whole3, log_total, weights[None, :],
     )
 
-    got3 = shift(term3, 2, (1,))
+    got3 = lax.ppermute(term3, "blk", pairs_of(2, (1,))[:-1] + [(loop - 1, 2)])
     from_core = swap(to_core)
     sent3, partial1, token = local_call(
         sums_body, [block, block32, TOKEN], queries, pair, coef, from_core
@@ -351,7 +354,7 @@
     square_all = pltpu.VMEM((groups * rows, groups * rows), BF16)
     *backs, token = local_call(
         functools.partial(hard_grads_body, groups), [back] * groups + [TOKEN],
-        *hard_coefs[::-1], *pieces[::-1], token, scratch=[square_all, square_all],
+        *hard_coefs, *pieces[::-1], token, scratch=[square_all, square_all],
     )
     backs = exchange(backs)
 
@@ -361,7 +364,7 @@
     pulled, base = local_call(
         base_body, [block32, block32],
         queries, pair, passages, next1, next3_even, next3_odd, coef, from_core,
-        weights[None, :], own3, token, flops=LONG, scratch=[pltpu.VMEM((rows, 5 * rows), BF16)],
+        weights[None, :], own3, token, got3, flops=LONG, scratch=[pltpu.VMEM((rows, 5 * rows), BF16)],
     )
     held = pltpu.VMEM((rows, width), BF16)
     grad_queries, almost = local_call(

time: 83 us -> 83 us (level)
  waiting for transfers between devices: 41.1 us -> 39.7 us
  starting transfers between devices: 27.6 us -> 28.8 us
    ppermute x6, waiting for transfers between devices: 27.3 us -> 18.8 us  [the longest x5 18.8 us: shift(): return lax.ppermute(array, 'blk', pairs_of(by, which))]
    ppermute x12, waiting for transfers between devices: 13.8 us -> 20 us  [over_groups(): return lax.ppermute(array, 'grp', [(i, i ^ r) for i in range(groups)])]
    ppermute x6, starting transfers between devices: 11.1 us -> 12.2 us  [the longest x5 11.4 us: shift(): return lax.ppermute(array, 'blk', pairs_of(by, which))]
    ppermute x2, waiting for transfers between devices: 0.01 us -> 0.9 us  [swap(): return lax.ppermute(array, 'blk', [(i, i ^ 1) for i in range(loop)])]
  transfers between devices with their start and end apart: 20 -> 20, of which waited for: 12 -> 16; matrix products, arithmetic and copies ran while one was open for 0% -> 0% of each run, Pallas kernels for 13% -> 13%
where the time goes in v12:
time: 83 us; the launch traced here: 82.8 us
  waiting for transfers between devices  39.7 us (48%)
  starting transfers between devices  28.8 us (35%)
  Pallas kernels  12.7 us (15%)
    ppermute x12, waiting for transfers between devices, over_groups(): return lax.ppermute(array, 'grp', [(i, i ^ r) for i in range(groups)])  20 us
    ppermute x5, waiting for transfers between devices, shift(): return lax.ppermute(array, 'blk', pairs_of(by, which))  18.8 us
    ppermute x12, starting transfers between devices, over_groups(): return lax.ppermute(array, 'grp', [(i, i ^ r) for i in range(groups)])  14.1 us
    pallas_call x15, Pallas kernels, local_call(): pl.pallas_call(body, out_shape=out_shape, in_specs=in_specs or [VMEM] * l...  12.7 us
    ppermute x5, starting transfers between devices, shift(): return lax.ppermute(array, 'blk', pairs_of(by, which))  11.4 us
    ppermute x2, starting transfers between devices, swap(): return lax.ppermute(array, 'blk', [(i, i ^ 1) for i in range(loop)])  2.52 us
  transfers between devices with their start and end apart: 20, of which 16 were waited for; matrix products, arithmetic and copies ran while one was open for 0% of the time, Pallas kernels for 13%

profile of v12, /device:TPU:0, one launch (start us, length us, event | category | flops | bytes accessed | tf_op | source)
XLA Modules:
  0.0 82.8 jit_solution(3482203216239160702)
XLA Ops:
  0.6 4.5 %collective-permute-start.3 = (bf16[128,4096]{1,0:T(8,128)(2,1)}, bf16[128,4096]{1,0:T(8,128)(2,1)S(1)}, u32[]{:S(2)}, u32[]{:S(2)}) collective-permute-start(bf16[128,4096]{1,0:T(8,128)(2,1)} %p_ref.1), channel_id=1, source_target_pairs={{0,7},{1,0},{2,1},{3,2},{4,3},{5,4},{6,5},{7,6},{8,15},{9,8},{10,9... | collective-permute-start | bytes 3145736 | tf_op jit(solution)/shard_map/ppermute | solution.py:290
  5.9 1.6 %shard_map.67 = (bf16[272,1024]{1,0:T(8,128)(2,1)S(1)}, bf16[272,1024]{1,0:T(8,128)(2,1)S(1)}, bf16[272,1024]{1,0:T(8,128)(2,1)S(1)}, bf16[272,1024]{1,0:T(8,128)(2,1)S(1)}, f32[8,128]{1,0:T(8,128)S(1)}) custom-call(bf16[128,4096]{1,0:T(8,128)(2,1)} %q_ref.9, bf16[128,4096]{1,0:T(8,128)(2,1)} %p_ref.1, s32[3,128]{1,0:T(4,128)S(1)} %bitcast.3), custom_call_target="tpu_custom_call" | custom-call | bytes 4331008 | tf_op jit(solution)/shard_map/pallas_call | solution.py:31
  7.5 2.5 %collective-permute-start = (bf16[272,1024]{1,0:T(8,128)(2,1)S(1)}, bf16[272,1024]{1,0:T(8,128)(2,1)S(1)}, u32[]{:S(2)}, u32[]{:S(2)}) collective-permute-start(bf16[272,1024]{1,0:T(8,128)(2,1)S(1)} %get-tuple-element.35), channel_id=1, source_target_pairs={{0,24},{8,16},{16,8},{24,0},{1,25},{9,17},{17,9},{25,1},{2,26},{10... | collective-permute-start | bytes 1671176 | tf_op jit(solution)/shard_map/ppermute | solution.py:296
  11.1 1.4 %collective-permute-start.4 = (bf16[128,4096]{1,0:T(8,128)(2,1)S(1)}, bf16[128,4096]{1,0:T(8,128)(2,1)S(1)}, u32[]{:S(2)}, u32[]{:S(2)}) collective-permute-start(bf16[128,4096]{1,0:T(8,128)(2,1)S(1)} %shard_map.69), channel_id=1, source_target_pairs={{1,6},{3,0},{5,2},{7,4},{9,14},{11,8},{13,10},{15,12},{17,22},{19,... | collective-permute-start | bytes 3145736 | tf_op jit(solution)/shard_map/ppermute | solution.py:290
  12.5 8.6 %collective-permute-done.3.source = bf16[128,4096]{1,0:T(8,128)(2,1)S(1)} collective-permute-done((bf16[128,4096]{1,0:T(8,128)(2,1)}, bf16[128,4096]{1,0:T(8,128)(2,1)S(1)}, u32[]{:S(2)}, u32[]{:S(2)}) %collective-permute-start.3) | collective-permute-done | bytes 1048608 | tf_op jit(solution)/shard_map/ppermute | solution.py:290
  21.2 0.7 collective-permute-start.9
  22.0 6.0 %collective-permute-done.4.refs_2_.e3_ref = bf16[128,4096]{1,0:T(8,128)(2,1)S(1)} collective-permute-done((bf16[128,4096]{1,0:T(8,128)(2,1)S(1)}, bf16[128,4096]{1,0:T(8,128)(2,1)S(1)}, u32[]{:S(2)}, u32[]{:S(2)}) %collective-permute-start.4) | collective-permute-done | bytes 1048608 | tf_op jit(solution)/shard_map/ppermute | solution.py:290
  28.1 1.2 %collective-permute-start.8 = (bf16[128,8192]{1,0:T(8,128)(2,1)S(1)}, bf16[128,8192]{1,0:T(8,128)(2,1)S(1)}, u32[]{:S(2)}, u32[]{:S(2)}) collective-permute-start(bf16[128,8192]{1,0:T(8,128)(2,1)S(1)} %shard_map.72), channel_id=1, source_target_pairs={{0,1},{1,0},{2,3},{3,2},{4,5},{5,4},{6,7},{7,6},{8,9},{9,8},{10,11... | collective-permute-start | bytes 6291464 | tf_op jit(solution)/shard_map/ppermute | solution.py:293
  29.3 1.0 %shard_map.70 = (f32[128,128]{1,0:T(8,128)S(1)}, f32[128,128]{1,0:T(8,128)S(1)}, f32[128,128]{1,0:T(8,128)S(1)}) custom-call(bf16[128,4096]{1,0:T(8,128)(2,1)S(1)} %copy-done, bf16[128,4096]{1,0:T(8,128)(2,1)S(1)} %copy-done.1, bf16[128,4096]{1,0:T(8,128)(2,1)S(1)} %shard_map.68.refs_1_.n1_ref, bf16[128,4096]{1,0:T(8,128)(2,1)S(1)} %collective-permute-done.4.refs_2_.e3_ref), custom_call_target="tpu_custom_call" | custom-call | bytes 4390912 | tf_op jit(solution)/shard_map/pallas_call | solution.py:31
  30.3 1.9 %collective-permute-done.1.refs_1_.refs_5_ = bf16[272,1024]{1,0:T(8,128)(2,1)S(1)} collective-permute-done((bf16[272,1024]{1,0:T(8,128)(2,1)S(1)}, bf16[272,1024]{1,0:T(8,128)(2,1)S(1)}, u32[]{:S(2)}, u32[]{:S(2)}) %collective-permute-start.1) | collective-permute-done | bytes 557088 | tf_op jit(solution)/shard_map/ppermute | solution.py:296
  32.5 1.2 %shard_map.71 = (f32[3,128]{1,0:T(4,128)S(1)}, f32[3,128]{1,0:T(4,128)S(1)}, f32[3,128]{1,0:T(4,128)S(1)}, f32[3,128]{1,0:T(4,128)S(1)}) custom-call(bf16[272,1024]{1,0:T(8,128)(2,1)S(1)} %collective-permute-done.refs_0_.refs_4_, bf16[272,1024]{1,0:T(8,128)(2,1)S(1)} %collective-permute-done.1.refs_1_.refs_5_, ...), custom_call_target="tpu_custom_call" | custom-call | flops 49999998976 | bytes 2299904 | tf_op jit(solution)/shard_map/pallas_call | solution.py:31
  33.6 1.6 %collective-permute-start.5 = (f32[3,128]{1,0:T(4,128)S(1)}, f32[3,128]{1,0:T(4,128)S(1)}, u32[]{:S(2)}, u32[]{:S(2)}) collective-permute-start(f32[3,128]{1,0:T(4,128)S(1)} %get-tuple-element.41), channel_id=1, source_target_pairs={{0,24},{8,16},{16,8},{24,0},{1,25},{9,17},{17,9},{25,1},{2,26},{10... | collective-permute-start | bytes 4616 | tf_op jit(solution)/shard_map/ppermute | solution.py:296
  35.2 1.4 %collective-permute-start.6 = (f32[3,128]{1,0:T(4,128)S(1)}, f32[3,128]{1,0:T(4,128)S(1)}, u32[]{:S(2)}, u32[]{:S(2)}) collective-permute-start(f32[3,128]{1,0:T(4,128)S(1)} %get-tuple-element.42), channel_id=1, source_target_pairs={{0,16},{8,24},{16,0},{24,8},{1,17},{9,25},{17,1},{25,9},{2,18},{10... | collective-permute-start | bytes 4616 | tf_op jit(solution)/shard_map/ppermute | solution.py:296
  38.8 1.4 %collective-permute-done.7.refs_2_ = f32[3,128]{1,0:T(4,128)S(1)} collective-permute-done((f32[3,128]{1,0:T(4,128)S(1)}, f32[3,128]{1,0:T(4,128)S(1)}, u32[]{:S(2)}, u32[]{:S(2)}) %collective-permute-start.7) | collective-permute-done | bytes 1568 | tf_op jit(solution)/shard_map/ppermute | solution.py:296
  40.2 0.9 %shard_map.74 = (f32[1,128]{1,0:T(1,128)S(1)}, f32[128,128]{1,0:T(8,128)S(1)}, bf16[128,4096]{1,0:T(8,128)(2,1)S(1)}) custom-call(f32[3,128]{1,0:T(4,128)S(1)} %collective-permute-done.5.refs_0_, f32[3,128]{1,0:T(4,128)S(1)} %collective-permute-done.6.refs_1_, f32[3,128]{1,0:T(4,128)S(1)} %collective-permute-done.7.refs_2_, ...), custom_call_target="tpu_custom_call" | custom-call | bytes 3480576 | tf_op jit(solution)/shard_map/pallas_call | solution.py:31
  41.2 0.7 collective-permute-start.12
  42.5 1.3 %collective-permute-start.10 = (bf16[128,256]{1,0:T(8,128)(2,1)S(1)}, bf16[128,256]{1,0:T(8,128)(2,1)S(1)}, u32[]{:S(2)}, u32[]{:S(2)}) collective-permute-start(bf16[128,256]{1,0:T(8,128)(2,1)S(1)} %get-tuple-element.51), channel_id=1, source_target_pairs={{0,1},{1,0},{2,3},{3,2},{4,5},{5,4},{6,7},{7,6},{8,9},{9,8},{10,11... | collective-permute-start | bytes 196616 | tf_op jit(solution)/shard_map/ppermute | solution.py:293
  43.8 0.9 %collective-permute-done.10.swap_ref = bf16[128,256]{1,0:T(8,128)(2,1)S(1)} collective-permute-done((bf16[128,256]{1,0:T(8,128)(2,1)S(1)}, bf16[128,256]{1,0:T(8,128)(2,1)S(1)}, u32[]{:S(2)}, u32[]{:S(2)}) %collective-permute-start.10) | collective-permute-done | bytes 65568 | tf_op jit(solution)/shard_map/ppermute | solution.py:293
  45.2 3.4 %collective-permute-start.11 = (bf16[128,4096]{1,0:T(8,128)(2,1)S(1)}, bf16[128,4096]{1,0:T(8,128)(2,1)S(1)}, u32[]{:S(2)}, u32[]{:S(2)}) collective-permute-start(bf16[128,4096]{1,0:T(8,128)(2,1)S(1)} %get-tuple-element.52), channel_id=1, source_target_pairs={{0,3},{2,5},{4,7},{6,1},{8,11},{10,13},{12,15},{14,9},{16,19},{18,... | collective-permute-start | bytes 3145736 | tf_op jit(solution)/shard_map/ppermute | solution.py:290
  48.6 2.8 %collective-permute-start.15 = (f32[3,128]{1,0:T(4,128)S(1)}, f32[3,128]{1,0:T(4,128)S(1)}, u32[]{:S(2)}, u32[]{:S(2)}) collective-permute-start(f32[3,128]{1,0:T(4,128)S(1)} %get-tuple-element.58.refs_0_), channel_id=1, source_target_pairs={{0,24},{8,16},{16,8},{24,0},{1,25},{9,17},{17,9},{25,1},{2,26},{10... | collective-permute-start | bytes 4616 | tf_op jit(solution)/shard_map/ppermute | solution.py:296
  52.2 1.0 %collective-permute-done.15.refs_3_ = f32[3,128]{1,0:T(4,128)S(1)} collective-permute-done((f32[3,128]{1,0:T(4,128)S(1)}, f32[3,128]{1,0:T(4,128)S(1)}, u32[]{:S(2)}, u32[]{:S(2)}) %collective-permute-start.15) | collective-permute-done | bytes 1568 | tf_op jit(solution)/shard_map/ppermute | solution.py:296
  53.2 1.8 %collective-permute-done.14.refs_2_ = f32[3,128]{1,0:T(4,128)S(1)} collective-permute-done((f32[3,128]{1,0:T(4,128)S(1)}, f32[3,128]{1,0:T(4,128)S(1)}, u32[]{:S(2)}, u32[]{:S(2)}) %collective-permute-start.14) | collective-permute-done | bytes 1568 | tf_op jit(solution)/shard_map/ppermute | solution.py:296
  55.2 2.1 %shard_map.79 = (bf16[256,1024]{1,0:T(8,128)(2,1)S(1)}, bf16[256,1024]{1,0:T(8,128)(2,1)S(1)}, bf16[256,1024]{1,0:T(8,128)(2,1)S(1)}, bf16[256,1024]{1,0:T(8,128)(2,1)S(1)}, f32[8,128]{1,0:T(8,128)}) custom-call(f32[3,128]{1,0:T(4,128)S(1)} %get-tuple-element.58.refs_0_, f32[3,128]{1,0:T(4,128)S(1)} %collective-permute-done.13.refs_1_, ...), custom_call_target="tpu_custom_call" | custom-call | bytes 4339712 | tf_op jit(solution)/shard_map/pallas_call | solution.py:31
  57.3 1.5 %collective-permute-start.16 = (bf16[256,1024]{1,0:T(8,128)(2,1)S(1)}, bf16[256,1024]{1,0:T(8,128)(2,1)S(1)}, u32[]{:S(2)}, u32[]{:S(2)}) collective-permute-start(bf16[256,1024]{1,0:T(8,128)(2,1)S(1)} %get-tuple-element.60), channel_id=1, source_target_pairs={{0,24},{8,16},{16,8},{24,0},{1,25},{9,17},{17,9},{25,1},{2,26},{10... | collective-permute-start | bytes 1572872 | tf_op jit(solution)/shard_map/ppermute | solution.py:296
  59.3 1.4 %collective-permute-start.18 = (bf16[256,1024]{1,0:T(8,128)(2,1)S(1)}, bf16[256,1024]{1,0:T(8,128)(2,1)S(1)}, u32[]{:S(2)}, u32[]{:S(2)}) collective-permute-start(bf16[256,1024]{1,0:T(8,128)(2,1)S(1)} %get-tuple-element.62), channel_id=1, source_target_pairs={{0,8},{8,0},{16,24},{24,16},{1,9},{9,1},{17,25},{25,17},{2,10},{10... | collective-permute-start | bytes 1572872 | tf_op jit(solution)/shard_map/ppermute | solution.py:296
  60.9 1.3 %collective-permute-start.19 = (bf16[128,4096]{1,0:T(8,128)(2,1)S(1)}, bf16[128,4096]{1,0:T(8,128)(2,1)S(1)}, u32[]{:S(2)}, u32[]{:S(2)}) collective-permute-start(bf16[128,4096]{1,0:T(8,128)(2,1)S(1)} %get-tuple-element.66), channel_id=1, source_target_pairs={{1,2},{3,4},{5,6},{7,0},{9,10},{11,12},{13,14},{15,8},{17,18},{19,... | collective-permute-start | bytes 3145736 | tf_op jit(solution)/shard_map/ppermute | solution.py:290
  62.2 3.8 %collective-permute-done.11.own3_ref = bf16[128,4096]{1,0:T(8,128)(2,1)S(1)} collective-permute-done((bf16[128,4096]{1,0:T(8,128)(2,1)S(1)}, bf16[128,4096]{1,0:T(8,128)(2,1)S(1)}, u32[]{:S(2)}, u32[]{:S(2)}) %collective-permute-start.11) | collective-permute-done | bytes 1048608 | tf_op jit(solution)/shard_map/ppermute | solution.py:290
  66.1 1.9 %shard_map.78 = (f32[128,4096]{1,0:T(8,128)S(1)}, f32[128,4096]{1,0:T(8,128)S(1)}) custom-call(bf16[128,4096]{1,0:T(8,128)(2,1)S(1)} %copy-done, bf16[128,8192]{1,0:T(8,128)(2,1)S(1)} %collective-permute-done.8.pair_ref, bf16[128,4096]{1,0:T(8,128)(2,1)S(1)} %copy-done.1, bf16[128,4096]{1,0:T(8,128)(2,1)S(1)} %shard_map.68.refs_1_.n1_ref, ...), custom_call_target="tpu_custom_call" | custom-call | flops 49999998976 | bytes 13832704 | tf_op jit(solution)/shard_map/pallas_call | solution.py:31
  67.9 5.1 %collective-permute-done.16.refs_0_ = bf16[256,1024]{1,0:T(8,128)(2,1)S(1)} collective-permute-done((bf16[256,1024]{1,0:T(8,128)(2,1)S(1)}, bf16[256,1024]{1,0:T(8,128)(2,1)S(1)}, u32[]{:S(2)}, u32[]{:S(2)}) %collective-permute-start.16) | collective-permute-done | bytes 524320 | tf_op jit(solution)/shard_map/ppermute | solution.py:296
  73.0 6.8 %collective-permute-done.17.refs_1_ = bf16[256,1024]{1,0:T(8,128)(2,1)S(1)} collective-permute-done((bf16[256,1024]{1,0:T(8,128)(2,1)S(1)}, bf16[256,1024]{1,0:T(8,128)(2,1)S(1)}, u32[]{:S(2)}, u32[]{:S(2)}) %collective-permute-start.17) | collective-permute-done | bytes 524320 | tf_op jit(solution)/shard_map/ppermute | solution.py:296
  80.1 1.2 %shard_map.80 = (bf16[128,4096]{1,0:T(8,128)(2,1)}, f32[128,4096]{1,0:T(8,128)S(1)}) custom-call(f32[128,4096]{1,0:T(8,128)S(1)} %get-tuple-element.56.pulled, f32[128,4096]{1,0:T(8,128)S(1)} %get-tuple-element.57.base, bf16[256,1024]{1,0:T(8,128)(2,1)S(1)} %collective-permute-done.16.refs_0_, bf16[256,1024]{1,0:T(8,128)(2,1)S(1)} %collective-permute-done.17.refs_1_, ...), custom_call_target="tpu_custom_call" | custom-call | bytes 9437184 | tf_op jit(solution)/shard_map/pallas_call | solution.py:31
  81.7 1.1 %shard_map.81 = bf16[128,4096]{1,0:T(8,128)(2,1)} custom-call(f32[128,4096]{1,0:T(8,128)S(1)} %get-tuple-element.65.almost, bf16[128,4096]{1,0:T(8,128)(2,1)S(1)} %collective-permute-done.19.own1), custom_call_target="tpu_custom_call" | custom-call | bytes 4194304 | tf_op jit(solution)/shard_map/pallas_call | solution.py:31
  (31 shorter events, 7.9 us)
Async XLA Ops:
  0.6 10.4 %copy-start.1 = (bf16[128,4096]{1,0:T(8,128)(2,1)S(1)}, bf16[128,4096]{1,0:T(8,128)(2,1)}, u32[]{:S(2)}) copy-start(bf16[128,4096]{1,0:T(8,128)(2,1)} %p_ref.1) | copy-start | bytes 3145732
  0.6 20.5 %collective-permute-start.3 = (bf16[128,4096]{1,0:T(8,128)(2,1)}, bf16[128,4096]{1,0:T(8,128)(2,1)S(1)}, u32[]{:S(2)}, u32[]{:S(2)}) collective-permute-start(bf16[128,4096]{1,0:T(8,128)(2,1)} %p_ref.1), channel_id=1, source_target_pairs={{0,7},{1,0},{2,1},{3,2},{4,3},{5,4},{6,5},{7,6},{8,15},{9,8},{10,9... | collective-permute-start | bytes 3145736 | tf_op jit(solution)/shard_map/ppermute | solution.py:290
  5.2 0.7 copy-start.2
  7.5 22.8 %collective-permute-start = (bf16[272,1024]{1,0:T(8,128)(2,1)S(1)}, bf16[272,1024]{1,0:T(8,128)(2,1)S(1)}, u32[]{:S(2)}, u32[]{:S(2)}) collective-permute-start(bf16[272,1024]{1,0:T(8,128)(2,1)S(1)} %get-tuple-element.35), channel_id=1, source_target_pairs={{0,24},{8,16},{16,8},{24,0},{1,25},{9,17},{17,9},{25,1},{2,26},{10... | collective-permute-start | bytes 1671176 | tf_op jit(solution)/shard_map/ppermute | solution.py:296
  10.0 22.2 %collective-permute-start.1 = (bf16[272,1024]{1,0:T(8,128)(2,1)S(1)}, bf16[272,1024]{1,0:T(8,128)(2,1)S(1)}, u32[]{:S(2)}, u32[]{:S(2)}) collective-permute-start(bf16[272,1024]{1,0:T(8,128)(2,1)S(1)} %get-tuple-element.36), channel_id=1, source_target_pairs={{0,16},{8,24},{16,0},{24,8},{1,17},{9,25},{17,1},{25,9},{2,18},{10... | collective-permute-start | bytes 1671176 | tf_op jit(solution)/shard_map/ppermute | solution.py:296
  10.5 22.0 %collective-permute-start.2 = (bf16[272,1024]{1,0:T(8,128)(2,1)S(1)}, bf16[272,1024]{1,0:T(8,128)(2,1)S(1)}, u32[]{:S(2)}, u32[]{:S(2)}) collective-permute-start(bf16[272,1024]{1,0:T(8,128)(2,1)S(1)} %get-tuple-element.37), channel_id=1, source_target_pairs={{0,8},{8,0},{16,24},{24,16},{1,9},{9,1},{17,25},{25,17},{2,10},{10... | collective-permute-start | bytes 1671176 | tf_op jit(solution)/shard_map/ppermute | solution.py:296
  11.1 16.9 %copy-start = (bf16[128,4096]{1,0:T(8,128)(2,1)S(1)}, bf16[128,4096]{1,0:T(8,128)(2,1)}, u32[]{:S(2)}) copy-start(bf16[128,4096]{1,0:T(8,128)(2,1)} %q_ref.9) | copy-start | bytes 3145732
  11.1 16.8 %collective-permute-start.4 = (bf16[128,4096]{1,0:T(8,128)(2,1)S(1)}, bf16[128,4096]{1,0:T(8,128)(2,1)S(1)}, u32[]{:S(2)}, u32[]{:S(2)}) collective-permute-start(bf16[128,4096]{1,0:T(8,128)(2,1)S(1)} %shard_map.69), channel_id=1, source_target_pairs={{1,6},{3,0},{5,2},{7,4},{9,14},{11,8},{13,10},{15,12},{17,22},{19,... | collective-permute-start | bytes 3145736 | tf_op jit(solution)/shard_map/ppermute | solution.py:290
  21.2 19.0 %collective-permute-start.9 = (bf16[128,4096]{1,0:T(8,128)(2,1)S(1)}, bf16[128,4096]{1,0:T(8,128)(2,1)S(1)}, u32[]{:S(2)}, u32[]{:S(2)}) collective-permute-start(bf16[128,4096]{1,0:T(8,128)(2,1)S(1)} %shard_map.68.refs_1_.n1_ref), channel_id=1, source_target_pairs={{1,7},{3,1},{5,3},{7,5},{9,15},{11,9},{13,11},{15,13},{17,23},{19,... | collective-permute-start | bytes 3145736 | tf_op jit(solution)/shard_map/ppermute | solution.py:290
  28.1 9.1 %collective-permute-start.8 = (bf16[128,8192]{1,0:T(8,128)(2,1)S(1)}, bf16[128,8192]{1,0:T(8,128)(2,1)S(1)}, u32[]{:S(2)}, u32[]{:S(2)}) collective-permute-start(bf16[128,8192]{1,0:T(8,128)(2,1)S(1)} %shard_map.72), channel_id=1, source_target_pairs={{0,1},{1,0},{2,3},{3,2},{4,5},{5,4},{6,7},{7,6},{8,9},{9,8},{10,11... | collective-permute-start | bytes 6291464 | tf_op jit(solution)/shard_map/ppermute | solution.py:293
  33.6 6.6 %copy-start.3 = (f32[128]{0:T(128)S(1)}, f32[128]{0:T(128)}, u32[]{:S(2)}) copy-start(f32[128]{0:T(128)} %param.7) | copy-start | bytes 1540
  33.6 4.5 %collective-permute-start.5 = (f32[3,128]{1,0:T(4,128)S(1)}, f32[3,128]{1,0:T(4,128)S(1)}, u32[]{:S(2)}, u32[]{:S(2)}) collective-permute-start(f32[3,128]{1,0:T(4,128)S(1)} %get-tuple-element.41), channel_id=1, source_target_pairs={{0,24},{8,16},{16,8},{24,0},{1,25},{9,17},{17,9},{25,1},{2,26},{10... | collective-permute-start | bytes 4616 | tf_op jit(solution)/shard_map/ppermute | solution.py:296
  35.2 3.6 %collective-permute-start.6 = (f32[3,128]{1,0:T(4,128)S(1)}, f32[3,128]{1,0:T(4,128)S(1)}, u32[]{:S(2)}, u32[]{:S(2)}) collective-permute-start(f32[3,128]{1,0:T(4,128)S(1)} %get-tuple-element.42), channel_id=1, source_target_pairs={{0,16},{8,24},{16,0},{24,8},{1,17},{9,25},{17,1},{25,9},{2,18},{10... | collective-permute-start | bytes 4616 | tf_op jit(solution)/shard_map/ppermute | solution.py:296
  36.7 3.6 %collective-permute-start.7 = (f32[3,128]{1,0:T(4,128)S(1)}, f32[3,128]{1,0:T(4,128)S(1)}, u32[]{:S(2)}, u32[]{:S(2)}) collective-permute-start(f32[3,128]{1,0:T(4,128)S(1)} %get-tuple-element.43), channel_id=1, source_target_pairs={{0,8},{8,0},{16,24},{24,16},{1,9},{9,1},{17,25},{25,17},{2,10},{10... | collective-permute-start | bytes 4616 | tf_op jit(solution)/shard_map/ppermute | solution.py:296
  41.2 19.6 %collective-permute-start.12 = (bf16[128,4096]{1,0:T(8,128)(2,1)S(1)}, bf16[128,4096]{1,0:T(8,128)(2,1)S(1)}, u32[]{:S(2)}, u32[]{:S(2)}) collective-permute-start(bf16[128,4096]{1,0:T(8,128)(2,1)S(1)} %get-tuple-element.54), channel_id=1, source_target_pairs={{1,3},{3,5},{5,7},{7,2},{9,11},{11,13},{13,15},{15,10},{17,19},{19... | collective-permute-start | bytes 3145736 | tf_op jit(solution)/shard_map/ppermute | solution.py:346
  42.5 2.2 %collective-permute-start.10 = (bf16[128,256]{1,0:T(8,128)(2,1)S(1)}, bf16[128,256]{1,0:T(8,128)(2,1)S(1)}, u32[]{:S(2)}, u32[]{:S(2)}) collective-permute-start(bf16[128,256]{1,0:T(8,128)(2,1)S(1)} %get-tuple-element.51), channel_id=1, source_target_pairs={{0,1},{1,0},{2,3},{3,2},{4,5},{5,4},{6,7},{7,6},{8,9},{9,8},{10,11... | collective-permute-start | bytes 196616 | tf_op jit(solution)/shard_map/ppermute | solution.py:293
  45.2 20.9 %collective-permute-start.11 = (bf16[128,4096]{1,0:T(8,128)(2,1)S(1)}, bf16[128,4096]{1,0:T(8,128)(2,1)S(1)}, u32[]{:S(2)}, u32[]{:S(2)}) collective-permute-start(bf16[128,4096]{1,0:T(8,128)(2,1)S(1)} %get-tuple-element.52), channel_id=1, source_target_pairs={{0,3},{2,5},{4,7},{6,1},{8,11},{10,13},{12,15},{14,9},{16,19},{18,... | collective-permute-start | bytes 3145736 | tf_op jit(solution)/shard_map/ppermute | solution.py:290
  48.6 4.5 %collective-permute-start.15 = (f32[3,128]{1,0:T(4,128)S(1)}, f32[3,128]{1,0:T(4,128)S(1)}, u32[]{:S(2)}, u32[]{:S(2)}) collective-permute-start(f32[3,128]{1,0:T(4,128)S(1)} %get-tuple-element.58.refs_0_), channel_id=1, source_target_pairs={{0,24},{8,16},{16,8},{24,0},{1,25},{9,17},{17,9},{25,1},{2,26},{10... | collective-permute-start | bytes 4616 | tf_op jit(solution)/shard_map/ppermute | solution.py:296
  51.4 3.6 %collective-permute-start.14 = (f32[3,128]{1,0:T(4,128)S(1)}, f32[3,128]{1,0:T(4,128)S(1)}, u32[]{:S(2)}, u32[]{:S(2)}) collective-permute-start(f32[3,128]{1,0:T(4,128)S(1)} %get-tuple-element.58.refs_0_), channel_id=1, source_target_pairs={{0,16},{8,24},{16,0},{24,8},{1,17},{9,25},{17,1},{25,9},{2,18},{10... | collective-permute-start | bytes 4616 | tf_op jit(solution)/shard_map/ppermute | solution.py:296
  51.6 3.6 %collective-permute-start.13 = (f32[3,128]{1,0:T(4,128)S(1)}, f32[3,128]{1,0:T(4,128)S(1)}, u32[]{:S(2)}, u32[]{:S(2)}) collective-permute-start(f32[3,128]{1,0:T(4,128)S(1)} %get-tuple-element.58.refs_0_), channel_id=1, source_target_pairs={{0,8},{8,0},{16,24},{24,16},{1,9},{9,1},{17,25},{25,17},{2,10},{10... | collective-permute-start | bytes 4616 | tf_op jit(solution)/shard_map/ppermute | solution.py:296
  57.3 15.8 %collective-permute-start.16 = (bf16[256,1024]{1,0:T(8,128)(2,1)S(1)}, bf16[256,1024]{1,0:T(8,128)(2,1)S(1)}, u32[]{:S(2)}, u32[]{:S(2)}) collective-permute-start(bf16[256,1024]{1,0:T(8,128)(2,1)S(1)} %get-tuple-element.60), channel_id=1, source_target_pairs={{0,24},{8,16},{16,8},{24,0},{1,25},{9,17},{17,9},{25,1},{2,26},{10... | collective-permute-start | bytes 1572872 | tf_op jit(solution)/shard_map/ppermute | solution.py:296
  58.8 21.0 %collective-permute-start.17 = (bf16[256,1024]{1,0:T(8,128)(2,1)S(1)}, bf16[256,1024]{1,0:T(8,128)(2,1)S(1)}, u32[]{:S(2)}, u32[]{:S(2)}) collective-permute-start(bf16[256,1024]{1,0:T(8,128)(2,1)S(1)} %get-tuple-element.61), channel_id=1, source_target_pairs={{0,16},{8,24},{16,0},{24,8},{1,17},{9,25},{17,1},{25,9},{2,18},{10... | collective-permute-start | bytes 1572872 | tf_op jit(solution)/shard_map/ppermute | solution.py:296
  59.3 20.8 %collective-permute-start.18 = (bf16[256,1024]{1,0:T(8,128)(2,1)S(1)}, bf16[256,1024]{1,0:T(8,128)(2,1)S(1)}, u32[]{:S(2)}, u32[]{:S(2)}) collective-permute-start(bf16[256,1024]{1,0:T(8,128)(2,1)S(1)} %get-tuple-element.62), channel_id=1, source_target_pairs={{0,8},{8,0},{16,24},{24,16},{1,9},{9,1},{17,25},{25,17},{2,10},{10... | collective-permute-start | bytes 1572872 | tf_op jit(solution)/shard_map/ppermute | solution.py:296
  60.9 20.8 %collective-permute-start.19 = (bf16[128,4096]{1,0:T(8,128)(2,1)S(1)}, bf16[128,4096]{1,0:T(8,128)(2,1)S(1)}, u32[]{:S(2)}, u32[]{:S(2)}) collective-permute-start(bf16[128,4096]{1,0:T(8,128)(2,1)S(1)} %get-tuple-element.66), channel_id=1, source_target_pairs={{1,2},{3,4},{5,6},{7,0},{9,10},{11,12},{13,14},{15,8},{17,18},{19,... | collective-permute-start | bytes 3145736 | tf_op jit(solution)/shard_map/ppermute | solution.py:290

commit v13 on v12

--- a/solution.py
+++ b/solution.py
@@ -13,7 +13,7 @@
 F32 = jnp.float32
 CHUNK = 512
 TAIL = 16
-LONG, SOME = 5 * 10**10, 10 * 10**9
+LONG, SOME = 5 * 10**10, 16 * 10**9
 VMEM = pl.BlockSpec(memory_space=pltpu.VMEM)
 HBM = pl.BlockSpec(memory_space=pltpu.HBM)
 TOKEN = jax.ShapeDtypeStruct((8, 128), F32)

time: 83 us -> 87.6 us (1.055); the launches traced: 82.8 us -> 86.1 us
  waiting for transfers between devices: 39.7 us -> 45.2 us
  starting transfers between devices: 28.8 us -> 26.7 us
    ppermute x5, waiting for transfers between devices: 18.8 us -> 37.8 us  [shift(): return lax.ppermute(array, 'blk', pairs_of(by, which))]
    ppermute x12, waiting for transfers between devices: 20 us -> 7.35 us  [over_groups(): return lax.ppermute(array, 'grp', [(i, i ^ r) for i in range(groups)])]
    ppermute x5, starting transfers between devices: 11.4 us -> 9.33 us  [shift(): return lax.ppermute(array, 'blk', pairs_of(by, which))]
    ppermute x2, waiting for transfers between devices: 0.9 us -> 0.01 us  [swap(): return lax.ppermute(array, 'blk', [(i, i ^ 1) for i in range(loop)])]
  transfers between devices with their start and end apart: 20 -> 20, of which waited for: 16 -> 12; matrix products, arithmetic and copies ran while one was open for 0% -> 0% of each run, Pallas kernels for 13% -> 13%
where the time goes in v13:
time: 87.6 us; the launch traced here: 86.1 us
  waiting for transfers between devices  45.2 us (52%)
  starting transfers between devices  26.7 us (30%)
  Pallas kernels  12.8 us (15%)
    ppermute x5, waiting for transfers between devices, shift(): return lax.ppermute(array, 'blk', pairs_of(by, which))  37.8 us
    ppermute x12, starting transfers between devices, over_groups(): return lax.ppermute(array, 'grp', [(i, i ^ r) for i in range(groups)])  14.1 us
    pallas_call x15, Pallas kernels, local_call(): pl.pallas_call(body, out_shape=out_shape, in_specs=in_specs or [VMEM] * l...  12.8 us
    ppermute x5, starting transfers between devices, shift(): return lax.ppermute(array, 'blk', pairs_of(by, which))  9.33 us
    ppermute x12, waiting for transfers between devices, over_groups(): return lax.ppermute(array, 'grp', [(i, i ^ r) for i in range(groups)])  7.35 us
    ppermute x2, starting transfers between devices, swap(): return lax.ppermute(array, 'blk', [(i, i ^ 1) for i in range(loop)])  2.52 us
  transfers between devices with their start and end apart: 20, of which 12 were waited for; matrix products, arithmetic and copies ran while one was open for 0% of the time, Pallas kernels for 13%

profile of v13, /device:TPU:0, one launch (start us, length us, event | category | flops | bytes accessed | tf_op | source)
XLA Modules:
  0.0 86.1 jit_solution(15383036957001201745)
XLA Ops:
  0.6 4.5 %collective-permute-start.3 = (bf16[128,4096]{1,0:T(8,128)(2,1)}, bf16[128,4096]{1,0:T(8,128)(2,1)S(1)}, u32[]{:S(2)}, u32[]{:S(2)}) collective-permute-start(bf16[128,4096]{1,0:T(8,128)(2,1)} %p_ref.1), channel_id=1, source_target_pairs={{0,7},{1,0},{2,1},{3,2},{4,3},{5,4},{6,5},{7,6},{8,15},{9,8},{10,9... | collective-permute-start | bytes 3145736 | tf_op jit(solution)/shard_map/ppermute | solution.py:290
  5.2 0.7 copy-done.2
  5.9 1.6 %shard_map.67 = (bf16[272,1024]{1,0:T(8,128)(2,1)S(1)}, bf16[272,1024]{1,0:T(8,128)(2,1)S(1)}, bf16[272,1024]{1,0:T(8,128)(2,1)S(1)}, bf16[272,1024]{1,0:T(8,128)(2,1)S(1)}, f32[8,128]{1,0:T(8,128)S(1)}) custom-call(bf16[128,4096]{1,0:T(8,128)(2,1)} %q_ref.9, bf16[128,4096]{1,0:T(8,128)(2,1)} %p_ref.1, s32[3,128]{1,0:T(4,128)S(1)} %bitcast.3), custom_call_target="tpu_custom_call" | custom-call | bytes 4331008 | tf_op jit(solution)/shard_map/pallas_call | solution.py:31
  7.5 2.5 %collective-permute-start = (bf16[272,1024]{1,0:T(8,128)(2,1)S(1)}, bf16[272,1024]{1,0:T(8,128)(2,1)S(1)}, u32[]{:S(2)}, u32[]{:S(2)}) collective-permute-start(bf16[272,1024]{1,0:T(8,128)(2,1)S(1)} %get-tuple-element.35), channel_id=1, source_target_pairs={{0,24},{8,16},{16,8},{24,0},{1,25},{9,17},{17,9},{25,1},{2,26},{10... | collective-permute-start | bytes 1671176 | tf_op jit(solution)/shard_map/ppermute | solution.py:296
  11.1 1.4 %collective-permute-start.4 = (bf16[128,4096]{1,0:T(8,128)(2,1)S(1)}, bf16[128,4096]{1,0:T(8,128)(2,1)S(1)}, u32[]{:S(2)}, u32[]{:S(2)}) collective-permute-start(bf16[128,4096]{1,0:T(8,128)(2,1)S(1)} %shard_map.69), channel_id=1, source_target_pairs={{1,6},{3,0},{5,2},{7,4},{9,14},{11,8},{13,10},{15,12},{17,22},{19,... | collective-permute-start | bytes 3145736 | tf_op jit(solution)/shard_map/ppermute | solution.py:290
  12.5 8.6 %collective-permute-done.3.source = bf16[128,4096]{1,0:T(8,128)(2,1)S(1)} collective-permute-done((bf16[128,4096]{1,0:T(8,128)(2,1)}, bf16[128,4096]{1,0:T(8,128)(2,1)S(1)}, u32[]{:S(2)}, u32[]{:S(2)}) %collective-permute-start.3) | collective-permute-done | bytes 1048608 | tf_op jit(solution)/shard_map/ppermute | solution.py:290
  21.2 0.7 collective-permute-start.9
  22.0 6.0 %collective-permute-done.4.refs_2_.e3_ref = bf16[128,4096]{1,0:T(8,128)(2,1)S(1)} collective-permute-done((bf16[128,4096]{1,0:T(8,128)(2,1)S(1)}, bf16[128,4096]{1,0:T(8,128)(2,1)S(1)}, u32[]{:S(2)}, u32[]{:S(2)}) %collective-permute-start.4) | collective-permute-done | bytes 1048608 | tf_op jit(solution)/shard_map/ppermute | solution.py:290
  28.1 1.2 %collective-permute-start.8 = (bf16[128,8192]{1,0:T(8,128)(2,1)S(1)}, bf16[128,8192]{1,0:T(8,128)(2,1)S(1)}, u32[]{:S(2)}, u32[]{:S(2)}) collective-permute-start(bf16[128,8192]{1,0:T(8,128)(2,1)S(1)} %shard_map.72), channel_id=1, source_target_pairs={{0,1},{1,0},{2,3},{3,2},{4,5},{5,4},{6,7},{7,6},{8,9},{9,8},{10,11... | collective-permute-start | bytes 6291464 | tf_op jit(solution)/shard_map/ppermute | solution.py:293
  29.3 1.0 %shard_map.70 = (f32[128,128]{1,0:T(8,128)S(1)}, f32[128,128]{1,0:T(8,128)S(1)}, f32[128,128]{1,0:T(8,128)S(1)}) custom-call(bf16[128,4096]{1,0:T(8,128)(2,1)S(1)} %copy-done, bf16[128,4096]{1,0:T(8,128)(2,1)S(1)} %copy-done.1, bf16[128,4096]{1,0:T(8,128)(2,1)S(1)} %shard_map.68.refs_1_.n1_ref, bf16[128,4096]{1,0:T(8,128)(2,1)S(1)} %collective-permute-done.4.refs_2_.e3_ref), custom_call_target="tpu_custom_call" | custom-call | bytes 4390912 | tf_op jit(solution)/shard_map/pallas_call | solution.py:31
  30.3 1.9 %collective-permute-done.1.refs_1_.refs_5_ = bf16[272,1024]{1,0:T(8,128)(2,1)S(1)} collective-permute-done((bf16[272,1024]{1,0:T(8,128)(2,1)S(1)}, bf16[272,1024]{1,0:T(8,128)(2,1)S(1)}, u32[]{:S(2)}, u32[]{:S(2)}) %collective-permute-start.1) | collective-permute-done | bytes 557088 | tf_op jit(solution)/shard_map/ppermute | solution.py:296
  32.5 1.2 %shard_map.71 = (f32[3,128]{1,0:T(4,128)S(1)}, f32[3,128]{1,0:T(4,128)S(1)}, f32[3,128]{1,0:T(4,128)S(1)}, f32[3,128]{1,0:T(4,128)S(1)}) custom-call(bf16[272,1024]{1,0:T(8,128)(2,1)S(1)} %collective-permute-done.refs_0_.refs_4_, bf16[272,1024]{1,0:T(8,128)(2,1)S(1)} %collective-permute-done.1.refs_1_.refs_5_, ...), custom_call_target="tpu_custom_call" | custom-call | flops 49999998976 | bytes 2299904 | tf_op jit(solution)/shard_map/pallas_call | solution.py:31
  33.6 1.6 %collective-permute-start.5 = (f32[3,128]{1,0:T(4,128)S(1)}, f32[3,128]{1,0:T(4,128)S(1)}, u32[]{:S(2)}, u32[]{:S(2)}) collective-permute-start(f32[3,128]{1,0:T(4,128)S(1)} %get-tuple-element.41), channel_id=1, source_target_pairs={{0,24},{8,16},{16,8},{24,0},{1,25},{9,17},{17,9},{25,1},{2,26},{10... | collective-permute-start | bytes 4616 | tf_op jit(solution)/shard_map/ppermute | solution.py:296
  35.2 1.4 %collective-permute-start.6 = (f32[3,128]{1,0:T(4,128)S(1)}, f32[3,128]{1,0:T(4,128)S(1)}, u32[]{:S(2)}, u32[]{:S(2)}) collective-permute-start(f32[3,128]{1,0:T(4,128)S(1)} %get-tuple-element.42), channel_id=1, source_target_pairs={{0,16},{8,24},{16,0},{24,8},{1,17},{9,25},{17,1},{25,9},{2,18},{10... | collective-permute-start | bytes 4616 | tf_op jit(solution)/shard_map/ppermute | solution.py:296
  38.2 0.6 collective-permute-done.6.refs_1_
  38.8 1.4 %collective-permute-done.7.refs_2_ = f32[3,128]{1,0:T(4,128)S(1)} collective-permute-done((f32[3,128]{1,0:T(4,128)S(1)}, f32[3,128]{1,0:T(4,128)S(1)}, u32[]{:S(2)}, u32[]{:S(2)}) %collective-permute-start.7) | collective-permute-done | bytes 1568 | tf_op jit(solution)/shard_map/ppermute | solution.py:296
  40.2 0.9 %shard_map.74 = (f32[1,128]{1,0:T(1,128)S(1)}, f32[128,128]{1,0:T(8,128)S(1)}, bf16[128,4096]{1,0:T(8,128)(2,1)S(1)}) custom-call(f32[3,128]{1,0:T(4,128)S(1)} %collective-permute-done.5.refs_0_, f32[3,128]{1,0:T(4,128)S(1)} %collective-permute-done.6.refs_1_, f32[3,128]{1,0:T(4,128)S(1)} %collective-permute-done.7.refs_2_, ...), custom_call_target="tpu_custom_call" | custom-call | bytes 3480576 | tf_op jit(solution)/shard_map/pallas_call | solution.py:31
  41.2 0.7 collective-permute-start.12
  42.5 1.3 %collective-permute-start.10 = (bf16[128,256]{1,0:T(8,128)(2,1)S(1)}, bf16[128,256]{1,0:T(8,128)(2,1)S(1)}, u32[]{:S(2)}, u32[]{:S(2)}) collective-permute-start(bf16[128,256]{1,0:T(8,128)(2,1)S(1)} %get-tuple-element.51), channel_id=1, source_target_pairs={{0,1},{1,0},{2,3},{3,2},{4,5},{5,4},{6,7},{7,6},{8,9},{9,8},{10,11... | collective-permute-start | bytes 196616 | tf_op jit(solution)/shard_map/ppermute | solution.py:293
  43.8 2.7 %collective-permute-start.15 = (f32[3,128]{1,0:T(4,128)S(1)}, f32[3,128]{1,0:T(4,128)S(1)}, u32[]{:S(2)}, u32[]{:S(2)}) collective-permute-start(f32[3,128]{1,0:T(4,128)S(1)} %get-tuple-element.58.refs_0_), channel_id=1, source_target_pairs={{0,24},{8,16},{16,8},{24,0},{1,25},{9,17},{17,9},{25,1},{2,26},{10... | collective-permute-start | bytes 4616 | tf_op jit(solution)/shard_map/ppermute | solution.py:296
  46.7 0.6 collective-permute-start.13
  48.3 1.8 %collective-permute-done.14.refs_2_ = f32[3,128]{1,0:T(4,128)S(1)} collective-permute-done((f32[3,128]{1,0:T(4,128)S(1)}, f32[3,128]{1,0:T(4,128)S(1)}, u32[]{:S(2)}, u32[]{:S(2)}) %collective-permute-start.14) | collective-permute-done | bytes 1568 | tf_op jit(solution)/shard_map/ppermute | solution.py:296
  50.3 2.1 %shard_map.79 = (bf16[256,1024]{1,0:T(8,128)(2,1)S(1)}, bf16[256,1024]{1,0:T(8,128)(2,1)S(1)}, bf16[256,1024]{1,0:T(8,128)(2,1)S(1)}, bf16[256,1024]{1,0:T(8,128)(2,1)S(1)}, f32[8,128]{1,0:T(8,128)}) custom-call(f32[3,128]{1,0:T(4,128)S(1)} %get-tuple-element.58.refs_0_, f32[3,128]{1,0:T(4,128)S(1)} %collective-permute-done.13.refs_1_, ...), custom_call_target="tpu_custom_call" | custom-call | bytes 4339712 | tf_op jit(solution)/shard_map/pallas_call | solution.py:31
  52.4 1.5 %collective-permute-start.16 = (bf16[256,1024]{1,0:T(8,128)(2,1)S(1)}, bf16[256,1024]{1,0:T(8,128)(2,1)S(1)}, u32[]{:S(2)}, u32[]{:S(2)}) collective-permute-start(bf16[256,1024]{1,0:T(8,128)(2,1)S(1)} %get-tuple-element.60), channel_id=1, source_target_pairs={{0,24},{8,16},{16,8},{24,0},{1,25},{9,17},{17,9},{25,1},{2,26},{10... | collective-permute-start | bytes 1572872 | tf_op jit(solution)/shard_map/ppermute | solution.py:296
  54.4 1.4 %collective-permute-start.18 = (bf16[256,1024]{1,0:T(8,128)(2,1)S(1)}, bf16[256,1024]{1,0:T(8,128)(2,1)S(1)}, u32[]{:S(2)}, u32[]{:S(2)}) collective-permute-start(bf16[256,1024]{1,0:T(8,128)(2,1)S(1)} %get-tuple-element.62), channel_id=1, source_target_pairs={{0,8},{8,0},{16,24},{24,16},{1,9},{9,1},{17,25},{25,17},{2,10},{10... | collective-permute-start | bytes 1572872 | tf_op jit(solution)/shard_map/ppermute | solution.py:296
  55.9 1.3 %collective-permute-start.11 = (bf16[128,4096]{1,0:T(8,128)(2,1)S(1)}, bf16[128,4096]{1,0:T(8,128)(2,1)S(1)}, u32[]{:S(2)}, u32[]{:S(2)}) collective-permute-start(bf16[128,4096]{1,0:T(8,128)(2,1)S(1)} %get-tuple-element.52), channel_id=1, source_target_pairs={{0,3},{2,5},{4,7},{6,1},{8,11},{10,13},{12,15},{14,9},{16,19},{18,... | collective-permute-start | bytes 3145736 | tf_op jit(solution)/shard_map/ppermute | solution.py:290
  57.5 1.3 %collective-permute-start.19 = (bf16[128,4096]{1,0:T(8,128)(2,1)S(1)}, bf16[128,4096]{1,0:T(8,128)(2,1)S(1)}, u32[]{:S(2)}, u32[]{:S(2)}) collective-permute-start(bf16[128,4096]{1,0:T(8,128)(2,1)S(1)} %get-tuple-element.66), channel_id=1, source_target_pairs={{1,2},{3,4},{5,6},{7,0},{9,10},{11,12},{13,14},{15,8},{17,18},{19,... | collective-permute-start | bytes 3145736 | tf_op jit(solution)/shard_map/ppermute | solution.py:290
  58.8 17.7 %collective-permute-done.11.own3_ref = bf16[128,4096]{1,0:T(8,128)(2,1)S(1)} collective-permute-done((bf16[128,4096]{1,0:T(8,128)(2,1)S(1)}, bf16[128,4096]{1,0:T(8,128)(2,1)S(1)}, u32[]{:S(2)}, u32[]{:S(2)}) %collective-permute-start.11) | collective-permute-done | bytes 1048608 | tf_op jit(solution)/shard_map/ppermute | solution.py:290
  76.4 1.9 %shard_map.78 = (f32[128,4096]{1,0:T(8,128)S(1)}, f32[128,4096]{1,0:T(8,128)S(1)}) custom-call(bf16[128,4096]{1,0:T(8,128)(2,1)S(1)} %copy-done, bf16[128,8192]{1,0:T(8,128)(2,1)S(1)} %collective-permute-done.8.pair_ref, bf16[128,4096]{1,0:T(8,128)(2,1)S(1)} %copy-done.1, bf16[128,4096]{1,0:T(8,128)(2,1)S(1)} %shard_map.68.refs_1_.n1_ref, ...), custom_call_target="tpu_custom_call" | custom-call | flops 49999998976 | bytes 13832704 | tf_op jit(solution)/shard_map/pallas_call | solution.py:31
  78.3 1.2 %shard_map.80 = (bf16[128,4096]{1,0:T(8,128)(2,1)}, f32[128,4096]{1,0:T(8,128)S(1)}) custom-call(f32[128,4096]{1,0:T(8,128)S(1)} %get-tuple-element.56.pulled, f32[128,4096]{1,0:T(8,128)S(1)} %get-tuple-element.57.base, bf16[256,1024]{1,0:T(8,128)(2,1)S(1)} %collective-permute-done.16.refs_0_, bf16[256,1024]{1,0:T(8,128)(2,1)S(1)} %collective-permute-done.17.refs_1_, ...), custom_call_target="tpu_custom_call" | custom-call | bytes 9437184 | tf_op jit(solution)/shard_map/pallas_call | solution.py:31
  79.6 5.5 %collective-permute-done.19.own1 = bf16[128,4096]{1,0:T(8,128)(2,1)S(1)} collective-permute-done((bf16[128,4096]{1,0:T(8,128)(2,1)S(1)}, bf16[128,4096]{1,0:T(8,128)(2,1)S(1)}, u32[]{:S(2)}, u32[]{:S(2)}) %collective-permute-start.19) | collective-permute-done | bytes 1048608 | tf_op jit(solution)/shard_map/ppermute | solution.py:290
  85.1 1.1 %shard_map.81 = bf16[128,4096]{1,0:T(8,128)(2,1)} custom-call(f32[128,4096]{1,0:T(8,128)S(1)} %get-tuple-element.65.almost, bf16[128,4096]{1,0:T(8,128)(2,1)S(1)} %collective-permute-done.19.own1), custom_call_target="tpu_custom_call" | custom-call | bytes 4194304 | tf_op jit(solution)/shard_map/pallas_call | solution.py:31
  (31 shorter events, 5.9 us)
Async XLA Ops:
  0.6 10.4 %copy-start.1 = (bf16[128,4096]{1,0:T(8,128)(2,1)S(1)}, bf16[128,4096]{1,0:T(8,128)(2,1)}, u32[]{:S(2)}) copy-start(bf16[128,4096]{1,0:T(8,128)(2,1)} %p_ref.1) | copy-start | bytes 3145732
  0.6 20.5 %collective-permute-start.3 = (bf16[128,4096]{1,0:T(8,128)(2,1)}, bf16[128,4096]{1,0:T(8,128)(2,1)S(1)}, u32[]{:S(2)}, u32[]{:S(2)}) collective-permute-start(bf16[128,4096]{1,0:T(8,128)(2,1)} %p_ref.1), channel_id=1, source_target_pairs={{0,7},{1,0},{2,1},{3,2},{4,3},{5,4},{6,5},{7,6},{8,15},{9,8},{10,9... | collective-permute-start | bytes 3145736 | tf_op jit(solution)/shard_map/ppermute | solution.py:290
  5.2 0.7 copy-start.2
  7.5 22.8 %collective-permute-start = (bf16[272,1024]{1,0:T(8,128)(2,1)S(1)}, bf16[272,1024]{1,0:T(8,128)(2,1)S(1)}, u32[]{:S(2)}, u32[]{:S(2)}) collective-permute-start(bf16[272,1024]{1,0:T(8,128)(2,1)S(1)} %get-tuple-element.35), channel_id=1, source_target_pairs={{0,24},{8,16},{16,8},{24,0},{1,25},{9,17},{17,9},{25,1},{2,26},{10... | collective-permute-start | bytes 1671176 | tf_op jit(solution)/shard_map/ppermute | solution.py:296
  10.0 22.2 %collective-permute-start.1 = (bf16[272,1024]{1,0:T(8,128)(2,1)S(1)}, bf16[272,1024]{1,0:T(8,128)(2,1)S(1)}, u32[]{:S(2)}, u32[]{:S(2)}) collective-permute-start(bf16[272,1024]{1,0:T(8,128)(2,1)S(1)} %get-tuple-element.36), channel_id=1, source_target_pairs={{0,16},{8,24},{16,0},{24,8},{1,17},{9,25},{17,1},{25,9},{2,18},{10... | collective-permute-start | bytes 1671176 | tf_op jit(solution)/shard_map/ppermute | solution.py:296
  10.5 22.0 %collective-permute-start.2 = (bf16[272,1024]{1,0:T(8,128)(2,1)S(1)}, bf16[272,1024]{1,0:T(8,128)(2,1)S(1)}, u32[]{:S(2)}, u32[]{:S(2)}) collective-permute-start(bf16[272,1024]{1,0:T(8,128)(2,1)S(1)} %get-tuple-element.37), channel_id=1, source_target_pairs={{0,8},{8,0},{16,24},{24,16},{1,9},{9,1},{17,25},{25,17},{2,10},{10... | collective-permute-start | bytes 1671176 | tf_op jit(solution)/shard_map/ppermute | solution.py:296
  11.1 16.9 %copy-start = (bf16[128,4096]{1,0:T(8,128)(2,1)S(1)}, bf16[128,4096]{1,0:T(8,128)(2,1)}, u32[]{:S(2)}) copy-start(bf16[128,4096]{1,0:T(8,128)(2,1)} %q_ref.9) | copy-start | bytes 3145732
  11.1 16.8 %collective-permute-start.4 = (bf16[128,4096]{1,0:T(8,128)(2,1)S(1)}, bf16[128,4096]{1,0:T(8,128)(2,1)S(1)}, u32[]{:S(2)}, u32[]{:S(2)}) collective-permute-start(bf16[128,4096]{1,0:T(8,128)(2,1)S(1)} %shard_map.69), channel_id=1, source_target_pairs={{1,6},{3,0},{5,2},{7,4},{9,14},{11,8},{13,10},{15,12},{17,22},{19,... | collective-permute-start | bytes 3145736 | tf_op jit(solution)/shard_map/ppermute | solution.py:290
  21.2 19.0 %collective-permute-start.9 = (bf16[128,4096]{1,0:T(8,128)(2,1)S(1)}, bf16[128,4096]{1,0:T(8,128)(2,1)S(1)}, u32[]{:S(2)}, u32[]{:S(2)}) collective-permute-start(bf16[128,4096]{1,0:T(8,128)(2,1)S(1)} %shard_map.68.refs_1_.n1_ref), channel_id=1, source_target_pairs={{1,7},{3,1},{5,3},{7,5},{9,15},{11,9},{13,11},{15,13},{17,23},{19,... | collective-permute-start | bytes 3145736 | tf_op jit(solution)/shard_map/ppermute | solution.py:290
  28.1 9.1 %collective-permute-start.8 = (bf16[128,8192]{1,0:T(8,128)(2,1)S(1)}, bf16[128,8192]{1,0:T(8,128)(2,1)S(1)}, u32[]{:S(2)}, u32[]{:S(2)}) collective-permute-start(bf16[128,8192]{1,0:T(8,128)(2,1)S(1)} %shard_map.72), channel_id=1, source_target_pairs={{0,1},{1,0},{2,3},{3,2},{4,5},{5,4},{6,7},{7,6},{8,9},{9,8},{10,11... | collective-permute-start | bytes 6291464 | tf_op jit(solution)/shard_map/ppermute | solution.py:293
  33.6 6.6 %copy-start.3 = (f32[128]{0:T(128)S(1)}, f32[128]{0:T(128)}, u32[]{:S(2)}) copy-start(f32[128]{0:T(128)} %param.7) | copy-start | bytes 1540
  33.6 4.5 %collective-permute-start.5 = (f32[3,128]{1,0:T(4,128)S(1)}, f32[3,128]{1,0:T(4,128)S(1)}, u32[]{:S(2)}, u32[]{:S(2)}) collective-permute-start(f32[3,128]{1,0:T(4,128)S(1)} %get-tuple-element.41), channel_id=1, source_target_pairs={{0,24},{8,16},{16,8},{24,0},{1,25},{9,17},{17,9},{25,1},{2,26},{10... | collective-permute-start | bytes 4616 | tf_op jit(solution)/shard_map/ppermute | solution.py:296
  35.2 3.6 %collective-permute-start.6 = (f32[3,128]{1,0:T(4,128)S(1)}, f32[3,128]{1,0:T(4,128)S(1)}, u32[]{:S(2)}, u32[]{:S(2)}) collective-permute-start(f32[3,128]{1,0:T(4,128)S(1)} %get-tuple-element.42), channel_id=1, source_target_pairs={{0,16},{8,24},{16,0},{24,8},{1,17},{9,25},{17,1},{25,9},{2,18},{10... | collective-permute-start | bytes 4616 | tf_op jit(solution)/shard_map/ppermute | solution.py:296
  36.7 3.6 %collective-permute-start.7 = (f32[3,128]{1,0:T(4,128)S(1)}, f32[3,128]{1,0:T(4,128)S(1)}, u32[]{:S(2)}, u32[]{:S(2)}) collective-permute-start(f32[3,128]{1,0:T(4,128)S(1)} %get-tuple-element.43), channel_id=1, source_target_pairs={{0,8},{8,0},{16,24},{24,16},{1,9},{9,1},{17,25},{25,17},{2,10},{10... | collective-permute-start | bytes 4616 | tf_op jit(solution)/shard_map/ppermute | solution.py:296
  41.2 16.0 %collective-permute-start.12 = (bf16[128,4096]{1,0:T(8,128)(2,1)S(1)}, bf16[128,4096]{1,0:T(8,128)(2,1)S(1)}, u32[]{:S(2)}, u32[]{:S(2)}) collective-permute-start(bf16[128,4096]{1,0:T(8,128)(2,1)S(1)} %get-tuple-element.54), channel_id=1, source_target_pairs={{1,3},{3,5},{5,7},{7,2},{9,11},{11,13},{13,15},{15,10},{17,19},{19... | collective-permute-start | bytes 3145736 | tf_op jit(solution)/shard_map/ppermute | solution.py:346
  42.5 4.8 %collective-permute-start.10 = (bf16[128,256]{1,0:T(8,128)(2,1)S(1)}, bf16[128,256]{1,0:T(8,128)(2,1)S(1)}, u32[]{:S(2)}, u32[]{:S(2)}) collective-permute-start(bf16[128,256]{1,0:T(8,128)(2,1)S(1)} %get-tuple-element.51), channel_id=1, source_target_pairs={{0,1},{1,0},{2,3},{3,2},{4,5},{5,4},{6,7},{7,6},{8,9},{9,8},{10,11... | collective-permute-start | bytes 196616 | tf_op jit(solution)/shard_map/ppermute | solution.py:293
  43.8 4.5 %collective-permute-start.15 = (f32[3,128]{1,0:T(4,128)S(1)}, f32[3,128]{1,0:T(4,128)S(1)}, u32[]{:S(2)}, u32[]{:S(2)}) collective-permute-start(f32[3,128]{1,0:T(4,128)S(1)} %get-tuple-element.58.refs_0_), channel_id=1, source_target_pairs={{0,24},{8,16},{16,8},{24,0},{1,25},{9,17},{17,9},{25,1},{2,26},{10... | collective-permute-start | bytes 4616 | tf_op jit(solution)/shard_map/ppermute | solution.py:296
  46.5 3.6 %collective-permute-start.14 = (f32[3,128]{1,0:T(4,128)S(1)}, f32[3,128]{1,0:T(4,128)S(1)}, u32[]{:S(2)}, u32[]{:S(2)}) collective-permute-start(f32[3,128]{1,0:T(4,128)S(1)} %get-tuple-element.58.refs_0_), channel_id=1, source_target_pairs={{0,16},{8,24},{16,0},{24,8},{1,17},{9,25},{17,1},{25,9},{2,18},{10... | collective-permute-start | bytes 4616 | tf_op jit(solution)/shard_map/ppermute | solution.py:296
  46.7 3.6 %collective-permute-start.13 = (f32[3,128]{1,0:T(4,128)S(1)}, f32[3,128]{1,0:T(4,128)S(1)}, u32[]{:S(2)}, u32[]{:S(2)}) collective-permute-start(f32[3,128]{1,0:T(4,128)S(1)} %get-tuple-element.58.refs_0_), channel_id=1, source_target_pairs={{0,8},{8,0},{16,24},{24,16},{1,9},{9,1},{17,25},{25,17},{2,10},{10... | collective-permute-start | bytes 4616 | tf_op jit(solution)/shard_map/ppermute | solution.py:296
  52.4 25.9 %collective-permute-start.16 = (bf16[256,1024]{1,0:T(8,128)(2,1)S(1)}, bf16[256,1024]{1,0:T(8,128)(2,1)S(1)}, u32[]{:S(2)}, u32[]{:S(2)}) collective-permute-start(bf16[256,1024]{1,0:T(8,128)(2,1)S(1)} %get-tuple-element.60), channel_id=1, source_target_pairs={{0,24},{8,16},{16,8},{24,0},{1,25},{9,17},{17,9},{25,1},{2,26},{10... | collective-permute-start | bytes 1572872 | tf_op jit(solution)/shard_map/ppermute | solution.py:296
  53.9 24.5 %collective-permute-start.17 = (bf16[256,1024]{1,0:T(8,128)(2,1)S(1)}, bf16[256,1024]{1,0:T(8,128)(2,1)S(1)}, u32[]{:S(2)}, u32[]{:S(2)}) collective-permute-start(bf16[256,1024]{1,0:T(8,128)(2,1)S(1)} %get-tuple-element.61), channel_id=1, source_target_pairs={{0,16},{8,24},{16,0},{24,8},{1,17},{9,25},{17,1},{25,9},{2,18},{10... | collective-permute-start | bytes 1572872 | tf_op jit(solution)/shard_map/ppermute | solution.py:296
  54.4 23.9 %collective-permute-start.18 = (bf16[256,1024]{1,0:T(8,128)(2,1)S(1)}, bf16[256,1024]{1,0:T(8,128)(2,1)S(1)}, u32[]{:S(2)}, u32[]{:S(2)}) collective-permute-start(bf16[256,1024]{1,0:T(8,128)(2,1)S(1)} %get-tuple-element.62), channel_id=1, source_target_pairs={{0,8},{8,0},{16,24},{24,16},{1,9},{9,1},{17,25},{25,17},{2,10},{10... | collective-permute-start | bytes 1572872 | tf_op jit(solution)/shard_map/ppermute | solution.py:296
  55.9 20.6 %collective-permute-start.11 = (bf16[128,4096]{1,0:T(8,128)(2,1)S(1)}, bf16[128,4096]{1,0:T(8,128)(2,1)S(1)}, u32[]{:S(2)}, u32[]{:S(2)}) collective-permute-start(bf16[128,4096]{1,0:T(8,128)(2,1)S(1)} %get-tuple-element.52), channel_id=1, source_target_pairs={{0,3},{2,5},{4,7},{6,1},{8,11},{10,13},{12,15},{14,9},{16,19},{18,... | collective-permute-start | bytes 3145736 | tf_op jit(solution)/shard_map/ppermute | solution.py:290
  57.5 27.6 %collective-permute-start.19 = (bf16[128,4096]{1,0:T(8,128)(2,1)S(1)}, bf16[128,4096]{1,0:T(8,128)(2,1)S(1)}, u32[]{:S(2)}, u32[]{:S(2)}) collective-permute-start(bf16[128,4096]{1,0:T(8,128)(2,1)S(1)} %get-tuple-element.66), channel_id=1, source_target_pairs={{1,2},{3,4},{5,6},{7,0},{9,10},{11,12},{13,14},{15,8},{17,18},{19,... | collective-permute-start | bytes 3145736 | tf_op jit(solution)/shard_map/ppermute | solution.py:290

commit v14 on v10

--- a/solution.py
+++ b/solution.py
@@ -87,7 +87,7 @@
 
 
 def hard_scores_body(groups, *refs):
-    pieces, outs = refs[:groups][::-1], refs[groups + 1 :]
+    pieces, outs = [*refs[2 : groups + 1][::-1], refs[0]], refs[groups + 1 :]
     rows = outs[0].shape[1]
     ids = lax.broadcasted_iota(jnp.int32, (rows, rows), 0)
     for r in range(groups):
@@ -325,7 +325,7 @@
 
     s0, s1, s3 = local_call(scores_body, [square] * 3, queries, passages, next1, next3_even)
     parts = local_call(
-        functools.partial(hard_scores_body, groups), [triple] * groups, *pieces[::-1], s0, flops=LONG
+        functools.partial(hard_scores_body, groups), [triple] * groups, pieces[-1], s0, *pieces[-2::-1], flops=LONG
     )
     (s2,) = local_call(last_score_body, [square], queries, pair)
     parts = exchange(parts)

time: 83 us -> 83.3 us (level)
  waiting for transfers between devices: 41.1 us -> 40 us
  starting transfers between devices: 27.6 us -> 28.7 us
    ppermute x6, waiting for transfers between devices: 27.3 us -> 25.8 us  [shift(): return lax.ppermute(array, 'blk', pairs)]
    ppermute x12, starting transfers between devices: 14.1 us -> 15.4 us  [over_groups(): return lax.ppermute(array, 'grp', [(i, i ^ r) for i in range(groups)])]
where the time goes in v14:
time: 83.3 us; the launch traced here: 82.7 us
  waiting for transfers between devices  40 us (48%)
  starting transfers between devices  28.7 us (34%)
  Pallas kernels  12.5 us (15%)
    ppermute x6, waiting for transfers between devices, shift(): return lax.ppermute(array, 'blk', pairs)  25.8 us
    ppermute x12, starting transfers between devices, over_groups(): return lax.ppermute(array, 'grp', [(i, i ^ r) for i in range(groups)])  15.4 us
    ppermute x12, waiting for transfers between devices, over_groups(): return lax.ppermute(array, 'grp', [(i, i ^ r) for i in range(groups)])  14.1 us
    pallas_call x15, Pallas kernels, local_call(): pl.pallas_call(body, out_shape=out_shape, in_specs=in_specs or [VMEM] * l...  12.5 us
    ppermute x6, starting transfers between devices, shift(): return lax.ppermute(array, 'blk', pairs)  10.9 us
    ppermute x2, starting transfers between devices, swap(): return lax.ppermute(array, 'blk', [(i, i ^ 1) for i in range(loop)])  2.43 us
  transfers between devices with their start and end apart: 20, of which 12 were waited for; matrix products, arithmetic and copies ran while one was open for 0% of the time, Pallas kernels for 13%

profile of v14, /device:TPU:0, one launch (start us, length us, event | category | flops | bytes accessed | tf_op | source)
XLA Modules:
  0.0 82.7 jit_solution(2693693076161464877)
XLA Ops:
  0.6 4.5 %collective-permute-start.1 = (bf16[128,4096]{1,0:T(8,128)(2,1)}, bf16[128,4096]{1,0:T(8,128)(2,1)S(1)}, u32[]{:S(2)}, u32[]{:S(2)}) collective-permute-start(bf16[128,4096]{1,0:T(8,128)(2,1)} %p_ref.1), channel_id=1, source_target_pairs={{0,7},{1,0},{2,1},{3,2},{4,3},{5,4},{6,5},{7,6},{8,15},{9,8},{10,9... | collective-permute-start | bytes 3145736 | tf_op jit(solution)/shard_map/ppermute | solution.py:287
  5.2 0.7 copy-done.2
  5.9 1.6 %shard_map.67 = (bf16[272,1024]{1,0:T(8,128)(2,1)S(1)}, bf16[272,1024]{1,0:T(8,128)(2,1)S(1)}, bf16[272,1024]{1,0:T(8,128)(2,1)S(1)}, bf16[272,1024]{1,0:T(8,128)(2,1)S(1)}, f32[8,128]{1,0:T(8,128)S(1)}) custom-call(bf16[128,4096]{1,0:T(8,128)(2,1)} %q_ref.9, bf16[128,4096]{1,0:T(8,128)(2,1)} %p_ref.1, s32[3,128]{1,0:T(4,128)S(1)} %bitcast.3), custom_call_target="tpu_custom_call" | custom-call | bytes 4331008 | tf_op jit(solution)/shard_map/pallas_call | solution.py:31
  7.5 2.5 %collective-permute-start = (bf16[272,1024]{1,0:T(8,128)(2,1)S(1)}, bf16[272,1024]{1,0:T(8,128)(2,1)S(1)}, u32[]{:S(2)}, u32[]{:S(2)}) collective-permute-start(bf16[272,1024]{1,0:T(8,128)(2,1)S(1)} %get-tuple-element.35), channel_id=1, source_target_pairs={{0,24},{8,16},{16,8},{24,0},{1,25},{9,17},{17,9},{25,1},{2,26},{10... | collective-permute-start | bytes 1671176 | tf_op jit(solution)/shard_map/ppermute | solution.py:293
  10.0 1.3 %collective-permute-start.2 = (bf16[128,4096]{1,0:T(8,128)(2,1)S(1)}, bf16[128,4096]{1,0:T(8,128)(2,1)S(1)}, u32[]{:S(2)}, u32[]{:S(2)}) collective-permute-start(bf16[128,4096]{1,0:T(8,128)(2,1)S(1)} %shard_map.69), channel_id=1, source_target_pairs={{1,6},{3,0},{5,2},{7,4},{9,14},{11,8},{13,10},{15,12},{17,22},{19,... | collective-permute-start | bytes 3145736 | tf_op jit(solution)/shard_map/ppermute | solution.py:287
  11.3 0.6 collective-permute-start.3
  12.5 9.9 %collective-permute-done.1.source = bf16[128,4096]{1,0:T(8,128)(2,1)S(1)} collective-permute-done((bf16[128,4096]{1,0:T(8,128)(2,1)}, bf16[128,4096]{1,0:T(8,128)(2,1)S(1)}, u32[]{:S(2)}, u32[]{:S(2)}) %collective-permute-start.1) | collective-permute-done | bytes 1048608 | tf_op jit(solution)/shard_map/ppermute | solution.py:287
  22.4 0.7 collective-permute-start.9
  23.2 4.8 %collective-permute-done.2.refs_2_.e3_ref = bf16[128,4096]{1,0:T(8,128)(2,1)S(1)} collective-permute-done((bf16[128,4096]{1,0:T(8,128)(2,1)S(1)}, bf16[128,4096]{1,0:T(8,128)(2,1)S(1)}, u32[]{:S(2)}, u32[]{:S(2)}) %collective-permute-start.2) | collective-permute-done | bytes 1048608 | tf_op jit(solution)/shard_map/ppermute | solution.py:287
  28.1 1.2 %collective-permute-start.8 = (bf16[128,8192]{1,0:T(8,128)(2,1)S(1)}, bf16[128,8192]{1,0:T(8,128)(2,1)S(1)}, u32[]{:S(2)}, u32[]{:S(2)}) collective-permute-start(bf16[128,8192]{1,0:T(8,128)(2,1)S(1)} %shard_map.72), channel_id=1, source_target_pairs={{0,1},{1,0},{2,3},{3,2},{4,5},{5,4},{6,7},{7,6},{8,9},{9,8},{10,11... | collective-permute-start | bytes 6291464 | tf_op jit(solution)/shard_map/ppermute | solution.py:290
  29.3 1.0 %shard_map.70 = (f32[128,128]{1,0:T(8,128)S(1)}, f32[128,128]{1,0:T(8,128)S(1)}, f32[128,128]{1,0:T(8,128)S(1)}) custom-call(bf16[128,4096]{1,0:T(8,128)(2,1)S(1)} %copy-done, bf16[128,4096]{1,0:T(8,128)(2,1)S(1)} %copy-done.1, bf16[128,4096]{1,0:T(8,128)(2,1)S(1)} %shard_map.68.refs_1_.n1_ref, bf16[128,4096]{1,0:T(8,128)(2,1)S(1)} %collective-permute-done.2.refs_2_.e3_ref), custom_call_target="tpu_custom_call" | custom-call | bytes 4390912 | tf_op jit(solution)/shard_map/pallas_call | solution.py:31
  30.3 1.9 %collective-permute-done.3.refs_2_.refs_5_ = bf16[272,1024]{1,0:T(8,128)(2,1)S(1)} collective-permute-done((bf16[272,1024]{1,0:T(8,128)(2,1)S(1)}, bf16[272,1024]{1,0:T(8,128)(2,1)S(1)}, u32[]{:S(2)}, u32[]{:S(2)}) %collective-permute-start.3) | collective-permute-done | bytes 557088 | tf_op jit(solution)/shard_map/ppermute | solution.py:293
  32.5 1.2 %shard_map.71 = (f32[3,128]{1,0:T(4,128)S(1)}, f32[3,128]{1,0:T(4,128)S(1)}, f32[3,128]{1,0:T(4,128)S(1)}, f32[3,128]{1,0:T(4,128)S(1)}) custom-call(bf16[272,1024]{1,0:T(8,128)(2,1)S(1)} %collective-permute-done.refs_0_.refs_4_, f32[128,128]{1,0:T(8,128)S(1)} %get-tuple-element.37.refs_1_.refs_5_.refs_4_, ...), custom_call_target="tpu_custom_call" | custom-call | flops 49999998976 | bytes 2299904 | tf_op jit(solution)/shard_map/pallas_call | solution.py:31
  33.6 2.4 %collective-permute-start.5 = (f32[3,128]{1,0:T(4,128)S(1)}, f32[3,128]{1,0:T(4,128)S(1)}, u32[]{:S(2)}, u32[]{:S(2)}) collective-permute-start(f32[3,128]{1,0:T(4,128)S(1)} %get-tuple-element.41), channel_id=1, source_target_pairs={{0,24},{8,16},{16,8},{24,0},{1,25},{9,17},{17,9},{25,1},{2,26},{10... | collective-permute-start | bytes 4616 | tf_op jit(solution)/shard_map/ppermute | solution.py:293
  36.0 0.6 collective-permute-start.6
  38.2 1.4 %collective-permute-done.6.refs_1_ = f32[3,128]{1,0:T(4,128)S(1)} collective-permute-done((f32[3,128]{1,0:T(4,128)S(1)}, f32[3,128]{1,0:T(4,128)S(1)}, u32[]{:S(2)}, u32[]{:S(2)}) %collective-permute-start.6) | collective-permute-done | bytes 1568 | tf_op jit(solution)/shard_map/ppermute | solution.py:293
  39.6 0.6 collective-permute-done.7.refs_2_
  40.2 0.9 %shard_map.74 = (f32[1,128]{1,0:T(1,128)S(1)}, f32[128,128]{1,0:T(8,128)S(1)}, bf16[128,4096]{1,0:T(8,128)(2,1)S(1)}) custom-call(f32[3,128]{1,0:T(4,128)S(1)} %collective-permute-done.5.refs_0_, f32[3,128]{1,0:T(4,128)S(1)} %collective-permute-done.6.refs_1_, f32[3,128]{1,0:T(4,128)S(1)} %collective-permute-done.7.refs_2_, ...), custom_call_target="tpu_custom_call" | custom-call | bytes 3480576 | tf_op jit(solution)/shard_map/pallas_call | solution.py:31
  41.2 0.7 collective-permute-start.12
  42.5 1.2 %collective-permute-start.10 = (bf16[128,256]{1,0:T(8,128)(2,1)S(1)}, bf16[128,256]{1,0:T(8,128)(2,1)S(1)}, u32[]{:S(2)}, u32[]{:S(2)}) collective-permute-start(bf16[128,256]{1,0:T(8,128)(2,1)S(1)} %get-tuple-element.51), channel_id=1, source_target_pairs={{0,1},{1,0},{2,3},{3,2},{4,5},{5,4},{6,7},{7,6},{8,9},{9,8},{10,11... | collective-permute-start | bytes 196616 | tf_op jit(solution)/shard_map/ppermute | solution.py:290
  43.7 4.2 %collective-permute-start.13 = (f32[3,128]{1,0:T(4,128)S(1)}, f32[3,128]{1,0:T(4,128)S(1)}, u32[]{:S(2)}, u32[]{:S(2)}) collective-permute-start(f32[3,128]{1,0:T(4,128)S(1)} %get-tuple-element.58.refs_3_), channel_id=1, source_target_pairs={{0,24},{8,16},{16,8},{24,0},{1,25},{9,17},{17,9},{25,1},{2,26},{10... | collective-permute-start | bytes 4616 | tf_op jit(solution)/shard_map/ppermute | solution.py:293
  48.9 2.3 %collective-permute-start.11 = (bf16[128,4096]{1,0:T(8,128)(2,1)S(1)}, bf16[128,4096]{1,0:T(8,128)(2,1)S(1)}, u32[]{:S(2)}, u32[]{:S(2)}) collective-permute-start(bf16[128,4096]{1,0:T(8,128)(2,1)S(1)} %get-tuple-element.52), channel_id=1, source_target_pairs={{0,3},{2,5},{4,7},{6,1},{8,11},{10,13},{12,15},{14,9},{16,19},{18,... | collective-permute-start | bytes 3145736 | tf_op jit(solution)/shard_map/ppermute | solution.py:287
  51.5 2.1 %shard_map.79 = (bf16[256,1024]{1,0:T(8,128)(2,1)S(1)}, bf16[256,1024]{1,0:T(8,128)(2,1)S(1)}, bf16[256,1024]{1,0:T(8,128)(2,1)S(1)}, bf16[256,1024]{1,0:T(8,128)(2,1)S(1)}, f32[8,128]{1,0:T(8,128)}) custom-call(f32[3,128]{1,0:T(4,128)S(1)} %collective-permute-done.13.refs_0_, f32[3,128]{1,0:T(4,128)S(1)} %collective-permute-done.14.refs_1_, ...), custom_call_target="tpu_custom_call" | custom-call | bytes 4339712 | tf_op jit(solution)/shard_map/pallas_call | solution.py:31
  53.6 2.4 %collective-permute-start.16 = (bf16[256,1024]{1,0:T(8,128)(2,1)S(1)}, bf16[256,1024]{1,0:T(8,128)(2,1)S(1)}, u32[]{:S(2)}, u32[]{:S(2)}) collective-permute-start(bf16[256,1024]{1,0:T(8,128)(2,1)S(1)} %get-tuple-element.60), channel_id=1, source_target_pairs={{0,24},{8,16},{16,8},{24,0},{1,25},{9,17},{17,9},{25,1},{2,26},{10... | collective-permute-start | bytes 1572872 | tf_op jit(solution)/shard_map/ppermute | solution.py:293
  56.3 0.8 collective-permute-start.18
  57.2 1.3 %collective-permute-start.19 = (bf16[128,4096]{1,0:T(8,128)(2,1)S(1)}, bf16[128,4096]{1,0:T(8,128)(2,1)S(1)}, u32[]{:S(2)}, u32[]{:S(2)}) collective-permute-start(bf16[128,4096]{1,0:T(8,128)(2,1)S(1)} %get-tuple-element.66), channel_id=1, source_target_pairs={{1,2},{3,4},{5,6},{7,0},{9,10},{11,12},{13,14},{15,8},{17,18},{19,... | collective-permute-start | bytes 3145736 | tf_op jit(solution)/shard_map/ppermute | solution.py:287
  58.5 9.1 %collective-permute-done.11.own3_ref = bf16[128,4096]{1,0:T(8,128)(2,1)S(1)} collective-permute-done((bf16[128,4096]{1,0:T(8,128)(2,1)S(1)}, bf16[128,4096]{1,0:T(8,128)(2,1)S(1)}, u32[]{:S(2)}, u32[]{:S(2)}) %collective-permute-start.11) | collective-permute-done | bytes 1048608 | tf_op jit(solution)/shard_map/ppermute | solution.py:287
  67.7 1.7 %shard_map.78 = (f32[128,4096]{1,0:T(8,128)S(1)}, f32[128,4096]{1,0:T(8,128)S(1)}) custom-call(bf16[128,4096]{1,0:T(8,128)(2,1)S(1)} %copy-done, bf16[128,8192]{1,0:T(8,128)(2,1)S(1)} %collective-permute-done.8.pair_ref, bf16[128,4096]{1,0:T(8,128)(2,1)S(1)} %copy-done.1, bf16[128,4096]{1,0:T(8,128)(2,1)S(1)} %shard_map.68.refs_1_.n1_ref, ...), custom_call_target="tpu_custom_call" | custom-call | flops 49999998976 | bytes 12784128 | tf_op jit(solution)/shard_map/pallas_call | solution.py:31
  69.4 8.7 %collective-permute-done.17.refs_1_ = bf16[256,1024]{1,0:T(8,128)(2,1)S(1)} collective-permute-done((bf16[256,1024]{1,0:T(8,128)(2,1)S(1)}, bf16[256,1024]{1,0:T(8,128)(2,1)S(1)}, u32[]{:S(2)}, u32[]{:S(2)}) %collective-permute-start.17) | collective-permute-done | bytes 524320 | tf_op jit(solution)/shard_map/ppermute | solution.py:293
  78.4 1.2 %shard_map.80 = (bf16[128,4096]{1,0:T(8,128)(2,1)}, f32[128,4096]{1,0:T(8,128)S(1)}) custom-call(f32[128,4096]{1,0:T(8,128)S(1)} %get-tuple-element.56.pulled, f32[128,4096]{1,0:T(8,128)S(1)} %get-tuple-element.57.base, bf16[256,1024]{1,0:T(8,128)(2,1)S(1)} %collective-permute-done.16.refs_0_, bf16[256,1024]{1,0:T(8,128)(2,1)S(1)} %collective-permute-done.17.refs_1_, ...), custom_call_target="tpu_custom_call" | custom-call | bytes 9437184 | tf_op jit(solution)/shard_map/pallas_call | solution.py:31
  79.6 2.0 %collective-permute-done.19.own1 = bf16[128,4096]{1,0:T(8,128)(2,1)S(1)} collective-permute-done((bf16[128,4096]{1,0:T(8,128)(2,1)S(1)}, bf16[128,4096]{1,0:T(8,128)(2,1)S(1)}, u32[]{:S(2)}, u32[]{:S(2)}) %collective-permute-start.19) | collective-permute-done | bytes 1048608 | tf_op jit(solution)/shard_map/ppermute | solution.py:287
  81.7 1.1 %shard_map.81 = bf16[128,4096]{1,0:T(8,128)(2,1)} custom-call(f32[128,4096]{1,0:T(8,128)S(1)} %get-tuple-element.65.almost, bf16[128,4096]{1,0:T(8,128)(2,1)S(1)} %collective-permute-done.19.own1), custom_call_target="tpu_custom_call" | custom-call | bytes 4194304 | tf_op jit(solution)/shard_map/pallas_call | solution.py:31
  (31 shorter events, 5.3 us)
Async XLA Ops:
  0.6 9.3 %copy-start.1 = (bf16[128,4096]{1,0:T(8,128)(2,1)S(1)}, bf16[128,4096]{1,0:T(8,128)(2,1)}, u32[]{:S(2)}) copy-start(bf16[128,4096]{1,0:T(8,128)(2,1)} %p_ref.1) | copy-start | bytes 3145732
  0.6 21.7 %collective-permute-start.1 = (bf16[128,4096]{1,0:T(8,128)(2,1)}, bf16[128,4096]{1,0:T(8,128)(2,1)S(1)}, u32[]{:S(2)}, u32[]{:S(2)}) collective-permute-start(bf16[128,4096]{1,0:T(8,128)(2,1)} %p_ref.1), channel_id=1, source_target_pairs={{0,7},{1,0},{2,1},{3,2},{4,3},{5,4},{6,5},{7,6},{8,15},{9,8},{10,9... | collective-permute-start | bytes 3145736 | tf_op jit(solution)/shard_map/ppermute | solution.py:287
  5.2 0.7 copy-start.2
  7.5 22.8 %collective-permute-start = (bf16[272,1024]{1,0:T(8,128)(2,1)S(1)}, bf16[272,1024]{1,0:T(8,128)(2,1)S(1)}, u32[]{:S(2)}, u32[]{:S(2)}) collective-permute-start(bf16[272,1024]{1,0:T(8,128)(2,1)S(1)} %get-tuple-element.35), channel_id=1, source_target_pairs={{0,24},{8,16},{16,8},{24,0},{1,25},{9,17},{17,9},{25,1},{2,26},{10... | collective-permute-start | bytes 1671176 | tf_op jit(solution)/shard_map/ppermute | solution.py:293
  10.0 17.9 %collective-permute-start.2 = (bf16[128,4096]{1,0:T(8,128)(2,1)S(1)}, bf16[128,4096]{1,0:T(8,128)(2,1)S(1)}, u32[]{:S(2)}, u32[]{:S(2)}) collective-permute-start(bf16[128,4096]{1,0:T(8,128)(2,1)S(1)} %shard_map.69), channel_id=1, source_target_pairs={{1,6},{3,0},{5,2},{7,4},{9,14},{11,8},{13,10},{15,12},{17,22},{19,... | collective-permute-start | bytes 3145736 | tf_op jit(solution)/shard_map/ppermute | solution.py:287
  11.3 20.8 %collective-permute-start.3 = (bf16[272,1024]{1,0:T(8,128)(2,1)S(1)}, bf16[272,1024]{1,0:T(8,128)(2,1)S(1)}, u32[]{:S(2)}, u32[]{:S(2)}) collective-permute-start(bf16[272,1024]{1,0:T(8,128)(2,1)S(1)} %get-tuple-element.38), channel_id=1, source_target_pairs={{0,16},{8,24},{16,0},{24,8},{1,17},{9,25},{17,1},{25,9},{2,18},{10... | collective-permute-start | bytes 1671176 | tf_op jit(solution)/shard_map/ppermute | solution.py:293
  11.9 16.0 %copy-start = (bf16[128,4096]{1,0:T(8,128)(2,1)S(1)}, bf16[128,4096]{1,0:T(8,128)(2,1)}, u32[]{:S(2)}) copy-start(bf16[128,4096]{1,0:T(8,128)(2,1)} %q_ref.9) | copy-start | bytes 3145732
  11.9 20.5 %collective-permute-start.4 = (bf16[272,1024]{1,0:T(8,128)(2,1)S(1)}, bf16[272,1024]{1,0:T(8,128)(2,1)S(1)}, u32[]{:S(2)}, u32[]{:S(2)}) collective-permute-start(bf16[272,1024]{1,0:T(8,128)(2,1)S(1)} %get-tuple-element.39), channel_id=1, source_target_pairs={{0,8},{8,0},{16,24},{24,16},{1,9},{9,1},{17,25},{25,17},{2,10},{10... | collective-permute-start | bytes 1671176 | tf_op jit(solution)/shard_map/ppermute | solution.py:293
  22.4 17.8 %collective-permute-start.9 = (bf16[128,4096]{1,0:T(8,128)(2,1)S(1)}, bf16[128,4096]{1,0:T(8,128)(2,1)S(1)}, u32[]{:S(2)}, u32[]{:S(2)}) collective-permute-start(bf16[128,4096]{1,0:T(8,128)(2,1)S(1)} %shard_map.68.refs_1_.n1_ref), channel_id=1, source_target_pairs={{1,7},{3,1},{5,3},{7,5},{9,15},{11,9},{13,11},{15,13},{17,23},{19,... | collective-permute-start | bytes 3145736 | tf_op jit(solution)/shard_map/ppermute | solution.py:287
  28.1 9.1 %collective-permute-start.8 = (bf16[128,8192]{1,0:T(8,128)(2,1)S(1)}, bf16[128,8192]{1,0:T(8,128)(2,1)S(1)}, u32[]{:S(2)}, u32[]{:S(2)}) collective-permute-start(bf16[128,8192]{1,0:T(8,128)(2,1)S(1)} %shard_map.72), channel_id=1, source_target_pairs={{0,1},{1,0},{2,3},{3,2},{4,5},{5,4},{6,7},{7,6},{8,9},{9,8},{10,11... | collective-permute-start | bytes 6291464 | tf_op jit(solution)/shard_map/ppermute | solution.py:290
  33.6 6.6 %copy-start.3 = (f32[128]{0:T(128)S(1)}, f32[128]{0:T(128)}, u32[]{:S(2)}) copy-start(f32[128]{0:T(128)} %param.7) | copy-start | bytes 1540
  33.6 4.5 %collective-permute-start.5 = (f32[3,128]{1,0:T(4,128)S(1)}, f32[3,128]{1,0:T(4,128)S(1)}, u32[]{:S(2)}, u32[]{:S(2)}) collective-permute-start(f32[3,128]{1,0:T(4,128)S(1)} %get-tuple-element.41), channel_id=1, source_target_pairs={{0,24},{8,16},{16,8},{24,0},{1,25},{9,17},{17,9},{25,1},{2,26},{10... | collective-permute-start | bytes 4616 | tf_op jit(solution)/shard_map/ppermute | solution.py:293
  36.0 3.6 %collective-permute-start.6 = (f32[3,128]{1,0:T(4,128)S(1)}, f32[3,128]{1,0:T(4,128)S(1)}, u32[]{:S(2)}, u32[]{:S(2)}) collective-permute-start(f32[3,128]{1,0:T(4,128)S(1)} %get-tuple-element.42), channel_id=1, source_target_pairs={{0,16},{8,24},{16,0},{24,8},{1,17},{9,25},{17,1},{25,9},{2,18},{10... | collective-permute-start | bytes 4616 | tf_op jit(solution)/shard_map/ppermute | solution.py:293
  36.7 3.6 %collective-permute-start.7 = (f32[3,128]{1,0:T(4,128)S(1)}, f32[3,128]{1,0:T(4,128)S(1)}, u32[]{:S(2)}, u32[]{:S(2)}) collective-permute-start(f32[3,128]{1,0:T(4,128)S(1)} %get-tuple-element.43), channel_id=1, source_target_pairs={{0,8},{8,0},{16,24},{24,16},{1,9},{9,1},{17,25},{25,17},{2,10},{10... | collective-permute-start | bytes 4616 | tf_op jit(solution)/shard_map/ppermute | solution.py:293
  41.2 15.9 %collective-permute-start.12 = (bf16[128,4096]{1,0:T(8,128)(2,1)S(1)}, bf16[128,4096]{1,0:T(8,128)(2,1)S(1)}, u32[]{:S(2)}, u32[]{:S(2)}) collective-permute-start(bf16[128,4096]{1,0:T(8,128)(2,1)S(1)} %get-tuple-element.54), channel_id=1, source_target_pairs={{1,3},{3,5},{5,7},{7,1},{9,11},{11,13},{13,15},{15,9},{17,19},{19,... | collective-permute-start | bytes 3145736 | tf_op jit(solution)/shard_map/ppermute | solution.py:287
  42.5 6.0 %collective-permute-start.10 = (bf16[128,256]{1,0:T(8,128)(2,1)S(1)}, bf16[128,256]{1,0:T(8,128)(2,1)S(1)}, u32[]{:S(2)}, u32[]{:S(2)}) collective-permute-start(bf16[128,256]{1,0:T(8,128)(2,1)S(1)} %get-tuple-element.51), channel_id=1, source_target_pairs={{0,1},{1,0},{2,3},{3,2},{4,5},{5,4},{6,7},{7,6},{8,9},{9,8},{10,11... | collective-permute-start | bytes 196616 | tf_op jit(solution)/shard_map/ppermute | solution.py:290
  43.7 7.5 %collective-permute-start.13 = (f32[3,128]{1,0:T(4,128)S(1)}, f32[3,128]{1,0:T(4,128)S(1)}, u32[]{:S(2)}, u32[]{:S(2)}) collective-permute-start(f32[3,128]{1,0:T(4,128)S(1)} %get-tuple-element.58.refs_3_), channel_id=1, source_target_pairs={{0,24},{8,16},{16,8},{24,0},{1,25},{9,17},{17,9},{25,1},{2,26},{10... | collective-permute-start | bytes 4616 | tf_op jit(solution)/shard_map/ppermute | solution.py:293
  47.9 3.6 %collective-permute-start.14 = (f32[3,128]{1,0:T(4,128)S(1)}, f32[3,128]{1,0:T(4,128)S(1)}, u32[]{:S(2)}, u32[]{:S(2)}) collective-permute-start(f32[3,128]{1,0:T(4,128)S(1)} %get-tuple-element.58.refs_3_), channel_id=1, source_target_pairs={{0,16},{8,24},{16,0},{24,8},{1,17},{9,25},{17,1},{25,9},{2,18},{10... | collective-permute-start | bytes 4616 | tf_op jit(solution)/shard_map/ppermute | solution.py:293
  47.9 3.6 %collective-permute-start.15 = (f32[3,128]{1,0:T(4,128)S(1)}, f32[3,128]{1,0:T(4,128)S(1)}, u32[]{:S(2)}, u32[]{:S(2)}) collective-permute-start(f32[3,128]{1,0:T(4,128)S(1)} %get-tuple-element.58.refs_3_), channel_id=1, source_target_pairs={{0,8},{8,0},{16,24},{24,16},{1,9},{9,1},{17,25},{25,17},{2,10},{10... | collective-permute-start | bytes 4616 | tf_op jit(solution)/shard_map/ppermute | solution.py:293
  48.9 18.7 %collective-permute-start.11 = (bf16[128,4096]{1,0:T(8,128)(2,1)S(1)}, bf16[128,4096]{1,0:T(8,128)(2,1)S(1)}, u32[]{:S(2)}, u32[]{:S(2)}) collective-permute-start(bf16[128,4096]{1,0:T(8,128)(2,1)S(1)} %get-tuple-element.52), channel_id=1, source_target_pairs={{0,3},{2,5},{4,7},{6,1},{8,11},{10,13},{12,15},{14,9},{16,19},{18,... | collective-permute-start | bytes 3145736 | tf_op jit(solution)/shard_map/ppermute | solution.py:287
  53.6 15.8 %collective-permute-start.16 = (bf16[256,1024]{1,0:T(8,128)(2,1)S(1)}, bf16[256,1024]{1,0:T(8,128)(2,1)S(1)}, u32[]{:S(2)}, u32[]{:S(2)}) collective-permute-start(bf16[256,1024]{1,0:T(8,128)(2,1)S(1)} %get-tuple-element.60), channel_id=1, source_target_pairs={{0,24},{8,16},{16,8},{24,0},{1,25},{9,17},{17,9},{25,1},{2,26},{10... | collective-permute-start | bytes 1572872 | tf_op jit(solution)/shard_map/ppermute | solution.py:293
  56.0 22.1 %collective-permute-start.17 = (bf16[256,1024]{1,0:T(8,128)(2,1)S(1)}, bf16[256,1024]{1,0:T(8,128)(2,1)S(1)}, u32[]{:S(2)}, u32[]{:S(2)}) collective-permute-start(bf16[256,1024]{1,0:T(8,128)(2,1)S(1)} %get-tuple-element.61), channel_id=1, source_target_pairs={{0,16},{8,24},{16,0},{24,8},{1,17},{9,25},{17,1},{25,9},{2,18},{10... | collective-permute-start | bytes 1572872 | tf_op jit(solution)/shard_map/ppermute | solution.py:293
  56.3 22.1 %collective-permute-start.18 = (bf16[256,1024]{1,0:T(8,128)(2,1)S(1)}, bf16[256,1024]{1,0:T(8,128)(2,1)S(1)}, u32[]{:S(2)}, u32[]{:S(2)}) collective-permute-start(bf16[256,1024]{1,0:T(8,128)(2,1)S(1)} %get-tuple-element.62), channel_id=1, source_target_pairs={{0,8},{8,0},{16,24},{24,16},{1,9},{9,1},{17,25},{25,17},{2,10},{10... | collective-permute-start | bytes 1572872 | tf_op jit(solution)/shard_map/ppermute | solution.py:293
  57.2 24.4 %collective-permute-start.19 = (bf16[128,4096]{1,0:T(8,128)(2,1)S(1)}, bf16[128,4096]{1,0:T(8,128)(2,1)S(1)}, u32[]{:S(2)}, u32[]{:S(2)}) collective-permute-start(bf16[128,4096]{1,0:T(8,128)(2,1)S(1)} %get-tuple-element.66), channel_id=1, source_target_pairs={{1,2},{3,4},{5,6},{7,0},{9,10},{11,12},{13,14},{15,8},{17,18},{19,... | collective-permute-start | bytes 3145736 | tf_op jit(solution)/shard_map/ppermute | solution.py:287
